TPU v7x, 32 devices: a whole 2x2x4 slice. The times are simulated.
32 devices in a mesh: rows: 8 (over z, y), strip: 4 (over x, core).
Axes of the slice: x: 2, y: 2, z: 4, core: 2. Of those that a mesh axis runs over, the one named last changes fastest.
Arguments:
- frames: bfloat16 [2048, 3, 64, 64], P('rows', None, 'strip'), may hold values from -4 to 4
- segment_ids: int32 [32, 64], P('rows'), may hold values from 0 to 3, never falling along the last dimension, each value on 1 to 32 neighbouring positions
- encode_one: bfloat16 [32, 3, 4, 4], replicated, may hold values from -1.25 to 1.25
- encode_two: bfloat16 [64, 32, 4, 4], replicated, may hold values from -0.375 to 0.375
- encode_three: bfloat16 [128, 64, 4, 4], replicated, may hold values from -0.25 to 0.25
- encode_four: bfloat16 [256, 128, 4, 4], replicated, may hold values from -0.1875 to 0.1875
- latent_head: bfloat16 [4096, 1024], P(None, 'strip'), may hold values from -0.1875 to 0.1875
- token_embed: bfloat16 [1024, 512], P('strip'), may hold values from -6 to 6
- positions: bfloat16 [64, 512], replicated, may hold values from -3 to 3
- norm_gains: float32 [2, 2, 512], replicated, may hold values from 0.5 to 1.5
- qkv_weight: bfloat16 [2, 512, 3, 512], P(None, None, None, 'strip'), may hold values from -0.25 to 0.25
- out_weight: bfloat16 [2, 512, 512], P(None, 'strip'), may hold values from -0.75 to 0.75
- up_weight: bfloat16 [2, 512, 2048], P(None, None, 'strip'), may hold values from -0.375 to 0.375
- down_weight: bfloat16 [2, 2048, 512], P(None, 'strip'), may hold values from -0.125 to 0.125
- decode_head: bfloat16 [1024, 4096], P('strip'), may hold values from -4 to 4
- decode_one: bfloat16 [128, 256, 4, 4], replicated, may hold values from -0.25 to 0.25
- decode_two: bfloat16 [64, 128, 4, 4], replicated, may hold values from -0.375 to 0.375
- decode_three: bfloat16 [32, 64, 4, 4], replicated, may hold values from -0.5 to 0.5
- decode_four: bfloat16 [3, 32, 4, 4], replicated, may hold values from -0.5 to 0.5
- token_cotangent: bfloat16 [2048, 512], P('rows'), may hold values from -6 to 6
- frame_cotangent: bfloat16 [2048, 3, 64, 64], P('rows', None, 'strip'), may hold values from -6 to 6
Outputs:
- tokens_out: bfloat16 [2048, 512], P('rows')
- recon_frames: bfloat16 [2048, 3, 64, 64], P('rows', None, 'strip')
- frames_grad: float32 [2048, 3, 64, 64], P('rows', None, 'strip')
- encode_one_grad: float32 [32, 3, 4, 4], replicated
- encode_two_grad: float32 [64, 32, 4, 4], replicated
- encode_three_grad: float32 [128, 64, 4, 4], replicated
- encode_four_grad: float32 [256, 128, 4, 4], replicated
- latent_head_grad: float32 [4096, 1024], P(None, 'strip')
- token_embed_grad: float32 [1024, 512], P('strip')
- positions_grad: float32 [64, 512], replicated
- norm_gains_grad: float32 [2, 2, 512], replicated
- qkv_weight_grad: float32 [2, 512, 3, 512], P(None, None, None, 'strip')
- out_weight_grad: float32 [2, 512, 512], P(None, 'strip')
- up_weight_grad: float32 [2, 512, 2048], P(None, None, 'strip')
- down_weight_grad: float32 [2, 2048, 512], P(None, 'strip')
- decode_head_grad: float32 [1024, 4096], P('strip')
- decode_one_grad: float32 [128, 256, 4, 4], replicated
- decode_two_grad: float32 [64, 128, 4, 4], replicated
- decode_three_grad: float32 [32, 64, 4, 4], replicated
- decode_four_grad: float32 [3, 32, 4, 4], replicated
Inputs may be any that keep to these rules, and one draw needn't show every extreme that they name: `segment_ids`: along a sequence of 64 steps the episode numbers never fall, and one episode spans at most 32 steps of a sequence.
All inputs are finite; a program needn't handle non-finite values.
Results may differ from a plain program's by a relative error of at most 0.035.
Values may be sent and summed in bfloat16 or wider, within the bound.
A program may use at most 320 MiB of HBM per device.

v0:
```python
import jax
import jax.numpy as jnp
from jax import lax
from jax.sharding import PartitionSpec as P

HEAD_DIM = 64
LCLASS = 32


EPS = 1e-05
SCALE = 0.125
NEG = -1e30
LAYOUT = ("NCHW", "OIHW", "NCHW")


def with_halo(block, sides, width):
    for axis, dim in sides:
        count = lax.axis_size(axis)
        forward = [(i, i + 1) for i in range(count - 1)]
        backward = [(target, source) for source, target in forward]
        low = lax.ppermute(
            lax.slice_in_dim(block, block.shape[dim] - width, None, axis=dim), axis, forward
        )
        high = lax.ppermute(lax.slice_in_dim(block, 0, width, axis=dim), axis, backward)
        block = jnp.concatenate([low, block, high], axis=dim)
    return block


def smooth_unit(values):
    return values * jax.nn.sigmoid(values)


def smooth_slope(values):
    squash = jax.nn.sigmoid(values)
    return squash * (1.0 + values * (1.0 - squash))


def encode_apply(extended, weight):
    return lax.conv_general_dilated(
        extended,
        weight,
        (2, 2),
        ((0, 0), (1, 1)),
        dimension_numbers=LAYOUT,
        preferred_element_type=jnp.float32,
    )


def decode_apply(extended, weight):
    return lax.conv_general_dilated(
        extended,
        weight,
        (1, 1),
        ((0, 0), (2, 2)),
        lhs_dilation=(2, 2),
        dimension_numbers=LAYOUT,
        preferred_element_type=jnp.float32,
    )


def turned(weight):
    return jnp.transpose(jnp.flip(weight, (2, 3)), (1, 0, 2, 3))


def kernel_taps(spread_maps, grad_pre, stride):
    out_rows = grad_pre.shape[2]
    out_cols = grad_pre.shape[3]
    row_taps = []
    for row_tap in range(4):
        col_taps = []
        for col_tap in range(4):
            patch = lax.slice(
                spread_maps,
                (0, 0, row_tap, col_tap),
                (
                    spread_maps.shape[0],
                    spread_maps.shape[1],
                    row_tap + stride * (out_rows - 1) + 1,
                    col_tap + stride * (out_cols - 1) + 1,
                ),
                (1, 1, stride, stride),
            )
            col_taps.append(
                jnp.einsum("nchw,nohw->oc", patch, grad_pre, preferred_element_type=jnp.float32)
            )
        row_taps.append(jnp.stack(col_taps, axis=-1))
    return jnp.stack(row_taps, axis=-2)


def encode_back(extended, weight, grad_pre):
    grad_ext = lax.conv_general_dilated(
        grad_pre,
        turned(weight),
        (1, 1),
        ((3, 3), (2, 2)),
        lhs_dilation=(2, 2),
        dimension_numbers=LAYOUT,
        preferred_element_type=jnp.float32,
    )
    zero_value = jnp.zeros((), extended.dtype)
    spread_maps = lax.pad(extended, zero_value, ((0, 0, 0), (0, 0, 0), (0, 0, 0), (1, 1, 0)))
    grad_weight = kernel_taps(spread_maps, grad_pre, 2)
    return (grad_ext, grad_weight)


def decode_back(extended, weight, grad_pre):
    grad_ext = lax.conv_general_dilated(
        grad_pre,
        turned(weight),
        (2, 2),
        ((3, 3), (1, 1)),
        dimension_numbers=LAYOUT,
        preferred_element_type=jnp.float32,
    )
    zero_value = jnp.zeros((), extended.dtype)
    spread_maps = lax.pad(extended, zero_value, ((0, 0, 0), (0, 0, 0), (0, 0, 1), (2, 2, 1)))
    grad_weight = kernel_taps(spread_maps, grad_pre, 1)
    return (grad_ext, grad_weight)


def extend_rows(maps):
    return with_halo(maps, (("strip", 2),), 1)


def settle_rows(grad_ext):
    edge_rows = jnp.concatenate([grad_ext[:, :, :1], grad_ext[:, :, -1:]], axis=2)
    arrived = with_halo(edge_rows.astype(jnp.bfloat16), (("strip", 2),), 1).astype(edge_rows.dtype)
    interior = grad_ext[:, :, 1:-1]
    interior = interior.at[:, :, :1].add(arrived[:, :, :1])
    return interior.at[:, :, -1:].add(arrived[:, :, -1:])


def strip_total(partial_value):
    return lax.psum(partial_value.astype(jnp.bfloat16), "strip").astype(jnp.float32)


def strip_grads(partial_value):
    return lax.psum(partial_value.astype(jnp.bfloat16), "strip").astype(jnp.float32)


def normalize(hidden):
    centred = hidden - jnp.mean(hidden, -1, keepdims=True)
    scale_inv = lax.rsqrt(jnp.mean(centred * centred, -1, keepdims=True) + EPS)
    return (centred * scale_inv, scale_inv)


def normalize_back(grad_normed, unit_rows, scale_inv, gain):
    grad_unit = grad_normed * gain
    grad_gain = jnp.sum(grad_normed * unit_rows, 0)
    grad_rows = scale_inv * (
        grad_unit
        - jnp.mean(grad_unit, -1, keepdims=True)
        - unit_rows * jnp.mean(grad_unit * unit_rows, -1, keepdims=True)
    )
    return (grad_gain, grad_rows)


def grouped_softmax(logits):
    frame_count = logits.shape[0]
    grouped = logits.reshape(frame_count, -1, LCLASS)
    shifted = grouped - jnp.max(grouped, -1, keepdims=True)
    raised = jnp.exp(shifted)
    return (raised / jnp.sum(raised, -1, keepdims=True)).reshape(frame_count, -1)


def make_mask(segment_ids):
    places = jnp.arange(segment_ids.shape[1])
    causal = places[:, None] >= places[None, :]
    return causal[None] & (segment_ids[:, :, None] == segment_ids[:, None, :])


def split_heads(flat_rows, sequences):
    return flat_rows.reshape(sequences, -1, flat_rows.shape[-1] // HEAD_DIM, HEAD_DIM)


def score_block(queries, keys_part, allowed):
    scores = (
        jnp.einsum("bqhe,bkhe->bhqk", queries, keys_part, preferred_element_type=jnp.float32)
        * SCALE
    )
    return jnp.where(allowed[:, None], scores, NEG)


def layer_forward(hidden, allowed, gain_pair, qkv_layer, out_layer, up_layer, down_layer):
    sequences = allowed.shape[0]
    unit_attn, inv_attn = normalize(hidden)
    normed_attn = (unit_attn * gain_pair[0]).astype(jnp.bfloat16)
    mixed = jnp.einsum(
        "td,dkh->tkh", normed_attn, qkv_layer, preferred_element_type=jnp.float32
    ).astype(jnp.bfloat16)
    queries = split_heads(mixed[:, 0], sequences)
    keys_part = split_heads(mixed[:, 1], sequences)
    vals_part = split_heads(mixed[:, 2], sequences)
    scores = score_block(queries, keys_part, allowed)
    top_score = jnp.max(scores, -1, keepdims=True)
    log_total = top_score + jnp.log(jnp.sum(jnp.exp(scores - top_score), -1, keepdims=True))
    chances = jnp.exp(scores - log_total).astype(jnp.bfloat16)
    attended = jnp.einsum("bhqk,bkhe->bqhe", chances, vals_part, preferred_element_type=jnp.float32)
    attended = attended.astype(jnp.bfloat16).reshape(hidden.shape[0], -1)
    middle = hidden + strip_total(jnp.dot(attended, out_layer, preferred_element_type=jnp.float32))
    unit_ffn, inv_ffn = normalize(middle)
    normed_ffn = (unit_ffn * gain_pair[1]).astype(jnp.bfloat16)
    before = jnp.dot(normed_ffn, up_layer, preferred_element_type=jnp.float32)
    inner_act = smooth_unit(before).astype(jnp.bfloat16)
    result = middle + strip_total(
        jnp.dot(inner_act, down_layer, preferred_element_type=jnp.float32)
    )
    kept_layer = (
        unit_attn,
        inv_attn,
        normed_attn,
        mixed,
        log_total,
        attended,
        unit_ffn,
        inv_ffn,
        normed_ffn,
        before,
        inner_act,
    )
    return (result, kept_layer)


def layer_backward(
    grad_hidden, allowed, gain_pair, qkv_layer, out_layer, up_layer, down_layer, kept_layer
):
    (
        unit_attn,
        inv_attn,
        normed_attn,
        mixed,
        log_total,
        attended,
        unit_ffn,
        inv_ffn,
        normed_ffn,
        before,
        inner_act,
    ) = kept_layer
    sequences = allowed.shape[0]
    token_count = grad_hidden.shape[0]
    grad_low = grad_hidden.astype(jnp.bfloat16)
    grad_down = jnp.dot(inner_act.T, grad_low, preferred_element_type=jnp.float32)
    grad_inner = jnp.dot(grad_low, down_layer.T, preferred_element_type=jnp.float32)
    grad_before = (grad_inner * smooth_slope(before)).astype(jnp.bfloat16)
    grad_up = jnp.dot(normed_ffn.T, grad_before, preferred_element_type=jnp.float32)
    grad_normed = strip_grads(jnp.dot(grad_before, up_layer.T, preferred_element_type=jnp.float32))
    gain_ffn, grad_mid = normalize_back(grad_normed, unit_ffn, inv_ffn, gain_pair[1])
    grad_middle = grad_hidden + grad_mid
    middle_low = grad_middle.astype(jnp.bfloat16)
    grad_project = jnp.dot(attended.T, middle_low, preferred_element_type=jnp.float32)
    grad_attended = jnp.dot(middle_low, out_layer.T, preferred_element_type=jnp.float32).astype(
        jnp.bfloat16
    )
    grad_attended = split_heads(grad_attended, sequences)
    queries = split_heads(mixed[:, 0], sequences)
    keys_part = split_heads(mixed[:, 1], sequences)
    vals_part = split_heads(mixed[:, 2], sequences)
    scores = score_block(queries, keys_part, allowed)
    chances = jnp.exp(scores - log_total)
    grad_vals = jnp.einsum(
        "bhqk,bqhe->bkhe",
        chances.astype(jnp.bfloat16),
        grad_attended,
        preferred_element_type=jnp.float32,
    )
    grad_chances = jnp.einsum(
        "bqhe,bkhe->bhqk", grad_attended, vals_part, preferred_element_type=jnp.float32
    )
    weighted_total = jnp.sum(chances * grad_chances, -1, keepdims=True)
    grad_scores = (chances * (grad_chances - weighted_total)).astype(jnp.bfloat16)
    grad_queries = (
        jnp.einsum("bhqk,bkhe->bqhe", grad_scores, keys_part, preferred_element_type=jnp.float32)
        * SCALE
    )
    grad_keys = (
        jnp.einsum("bhqk,bqhe->bkhe", grad_scores, queries, preferred_element_type=jnp.float32)
        * SCALE
    )
    grad_mixed = jnp.stack(
        [
            grad_queries.reshape(token_count, -1),
            grad_keys.reshape(token_count, -1),
            grad_vals.reshape(token_count, -1),
        ],
        axis=1,
    ).astype(jnp.bfloat16)
    grad_qkv = jnp.einsum(
        "td,tkh->dkh", normed_attn, grad_mixed, preferred_element_type=jnp.float32
    )
    grad_normed_attn = strip_grads(
        jnp.einsum("tkh,dkh->td", grad_mixed, qkv_layer, preferred_element_type=jnp.float32)
    )
    gain_attn, grad_first = normalize_back(grad_normed_attn, unit_attn, inv_attn, gain_pair[0])
    return (
        grad_middle + grad_first,
        jnp.stack([gain_attn, gain_ffn]),
        grad_qkv,
        grad_project,
        grad_up,
        grad_down,
    )


def run_forward(
    frames,
    segment_ids,
    encoders,
    latent_head,
    token_embed,
    positions,
    norm_gains,
    qkv_weight,
    out_weight,
    up_weight,
    down_weight,
    decode_head,
    decoders,
):
    frame_count = frames.shape[0]
    maps = frames
    encode_kept = []
    for weight in encoders:
        extended = extend_rows(maps)
        before = encode_apply(extended, weight)
        encode_kept.append((extended, before))
        maps = smooth_unit(before).astype(jnp.bfloat16)
    gathered = lax.all_gather(maps, "strip", axis=2, tiled=True)
    features = gathered.reshape(frame_count, -1)
    logits = jnp.dot(features, latent_head, preferred_element_type=jnp.float32)
    chances = grouped_softmax(logits)
    latent = chances.astype(jnp.bfloat16)
    embedded = strip_total(jnp.dot(latent, token_embed, preferred_element_type=jnp.float32))
    sequences = segment_ids.shape[0]
    hidden = (
        embedded.reshape(sequences, -1, embedded.shape[1]) + positions.astype(jnp.float32)[None]
    )
    hidden = hidden.reshape(frame_count, -1)
    allowed = make_mask(segment_ids)
    layer_kept = []
    for layer_index in range(qkv_weight.shape[0]):
        hidden, kept_layer = layer_forward(
            hidden,
            allowed,
            norm_gains[layer_index],
            qkv_weight[layer_index],
            out_weight[layer_index],
            up_weight[layer_index],
            down_weight[layer_index],
        )
        layer_kept.append(kept_layer)
    partial_maps = jnp.dot(latent, decode_head, preferred_element_type=jnp.float32).reshape(
        gathered.shape
    )
    decoded = lax.psum_scatter(
        partial_maps.astype(jnp.bfloat16), "strip", scatter_dimension=2, tiled=True
    ).astype(jnp.float32)
    dmaps = smooth_unit(decoded).astype(jnp.bfloat16)
    decode_kept = []
    for weight in decoders[:-1]:
        extended = extend_rows(dmaps)
        before = decode_apply(extended, weight)
        decode_kept.append((extended, before))
        dmaps = smooth_unit(before).astype(jnp.bfloat16)
    last_extended = extend_rows(dmaps)
    recon = decode_apply(last_extended, decoders[-1])
    state = {
        "encode_kept": encode_kept,
        "gathered": gathered,
        "chances": chances,
        "latent": latent,
        "allowed": allowed,
        "layer_kept": layer_kept,
        "decoded": decoded,
        "decode_kept": decode_kept,
        "last_extended": last_extended,
    }
    return (hidden, recon, state)


def run_backward(
    state,
    token_cotangent,
    frame_cotangent,
    encoders,
    latent_head,
    token_embed,
    norm_gains,
    qkv_weight,
    out_weight,
    up_weight,
    down_weight,
    decode_head,
    decoders,
):
    allowed = state["allowed"]
    grad_hidden = token_cotangent.astype(jnp.float32)
    layer_count = qkv_weight.shape[0]
    layer_grads = [None] * layer_count
    for layer_index in reversed(range(layer_count)):
        grad_hidden, gain_grad, qkv_grad, project_grad, up_grad, down_grad = layer_backward(
            grad_hidden,
            allowed,
            norm_gains[layer_index],
            qkv_weight[layer_index],
            out_weight[layer_index],
            up_weight[layer_index],
            down_weight[layer_index],
            state["layer_kept"][layer_index],
        )
        layer_grads[layer_index] = (gain_grad, qkv_grad, project_grad, up_grad, down_grad)
    stacked = [jnp.stack([entry[slot] for entry in layer_grads]) for slot in range(5)]
    sequences = allowed.shape[0]
    positions_grad = jnp.sum(grad_hidden.reshape(sequences, -1, grad_hidden.shape[1]), 0)
    embed_low = grad_hidden.astype(jnp.bfloat16)
    latent = state["latent"]
    frame_count = latent.shape[0]
    embed_grad = jnp.dot(latent.T, embed_low, preferred_element_type=jnp.float32)
    grad_latent = jnp.dot(embed_low, token_embed.T, preferred_element_type=jnp.float32)
    decode_kept = state["decode_kept"]
    decode_grads = [None, None, None, None]
    grad_ext, decode_grads[3] = decode_back(state["last_extended"], decoders[3], frame_cotangent)
    for depth_index in (2, 1, 0):
        grad_maps = settle_rows(grad_ext)
        extended, before = decode_kept[depth_index]
        grad_pre = (grad_maps * smooth_slope(before)).astype(jnp.bfloat16)
        grad_ext, decode_grads[depth_index] = decode_back(extended, decoders[depth_index], grad_pre)
    grad_maps = settle_rows(grad_ext)
    grad_decoded = (grad_maps * smooth_slope(state["decoded"])).astype(jnp.bfloat16)
    spread_grads = lax.all_gather(grad_decoded, "strip", axis=2, tiled=True).reshape(
        frame_count, -1
    )
    head_grad = jnp.dot(latent.T, spread_grads, preferred_element_type=jnp.float32)
    grad_latent = grad_latent + jnp.dot(
        spread_grads, decode_head.T, preferred_element_type=jnp.float32
    )
    grouped = state["chances"].reshape(frame_count, -1, LCLASS)
    grad_grouped = grad_latent.reshape(grouped.shape)
    grad_logits = grouped * (grad_grouped - jnp.sum(grouped * grad_grouped, -1, keepdims=True))
    grad_logits = grad_logits.reshape(frame_count, -1).astype(jnp.bfloat16)
    gathered = state["gathered"]
    features = gathered.reshape(frame_count, -1)
    latent_grad = jnp.dot(features.T, grad_logits, preferred_element_type=jnp.float32)
    grad_features = jnp.dot(grad_logits, latent_head.T, preferred_element_type=jnp.float32).reshape(
        gathered.shape
    )
    grad_maps = lax.psum_scatter(
        grad_features.astype(jnp.bfloat16), "strip", scatter_dimension=2, tiled=True
    ).astype(jnp.float32)
    encode_kept = state["encode_kept"]
    encode_grads = [None, None, None, None]
    for depth_index in (3, 2, 1, 0):
        extended, before = encode_kept[depth_index]
        grad_pre = (grad_maps * smooth_slope(before)).astype(jnp.bfloat16)
        grad_ext, encode_grads[depth_index] = encode_back(extended, encoders[depth_index], grad_pre)
        grad_maps = settle_rows(grad_ext)
    others = [
        latent_grad,
        embed_grad,
        positions_grad,
        stacked[0],
        stacked[1],
        stacked[2],
        stacked[3],
        stacked[4],
        head_grad,
    ]
    return (grad_maps, encode_grads + decode_grads, others)


def flatten_all(parts, multiple):
    flat_vector = jnp.concatenate([part.reshape(-1) for part in parts])
    return jnp.pad(flat_vector, (0, -flat_vector.shape[0] % multiple))


def unflatten_all(flat_vector, parts):
    pieces = []
    offset = 0
    for part in parts:
        pieces.append(flat_vector[offset : offset + part.size].reshape(part.shape))
        offset = offset + part.size
    return pieces


def rows_total(parts):
    flat_vector = flatten_all(parts, lax.axis_size("rows"))
    shares = lax.psum_scatter(flat_vector, "rows", scatter_dimension=0, tiled=True)
    summed = lax.all_gather(shares.astype(jnp.bfloat16), "rows", axis=0, tiled=True).astype(
        shares.dtype
    )
    return unflatten_all(summed, parts)


def shards(
    frames,
    segment_ids,
    encode_one,
    encode_two,
    encode_three,
    encode_four,
    latent_head,
    token_embed,
    positions,
    norm_gains,
    qkv_weight,
    out_weight,
    up_weight,
    down_weight,
    decode_head,
    decode_one,
    decode_two,
    decode_three,
    decode_four,
    token_cotangent,
    frame_cotangent,
):
    encoders = (encode_one, encode_two, encode_three, encode_four)
    decoders = (decode_one, decode_two, decode_three, decode_four)
    hidden, recon, state = run_forward(
        frames,
        segment_ids,
        encoders,
        latent_head,
        token_embed,
        positions,
        norm_gains,
        qkv_weight,
        out_weight,
        up_weight,
        down_weight,
        decode_head,
        decoders,
    )
    again = lax.optimization_barrier(
        (
            frames,
            segment_ids,
            encoders,
            latent_head,
            token_embed,
            positions,
            norm_gains,
            qkv_weight,
            out_weight,
            up_weight,
            down_weight,
            decode_head,
            decoders,
        )
    )
    unused_hidden, unused_recon, state = run_forward(
        again[0],
        again[1],
        again[2],
        again[3],
        again[4],
        again[5],
        again[6],
        again[7],
        again[8],
        again[9],
        again[10],
        again[11],
        again[12],
    )
    frames_grad, conv_parts, others = run_backward(
        state,
        token_cotangent,
        frame_cotangent,
        encoders,
        latent_head,
        token_embed,
        norm_gains,
        qkv_weight,
        out_weight,
        up_weight,
        down_weight,
        decode_head,
        decoders,
    )
    conv_strip = (
        lax.psum(conv_parts[0].astype(jnp.bfloat16), "strip").astype(jnp.float32),
        lax.psum(conv_parts[1].astype(jnp.bfloat16), "strip").astype(jnp.float32),
        lax.psum(conv_parts[2].astype(jnp.bfloat16), "strip").astype(jnp.float32),
        lax.psum(conv_parts[3].astype(jnp.bfloat16), "strip").astype(jnp.float32),
        lax.psum(conv_parts[4].astype(jnp.bfloat16), "strip").astype(jnp.float32),
        lax.psum(conv_parts[5].astype(jnp.bfloat16), "strip").astype(jnp.float32),
        lax.psum(conv_parts[6].astype(jnp.bfloat16), "strip").astype(jnp.float32),
        lax.psum(conv_parts[7].astype(jnp.bfloat16), "strip").astype(jnp.float32),
    )
    summed = rows_total(list(conv_strip) + others)
    conv_done = summed[:8]
    other_done = summed[8:]
    return (
        hidden.astype(jnp.bfloat16),
        recon.astype(jnp.bfloat16),
        frames_grad,
        conv_done[0],
        conv_done[1],
        conv_done[2],
        conv_done[3],
        other_done[0],
        other_done[1],
        other_done[2],
        other_done[3],
        other_done[4],
        other_done[5],
        other_done[6],
        other_done[7],
        other_done[8],
        conv_done[4],
        conv_done[5],
        conv_done[6],
        conv_done[7],
    )


def solution(mesh):
    placed = (
        P("rows", None, "strip", None),
        P("rows", None),
        P(),
        P(),
        P(),
        P(),
        P(None, "strip"),
        P("strip", None),
        P(),
        P(),
        P(None, None, None, "strip"),
        P(None, "strip", None),
        P(None, None, "strip"),
        P(None, "strip", None),
        P("strip", None),
        P(),
        P(),
        P(),
        P(),
        P("rows", None),
        P("rows", None, "strip", None),
    )
    return jax.shard_map(
        shards,
        mesh=mesh,
        in_specs=placed,
        out_specs=(
            P("rows", None),
            P("rows", None, "strip", None),
            P("rows", None, "strip", None),
            P(),
            P(),
            P(),
            P(),
            P(None, "strip"),
            P("strip", None),
            P(),
            P(),
            P(None, None, None, "strip"),
            P(None, "strip", None),
            P(None, None, "strip"),
            P(None, "strip", None),
            P("strip", None),
            P(),
            P(),
            P(),
            P(),
        ),
        check_vma=False,
    )
```

profile of v0, /device:TPU:0, one launch (start us, length us, event | category | flops | bytes accessed | tf_op | source)
XLA Modules:
  0.0 3228.3 jit_solution(10427706919066091493)
XLA Ops:
  154.3 29.4 all-reduce.26.cloned.1.call-done
  194.1 29.0 all-reduce.28.cloned.1.call-done
  228.9 32.0 all-reduce.30.cloned.1.call-done
  276.9 31.1 all-reduce.32.cloned.1.call-done
  317.2 31.1 all-reduce.42.cloned.1.call-done
  374.1 33.3 %all-reduce.40.cloned.1.call-done = (bf16[256,512]{1,0:T(8,128)(2,1)}, bf16[256,512]{1,0:T(8,128)(2,1)}) async-done(((bf16[256,512]{1,0:T(8,128)(2,1)}, bf16[256,512]{1,0:T(8,128)(2,1)}), (bf16[256,512]{1,0:T(8,128)(2,1)}, bf16[256,512]{1,0:T(8,128)(2,1)})) %all-reduce.40.cloned.1.call-update) | async-done | bytes 524304 | tf_op jit(solution)/shard_map/psum | solution.py:134
  425.4 25.4 all-reduce.38.cloned.1.call-done
  516.7 24.4 reduce-scatter.6.cloned.1.call-done
  599.6 13.5 pad.63
  635.5 49.4 %pad.64 = bf16[256,64,11,35]{0,1,3,2:T(8,128)(2,1)} pad(bf16[256,64,6,16]{0,1,3,2:T(8,128)(2,1)} %pad_maximum_fusion.3, bf16[]{:T(256)} %constant.439.clone.1), padding=0_0_0x0_0_0x0_0_1x2_2_1 | pad | bytes 15761410 | tf_op jit(solution)/shard_map/pad | solution.py:116
  812.3 16.8 reshape.1114
  867.3 25.0 copy.470
  892.4 61.8 %reshape.1112 = bf16[524288]{0:T(1024)(128)(2,1)} reshape(bf16[128,256,4,4]{3,2,1,0:T(4,128)(2,1)} %copy.470) | data formatting | bytes 2097152 | tf_op jit(solution)/shard_map/reshape | solution.py:472
  978.6 26.4 copy.453
  1004.9 61.8 %reshape.1110 = bf16[524288]{0:T(1024)(128)(2,1)} reshape(bf16[256,128,4,4]{3,2,1,0:T(4,128)(2,1)} %copy.453) | data formatting | bytes 2097152 | tf_op jit(solution)/shard_map/reshape | solution.py:472
  1088.9 14.1 copy.436
  1103.0 16.8 reshape.1091
  1198.5 148.4 %pad.65 = bf16[256,32,19,67]{0,1,3,2:T(8,128)(2,1)} pad(bf16[256,32,10,32]{0,1,3,2:T(8,128)(2,1)} %pad_maximum_fusion.1, bf16[]{:T(256)} %constant.439.clone.1), padding=0_0_0x0_0_0x0_0_1x2_2_1 | pad | bytes 26099714 | tf_op jit(solution)/shard_map/pad | solution.py:116
  1522.0 19.1 dynamic-update-slice.49
  1541.1 18.1 dynamic-update-slice.50
  1578.9 800.1 %all-reduce.43 = bf16[5215232]{0:T(1024)(128)(2,1)} all-reduce(f32[5215232]{0:T(1024)} %constant_dynamic-update-slice_fusion.10), channel_id=5, replica_groups=mesh['rows'=8,'strip'=4] {'rows'}, use_global_device_ids=true, to_apply=%region_68.69.clone | all-reduce | flops 5215232 | bytes 31291392
  2381.0 15.6 reshape.1141
  2460.5 27.3 fusion.1268
  2492.7 24.9 fusion.149
  2523.5 271.4 %all-gather.12.cloned.1.call-done = bf16[8,1,651904]{2,1,0:T(2,128)(2,1)} async-done(((bf16[1,1,651904]{2,1,0:T(2,128)(2,1)}), bf16[8,1,651904]{2,1,0:T(2,128)(2,1)}) %all-gather.12.cloned.1.call-update) | async-done | bytes 10430480 | tf_op jit(solution)/shard_map/all_gather | solution.py:488
  2794.9 24.0 convert_element_type.493
  2829.2 89.4 %reshape.1132 = f32[256,128,4,4]{3,2,1,0:T(4,128)} reshape(f32[524288]{0:T(1024)} %get-tuple-element.373) | data formatting | bytes 4194304 | tf_op jit(solution)/shard_map/reshape | solution.py:480
  2918.6 48.4 %copy.498 = f32[256,128,4,4]{1,3,2,0:T(4,128)} copy(f32[256,128,4,4]{3,2,1,0:T(4,128)} %reshape.1132) | data formatting | bytes 4194304
  2966.9 88.4 %reshape.1138 = f32[128,256,4,4]{3,2,1,0:T(4,128)} reshape(f32[524288]{0:T(1024)S(1)} %copy-done.48) | data formatting | bytes 4194304 | tf_op jit(solution)/shard_map/reshape | solution.py:480
  3055.3 48.4 %copy.500 = f32[128,256,4,4]{1,3,2,0:T(4,128)} copy(f32[128,256,4,4]{3,2,1,0:T(4,128)} %reshape.1138) | data formatting | bytes 4194304
  3103.7 23.1 reshape.1131
  3139.9 23.1 reshape.1139
  (1056 shorter events, 1018.2 us)
Async XLA Ops:
  7.2 118.4 %all-gather.8.cloned.1.call-start = ((), (), s32[]{:S(2)}) async-start(), calls=%async_computation.5 | async-start | bytes 2621440 | tf_op jit(solution)/shard_map/all_gather | solution.py:328
  39.2 15.9 collective-permute-start.20
  59.0 16.7 collective-permute-start.22
  78.2 70.6 %all-gather.6.cloned.1.call-start = ((), (), s32[]{:S(2)}) async-start(), calls=%async_computation.3 | async-start | bytes 2621440 | tf_op jit(solution)/shard_map/all_gather | solution.py:328
  119.0 64.7 %all-reduce.26.cloned.1.call-start = ((), (), s32[]{:S(2)}) async-start(), calls=%async_computation.6 | async-start | bytes 524288 | tf_op jit(solution)/shard_map/psum | solution.py:134
  139.7 83.4 %all-reduce.28.cloned.1.call-start = ((), (), s32[]{:S(2)}) async-start(), calls=%async_computation.7 | async-start | bytes 524288 | tf_op jit(solution)/shard_map/psum | solution.py:134
  191.0 69.9 %all-reduce.30.cloned.1.call-start = ((), (), s32[]{:S(2)}) async-start(), calls=%async_computation.8 | async-start | bytes 524288 | tf_op jit(solution)/shard_map/psum | solution.py:134
  228.8 79.2 %all-reduce.32.cloned.1.call-start = ((), (), s32[]{:S(2)}) async-start(), calls=%async_computation.9 | async-start | bytes 524288 | tf_op jit(solution)/shard_map/psum | solution.py:134
  275.9 72.4 %all-reduce.42.cloned.1.call-start = ((), (), s32[]{:S(2)}) async-start(), calls=%async_computation.18 | async-start | bytes 1048576 | tf_op jit(solution)/shard_map/psum | solution.py:134
  315.0 92.5 %all-reduce.40.cloned.1.call-start = ((), (), s32[]{:S(2)}) async-start(), calls=%async_computation.17 | async-start | bytes 1048576 | tf_op jit(solution)/shard_map/psum | solution.py:134
  373.9 76.9 %all-reduce.38.cloned.1.call-start = ((), (), s32[]{:S(2)}) async-start(), calls=%async_computation.16 | async-start | bytes 1048576 | tf_op jit(solution)/shard_map/psum | solution.py:134
  417.3 97.5 %all-reduce.36.cloned.1.call-start = ((), (), s32[]{:S(2)}) async-start(), calls=%async_computation.15 | async-start | bytes 1048576 | tf_op jit(solution)/shard_map/psum | solution.py:134
  472.4 68.6 %reduce-scatter.6.cloned.1.call-start = ((), (), s32[]{:S(2)}) async-start(), calls=%async_computation.10 | async-start | bytes 2621440 | tf_op jit(solution)/shard_map/reduce_scatter | solution.py:355
  475.8 357.7 %all-gather.10.cloned.1.call-start = ((), (), s32[]{:S(2)}) async-start(), calls=%async_computation.11 | async-start | bytes 2621440 | tf_op jit(solution)/shard_map/all_gather | solution.py:430
  486.3 15.9 collective-permute-start.24
  575.8 37.3 %collective-permute-start.30 = (bf16[256,64,1,16]{0,1,3,2:T(8,128)(2,1)}, bf16[256,64,1,16]{0,1,3,2:T(8,128)(2,1)}, u32[]{:S(2)}, u32[]{:S(2)}) collective-permute-start(bf16[256,64,1,16]{0,1,3,2:T(8,128)(2,1)} %get-tuple-element.402), channel_id=1, source_target_pairs={{0,1},{1,2},{2,3},{4,5},{5,6},{6,7},{8,9},{9,10},{10,11},{12,13},{... | collective-permute-start | bytes 1572872 | tf_op jit(solution)/shard_map/ppermute | solution.py:21
  585.2 27.9 collective-permute-start.31
  731.2 16.7 collective-permute-start.32
  793.7 160.5 %reduce-scatter.8.cloned.1.call-start = ((), (), s32[]{:S(2)}) async-start(), calls=%async_computation.12 | async-start | bytes 2621440 | tf_op jit(solution)/shard_map/reduce_scatter | solution.py:447
  848.5 665.8 %all-reduce.34.cloned.1.call-start = ((), (), s32[]{:S(2)}) async-start(), calls=%async_computation.14 | async-start | bytes 6029312 | tf_op jit(solution)/shard_map/psum | solution.py:134
  965.4 101.3 %collective-permute-start.38 = (bf16[256,128,1,8]{1,0,3,2:T(8,128)(2,1)S(1)}, bf16[256,128,1,8]{1,0,3,2:T(8,128)(2,1)}, u32[]{:S(2)}, u32[]{:S(2)}) collective-permute-start(bf16[256,128,1,8]{1,0,3,2:T(8,128)(2,1)S(1)} %get-tuple-element.398), channel_id=1, source_target_pairs={{0,1},{1,2},{2,3},{4,5},{5,6},{6,7},{8,9},{9,10},{10,11},{12,13},{... | collective-permute-start | bytes 1572872 | tf_op jit(solution)/shard_map/ppermute | solution.py:21
  975.4 91.3 %collective-permute-start.39 = (bf16[256,128,1,8]{1,0,3,2:T(8,128)(2,1)S(1)}, bf16[256,128,1,8]{1,0,3,2:T(8,128)(2,1)}, u32[]{:S(2)}, u32[]{:S(2)}) collective-permute-start(bf16[256,128,1,8]{1,0,3,2:T(8,128)(2,1)S(1)} %get-tuple-element.399), channel_id=1, source_target_pairs={{1,0},{2,1},{3,2},{5,4},{6,5},{7,6},{9,8},{10,9},{11,10},{13,12},{... | collective-permute-start | bytes 1572872 | tf_op jit(solution)/shard_map/ppermute | solution.py:24
  1081.6 38.2 %collective-permute-start.40 = (bf16[256,64,1,16]{0,1,3,2:T(8,128)(2,1)S(1)}, bf16[256,64,1,16]{0,1,3,2:T(8,128)(2,1)S(1)}, u32[]{:S(2)}, u32[]{:S(2)}) collective-permute-start(bf16[256,64,1,16]{0,1,3,2:T(8,128)(2,1)S(1)} %get-tuple-element.390), channel_id=1, source_target_pairs={{0,1},{1,2},{2,3},{4,5},{5,6},{6,7},{8,9},{9,10},{10,11},{12,13},{... | collective-permute-start | bytes 1572872 | tf_op jit(solution)/shard_map/ppermute | solution.py:21
  1084.6 35.2 %collective-permute-start.41 = (bf16[256,64,1,16]{0,1,3,2:T(8,128)(2,1)S(1)}, bf16[256,64,1,16]{0,1,3,2:T(8,128)(2,1)S(1)}, u32[]{:S(2)}, u32[]{:S(2)}) collective-permute-start(bf16[256,64,1,16]{0,1,3,2:T(8,128)(2,1)S(1)} %get-tuple-element.391), channel_id=1, source_target_pairs={{1,0},{2,1},{3,2},{5,4},{6,5},{7,6},{9,8},{10,9},{11,10},{13,12},{... | collective-permute-start | bytes 1572872 | tf_op jit(solution)/shard_map/ppermute | solution.py:24
  1149.9 1246.8 %reduce-scatter.4.cloned.1.call-start = ((), (), s32[]{:S(2)}) async-start(), calls=%async_computation.4 | async-start | bytes 2621440 | tf_op jit(solution)/shard_map/reduce_scatter | solution.py:355
  1163.4 1631.5 %all-gather.12.cloned.1.call-start = ((), (), s32[]{:S(2)}) async-start(), calls=%async_computation.13 | async-start | bytes 23468544 | tf_op jit(solution)/shard_map/all_gather | solution.py:488
  1175.8 16.9 collective-permute-start.46
  1460.8 16.0 collective-permute-start.42
  2450.0 42.7 %collective-permute-start.14 = (bf16[256,32,1,32]{0,1,3,2:T(8,128)(2,1)S(1)}, bf16[256,32,1,32]{0,1,3,2:T(8,128)(2,1)S(1)}, u32[]{:S(2)}, u32[]{:S(2)}) collective-permute-start(bf16[256,32,1,32]{0,1,3,2:T(8,128)(2,1)S(1)} %get-tuple-element.384), channel_id=1, source_target_pairs={{0,1},{1,2},{2,3},{4,5},{5,6},{6,7},{8,9},{9,10},{10,11},{12,13},{... | collective-permute-start | bytes 1572872 | tf_op jit(solution)/shard_map/ppermute | solution.py:21
  2459.0 33.7 %collective-permute-start.15 = (bf16[256,32,1,32]{0,1,3,2:T(8,128)(2,1)S(1)}, bf16[256,32,1,32]{0,1,3,2:T(8,128)(2,1)S(1)}, u32[]{:S(2)}, u32[]{:S(2)}) collective-permute-start(bf16[256,32,1,32]{0,1,3,2:T(8,128)(2,1)S(1)} %get-tuple-element.385), channel_id=1, source_target_pairs={{1,0},{2,1},{3,2},{5,4},{6,5},{7,6},{9,8},{10,9},{11,10},{13,12},{... | collective-permute-start | bytes 1572872 | tf_op jit(solution)/shard_map/ppermute | solution.py:24
  2487.9 32.1 collective-permute-start.44
  2491.0 29.1 collective-permute-start.45
  (232 other events, 3243.0 us)
Sparse Core Ops, SparseCore 0:
  78.4 28.3 all-gather.7
  119.1 29.6 all-gather.5
  151.7 31.9 all-reduce.25
  191.1 31.9 all-reduce.27
  228.9 31.9 all-reduce.29
  276.0 31.9 all-reduce.31
  315.1 33.1 all-reduce.41
  374.0 33.3 all-reduce.39
  417.4 33.3 all-reduce.37
  472.6 33.9 all-reduce.35
  509.6 31.4 reduce-scatter.5
  793.8 29.1 all-gather.9
  848.7 38.1 reduce-scatter.7
  1150.0 70.1 all-reduce.33
  1223.2 31.5 reduce-scatter.3
  2396.8 398.0 all-gather.11
where the time goes:
time: 3270 us; the launch traced here: 3230 us
  local copies, waits for them, and re-layouts  1070 us (33%)
  blocking collectives  809 us (25%)
  waiting for transfers between devices  537 us (16%)
  matrix products  483 us (15%)
  starting transfers between devices  176 us (5%)
  other arithmetic  131 us (4%)
    unnamed x1, blocking collectives  800 us
    all_gather x1, waiting for transfers between devices, rows_total(): lax.all_gather(shares.astype(jnp.bfloat16), 'rows', axis=0, tiled=True)  271 us
    reshape x11, local copies, waits for them, and re-layouts, unflatten_all(): pieces.append(flat_vector[offset:offset + part.size].reshape(part.shape))  244 us
    unnamed x440, local copies, waits for them, and re-layouts  238 us
    dot_general x128, matrix products, kernel_taps(): jnp.einsum('nchw,nohw->oc', patch, grad_pre, preferred_element_type=jnp.f...  228 us
    pad x4, local copies, waits for them, and re-layouts, decode_back(): lax.pad(extended, zero_value, ((0, 0, 0), (0, 0, 0), (0, 0, 1), (2, 2, 1)))  218 us
    psum x9, waiting for transfers between devices, strip_total(): lax.psum(partial_value.astype(jnp.bfloat16), 'strip').astype(jnp.float32)  211 us
    reshape x9, local copies, waits for them, and re-layouts, flatten_all(): flat_vector = jnp.concatenate([part.reshape(-1) for part in parts])  172 us
  transfers between devices with their start and end apart: 64, of which 24 were waited for; matrix products, arithmetic and copies ran while one was open for 28% of the time, Pallas kernels for 0%

commit v1 on v0

v1 whole, which is shorter than its diff:
```python
import functools

import jax
import jax.numpy as jnp
from jax import lax
from jax.experimental import pallas as pl
from jax.experimental.pallas import tpu as pltpu
from jax.sharding import PartitionSpec as P

HEAD_DIM = 64
LCLASS = 32
EPS = 1e-05
SCALE = 0.125
NEG = -1e30
F32 = jnp.float32
BF = jnp.bfloat16
NF = 64
MIB = 1 << 20
MESH = pl.DeviceIdType.MESH


def canon_T(we, a):
    _,_,c,o=we.shape
    flat=we.reshape(4,4*c,o)
    cols=[]
    for j in range(a):
        top=(a+2*j-1)*c
        cols.append(jnp.pad(flat,((0,0),(top,512-top-4*c),(0,0))))
    return jnp.concatenate(cols,axis=2)

def canon_U(T, a):
    Tt=jnp.swapaxes(T,1,2)
    z=jnp.zeros_like(Tt[:,:,:128])
    left=jnp.concatenate([Tt[:,:,384:512],z],axis=2)
    mid=Tt[:,:,128:384]
    right=jnp.concatenate([z,Tt[:,:,0:128]],axis=2)
    if a>1:
        left=left[:,128:]; right=right[:,:128]
    U=jnp.concatenate([left,mid,right],axis=1)
    return jnp.stack([jnp.concatenate([U[1],U[3]]),jnp.concatenate([U[0],U[2]])])

def outer_A(we):
    w=jnp.arange(64)[:,None]; j=jnp.arange(32)[None,:]
    kw=w-2*j+1
    hot=(kw[None]==jnp.arange(4)[:,None,None]).astype(we.dtype)
    full=jnp.einsum("kwj,hkco->hcwjo",hot,we,preferred_element_type=F32).astype(we.dtype)
    full=full.reshape(4,192,1024)
    z=jnp.zeros_like(full[0])
    return jnp.stack([jnp.concatenate([z,full[0]]),jnp.concatenate([full[1],full[2]]),jnp.concatenate([full[3],z])])

def outer_B(A):
    return jnp.swapaxes(A,1,2).reshape(3072,384)

def gt_to_we(GT, a, c, o):
    tot=0
    for j in range(a):
        s=(a+2*j-1)*c
        tot=tot+GT[:,j*o:(j+1)*o,s:s+4*c]
    return tot

def red_to_we(red):
    r=red.reshape(3,32,2,3,64)[...,:4]
    r=r.transpose(0,2,3,4,1)
    return jnp.stack([r[0,1],r[1,0],r[1,1],r[2,0]])

def sig(z): return 1.0/(1.0+jnp.exp(-z))

def zero_big(ref,rows):
    z=jnp.zeros((NF,1280),BF)
    ref[0,0]=z; ref[rows//2,1]=z
    e=jnp.zeros((rows//2+1,2,NF,128),BF)
    ref[:,:,:,0:128]=e; ref[:,:,:,1152:1280]=e

def zero_small(ref,rows,pad):
    z=jnp.zeros((NF,1024+2*pad),BF)
    ref[0]=z; ref[rows+1]=z
    if pad:
        e=jnp.zeros((rows+2,NF,pad),BF)
        ref[:,:,0:pad]=e; ref[:,:,1024+pad:]=e

def put_big(ref,half0,rows,q,val):
    v=val.reshape(rows,NF,256)
    for t in range(rows):
        ref[half0+(t+1)//2,(t+1)%2,:,128+256*q:384+256*q]=v[t]

def loop(n,body):
    if n==1: body(0)
    else:
        def step(g,c):
            body(g); return c
        lax.fori_loop(0,n,step,0)

def down(src,t_ref,rows,per,emit):
    def body(g):
        i0=g*per
        for q in range(4):
            lhs=jnp.concatenate([src[pl.ds(i0+kh//2,per),kh%2,:,256*q:256*q+512].reshape(per*NF,512) for kh in range(4)],axis=1)
            emit(i0,g*(per//2),q,jnp.dot(lhs,t_ref[...],preferred_element_type=F32))
    loop(rows//per,body)

def up(src,u_ref,rows,per,emit):
    k=u_ref.shape[1]//2
    def body(g):
        m0=g*per
        for q in range(4):
            for odd in range(2):
                lhs=jnp.concatenate([src[pl.ds(m0+1+odd-s,per),:,256*q:256*q+k].reshape(per*NF,k) for s in range(2)],axis=1)
                emit(m0,odd,q,jnp.dot(lhs,u_ref[odd],preferred_element_type=F32).reshape(per,NF,256))
    loop(rows//per,body)

def turn(src,dst,rows,pad):
    for q in range(4):
        dst[256*q:256*q+256,:]=src[1:rows+1,:,pad+256*q:pad+256*q+256].reshape(rows*NF,256).T

def grad_w(big,yt,rows,out):
    def body(kh,half):
        acc=jnp.zeros((256,512),F32)
        for q in range(4):
            win=big[pl.ds(half,rows),kh-2*half,:,256*q:256*q+512].reshape(rows*NF,512)
            acc=acc+jnp.dot(yt[256*q:256*q+256,:],win,preferred_element_type=F32)
        out[kh]=acc
    for kh in range(4): body(kh,kh//2)

def outer_down(xp,a_ref,emit,per=4):
    def body(g):
        i0=g*per
        lhs=jnp.concatenate([xp[pl.ds(i0+d,per)].reshape(per*NF,384) for d in range(3)],axis=1)
        for q in range(4):
            emit(i0,g*(per//2),q,jnp.dot(lhs,a_ref[:,256*q:256*q+256],preferred_element_type=F32))
    loop(32//per,body)

def outer_up(yp,b_ref,emit,per=4):
    def body(g):
        i0=g*per
        lhs=jnp.concatenate([yp[pl.ds(i0+2-d,per)].reshape(per*NF,1024) for d in range(3)],axis=1)
        emit(i0,jnp.dot(lhs,b_ref[...],preferred_element_type=F32).reshape(per,NF,384))
    loop(32//per,body)

def outer_grad(xp,yt,red):
    lane=lax.broadcasted_iota(jnp.int32,(32,384),1)%64
    for d in range(3):
        x=xp[d:d+32].reshape(32*NF,384)
        tot=jnp.zeros((32,384),F32)
        for jb in range(4):
            g=jnp.dot(yt[256*jb:256*jb+256,:],x,preferred_element_type=F32)
            for jj in range(8):
                j=8*jb+jj
                v=pltpu.roll(g[32*jj:32*jj+32],(385-2*j)%384,1)
                if j==0: v=jnp.where(lane==0,0.0,v)
                if j==31: v=jnp.where(lane==3,0.0,v)
                tot=tot+v
        red[d]=tot

def enc_fwd_kernel(xp,a,t2,t3,t4,z1,z2,z3,z4,feat,m1,m2,m3):
    zero_big(m1,32); zero_big(m2,16); zero_big(m3,8)
    def keep(z,m):
        def emit(i0,half0,q,acc):
            rows=acc.shape[0]//NF
            z[pl.ds(i0,rows),:,256*q:256*q+256]=acc.astype(BF).reshape(rows,NF,256)
            val=(acc*sig(acc)).astype(BF)
            if m is None: feat[pl.ds(i0,rows),:,256*q:256*q+256]=val.reshape(rows,NF,256)
            else: put_big(m,half0,rows,q,val)
        return emit
    outer_down(xp,a,keep(z1,m1))
    down(m1,t2,16,4,keep(z2,m2))
    down(m2,t3,8,4,keep(z3,m3))
    down(m3,t4,4,4,keep(z4,None))

def enc_bwd_kernel(xp,z1,z2,z3,z4,df,u2,u3,u4,b,dx,g2,g3,g4,red,m1,m2,m3,s1,s2,s3,s4,yt1,yt2,yt3,yt4):
    zero_big(m1,32); zero_big(m2,16); zero_big(m3,8)
    zero_small(s1,32,0); zero_small(s2,16,128); zero_small(s3,8,128); zero_small(s4,4,256)
    z=z4[...].astype(F32); s=sig(z)
    s4[1:5,:,256:1280]=(df[...].astype(F32)*(s*(1.0+z*(1.0-s)))).astype(BF)
    def back(z_ref,m,dst,pad):
        def emit(m0,odd,q,acc):
            per=acc.shape[0]
            for t in range(per):
                h=2*(m0+t)+odd
                zz=z_ref[h,:,256*q:256*q+256].astype(F32)
                ss=sig(zz); mm=zz*ss
                dst[h+1,:,pad+256*q:pad+256*q+256]=(acc[t]*(ss+mm*(1.0-ss))).astype(BF)
                m[m0+t+odd,1-odd,:,128+256*q:384+256*q]=mm.astype(BF)
        return emit
    up(s4,u4,4,4,back(z3,m3,s3,128))
    turn(s4,yt4,4,256); grad_w(m3,yt4,4,g4)
    up(s3,u3,8,4,back(z2,m2,s2,128))
    turn(s3,yt3,8,128); grad_w(m2,yt3,8,g3)
    up(s2,u2,16,4,back(z1,m1,s1,0))
    turn(s2,yt2,16,128); grad_w(m1,yt2,16,g2)
    def put(i0,acc): dx[pl.ds(i0,acc.shape[0])]=acc.astype(BF)
    outer_up(s1,b,put)
    turn(s1,yt1,32,0); outer_grad(xp,yt1,red)

def dec_fwd_kernel(dec,u4,u3,u2,b,recon,p3,p2,p1,s4,s3,s2,s1):
    zero_small(s1,32,0); zero_small(s2,16,128); zero_small(s3,8,128); zero_small(s4,4,256)
    z=dec[...].astype(F32)
    s4[1:5,:,256:1280]=(z*sig(z)).astype(BF)
    def fwd(p,dst,pad):
        def emit(m0,odd,q,acc):
            for t in range(acc.shape[0]):
                h=2*(m0+t)+odd
                v=acc[t]
                p[h,:,256*q:256*q+256]=v.astype(BF)
                dst[h+1,:,pad+256*q:pad+256*q+256]=(v*sig(v)).astype(BF)
        return emit
    up(s4,u4,4,4,fwd(p3,s3,128))
    up(s3,u3,8,4,fwd(p2,s2,128))
    up(s2,u2,16,4,fwd(p1,s1,0))
    def put(i0,acc): recon[pl.ds(i0,acc.shape[0])]=acc.astype(BF)
    outer_up(s1,b,put)

def dec_bwd_kernel(cp,dec,p3,p2,p1,a,t2,t3,t4,gdec,g2,g3,g4,red,d1,d2,d3,s,yt1,yt2,yt3,yt4):
    zero_big(d1,32); zero_big(d2,16); zero_big(d3,8)
    def maps(p,rows,yt):
        for q in range(4):
            zz=p[:,:,256*q:256*q+256].reshape(rows*NF,256).astype(F32)
            yt[256*q:256*q+256,:]=(zz*sig(zz)).astype(BF).T
    def back(p,dst):
        def emit(i0,half0,q,acc):
            rows=acc.shape[0]//NF
            zz=p[pl.ds(i0,rows),:,256*q:256*q+256].astype(F32).reshape(rows*NF,256)
            ss=sig(zz)
            val=(acc*(ss*(1.0+zz*(1.0-ss)))).astype(BF)
            if dst is None: gdec[pl.ds(i0,rows),:,256*q:256*q+256]=val.reshape(rows,NF,256)
            else: put_big(dst,half0,rows,q,val)
        return emit
    maps(p1,32,yt1); outer_grad(cp,yt1,red)
    outer_down(cp,a,back(p1,d1))
    maps(p2,16,yt2); grad_w(d1,yt2,16,g2)
    down(d1,t2,16,4,back(p2,d2))
    maps(p3,8,yt3); grad_w(d2,yt3,8,g3)
    down(d2,t3,8,4,back(p3,d3))
    maps(dec,4,yt4); grad_w(d3,yt4,4,g4)
    down(d3,t4,4,4,back(dec,None))

def S(shape,dt=BF): return jax.ShapeDtypeStruct(shape,dt)
def V(shape,dt=BF): return pltpu.VMEM(shape,dt)
VM=lambda n:[pl.BlockSpec(memory_space=pltpu.VMEM)]*n
def run(kernel,outs,scratch,args,name,lim=60,flops=10**10):
    return pl.pallas_call(kernel,out_shape=outs,in_specs=VM(len(args)),out_specs=tuple(VM(len(outs))),
        scratch_shapes=scratch,compiler_params=pltpu.CompilerParams(vmem_limit_bytes=lim*MIB),
        cost_estimate=pl.CostEstimate(flops=flops,bytes_accessed=20*MIB,transcendentals=0),name=name)(*args)
big=lambda h:V((h//2+1,2,NF,1280))
def enc_fwd(xp,a,t2,t3,t4):
    return run(enc_fwd_kernel,(S((32,NF,1024)),S((16,NF,1024)),S((8,NF,1024)),S((4,NF,1024)),S((4,NF,1024))),
      [big(32),big(16),big(8)],(xp,a,t2,t3,t4),"encode")
GS=tuple([S((4,256,512),F32)]*3+[S((3,32,384),F32)])
small=lambda h,p:V((h+2,NF,1024+2*p))
yts=[V((1024,32*NF)),V((1024,16*NF)),V((1024,8*NF)),V((1024,4*NF))]
def enc_bwd(xp,z1,z2,z3,z4,df,u2,u3,u4,b):
    return run(enc_bwd_kernel,(S((32,NF,384)),)+GS,[big(32),big(16),big(8),small(32,0),small(16,128),small(8,128),small(4,256)]+yts,
      (xp,z1,z2,z3,z4,df,u2,u3,u4,b),"encode_back")
def dec_fwd(dec,u4,u3,u2,b):
    return run(dec_fwd_kernel,(S((32,NF,384)),S((8,NF,1024)),S((16,NF,1024)),S((32,NF,1024))),
      [small(4,256),small(8,128),small(16,128),small(32,0)],(dec,u4,u3,u2,b),"decode")
def dec_bwd(cp,dec,p3,p2,p1,a,t2,t3,t4):
    return run(dec_bwd_kernel,(S((4,NF,1024)),)+GS,[big(32),big(16),big(8),V((8,128))]+yts,
      (cp,dec,p3,p2,p1,a,t2,t3,t4),"decode_back")


def greet(me):
    barrier = pltpu.get_barrier_semaphore()
    row = lax.axis_index("rows")
    for k in range(1, 4):
        pl.semaphore_signal(
            barrier, inc=1, device_id=(row, lax.rem(me + k, 4)), device_id_type=MESH
        )
    pl.semaphore_wait(barrier, 3)


def frames_in_kernel(x, out, stage, send_sem, recv_sem):
    me = lax.axis_index("strip")
    row = lax.axis_index("rows")
    out[0] = jnp.zeros((NF, 384), BF)
    out[33] = jnp.zeros((NF, 384), BF)

    def turn_rows(i, carry):
        block = jnp.concatenate(
            [x[c, 2 * i + p] for p in range(2) for c in range(3)], axis=0
        )
        flat = block.T
        for k in range(4):
            first = NF * ((k % 2) * 2 + k // 2)
            stage[k, i] = flat[first : first + NF]
        return carry

    lax.fori_loop(0, 8, turn_rows, 0)
    greet(me)
    copies = []
    for k in range(1, 4):
        to = lax.rem(me + k, 4)
        copies.append(
            pltpu.make_async_remote_copy(
                src_ref=stage.at[to],
                dst_ref=out.at[pl.ds(1 + 8 * me, 8)],
                send_sem=send_sem.at[k - 1],
                recv_sem=recv_sem.at[k - 1],
                device_id=(row, to),
                device_id_type=MESH,
            )
        )
    for copy in copies:
        copy.start()
    out[pl.ds(1 + 8 * me, 8)] = stage[me]
    for copy in copies:
        copy.wait()


def frames_out_kernel(y, out, got, send_sem, recv_sem):
    me = lax.axis_index("strip")
    row = lax.axis_index("rows")
    greet(me)
    copies = []
    for k in range(1, 4):
        to = lax.rem(me + k, 4)
        copies.append(
            pltpu.make_async_remote_copy(
                src_ref=y.at[pl.ds(8 * to, 8)],
                dst_ref=got.at[me],
                send_sem=send_sem.at[k - 1],
                recv_sem=recv_sem.at[k - 1],
                device_id=(row, to),
                device_id_type=MESH,
            )
        )
    for copy in copies:
        copy.start()
    got[me] = y[pl.ds(8 * me, 8)]
    for copy in copies:
        copy.wait()

    def turn_rows(i, carry):
        block = jnp.concatenate([got[(b % 2) * 2 + b // 2, i] for b in range(4)], axis=0)
        flat = block.T.astype(out.dtype)
        for p in range(2):
            for c in range(3):
                first = 64 * (3 * p + c)
                out[c, 2 * i + p] = flat[first : first + 64]
        return carry

    lax.fori_loop(0, 8, turn_rows, 0)


def frames_in(block, ident):
    return pl.pallas_call(
        frames_in_kernel,
        out_shape=jax.ShapeDtypeStruct((34, NF, 384), BF),
        in_specs=VM(1),
        out_specs=VM(1)[0],
        scratch_shapes=[
            pltpu.VMEM((4, 8, NF, 384), BF),
            pltpu.SemaphoreType.DMA((3,)),
            pltpu.SemaphoreType.DMA((3,)),
        ],
        compiler_params=pltpu.CompilerParams(
            collective_id=ident, has_side_effects=True, vmem_limit_bytes=32 * MIB
        ),
        name="frames_in",
    )(jnp.transpose(block, (1, 2, 3, 0)))


def frames_out(pairs, dtype, ident):
    flat = pl.pallas_call(
        frames_out_kernel,
        out_shape=jax.ShapeDtypeStruct((3, 16, 64, 256), dtype),
        in_specs=VM(1),
        out_specs=VM(1)[0],
        scratch_shapes=[
            pltpu.VMEM((4, 8, NF, 384), BF),
            pltpu.SemaphoreType.DMA((3,)),
            pltpu.SemaphoreType.DMA((3,)),
        ],
        compiler_params=pltpu.CompilerParams(
            collective_id=ident, has_side_effects=True, vmem_limit_bytes=32 * MIB
        ),
        name="frames_out",
    )(pairs)
    return jnp.transpose(flat, (3, 0, 1, 2))


def across(value):
    return lax.ppermute(value, "strip", [(0, 2), (2, 0), (1, 3), (3, 1)])


def beside(value):
    return lax.ppermute(value, "strip", [(0, 1), (1, 0), (2, 3), (3, 2)])


def pair_total(partial_value):
    low = partial_value.astype(BF)
    got = across(low)
    half = low.shape[0] // 2
    got = jnp.concatenate([got[half:], got[:half]], axis=0)
    return low.astype(F32) + got.astype(F32)


def fold(full, axis):
    half = full.shape[axis] // 2
    own = lax.slice_in_dim(full, 0, half, axis=axis)
    other = lax.slice_in_dim(full, half, 2 * half, axis=axis)
    return own + beside(other.astype(BF)).astype(F32)


def with_sibling(shard, axis):
    return jnp.concatenate([shard, beside(shard)], axis=axis)


def normalize(hidden):
    centred = hidden - jnp.mean(hidden, -1, keepdims=True)
    scale_inv = lax.rsqrt(jnp.mean(centred * centred, -1, keepdims=True) + EPS)
    return (centred * scale_inv, scale_inv)


def normalize_back(grad_normed, unit_rows, scale_inv, gain):
    grad_unit = grad_normed * gain
    grad_gain = jnp.sum(grad_normed * unit_rows, 0)
    grad_rows = scale_inv * (
        grad_unit
        - jnp.mean(grad_unit, -1, keepdims=True)
        - unit_rows * jnp.mean(grad_unit * unit_rows, -1, keepdims=True)
    )
    return (grad_gain, grad_rows)


def grouped_softmax(logits):
    frame_count = logits.shape[0]
    grouped = logits.reshape(frame_count, -1, LCLASS)
    shifted = grouped - jnp.max(grouped, -1, keepdims=True)
    raised = jnp.exp(shifted)
    return (raised / jnp.sum(raised, -1, keepdims=True)).reshape(frame_count, -1)


def make_mask(segment_ids):
    places = jnp.arange(segment_ids.shape[1])
    causal = places[:, None] >= places[None, :]
    return causal[None] & (segment_ids[:, :, None] == segment_ids[:, None, :])


def split_heads(flat_rows, sequences):
    return flat_rows.reshape(sequences, -1, flat_rows.shape[-1] // HEAD_DIM, HEAD_DIM)


def score_block(queries, keys_part, allowed):
    scores = (
        jnp.einsum("bqhe,bkhe->bhqk", queries, keys_part, preferred_element_type=F32) * SCALE
    )
    return jnp.where(allowed[:, None], scores, NEG)


def mm(a, b):
    return jnp.dot(a, b, preferred_element_type=F32)


def mm_t(a, b):
    return lax.dot_general(a, b, (((1,), (1,)), ((), ())), preferred_element_type=F32)


def t_mm(a, b):
    return lax.dot_general(a, b, (((0,), (0,)), ((), ())), preferred_element_type=F32)


def layer_forward(hidden, allowed, gain_pair, qkv_layer, out_layer, up_layer, down_layer):
    sequences = allowed.shape[0]
    unit_attn, inv_attn = normalize(hidden)
    normed_attn = (unit_attn * gain_pair[0]).astype(BF)
    mixed = [mm(normed_attn, qkv_layer[:, k]).astype(BF) for k in range(3)]
    queries, keys_part, vals_part = [split_heads(part, sequences) for part in mixed]
    scores = score_block(queries, keys_part, allowed)
    top_score = jnp.max(scores, -1, keepdims=True)
    raised = jnp.exp(scores - top_score)
    chances = raised / jnp.sum(raised, -1, keepdims=True)
    attended = jnp.einsum(
        "bhqk,bkhe->bqhe", chances.astype(BF), vals_part, preferred_element_type=F32
    )
    attended = attended.astype(BF).reshape(hidden.shape[0], -1)
    middle = hidden + pair_total(mm(attended, out_layer))
    unit_ffn, inv_ffn = normalize(middle)
    normed_ffn = (unit_ffn * gain_pair[1]).astype(BF)
    before = mm(normed_ffn, up_layer)
    inner_act = (before * sig(before)).astype(BF)
    result = middle + pair_total(mm(inner_act, down_layer))
    kept = (
        unit_attn,
        inv_attn,
        normed_attn,
        (queries, keys_part, vals_part),
        chances,
        attended,
        unit_ffn,
        inv_ffn,
        normed_ffn,
        before,
        inner_act,
    )
    return (result, kept)


def layer_backward(
    grad_hidden, allowed, gain_pair, qkv_layer, out_layer, up_layer, down_layer, kept
):
    (
        unit_attn,
        inv_attn,
        normed_attn,
        mixed,
        chances,
        attended,
        unit_ffn,
        inv_ffn,
        normed_ffn,
        before,
        inner_act,
    ) = kept
    token_count = grad_hidden.shape[0]
    grad_low = grad_hidden.astype(BF)
    grad_down = t_mm(inner_act, grad_low)
    grad_inner = mm_t(grad_low, down_layer)
    squash = sig(before)
    grad_before = (grad_inner * (squash * (1.0 + before * (1.0 - squash)))).astype(BF)
    grad_up = t_mm(normed_ffn, grad_before)
    grad_normed = pair_total(mm_t(grad_before, up_layer))
    gain_ffn, grad_mid = normalize_back(grad_normed, unit_ffn, inv_ffn, gain_pair[1])
    grad_middle = grad_hidden + grad_mid
    middle_low = grad_middle.astype(BF)
    grad_project = t_mm(attended, middle_low)
    sequences = allowed.shape[0]
    grad_attended = split_heads(mm_t(middle_low, out_layer).astype(BF), sequences)
    queries, keys_part, vals_part = mixed
    grad_vals = jnp.einsum(
        "bhqk,bqhe->bkhe", chances.astype(BF), grad_attended, preferred_element_type=F32
    )
    grad_chances = jnp.einsum(
        "bqhe,bkhe->bhqk", grad_attended, vals_part, preferred_element_type=F32
    )
    weighted_total = jnp.sum(chances * grad_chances, -1, keepdims=True)
    grad_scores = (chances * (grad_chances - weighted_total)).astype(BF)
    grad_queries = SCALE * jnp.einsum(
        "bhqk,bkhe->bqhe", grad_scores, keys_part, preferred_element_type=F32
    )
    grad_keys = SCALE * jnp.einsum(
        "bhqk,bqhe->bkhe", grad_scores, queries, preferred_element_type=F32
    )
    grad_mixed = [
        part.reshape(token_count, -1).astype(BF) for part in (grad_queries, grad_keys, grad_vals)
    ]
    grad_qkv = jnp.stack([t_mm(normed_attn, part) for part in grad_mixed])
    grad_normed_attn = pair_total(
        sum(mm_t(part, qkv_layer[:, k]) for k, part in enumerate(grad_mixed))
    )
    gain_attn, grad_first = normalize_back(grad_normed_attn, unit_attn, inv_attn, gain_pair[0])
    return (
        grad_middle + grad_first,
        jnp.stack([gain_attn, gain_ffn]),
        grad_qkv,
        grad_project,
        grad_up,
        grad_down,
    )


def rows_total(parts):
    count = lax.axis_size("rows")
    flat = jnp.concatenate([part.astype(BF) for part in parts], axis=0)
    total = flat.shape[0]
    flat = jnp.pad(flat, ((0, -total % (16 * count)), (0, 0)))
    share = lax.psum_scatter(flat, "rows", scatter_dimension=0, tiled=True)
    whole = lax.all_gather(share, "rows", axis=0, tiled=True)
    pieces = []
    offset = 0
    for part in parts:
        pieces.append(whole[offset : offset + part.shape[0]])
        offset = offset + part.shape[0]
    return pieces


def pack_kernels(outer, first, second, third):
    parts = [
        jnp.concatenate([third[:, :, :256], third[:, :, 256:]], axis=1).reshape(2048, 256),
        second.reshape(512, 256),
        jnp.concatenate([first[:2], first[2:]], axis=2).reshape(128, 256),
        jnp.pad(outer.reshape(6, 256), ((0, 122), (0, 0))),
    ]
    return jnp.concatenate(parts, axis=0)


def unpack_kernels(flat):
    third = flat[:2048].reshape(4, 512, 256)
    third = jnp.concatenate([third[:, :256], third[:, 256:]], axis=2)
    second = flat[2048:2560].reshape(4, 128, 256)
    first = flat[2560:2688].reshape(2, 64, 256)
    first = jnp.concatenate([first[:, :, :128], first[:, :, 128:]], axis=0)
    outer = flat[2688:2694].reshape(4, 3, 4, 32)
    return (outer, first, second, third)


def strip_share(flat, x, core):
    half = flat.shape[0] // 2
    low = flat.astype(BF)
    mine = lax.dynamic_slice_in_dim(low, core * half, half)
    theirs = lax.dynamic_slice_in_dim(low, (1 - core) * half, half)
    summed = mine.astype(F32) + beside(theirs).astype(F32)
    low = summed.astype(BF)
    half = half // 2
    mine = lax.dynamic_slice_in_dim(low, x * half, half)
    theirs = lax.dynamic_slice_in_dim(low, (1 - x) * half, half)
    return mine.astype(F32) + across(theirs).astype(F32)


def strip_whole(share, x, core):
    got = across(share)
    half = jnp.where(
        x == 0, jnp.concatenate([share, got]), jnp.concatenate([got, share])
    )
    got = beside(half)
    return jnp.where(
        core == 0, jnp.concatenate([half, got]), jnp.concatenate([got, half])
    )


def features_first(weight):
    return weight.reshape(256, 16, -1).transpose(1, 0, 2).reshape(weight.shape)


def channels_first(weight):
    return weight.reshape(16, 256, -1).transpose(1, 0, 2).reshape(weight.shape)


def shards(
    frames,
    segment_ids,
    encode_one,
    encode_two,
    encode_three,
    encode_four,
    latent_head,
    token_embed,
    positions,
    norm_gains,
    qkv_weight,
    out_weight,
    up_weight,
    down_weight,
    decode_head,
    decode_one,
    decode_two,
    decode_three,
    decode_four,
    token_cotangent,
    frame_cotangent,
):
    strip = lax.axis_index("strip")
    x, core = strip // 2, strip % 2
    layers = qkv_weight.shape[0]

    enc = [w.transpose(2, 3, 1, 0) for w in (encode_one, encode_two, encode_three, encode_four)]
    dec = [
        jnp.flip(w, (2, 3)).transpose(2, 3, 0, 1)
        for w in (decode_four, decode_three, decode_two, decode_one)
    ]
    folds = (4, 2, 1)
    enc_a = outer_A(enc[0])
    dec_a = outer_A(dec[0])
    enc_b, dec_b = outer_B(enc_a), outer_B(dec_a)
    enc_a, dec_a = enc_a.reshape(1152, 1024), dec_a.reshape(1152, 1024)
    enc_t = [canon_T(w, a) for w, a in zip(enc[1:], folds)]
    dec_t = [canon_T(w, a) for w, a in zip(dec[1:], folds)]
    enc_u = [canon_U(t, a) for t, a in zip(enc_t, folds)]
    dec_u = [canon_U(t, a) for t, a in zip(dec_t, folds)]
    enc_t = [t.reshape(2048, 256) for t in enc_t]
    dec_t = [t.reshape(2048, 256) for t in dec_t]

    head_in = with_sibling(features_first(latent_head), 1)
    head_out = with_sibling(features_first(decode_head.T), 1)
    embed = with_sibling(token_embed, 0)
    qkv = with_sibling(qkv_weight, 3)
    project = with_sibling(out_weight, 1)
    widen = with_sibling(up_weight, 2)
    narrow = with_sibling(down_weight, 1)

    pixels = frames_in(frames, 1)
    z1, z2, z3, z4, feat = enc_fwd(pixels, enc_a, *enc_t)
    feat = jnp.concatenate([feat, across(feat)], axis=1)
    head_in4 = head_in.reshape(4, 1024, 512)
    logits = sum(mm(feat[h], head_in4[h]) for h in range(4))
    chances = grouped_softmax(logits)
    latent = chances.astype(BF)

    head_out4 = head_out.reshape(4, 1024, 512)
    spread = jnp.stack([mm_t(latent, head_out4[h]) for h in range(4)]).astype(BF)
    decoded = (
        spread[:, :NF].astype(F32) + across(spread[:, NF:]).astype(F32)
    ).astype(BF)
    recon_pairs, p3, p2, p1 = dec_fwd(decoded, dec_u[2], dec_u[1], dec_u[0], dec_b)
    recon = frames_out(recon_pairs, BF, 3)

    first = 2 * core
    def mine(array, size):
        own = lax.dynamic_slice_in_dim(array, (first + x) * size, size)
        other = lax.dynamic_slice_in_dim(array, (first + 1 - x) * size, size)
        return jnp.concatenate([own, other], axis=0)
    segments = mine(segment_ids, 1)
    allowed = make_mask(segments)
    embedded = pair_total(mm(latent, embed))
    hidden = embedded.reshape(2, NF, -1) + positions.astype(F32)[None]
    hidden = hidden.reshape(2 * NF, -1)
    kept_layers = []
    for k in range(layers):
        hidden, kept = layer_forward(
            hidden, allowed, norm_gains[k], qkv[k], project[k], widen[k], narrow[k]
        )
        kept_layers.append(kept)
    tokens = hidden.astype(BF)
    tokens = jnp.where(
        x == 0, tokens, jnp.concatenate([tokens[NF:], tokens[:NF]], axis=0)
    )
    other_tokens = beside(tokens)
    tokens_out = jnp.where(
        core == 0,
        jnp.concatenate([tokens, other_tokens]),
        jnp.concatenate([other_tokens, tokens]),
    )
    grad_hidden = mine(token_cotangent, NF).astype(F32)
    layer_grads = [None] * layers
    for k in reversed(range(layers)):
        grad_hidden, *layer_grads[k] = layer_backward(
            grad_hidden,
            allowed,
            norm_gains[k],
            qkv[k],
            project[k],
            widen[k],
            narrow[k],
            kept_layers[k],
        )
    gains, g_qkv, g_project, g_widen, g_narrow = [
        jnp.stack([entry[slot] for entry in layer_grads]) for slot in range(5)
    ]
    g_positions = grad_hidden[:NF] + grad_hidden[NF:]
    embed_low = grad_hidden.astype(BF)
    g_embed = fold(t_mm(latent, embed_low), 0)
    grad_latent = mm_t(embed_low, embed)
    g_qkv = fold(g_qkv, 3)
    g_project = fold(g_project, 1)
    g_widen = fold(g_widen, 2)
    g_narrow = fold(g_narrow, 1)
    small = jnp.concatenate([g_positions, gains.reshape(-1, 512)], axis=0)
    small = small + beside(small.astype(BF)).astype(F32)

    hints = frames_in(frame_cotangent, 2)
    g_decoded, h2, h3, h4, h_outer = dec_bwd(hints, decoded, p3, p2, p1, dec_a, *dec_t)
    g_spread = jnp.concatenate([g_decoded, across(g_decoded)], axis=1)
    g_head_out = fold(jnp.concatenate([t_mm(g_spread[h], latent) for h in range(4)]), 1)
    grad_latent = grad_latent + sum(mm(g_spread[h], head_out4[h]) for h in range(4))
    dec_flat = pack_kernels(
        red_to_we(h_outer),
        gt_to_we(h2, 4, 32, 64),
        gt_to_we(h3, 2, 64, 128),
        gt_to_we(h4, 1, 128, 256),
    )
    dec_share = strip_share(dec_flat, x, core)

    early_wide = rows_total(
        [
            g_widen.reshape(-1, 512),
            g_narrow.reshape(-1, 512),
            g_project.reshape(-1, 512),
            g_embed,
            small,
        ]
    )
    qkv_rows = jnp.concatenate([g_qkv[0], g_qkv[1]], axis=-1).reshape(-1, 256)
    early = rows_total([g_head_out, qkv_rows, dec_share])

    grouped = chances.reshape(2 * NF, -1, LCLASS)
    grad_grouped = grad_latent.reshape(grouped.shape)
    grad_logits = grouped * (grad_grouped - jnp.sum(grouped * grad_grouped, -1, keepdims=True))
    grad_logits = grad_logits.reshape(2 * NF, -1).astype(BF)
    g_head_in = fold(jnp.concatenate([t_mm(feat[h], grad_logits) for h in range(4)]), 1)
    g_feat = jnp.stack([mm_t(grad_logits, head_in4[h]) for h in range(4)]).astype(BF)
    g_feat = (g_feat[:, :NF].astype(F32) + across(g_feat[:, NF:]).astype(F32)).astype(BF)
    d_pairs, e2, e3, e4, e_outer = enc_bwd(pixels, z1, z2, z3, z4, g_feat, *enc_u, enc_b)
    frames_grad = frames_out(d_pairs, F32, 4)
    enc_flat = pack_kernels(
        red_to_we(e_outer),
        gt_to_we(e2, 4, 32, 64),
        gt_to_we(e3, 2, 64, 128),
        gt_to_we(e4, 1, 128, 256),
    )
    enc_share = strip_share(enc_flat, x, core)
    late = rows_total([g_head_in, enc_share])

    def of_encoder(part, c, o):
        return part.astype(F32).reshape(4, o, 4, c).transpose(1, 3, 0, 2)

    def of_decoder(part, c, o):
        return jnp.flip(part.astype(F32).reshape(4, o, 4, c), (0, 2)).transpose(3, 1, 0, 2)

    k1, k2, k3, k4 = unpack_kernels(strip_whole(late[1], x, core))
    j1, j2, j3, j4 = unpack_kernels(strip_whole(early[2], x, core))
    r_qkv = early[1].astype(F32).reshape(3, 512, 2, 128).transpose(2, 1, 0, 3)
    return (
        tokens_out,
        recon,
        frames_grad,
        k1.astype(F32).transpose(3, 1, 0, 2),
        of_encoder(k2, 32, 64),
        of_encoder(k3, 64, 128),
        of_encoder(k4, 128, 256),
        channels_first(late[0].astype(F32)),
        early_wide[3].astype(F32),
        early_wide[4][:NF].astype(F32),
        early_wide[4][NF:].astype(F32).reshape(norm_gains.shape),
        r_qkv,
        early_wide[2].astype(F32).reshape(out_weight.shape),
        early_wide[0].astype(F32).reshape(up_weight.shape),
        early_wide[1].astype(F32).reshape(down_weight.shape),
        channels_first(early[0].astype(F32)).T,
        of_decoder(j4, 128, 256),
        of_decoder(j3, 64, 128),
        of_decoder(j2, 32, 64),
        jnp.flip(j1.astype(F32), (0, 2)).transpose(1, 3, 0, 2),
    )


def solution(mesh):
    placed = (
        P("rows", None, "strip", None),
        P("rows", None),
        P(),
        P(),
        P(),
        P(),
        P(None, "strip"),
        P("strip", None),
        P(),
        P(),
        P(None, None, None, "strip"),
        P(None, "strip", None),
        P(None, None, "strip"),
        P(None, "strip", None),
        P("strip", None),
        P(),
        P(),
        P(),
        P(),
        P("rows", None),
        P("rows", None, "strip", None),
    )
    return jax.shard_map(
        shards,
        mesh=mesh,
        in_specs=placed,
        out_specs=(
            P("rows", None),
            P("rows", None, "strip", None),
            P("rows", None, "strip", None),
            P(),
            P(),
            P(),
            P(),
            P(None, "strip"),
            P("strip", None),
            P(),
            P(),
            P(None, None, None, "strip"),
            P(None, "strip", None),
            P(None, None, "strip"),
            P(None, "strip", None),
            P("strip", None),
            P(),
            P(),
            P(),
            P(),
        ),
        check_vma=False,
    )
```

time: 3270 us -> 972 us (0.30); the launches traced: 3230 us -> 965 us
  local copies, waits for them, and re-layouts: 1070 us -> 230 us
  blocking collectives: 809 us -> 0 us
  matrix products: 483 us -> 62.5 us
  waiting for transfers between devices: 537 us -> 304 us
  Pallas kernels: 0 us -> 211 us
  starting transfers between devices: 176 us -> 25.9 us
    unnamed x1 -> x0, blocking collectives: 800 us -> none
    reshape x27 -> x16, local copies, waits for them, and re-layouts: 427 us -> 12.1 us  [the longest x1 4.44 us: channels_first(): return weight.reshape(16, 256, -1).transpose(1, 0, 2).reshape(weight.shape)]
    dot_general x173 -> x69, matrix products: 289 us -> 53.3 us  [the longest x21 16.9 us: mm_t(): lax.dot_general(a, b, (((1,), (1,)), ((), ())), preferred_element_type=F32)]
    pad x4 -> x1, local copies, waits for them, and re-layouts: 218 us -> 1.71 us  [rows_total(): flat = jnp.pad(flat, ((0, -total % (16 * count)), (0, 0)))]
    psum x9 -> x0, waiting for transfers between devices: 211 us -> none  [strip_total(): lax.psum(partial_value.astype(jnp.bfloat16), 'strip').astype(jnp.float32)]
    pallas_call x0 -> x8, Pallas kernels: none -> 211 us  [the longest x4 130 us: run(): pl.pallas_call(kernel, out_shape=outs, in_specs=VM(len(args)), out_specs=...]
    conv_general_dilated x23 -> x0, matrix products: 176 us -> none  [the longest x7 68.6 us: decode_apply(): lax.conv_general_dilated(extended, weight, (1, 1), ((0, 0), (2, 2)), lhs_...]
    all_gather x4 -> x3, waiting for transfers between devices: 280 us -> 105 us  [rows_total(): whole = lax.all_gather(share, 'rows', axis=0, tiled=True)]
  transfers between devices with their start and end apart: 64 -> 43, of which waited for: 24 -> 16; matrix products, arithmetic and copies ran while one was open for 28% -> 31% of each run, Pallas kernels for 0% -> 17%
where the time goes in v1:
time: 972 us; the launch traced here: 965 us
  waiting for transfers between devices  304 us (31%)
  local copies, waits for them, and re-layouts  230 us (24%)
  Pallas kernels  211 us (22%)
  other arithmetic  114 us (12%)
  matrix products  62.5 us (6%)
  starting transfers between devices  25.9 us (3%)
  between operations  18 us (2%)
    reduce_scatter x3, waiting for transfers between devices, rows_total(): share = lax.psum_scatter(flat, 'rows', scatter_dimension=0, tiled=True)  164 us
    pallas_call x4, Pallas kernels, run(): pl.pallas_call(kernel, out_shape=outs, in_specs=VM(len(args)), out_specs=...  130 us
    all_gather x3, waiting for transfers between devices, rows_total(): whole = lax.all_gather(share, 'rows', axis=0, tiled=True)  105 us
    unnamed x471, local copies, waits for them, and re-layouts  64.9 us
    pallas_call x2, Pallas kernels, frames_out(): pl.pallas_call(frames_out_kernel, out_shape=jax.ShapeDtypeStruct((3, 16,...  40.4 us
    pallas_call x2, Pallas kernels, frames_in(): pl.pallas_call(frames_in_kernel, out_shape=jax.ShapeDtypeStruct((34, NF,...  40.1 us
    ppermute x17, waiting for transfers between devices, across(): return lax.ppermute(value, 'strip', [(0, 2), (2, 0), (1, 3), (3, 1)])  34.7 us
  transfers between devices with their start and end apart: 43, of which 16 were waited for; matrix products, arithmetic and copies ran while one was open for 31% of the time, Pallas kernels for 17%

profile of v1, /device:TPU:0, one launch (start us, length us, event | category | flops | bytes accessed | tf_op | source)
XLA Modules:
  0.0 964.9 jit_solution(17533468876378668715)
XLA Ops:
  18.0 2.8 copy.322
  25.4 21.2 %frames_in.2.xp = bf16[34,64,384]{2,1,0:T(8,128)(2,1)S(1)} custom-call(bf16[3,16,64,256]{3,2,1,0:T(8,128)(2,1)S(1)} %bitcast.530), custom_call_target="tpu_custom_call" | custom-call | tf_op jit(solution)/shard_map/frames_in/pallas_call | solution.py:345
  49.4 21.8 %encode.1 = (bf16[32,64,1024]{2,1,0:T(8,128)(2,1)}, bf16[16,64,1024]{2,1,0:T(8,128)(2,1)}, bf16[8,64,1024]{2,1,0:T(8,128)(2,1)}, bf16[4,64,1024]{2,1,0:T(8,128)(2,1)}, bf16[4,64,1024]{2,1,0:T(8,128)(2,1)}) custom-call(bf16[34,64,384]{2,1,0:T(8,128)(2,1)} %copy-done.3, bf16[1152,1024]{1,0:T(8,128)(2,1)} %bitcast.558, bf16[2048,256]{1,0:T(8,128)(2,1)} %bitcast.572, ...), custom_call_target="tpu_custom_call" | custom-call | flops 10000000000 | bytes 20971520 | tf_op jit(solution)/shard_map/encode/pallas_call | solution.py:240
  76.6 4.9 rev.32
  142.4 4.1 copy.348
  146.5 3.7 copy.349
  156.3 18.8 %frames_in.3.cp = bf16[34,64,384]{2,1,0:T(8,128)(2,1)S(1)} custom-call(bf16[3,16,64,256]{3,2,1,0:T(8,128)(2,1)S(1)} %bitcast.531), custom_call_target="tpu_custom_call" | custom-call | tf_op jit(solution)/shard_map/frames_in/pallas_call | solution.py:345
  216.2 3.4 collective-permute-done.6
  224.3 2.8 collective-permute-done.9
  243.2 24.0 %decode.1 = (bf16[32,64,384]{2,1,0:T(8,128)(2,1)}, bf16[8,64,1024]{2,1,0:T(8,128)(2,1)}, bf16[16,64,1024]{2,1,0:T(8,128)(2,1)}, bf16[32,64,1024]{2,1,0:T(8,128)(2,1)}) custom-call(bf16[4,64,1024]{2,1,0:T(8,128)(2,1)} %add_convert_fusion.3.dec, bf16[2,1536,256]{2,1,0:T(8,128)(2,1)} %pad_maximum_fusion.7.u4, bf16[2,1024,256]{2,1,0:T(8,128)(2,1)} %pad_maximum_fusion.13.u3, ...), custom_call_target="tpu_custom_call" | custom-call | flops 10000000000 | bytes 20971520 | tf_op jit(solution)/shard_map/decode/pallas_call | solution.py:240
  267.2 41.2 %decode_back.1 = (bf16[4,64,1024]{2,1,0:T(8,128)(2,1)}, f32[4,256,512]{2,1,0:T(8,128)}, f32[4,256,512]{2,1,0:T(8,128)}, f32[4,256,512]{2,1,0:T(8,128)}, f32[3,32,384]{2,1,0:T(8,128)}) custom-call(bf16[34,64,384]{2,1,0:T(8,128)(2,1)} %copy-done.4, bf16[4,64,1024]{2,1,0:T(8,128)(2,1)} %add_convert_fusion.3.dec, bf16[8,64,1024]{2,1,0:T(8,128)(2,1)} %get-tuple-element.45.p3, ...), custom_call_target="tpu_custom_call" | custom-call | flops 10000000000 | bytes 20971520 | tf_op jit(solution)/shard_map/decode_back/pallas_call | solution.py:240
  410.2 3.3 copy-done.9
  418.3 43.3 %encode_back.1 = (bf16[32,64,384]{2,1,0:T(8,128)(2,1)}, f32[4,256,512]{2,1,0:T(8,128)}, f32[4,256,512]{2,1,0:T(8,128)}, f32[4,256,512]{2,1,0:T(8,128)}, f32[3,32,384]{2,1,0:T(8,128)}) custom-call(bf16[34,64,384]{2,1,0:T(8,128)(2,1)} %copy-done.3, bf16[32,64,1024]{2,1,0:T(8,128)(2,1)} %get-tuple-element.41.z1, bf16[16,64,1024]{2,1,0:T(8,128)(2,1)} %get-tuple-element.42.z2, ...), custom_call_target="tpu_custom_call" | custom-call | flops 10000000000 | bytes 20971520 | tf_op jit(solution)/shard_map/encode_back/pallas_call | solution.py:240
  472.5 8.4 collective-permute-done.23
  520.8 9.4 collective-permute-done.34
  531.4 13.6 %fusion.12 = bf16[6400,256]{1,0:T(8,128)(2,1)} fusion(bf16[704,256]{1,0:T(8,128)(2,1)S(1)} %add_convert_fusion.4, bf16[4096,256]{1,0:T(8,128)(2,1)S(1)} %fusion.9, bf16[1536,128]{1,0:T(8,128)(2,1)S(1)} %bitcast.566, bf16[1536,128]{1,0:T(8,128)(2,1)S(1)} %bitcast.565), kind=kLoop, calls=%fused_computation.37 | loop fusion | flops 21299200 | bytes 6520832 | tf_op jit(solution)/shard_map/concatenate | solution.py:563
  545.0 10.8 %reduce-scatter.4.cloned.1.call-done = bf16[608,256]{1,0:T(8,128)(2,1)} async-done(((bf16[4864,256]{1,0:T(8,128)(2,1)}), bf16[608,256]{1,0:T(8,128)(2,1)}) %reduce-scatter.4.cloned.1.call-update) | async-done | bytes 311312 | tf_op jit(solution)/shard_map/reduce_scatter | solution.py:566
  555.9 74.1 %reduce-scatter.6.cloned.1.call-done = bf16[336,512]{1,0:T(8,128)(2,1)} async-done(((bf16[2688,512]{1,0:T(8,128)(2,1)}), bf16[336,512]{1,0:T(8,128)(2,1)}) %reduce-scatter.6.cloned.1.call-update) | async-done | bytes 344080 | tf_op jit(solution)/shard_map/reduce_scatter | solution.py:566
  630.2 79.6 %reduce-scatter.8.cloned.1.call-done = bf16[800,256]{1,0:T(8,128)(2,1)} async-done(((bf16[6400,256]{1,0:T(8,128)(2,1)}), bf16[800,256]{1,0:T(8,128)(2,1)}) %reduce-scatter.8.cloned.1.call-update) | async-done | bytes 409616 | tf_op jit(solution)/shard_map/reduce_scatter | solution.py:566
  710.0 19.8 %frames_out.2 = bf16[3,16,64,256]{3,2,1,0:T(8,128)(2,1)S(1)} custom-call(bf16[32,64,384]{2,1,0:T(8,128)(2,1)S(1)} %copy-done.7), custom_call_target="tpu_custom_call" | custom-call | tf_op jit(solution)/shard_map/frames_out/pallas_call | solution.py:363
  732.1 20.6 %frames_out.3 = f32[3,16,64,256]{3,2,1,0:T(8,128)S(1)} custom-call(bf16[32,64,384]{2,1,0:T(8,128)(2,1)S(1)} %copy-done.8), custom_call_target="tpu_custom_call" | custom-call | tf_op jit(solution)/shard_map/frames_out/pallas_call | solution.py:363
  752.7 11.5 %all-gather.4.cloned.1.call-done = bf16[4864,256]{1,0:T(8,128)(2,1)} async-done(((bf16[608,256]{1,0:T(8,128)(2,1)}), bf16[4864,256]{1,0:T(8,128)(2,1)}) %all-gather.4.cloned.1.call-update) | async-done | bytes 2490384 | tf_op jit(solution)/shard_map/all_gather | solution.py:567
  766.8 54.1 %all-gather.6.cloned.1.call-done = bf16[2688,512]{1,0:T(8,128)(2,1)} async-done(((bf16[336,512]{1,0:T(8,128)(2,1)}), bf16[2688,512]{1,0:T(8,128)(2,1)}) %all-gather.6.cloned.1.call-update) | async-done | bytes 2752528 | tf_op jit(solution)/shard_map/all_gather | solution.py:567
  835.5 4.4 copy.407
  844.2 39.3 %all-gather.8.cloned.1.call-done = bf16[6400,256]{1,0:T(8,128)(2,1)} async-done(((bf16[800,256]{1,0:T(8,128)(2,1)}), bf16[6400,256]{1,0:T(8,128)(2,1)}) %all-gather.8.cloned.1.call-update) | async-done | bytes 3276816 | tf_op jit(solution)/shard_map/all_gather | solution.py:567
  907.9 3.5 convert_bitcast_fusion.3
  913.0 3.2 copy.413
  916.2 5.6 copy.422
  924.2 3.1 reshape.558
  927.3 2.7 copy.473
  941.6 2.7 copy.423
  953.4 2.7 copy.489
  (960 shorter events, 382.6 us)
Async XLA Ops:
  7.2 548.6 %reduce-scatter.4.cloned.1.call-start = ((), (), s32[]{:S(2)}) async-start(), calls=%async_computation.3 | async-start | bytes 2801664 | tf_op jit(solution)/shard_map/reduce_scatter | solution.py:566
  71.1 112.0 %collective-permute-start = (bf16[4,64,1024]{2,1,0:T(8,128)(2,1)}, bf16[4,64,1024]{2,1,0:T(8,128)(2,1)}, u32[]{:S(2)}, u32[]{:S(2)}) collective-permute-start(bf16[4,64,1024]{2,1,0:T(8,128)(2,1)} %get-tuple-element.39), channel_id=1, source_target_pairs={{0,2},{2,0},{1,3},{3,1},{4,6},{6,4},{5,7},{7,5},{8,10},{10,8},{9,1... | collective-permute-start | bytes 1572872 | tf_op jit(solution)/shard_map/ppermute | solution.py:382
  73.6 116.8 %collective-permute-start.1 = (bf16[4096,256]{1,0:T(8,128)(2,1)}, bf16[4096,256]{1,0:T(8,128)(2,1)}, u32[]{:S(2)}, u32[]{:S(2)}) collective-permute-start(bf16[4096,256]{1,0:T(8,128)(2,1)} %bitcast.22), channel_id=1, source_target_pairs={{0,1},{1,0},{2,3},{3,2},{4,5},{5,4},{6,7},{7,6},{8,9},{9,8},{10,11... | collective-permute-start | bytes 6291464 | tf_op jit(solution)/shard_map/ppermute | solution.py:386
  75.2 101.1 %collective-permute-start.2 = (bf16[256,512]{1,0:T(8,128)(2,1)}, bf16[256,512]{1,0:T(8,128)(2,1)}, u32[]{:S(2)}, u32[]{:S(2)}) collective-permute-start(bf16[256,512]{1,0:T(8,128)(2,1)} %param.28), channel_id=1, source_target_pairs={{0,1},{1,0},{2,3},{3,2},{4,5},{5,4},{6,7},{7,6},{8,9},{9,8},{10,11... | collective-permute-start | bytes 786440 | tf_op jit(solution)/shard_map/ppermute | solution.py:386
  75.2 109.3 %collective-permute-start.4 = (bf16[2,512,3,128]{3,1,2,0:T(8,128)(2,1)}, bf16[2,512,3,128]{3,1,2,0:T(8,128)(2,1)}, u32[]{:S(2)}, u32[]{:S(2)}) collective-permute-start(bf16[2,512,3,128]{3,1,2,0:T(8,128)(2,1)} %param.31), channel_id=1, source_target_pairs={{0,1},{1,0},{2,3},{3,2},{4,5},{5,4},{6,7},{7,6},{8,9},{9,8},{10,11... | collective-permute-start | bytes 2359304 | tf_op jit(solution)/shard_map/ppermute | solution.py:386
  75.7 103.7 %collective-permute-start.5 = (bf16[2,128,512]{2,1,0:T(8,128)(2,1)}, bf16[2,128,512]{2,1,0:T(8,128)(2,1)}, u32[]{:S(2)}, u32[]{:S(2)}) collective-permute-start(bf16[2,128,512]{2,1,0:T(8,128)(2,1)} %param.32), channel_id=1, source_target_pairs={{0,1},{1,0},{2,3},{3,2},{4,5},{5,4},{6,7},{7,6},{8,9},{9,8},{10,11... | collective-permute-start | bytes 786440 | tf_op jit(solution)/shard_map/ppermute | solution.py:386
  176.3 11.2 %collective-permute-start.7 = (bf16[2,512,512]{2,1,0:T(8,128)(2,1)}, bf16[2,512,512]{2,1,0:T(8,128)(2,1)S(1)}, u32[]{:S(2)}, u32[]{:S(2)}) collective-permute-start(bf16[2,512,512]{2,1,0:T(8,128)(2,1)} %param.33), channel_id=1, source_target_pairs={{0,1},{1,0},{2,3},{3,2},{4,5},{5,4},{6,7},{7,6},{8,9},{9,8},{10,11... | collective-permute-start | bytes 3145736 | tf_op jit(solution)/shard_map/ppermute | solution.py:386
  179.4 8.3 collective-permute-start.8
  183.1 13.6 %collective-permute-start.13 = (bf16[4096,256]{1,0:T(8,128)(2,1)}, bf16[4096,256]{1,0:T(8,128)(2,1)}, u32[]{:S(2)}, u32[]{:S(2)}) collective-permute-start(bf16[4096,256]{1,0:T(8,128)(2,1)} %bitcast.53), channel_id=1, source_target_pairs={{0,1},{1,0},{2,3},{3,2},{4,5},{5,4},{6,7},{7,6},{8,9},{9,8},{10,11... | collective-permute-start | bytes 6291464 | tf_op jit(solution)/shard_map/ppermute | solution.py:386
  223.7 17.4 %collective-permute-start.14 = (bf16[4,64,1024]{2,1,0:T(8,128)(2,1)}, bf16[4,64,1024]{2,1,0:T(8,128)(2,1)}, u32[]{:S(2)}, u32[]{:S(2)}) collective-permute-start(bf16[4,64,1024]{2,1,0:T(8,128)(2,1)} %slice.901), channel_id=1, source_target_pairs={{0,2},{2,0},{1,3},{3,1},{4,6},{6,4},{5,7},{7,5},{8,10},{10,8},{9,1... | collective-permute-start | bytes 1572872 | tf_op jit(solution)/shard_map/ppermute | solution.py:382
  239.1 75.6 %collective-permute-start.10 = (bf16[128,512]{1,0:T(8,128)(2,1)}, bf16[128,512]{1,0:T(8,128)(2,1)}, u32[]{:S(2)}, u32[]{:S(2)}) collective-permute-start(bf16[128,512]{1,0:T(8,128)(2,1)} %convolution_convert_fusion.14), channel_id=1, source_target_pairs={{0,2},{2,0},{1,3},{3,1},{4,6},{6,4},{5,7},{7,5},{8,10},{10,8},{9,1... | collective-permute-start | bytes 393224 | tf_op jit(solution)/shard_map/ppermute | solution.py:382
  308.4 84.0 %collective-permute-start.19 = (bf16[4,64,1024]{2,1,0:T(8,128)(2,1)}, bf16[4,64,1024]{2,1,0:T(8,128)(2,1)}, u32[]{:S(2)}, u32[]{:S(2)}) collective-permute-start(bf16[4,64,1024]{2,1,0:T(8,128)(2,1)} %get-tuple-element.48), channel_id=1, source_target_pairs={{0,2},{2,0},{1,3},{3,1},{4,6},{6,4},{5,7},{7,5},{8,10},{10,8},{9,1... | collective-permute-start | bytes 1572872 | tf_op jit(solution)/shard_map/ppermute | solution.py:382
  408.1 9.2 collective-permute-start.20
  415.2 65.8 %collective-permute-start.21 = (bf16[4096,256]{1,0:T(8,128)(2,1)}, bf16[4096,256]{1,0:T(8,128)(2,1)}, u32[]{:S(2)}, u32[]{:S(2)}) collective-permute-start(bf16[4096,256]{1,0:T(8,128)(2,1)} %slice.1248), channel_id=1, source_target_pairs={{0,1},{1,0},{2,3},{3,2},{4,5},{5,4},{6,7},{7,6},{8,9},{9,8},{10,11... | collective-permute-start | bytes 6291464 | tf_op jit(solution)/shard_map/ppermute | solution.py:386
  471.3 9.6 collective-permute-start.23
  485.2 144.8 %reduce-scatter.6.cloned.1.call-start = ((), (), s32[]{:S(2)}) async-start(), calls=%async_computation.5 | async-start | bytes 3096576 | tf_op jit(solution)/shard_map/reduce_scatter | solution.py:566
  486.5 30.7 %collective-permute-start.33 = (bf16[1408,256]{1,0:T(8,128)(2,1)}, bf16[1408,256]{1,0:T(8,128)(2,1)}, u32[]{:S(2)}, u32[]{:S(2)}) collective-permute-start(bf16[1408,256]{1,0:T(8,128)(2,1)} %constant_dynamic-slice_fusion.1), channel_id=1, source_target_pairs={{0,1},{1,0},{2,3},{3,2},{4,5},{5,4},{6,7},{7,6},{8,9},{9,8},{10,11... | collective-permute-start | bytes 2162696 | tf_op jit(solution)/shard_map/ppermute | solution.py:386
  493.2 12.6 %collective-permute-start.27 = (bf16[2,512,512]{2,1,0:T(8,128)(2,1)}, bf16[2,512,512]{2,1,0:T(8,128)(2,1)}, u32[]{:S(2)}, u32[]{:S(2)}) collective-permute-start(bf16[2,512,512]{2,1,0:T(8,128)(2,1)} %fusion.33), channel_id=1, source_target_pairs={{0,1},{1,0},{2,3},{3,2},{4,5},{5,4},{6,7},{7,6},{8,9},{9,8},{10,11... | collective-permute-start | bytes 3145736 | tf_op jit(solution)/shard_map/ppermute | solution.py:386
  495.9 12.0 %collective-permute-start.26 = (bf16[2,512,512]{2,1,0:T(8,128)(2,1)}, bf16[2,512,512]{2,1,0:T(8,128)(2,1)}, u32[]{:S(2)}, u32[]{:S(2)}) collective-permute-start(bf16[2,512,512]{2,1,0:T(8,128)(2,1)} %fusion.34), channel_id=1, source_target_pairs={{0,1},{1,0},{2,3},{3,2},{4,5},{5,4},{6,7},{7,6},{8,9},{9,8},{10,11... | collective-permute-start | bytes 3145736 | tf_op jit(solution)/shard_map/ppermute | solution.py:386
  502.7 7.5 collective-permute-start.30
  511.9 197.9 %reduce-scatter.8.cloned.1.call-start = ((), (), s32[]{:S(2)}) async-start(), calls=%async_computation.7 | async-start | bytes 3686400 | tf_op jit(solution)/shard_map/reduce_scatter | solution.py:566
  515.4 15.1 %collective-permute-start.31 = (bf16[4096,256]{1,0:T(8,128)(2,1)S(1)}, bf16[4096,256]{1,0:T(8,128)(2,1)S(1)}, u32[]{:S(2)}, u32[]{:S(2)}) collective-permute-start(bf16[4096,256]{1,0:T(8,128)(2,1)S(1)} %slice.1247), channel_id=1, source_target_pairs={{0,1},{1,0},{2,3},{3,2},{4,5},{5,4},{6,7},{7,6},{8,9},{9,8},{10,11... | collective-permute-start | bytes 6291464 | tf_op jit(solution)/shard_map/ppermute | solution.py:386
  517.1 13.2 %collective-permute-start.32 = (bf16[2,3,512,128]{3,2,1,0:T(8,128)(2,1)S(1)}, bf16[2,3,512,128]{3,2,1,0:T(8,128)(2,1)S(1)}, u32[]{:S(2)}, u32[]{:S(2)}) collective-permute-start(bf16[2,3,512,128]{3,2,1,0:T(8,128)(2,1)S(1)} %fusion.50), channel_id=1, source_target_pairs={{0,1},{1,0},{2,3},{3,2},{4,5},{5,4},{6,7},{7,6},{8,9},{9,8},{10,11... | collective-permute-start | bytes 2359304 | tf_op jit(solution)/shard_map/ppermute | solution.py:386
  519.7 10.5 %collective-permute-start.34 = (bf16[704,256]{1,0:T(8,128)(2,1)S(1)}, bf16[704,256]{1,0:T(8,128)(2,1)S(1)}, u32[]{:S(2)}, u32[]{:S(2)}) collective-permute-start(bf16[704,256]{1,0:T(8,128)(2,1)S(1)} %constant_dynamic-slice_fusion), channel_id=1, source_target_pairs={{0,2},{2,0},{1,3},{3,1},{4,6},{6,4},{5,7},{7,5},{8,10},{10,8},{9,1... | collective-permute-start | bytes 1081352 | tf_op jit(solution)/shard_map/ppermute | solution.py:382
  545.0 219.2 %all-gather.4.cloned.1.call-start = ((), (), s32[]{:S(2)}) async-start(), calls=%async_computation.4 | async-start | bytes 2801664 | tf_op jit(solution)/shard_map/all_gather | solution.py:567
  555.9 265.0 %all-gather.6.cloned.1.call-start = ((), (), s32[]{:S(2)}) async-start(), calls=%async_computation.6 | async-start | bytes 3096576 | tf_op jit(solution)/shard_map/all_gather | solution.py:567
  630.0 253.5 %all-gather.8.cloned.1.call-start = ((), (), s32[]{:S(2)}) async-start(), calls=%async_computation.8 | async-start | bytes 3686400 | tf_op jit(solution)/shard_map/all_gather | solution.py:567
  709.9 20.0 %collective-permute-start.12 = (bf16[128,512]{1,0:T(8,128)(2,1)S(1)}, bf16[128,512]{1,0:T(8,128)(2,1)S(1)}, u32[]{:S(2)}, u32[]{:S(2)}) collective-permute-start(bf16[128,512]{1,0:T(8,128)(2,1)S(1)} %maximum_select_fusion.5), channel_id=1, source_target_pairs={{0,1},{1,0},{2,3},{3,2},{4,5},{5,4},{6,7},{7,6},{8,9},{9,8},{10,11... | collective-permute-start | bytes 393224 | tf_op jit(solution)/shard_map/ppermute | solution.py:386
  765.2 59.2 %collective-permute-start.24 = (bf16[704,256]{1,0:T(8,128)(2,1)S(1)}, bf16[704,256]{1,0:T(8,128)(2,1)}, u32[]{:S(2)}, u32[]{:S(2)}) collective-permute-start(bf16[704,256]{1,0:T(8,128)(2,1)S(1)} %slice.973), channel_id=1, source_target_pairs={{0,2},{2,0},{1,3},{3,1},{4,6},{6,4},{5,7},{7,5},{8,10},{10,8},{9,1... | collective-permute-start | bytes 1081352 | tf_op jit(solution)/shard_map/ppermute | solution.py:382
  826.6 13.4 %collective-permute-start.25 = (bf16[1408,256]{1,0:T(8,128)(2,1)}, bf16[1408,256]{1,0:T(8,128)(2,1)}, u32[]{:S(2)}, u32[]{:S(2)}) collective-permute-start(bf16[1408,256]{1,0:T(8,128)(2,1)} %maximum_select_fusion.2), channel_id=1, source_target_pairs={{0,1},{1,0},{2,3},{3,2},{4,5},{5,4},{6,7},{7,6},{8,9},{9,8},{10,11... | collective-permute-start | bytes 2162696 | tf_op jit(solution)/shard_map/ppermute | solution.py:386
  884.5 9.4 collective-permute-start.35
  896.2 33.8 %collective-permute-start.36 = (bf16[1408,256]{1,0:T(8,128)(2,1)}, bf16[1408,256]{1,0:T(8,128)(2,1)}, u32[]{:S(2)}, u32[]{:S(2)}) collective-permute-start(bf16[1408,256]{1,0:T(8,128)(2,1)} %maximum_select_fusion.3), channel_id=1, source_target_pairs={{0,1},{1,0},{2,3},{3,2},{4,5},{5,4},{6,7},{7,6},{8,9},{9,8},{10,11... | collective-permute-start | bytes 2162696 | tf_op jit(solution)/shard_map/ppermute | solution.py:386
  (238 other events, 1302.2 us)
Sparse Core Ops, SparseCore 0:
  485.2 70.5 reduce-scatter.3
  560.4 69.5 reduce-scatter.5
  634.6 75.1 reduce-scatter.7
  711.9 52.3 all-gather.3
  766.2 54.5 all-gather.5
  822.9 60.5 all-gather.7

commit v2 on v1

--- a/solution.py
+++ b/solution.py
@@ -209,7 +209,11 @@
     def put(i0,acc): recon[pl.ds(i0,acc.shape[0])]=acc.astype(BF)
     outer_up(s1,b,put)
 
-def dec_bwd_kernel(cp,dec,p3,p2,p1,a,t2,t3,t4,gdec,g2,g3,g4,red,d1,d2,d3,s,yt1,yt2,yt3,yt4):
+def dec_bwd_kernel(c0,c1,c2,c3,dec,p3,p2,p1,a,t2,t3,t4,gdec,g2,g3,g4,red,d1,d2,d3,cp,yt1,yt2,yt3,yt4):
+    me=lax.axis_index("strip")
+    cp[0]=jnp.zeros((NF,384),BF); cp[33]=jnp.zeros((NF,384),BF)
+    for k,part in enumerate((c0,c1,c2,c3)):
+        cp[pl.ds(1+8*lax.rem(me+4-k,4),8)]=part[...]
     zero_big(d1,32); zero_big(d2,16); zero_big(d3,8)
     def maps(p,rows,yt):
         for q in range(4):
@@ -253,39 +257,38 @@
 def dec_fwd(dec,u4,u3,u2,b):
     return run(dec_fwd_kernel,(S((32,NF,384)),S((8,NF,1024)),S((16,NF,1024)),S((32,NF,1024))),
       [small(4,256),small(8,128),small(16,128),small(32,0)],(dec,u4,u3,u2,b),"decode")
-def dec_bwd(cp,dec,p3,p2,p1,a,t2,t3,t4):
-    return run(dec_bwd_kernel,(S((4,NF,1024)),)+GS,[big(32),big(16),big(8),V((8,128))]+yts,
-      (cp,dec,p3,p2,p1,a,t2,t3,t4),"decode_back")
-
-
-def greet(me):
+def dec_bwd(hints,dec,p3,p2,p1,a,t2,t3,t4):
+    return run(dec_bwd_kernel,(S((4,NF,1024)),)+GS,[big(32),big(16),big(8),V((34,NF,384))]+yts,
+      (*hints,dec,p3,p2,p1,a,t2,t3,t4),"decode_back")
+
+
+def first_frame(strip):
+    return NF * ((strip % 2) * 2 + strip // 2)
+
+
+def turned_rows(x, i):
+    return jnp.concatenate([x[c, 2 * i + p] for p in range(2) for c in range(3)], axis=0).T
+
+
+def frames_in_kernel(x, out, stage, send_sem, recv_sem):
+    me = lax.axis_index("strip")
+    row = lax.axis_index("rows")
+    out[0] = jnp.zeros((NF, 384), BF)
+    out[33] = jnp.zeros((NF, 384), BF)
+
+    def turn_rows(i, carry):
+        flat = turned_rows(x, i)
+        for k in range(4):
+            stage[k, i] = flat[first_frame(k) : first_frame(k) + NF]
+        return carry
+
+    lax.fori_loop(0, 8, turn_rows, 0)
     barrier = pltpu.get_barrier_semaphore()
-    row = lax.axis_index("rows")
     for k in range(1, 4):
         pl.semaphore_signal(
             barrier, inc=1, device_id=(row, lax.rem(me + k, 4)), device_id_type=MESH
         )
     pl.semaphore_wait(barrier, 3)
-
-
-def frames_in_kernel(x, out, stage, send_sem, recv_sem):
-    me = lax.axis_index("strip")
-    row = lax.axis_index("rows")
-    out[0] = jnp.zeros((NF, 384), BF)
-    out[33] = jnp.zeros((NF, 384), BF)
-
-    def turn_rows(i, carry):
-        block = jnp.concatenate(
-            [x[c, 2 * i + p] for p in range(2) for c in range(3)], axis=0
-        )
-        flat = block.T
-        for k in range(4):
-            first = NF * ((k % 2) * 2 + k // 2)
-            stage[k, i] = flat[first : first + NF]
-        return carry
-
-    lax.fori_loop(0, 8, turn_rows, 0)
-    greet(me)
     copies = []
     for k in range(1, 4):
         to = lax.rem(me + k, 4)
@@ -306,41 +309,6 @@
         copy.wait()
 
 
-def frames_out_kernel(y, out, got, send_sem, recv_sem):
-    me = lax.axis_index("strip")
-    row = lax.axis_index("rows")
-    greet(me)
-    copies = []
-    for k in range(1, 4):
-        to = lax.rem(me + k, 4)
-        copies.append(
-            pltpu.make_async_remote_copy(
-                src_ref=y.at[pl.ds(8 * to, 8)],
-                dst_ref=got.at[me],
-                send_sem=send_sem.at[k - 1],
-                recv_sem=recv_sem.at[k - 1],
-                device_id=(row, to),
-                device_id_type=MESH,
-            )
-        )
-    for copy in copies:
-        copy.start()
-    got[me] = y[pl.ds(8 * me, 8)]
-    for copy in copies:
-        copy.wait()
-
-    def turn_rows(i, carry):
-        block = jnp.concatenate([got[(b % 2) * 2 + b // 2, i] for b in range(4)], axis=0)
-        flat = block.T.astype(out.dtype)
-        for p in range(2):
-            for c in range(3):
-                first = 64 * (3 * p + c)
-                out[c, 2 * i + p] = flat[first : first + 64]
-        return carry
-
-    lax.fori_loop(0, 8, turn_rows, 0)
-
-
 def frames_in(block, ident):
     return pl.pallas_call(
         frames_in_kernel,
@@ -359,23 +327,512 @@
     )(jnp.transpose(block, (1, 2, 3, 0)))
 
 
-def frames_out(pairs, dtype, ident):
-    flat = pl.pallas_call(
-        frames_out_kernel,
-        out_shape=jax.ShapeDtypeStruct((3, 16, 64, 256), dtype),
+def turn_kernel(x, *out):
+    me = lax.axis_index("strip")
+
+    def turn_rows(i, carry):
+        flat = turned_rows(x, i)
+        for k in range(4):
+            part = flat[first_frame(k) : first_frame(k) + NF]
+            for step in range(4):
+
+                @pl.when(lax.rem(me + step, 4) == k)
+                def _():
+                    out[step][i] = part
+
+        return carry
+
+    lax.fori_loop(0, 8, turn_rows, 0)
+
+
+def frames_in_later(block):
+    parts = pl.pallas_call(
+        turn_kernel,
+        out_shape=(jax.ShapeDtypeStruct((8, NF, 384), BF),) * 4,
         in_specs=VM(1),
-        out_specs=VM(1)[0],
+        out_specs=tuple(VM(4)),
+        compiler_params=pltpu.CompilerParams(vmem_limit_bytes=32 * MIB),
+        name="turn",
+    )(jnp.transpose(block, (1, 2, 3, 0)))
+    return [parts[0]] + [
+        lax.ppermute(parts[k], "strip", [(s, (s + k) % 4) for s in range(4)]) for k in range(1, 4)
+    ]
+
+
+def finish_kernel(
+    count, chunks, v, recon, grad, total, recon_out, grad_out,
+    got, from_near, summed, from_far, strip_sems, near_sems, far_sems, back_sems, last_sems,
+):
+    me = lax.axis_index("strip")
+    row = lax.axis_index("rows")
+    half = count // 2
+    near, far = lax.rem(row, 2), lax.div(row, 2)
+    near_device = (row + 1 - 2 * near, me)
+    barrier = pltpu.get_barrier_semaphore()
+    strip_devices = [(row, lax.rem(me + k, 4)) for k in range(1, 4)]
+    far_places = [lax.rem(far + k, half) for k in range(1, half)]
+    far_devices = [(2 * place + near, me) for place in far_places]
+    for device in strip_devices + [near_device] + far_devices:
+        pl.semaphore_signal(barrier, inc=1, device_id=device, device_id_type=MESH)
+    pl.semaphore_wait(barrier, 3 + half)
+
+    def copy(src, dst, sems, index, device):
+        return pltpu.make_async_remote_copy(
+            src_ref=src,
+            dst_ref=dst,
+            send_sem=sems.at[(0,) + index],
+            recv_sem=sems.at[(1,) + index],
+            device_id=device,
+            device_id_type=MESH,
+        )
+
+    near_copies = [
+        copy(v.at[c, 1 - near], from_near.at[c], near_sems, (c,), near_device)
+        for c in range(chunks)
+    ]
+    for one in near_copies:
+        one.start()
+    strip_copies = []
+    for slot, pairs in enumerate((recon, grad)):
+        for k in range(1, 4):
+            to = lax.rem(me + k, 4)
+            strip_copies.append(
+                copy(
+                    pairs.at[pl.ds(8 * to, 8)],
+                    got.at[slot, me],
+                    strip_sems,
+                    (slot, k - 1),
+                    (row, to),
+                )
+            )
+    for one in strip_copies:
+        one.start()
+    for slot, pairs in enumerate((recon, grad)):
+        got[slot, me] = pairs[pl.ds(8 * me, 8)]
+
+    def turn(slot, out):
+        for one in strip_copies[3 * slot : 3 * slot + 3]:
+            one.wait()
+
+        def turn_rows(i, carry):
+            block = jnp.concatenate([got[slot, (b % 2) * 2 + b // 2, i] for b in range(4)], axis=0)
+            flat = block.T.astype(out.dtype)
+            for p in range(2):
+                for c in range(3):
+                    first = 64 * (3 * p + c)
+                    out[c, 2 * i + p] = flat[first : first + 64]
+            return carry
+
+        lax.fori_loop(0, 8, turn_rows, 0)
+
+    far_copies, back_copies, last_copies = {}, {}, {}
+
+    def stage_far(c):
+        near_copies[c].wait()
+        summed[c] = (v[c, near].astype(F32) + from_near[c].astype(F32)).astype(BF)
+        far_copies[c] = [
+            copy(summed.at[c, place], from_far.at[c, k], far_sems, (c, k), device)
+            for k, (place, device) in enumerate(zip(far_places, far_devices))
+        ]
+        for one in far_copies[c]:
+            one.start()
+
+    def stage_back(c):
+        for one in far_copies[c]:
+            one.wait()
+        whole = summed[c, far].astype(F32)
+        for k in range(half - 1):
+            whole = whole + from_far[c, k].astype(F32)
+        total[c, near, far] = whole.astype(BF)
+        back_copies[c] = [
+            copy(total.at[c, near, far], total.at[c, near, far], back_sems, (c, k), device)
+            for k, device in enumerate(far_devices)
+        ]
+        for one in back_copies[c]:
+            one.start()
+
+    def stage_last(c):
+        for one in back_copies[c]:
+            one.wait()
+        last_copies[c] = copy(
+            total.at[c, near], total.at[c, near], last_sems, (c,), near_device
+        )
+        last_copies[c].start()
+
+    for t in range(chunks + 2):
+        if t < chunks:
+            stage_far(t)
+        if t == 1:
+            turn(0, recon_out)
+        if t == 3:
+            turn(1, grad_out)
+        if 0 <= t - 1 < chunks:
+            stage_back(t - 1)
+        if 0 <= t - 2 < chunks:
+            stage_last(t - 2)
+    for c in range(chunks):
+        last_copies[c].wait()
+
+
+def finish(flat, recon, grad, chunks, ident):
+    count = lax.axis_size("rows")
+    half = count // 2
+    rows = flat.shape[0]
+    flat = jnp.pad(flat, ((0, -rows % (16 * count * chunks)), (0, 0)))
+    each = flat.shape[0] // (count * chunks)
+    shape = (chunks, 2, half, each, 256)
+    dma = pltpu.SemaphoreType.DMA
+    total, recon_out, grad_out = pl.pallas_call(
+        functools.partial(finish_kernel, count, chunks),
+        out_shape=(
+            jax.ShapeDtypeStruct(shape, BF),
+            jax.ShapeDtypeStruct((3, 16, 64, 256), BF),
+            jax.ShapeDtypeStruct((3, 16, 64, 256), F32),
+        ),
+        in_specs=VM(3),
+        out_specs=tuple(VM(3)),
         scratch_shapes=[
-            pltpu.VMEM((4, 8, NF, 384), BF),
-            pltpu.SemaphoreType.DMA((3,)),
-            pltpu.SemaphoreType.DMA((3,)),
+            pltpu.VMEM((2, 4, 8, NF, 384), BF),
+            pltpu.VMEM((chunks, half, each, 256), BF),
+            pltpu.VMEM((chunks, half, each, 256), BF),
+            pltpu.VMEM((chunks, half - 1, each, 256), BF),
+            dma((2, 2, 3)),
+            dma((2, chunks)),
+            dma((2, chunks, half - 1)),
+            dma((2, chunks, half - 1)),
+            dma((2, chunks)),
         ],
         compiler_params=pltpu.CompilerParams(
-            collective_id=ident, has_side_effects=True, vmem_limit_bytes=32 * MIB
+            collective_id=ident, has_side_effects=True, vmem_limit_bytes=56 * MIB
         ),
-        name="frames_out",
-    )(pairs)
-    return jnp.transpose(flat, (3, 0, 1, 2))
+        name="finish",
+    )(flat.reshape(shape), recon, grad)
+    return (
+        total.reshape(-1, 256)[:rows],
+        jnp.transpose(recon_out, (3, 0, 1, 2)),
+        jnp.transpose(grad_out, (3, 0, 1, 2)),
+    )
+
+
+def dot(a, b):
+    return jnp.dot(a, b, preferred_element_type=F32)
+
+
+def dot_nt(a, b):
+    return lax.dot_general(a, b, (((1,), (1,)), ((), ())), preferred_element_type=F32)
+
+
+def over_groups(values, join):
+    lanes = values.shape[1]
+    lane = lax.broadcasted_iota(jnp.int32, values.shape, 1)
+    for step in (1, 2, 4, 8, 16):
+        upper = lax.rem(lax.div(lane, step), 2) == 1
+        other = jnp.where(
+            upper, pltpu.roll(values, step, 1), pltpu.roll(values, lanes - step, 1)
+        )
+        values = join(values, other)
+    return values
+
+
+def unit_of(hidden):
+    centred = hidden - jnp.mean(hidden, -1, keepdims=True)
+    scale_inv = lax.rsqrt(jnp.mean(centred * centred, -1, keepdims=True) + EPS)
+    return centred * scale_inv, scale_inv
+
+
+def unit_back(grad_normed, unit_rows, scale_inv, gain):
+    grad_unit = grad_normed * gain
+    grad_gain = jnp.sum(grad_normed * unit_rows, 0, keepdims=True)
+    grad_rows = scale_inv * (
+        grad_unit
+        - jnp.mean(grad_unit, -1, keepdims=True)
+        - unit_rows * jnp.mean(grad_unit * unit_rows, -1, keepdims=True)
+    )
+    return grad_gain, grad_rows
+
+
+LAYER_ROWS = 1536
+
+
+def token_rows(layers):
+    return layers * LAYER_ROWS + 256 + NF + 16
+
+
+def middle_kernel(
+    layers,
+    feat, lh0, lh1, dh0, dh1, emb0, emb1, pos, gains, allow, cot,
+    qkv0, qkv1, proj0, proj1, up0, up1, down0, down1,
+    tokens, latent_out, chances_out, decoded, flat, grad_latent,
+    feat_got, feat_sems, keep, send, sent, spread_sems, parts, gots, pair_sems,
+    other, other_got, fold_sems, unit_a, unit_f, normed_a, normed_f, mixed, weights,
+    attended, before, inner, gain_rows,
+):
+    strip = lax.axis_index("strip")
+    row = lax.axis_index("rows")
+    partner = (row, lax.rem(strip + 2, 4))
+    sibling = (row, strip + 1 - 2 * lax.rem(strip, 2))
+    barrier = pltpu.get_barrier_semaphore()
+    for device in (partner, sibling):
+        pl.semaphore_signal(barrier, inc=1, device_id=device, device_id_type=MESH)
+    pl.semaphore_wait(barrier, 2)
+
+    def copy(src, dst, sems, index, device):
+        return pltpu.make_async_remote_copy(
+            src_ref=src,
+            dst_ref=dst,
+            send_sem=sems.at[0, index],
+            recv_sem=sems.at[1, index],
+            device_id=device,
+            device_id_type=MESH,
+        )
+
+    feat_copy = copy(feat, feat_got, feat_sems, 0, partner)
+    feat_copy.start()
+
+    def total_start(index, value):
+        parts[index] = value.astype(BF)
+        one = copy(parts.at[index], gots.at[index], pair_sems, index, partner)
+        one.start()
+        return one
+
+    def total_wait(index, one):
+        one.wait()
+        got = jnp.concatenate([gots[index, NF:], gots[index, :NF]], axis=0)
+        return parts[index].astype(F32) + got.astype(F32)
+
+    def logits_of(maps):
+        halves = []
+        for weight in (lh0, lh1):
+            total = jnp.zeros((NF, 256), F32)
+            for h in range(4):
+                total = total + dot(maps[h], weight[1024 * h : 1024 * h + 1024])
+            halves.append(total)
+        return jnp.concatenate(halves, axis=1)
+
+    mine = logits_of(feat)
+    feat_copy.wait()
+    logits = jnp.concatenate([mine, logits_of(feat_got)], axis=0)
+    raised = jnp.exp(logits - over_groups(logits, jnp.maximum))
+    chances = raised / over_groups(raised, jnp.add)
+    latent = chances.astype(BF)
+    chances_out[...] = chances
+    latent_out[...] = latent
+
+    waiting = total_start(0, dot(latent[:, :256], emb0[...]) + dot(latent[:, 256:], emb1[...]))
+    for hw in range(16):
+        lanes = slice(256 * (hw % 4), 256 * (hw % 4) + 256)
+        rows = slice(256 * hw, 256 * hw + 256)
+        value = dot_nt(latent[:, :256], dh0[rows]) + dot_nt(latent[:, 256:], dh1[rows])
+        value = value.astype(BF)
+        keep[hw // 4, :, lanes] = value[:NF]
+        send[hw // 4, :, lanes] = value[NF:]
+    spread_copy = copy(send, sent, spread_sems, 0, partner)
+    spread_copy.start()
+    embedded = total_wait(0, waiting)
+    place = pos[...].astype(F32)
+    hidden = embedded + jnp.concatenate([place, place], axis=0)
+    head_lane = lax.div(lax.broadcasted_iota(jnp.int32, (2 * NF, 128), 1), HEAD_DIM)
+    allowed = allow[...] > 0.5
+
+    def of_head(value, h):
+        return jnp.where(head_lane == h % 2, value, jnp.zeros_like(value))
+
+    def pair_lanes(h):
+        return slice(128 * (h // 2), 128 * (h // 2) + 128)
+
+    for k in range(layers):
+        unit, inv = unit_of(hidden)
+        unit_a[k] = jnp.concatenate([unit, jnp.broadcast_to(inv, (2 * NF, 128))], axis=1)
+        normed = (unit * gains[2 * k : 2 * k + 1]).astype(BF)
+        normed_a[k] = normed
+        for part in range(3):
+            mixed[k, part] = jnp.concatenate(
+                [dot(normed, qkv0[k, part]), dot(normed, qkv1[k, part])], axis=1
+            ).astype(BF)
+        for p in range(2):
+            both = jnp.zeros((2 * NF, 128), F32)
+            for h in (2 * p, 2 * p + 1):
+                lanes = pair_lanes(h)
+                scores = SCALE * dot_nt(of_head(mixed[k, 0, :, lanes], h), mixed[k, 1, :, lanes])
+                scores = jnp.where(allowed, scores, NEG)
+                lifted = jnp.exp(scores - jnp.max(scores, -1, keepdims=True))
+                weight = lifted / jnp.sum(lifted, -1, keepdims=True)
+                weights[k, h] = weight
+                both = both + of_head(dot(weight.astype(BF), mixed[k, 2, :, lanes]), h)
+            attended[k, :, 128 * p : 128 * p + 128] = both.astype(BF)
+        partial = dot(attended[k, :, :128], proj0[k]) + dot(attended[k, :, 128:], proj1[k])
+        middle = hidden + total_wait(2 * k + 1, total_start(2 * k + 1, partial))
+        unit, inv = unit_of(middle)
+        unit_f[k] = jnp.concatenate([unit, jnp.broadcast_to(inv, (2 * NF, 128))], axis=1)
+        normed = (unit * gains[2 * k + 1 : 2 * k + 2]).astype(BF)
+        normed_f[k] = normed
+        partial = jnp.zeros((2 * NF, 512), F32)
+        for side, (up, down) in enumerate(((up0, down0), (up1, down1))):
+            value = dot(normed, up[k])
+            before[k, :, 512 * side : 512 * side + 512] = value
+            act = (value * sig(value)).astype(BF)
+            inner[k, :, 512 * side : 512 * side + 512] = act
+            partial = partial + dot(act, down[k])
+        hidden = middle + total_wait(2 * k + 2, total_start(2 * k + 2, partial))
+    tokens[...] = hidden.astype(BF)
+
+    spread_copy.wait()
+    decoded[...] = (keep[...].astype(F32) + sent[...].astype(F32)).astype(BF)
+
+    fold_copies = []
+
+    def fold_start(first, count):
+        rows = pl.ds(first, count)
+        one = copy(other.at[rows], other_got.at[rows], fold_sems, len(fold_copies), sibling)
+        one.start()
+        fold_copies.append((first, count, one))
+
+    grad = cot[...].astype(F32)
+    for k in reversed(range(layers)):
+        base = LAYER_ROWS * k
+        index = 2 * layers + 1 + 2 * (layers - 1 - k)
+        low = grad.astype(BF)
+        partial = jnp.zeros((2 * NF, 512), F32)
+        grads = []
+        for side, (up, down) in enumerate(((up0, down0), (up1, down1))):
+            value = before[k, :, 512 * side : 512 * side + 512]
+            squash = sig(value)
+            slope = squash * (1.0 + value * (1.0 - squash))
+            grad_before = (dot_nt(low, down[k]) * slope).astype(BF)
+            grads.append(grad_before)
+            partial = partial + dot_nt(grad_before, up[k])
+        waiting = total_start(index, partial)
+        turned = normed_f[k].T
+        for side, dst in enumerate((flat, other)):
+            act = inner[k, :, 512 * side : 512 * side + 512]
+            dst[base : base + 512] = dot(act.T, low).astype(BF)
+            dst[base + 512 : base + 1024] = dot(turned, grads[side]).astype(BF)
+        grad_normed = total_wait(index, waiting)
+        gain_f, grad_rows = unit_back(
+            grad_normed, unit_f[k, :, :512], unit_f[k, :, 512:513], gains[2 * k + 1 : 2 * k + 2]
+        )
+        grad = grad + grad_rows
+        low = grad.astype(BF)
+        grad_mixed = [[], [], []]
+        for p, proj in enumerate((proj0, proj1)):
+            lanes = pair_lanes(2 * p)
+            grad_pair = dot_nt(low, proj[k]).astype(BF)
+            queries, keys, vals = mixed[k, 0, :, lanes], mixed[k, 1, :, lanes], mixed[k, 2, :, lanes]
+            g_queries = jnp.zeros((2 * NF, 128), F32)
+            g_keys, g_vals = g_queries, g_queries
+            for h in (2 * p, 2 * p + 1):
+                weight = weights[k, h]
+                grad_head = of_head(grad_pair, h)
+                g_vals = g_vals + dot(weight.astype(BF).T, grad_head)
+                grad_weight = dot_nt(grad_head, vals)
+                along = jnp.sum(weight * grad_weight, -1, keepdims=True)
+                grad_scores = (weight * (grad_weight - along)).astype(BF)
+                g_queries = g_queries + of_head(dot(grad_scores, keys), h)
+                g_keys = g_keys + dot(grad_scores.T, of_head(queries, h))
+            grad_mixed[0].append((SCALE * g_queries).astype(BF))
+            grad_mixed[1].append((SCALE * g_keys).astype(BF))
+            grad_mixed[2].append(g_vals.astype(BF))
+        partial = jnp.zeros((2 * NF, 512), F32)
+        for part in range(3):
+            for side, qkv in enumerate((qkv0, qkv1)):
+                partial = partial + dot_nt(grad_mixed[part][side], qkv[k, part])
+        waiting = total_start(index + 1, partial)
+        turned = normed_a[k].T
+        for side, dst in enumerate((flat, other)):
+            act = attended[k, :, 128 * side : 128 * side + 128]
+            dst[base + 1024 : base + 1152] = dot(act.T, low).astype(BF)
+            for part in range(3):
+                value = dot(turned, grad_mixed[part][side]).astype(BF)
+                first = base + 1152 + 128 * part
+                for b in range(4):
+                    dst[first : first + 128, 128 * b : 128 * b + 128] = value[
+                        128 * b : 128 * b + 128
+                    ]
+        fold_start(base, LAYER_ROWS)
+        grad_normed = total_wait(index + 1, waiting)
+        gain_a, grad_rows = unit_back(
+            grad_normed, unit_a[k, :, :512], unit_a[k, :, 512:513], gains[2 * k : 2 * k + 1]
+        )
+        grad = grad + grad_rows
+        gain_rows[2 * k : 2 * k + 1] = gain_a
+        gain_rows[2 * k + 1 : 2 * k + 2] = gain_f
+
+    base = LAYER_ROWS * layers
+    low = grad.astype(BF)
+    own_latent, other_latent = latent_out[:, :256], latent_out[:, 256:]
+    flat[base : base + 256] = dot(own_latent.T, low).astype(BF)
+    other[base : base + 256] = dot(other_latent.T, low).astype(BF)
+    small = jnp.concatenate(
+        [
+            grad[:NF] + grad[NF:],
+            gain_rows[...],
+            jnp.zeros((16 - 2 * layers, 512), F32),
+        ],
+        axis=0,
+    ).astype(BF)
+    flat[base + 256 : base + 256 + NF + 16] = small
+    other[base + 256 : base + 256 + NF + 16] = small
+    fold_start(base, 256 + NF + 16)
+    grad_latent[:, :256] = dot_nt(low, emb0[...])
+    grad_latent[:, 256:] = dot_nt(low, emb1[...])
+    for first, count, one in fold_copies:
+        one.wait()
+        for start in range(first, first + count, 16 * 7 if count % 112 == 0 else 16 * 8):
+            size = min(128 if count % 112 else 112, first + count - start)
+            rows = slice(start, start + size)
+            flat[rows] = (flat[rows].astype(F32) + other_got[rows].astype(F32)).astype(BF)
+    spare = flat.shape[0] - token_rows(layers)
+    if spare:
+        flat[token_rows(layers) :] = jnp.zeros((spare, 512), BF)
+
+
+def middle(layers, multiple, *args):
+    rows = token_rows(layers)
+    rows = rows + -rows % multiple
+    dma = pltpu.SemaphoreType.DMA
+    sums = 4 * layers + 1
+    t = 2 * NF
+    return pl.pallas_call(
+        functools.partial(middle_kernel, layers),
+        out_shape=(
+            S((t, 512)),
+            S((t, 512)),
+            S((t, 512), F32),
+            S((4, NF, 1024)),
+            S((rows, 512)),
+            S((t, 512), F32),
+        ),
+        in_specs=VM(len(args)),
+        out_specs=tuple(VM(6)),
+        scratch_shapes=[
+            V((4, NF, 1024)),
+            dma((2, 1)),
+            V((4, NF, 1024)),
+            V((4, NF, 1024)),
+            V((4, NF, 1024)),
+            dma((2, 1)),
+            V((sums, t, 512)),
+            V((sums, t, 512)),
+            dma((2, sums)),
+            V((rows, 512)),
+            V((rows, 512)),
+            dma((2, layers + 1)),
+            V((layers, t, 640), F32),
+            V((layers, t, 640), F32),
+            V((layers, t, 512)),
+            V((layers, t, 512)),
+            V((layers, 3, t, 256)),
+            V((layers, 4, t, t), F32),
+            V((layers, t, 256)),
+            V((layers, t, 1024), F32),
+            V((layers, t, 1024)),
+            V((2 * layers, 512), F32),
+        ],
+        compiler_params=pltpu.CompilerParams(
+            collective_id=3, has_side_effects=True, vmem_limit_bytes=56 * MIB
+        ),
+        name="middle",
+    )(*args)
 
 
 def across(value):
@@ -384,14 +841,6 @@
 
 def beside(value):
     return lax.ppermute(value, "strip", [(0, 1), (1, 0), (2, 3), (3, 2)])
-
-
-def pair_total(partial_value):
-    low = partial_value.astype(BF)
-    got = across(low)
-    half = low.shape[0] // 2
-    got = jnp.concatenate([got[half:], got[:half]], axis=0)
-    return low.astype(F32) + got.astype(F32)
 
 
 def fold(full, axis):
@@ -401,52 +850,12 @@
     return own + beside(other.astype(BF)).astype(F32)
 
 
-def with_sibling(shard, axis):
-    return jnp.concatenate([shard, beside(shard)], axis=axis)
-
-
-def normalize(hidden):
-    centred = hidden - jnp.mean(hidden, -1, keepdims=True)
-    scale_inv = lax.rsqrt(jnp.mean(centred * centred, -1, keepdims=True) + EPS)
-    return (centred * scale_inv, scale_inv)
-
-
-def normalize_back(grad_normed, unit_rows, scale_inv, gain):
-    grad_unit = grad_normed * gain
-    grad_gain = jnp.sum(grad_normed * unit_rows, 0)
-    grad_rows = scale_inv * (
-        grad_unit
-        - jnp.mean(grad_unit, -1, keepdims=True)
-        - unit_rows * jnp.mean(grad_unit * unit_rows, -1, keepdims=True)
-    )
-    return (grad_gain, grad_rows)
-
-
-def grouped_softmax(logits):
-    frame_count = logits.shape[0]
-    grouped = logits.reshape(frame_count, -1, LCLASS)
-    shifted = grouped - jnp.max(grouped, -1, keepdims=True)
-    raised = jnp.exp(shifted)
-    return (raised / jnp.sum(raised, -1, keepdims=True)).reshape(frame_count, -1)
-
-
 def make_mask(segment_ids):
     places = jnp.arange(segment_ids.shape[1])
     causal = places[:, None] >= places[None, :]
     return causal[None] & (segment_ids[:, :, None] == segment_ids[:, None, :])
 
 
-def split_heads(flat_rows, sequences):
-    return flat_rows.reshape(sequences, -1, flat_rows.shape[-1] // HEAD_DIM, HEAD_DIM)
-
-
-def score_block(queries, keys_part, allowed):
-    scores = (
-        jnp.einsum("bqhe,bkhe->bhqk", queries, keys_part, preferred_element_type=F32) * SCALE
-    )
-    return jnp.where(allowed[:, None], scores, NEG)
-
-
 def mm(a, b):
     return jnp.dot(a, b, preferred_element_type=F32)
 
@@ -459,118 +868,26 @@
     return lax.dot_general(a, b, (((0,), (0,)), ((), ())), preferred_element_type=F32)
 
 
-def layer_forward(hidden, allowed, gain_pair, qkv_layer, out_layer, up_layer, down_layer):
-    sequences = allowed.shape[0]
-    unit_attn, inv_attn = normalize(hidden)
-    normed_attn = (unit_attn * gain_pair[0]).astype(BF)
-    mixed = [mm(normed_attn, qkv_layer[:, k]).astype(BF) for k in range(3)]
-    queries, keys_part, vals_part = [split_heads(part, sequences) for part in mixed]
-    scores = score_block(queries, keys_part, allowed)
-    top_score = jnp.max(scores, -1, keepdims=True)
-    raised = jnp.exp(scores - top_score)
-    chances = raised / jnp.sum(raised, -1, keepdims=True)
-    attended = jnp.einsum(
-        "bhqk,bkhe->bqhe", chances.astype(BF), vals_part, preferred_element_type=F32
-    )
-    attended = attended.astype(BF).reshape(hidden.shape[0], -1)
-    middle = hidden + pair_total(mm(attended, out_layer))
-    unit_ffn, inv_ffn = normalize(middle)
-    normed_ffn = (unit_ffn * gain_pair[1]).astype(BF)
-    before = mm(normed_ffn, up_layer)
-    inner_act = (before * sig(before)).astype(BF)
-    result = middle + pair_total(mm(inner_act, down_layer))
-    kept = (
-        unit_attn,
-        inv_attn,
-        normed_attn,
-        (queries, keys_part, vals_part),
-        chances,
-        attended,
-        unit_ffn,
-        inv_ffn,
-        normed_ffn,
-        before,
-        inner_act,
-    )
-    return (result, kept)
-
-
-def layer_backward(
-    grad_hidden, allowed, gain_pair, qkv_layer, out_layer, up_layer, down_layer, kept
-):
-    (
-        unit_attn,
-        inv_attn,
-        normed_attn,
-        mixed,
-        chances,
-        attended,
-        unit_ffn,
-        inv_ffn,
-        normed_ffn,
-        before,
-        inner_act,
-    ) = kept
-    token_count = grad_hidden.shape[0]
-    grad_low = grad_hidden.astype(BF)
-    grad_down = t_mm(inner_act, grad_low)
-    grad_inner = mm_t(grad_low, down_layer)
-    squash = sig(before)
-    grad_before = (grad_inner * (squash * (1.0 + before * (1.0 - squash)))).astype(BF)
-    grad_up = t_mm(normed_ffn, grad_before)
-    grad_normed = pair_total(mm_t(grad_before, up_layer))
-    gain_ffn, grad_mid = normalize_back(grad_normed, unit_ffn, inv_ffn, gain_pair[1])
-    grad_middle = grad_hidden + grad_mid
-    middle_low = grad_middle.astype(BF)
-    grad_project = t_mm(attended, middle_low)
-    sequences = allowed.shape[0]
-    grad_attended = split_heads(mm_t(middle_low, out_layer).astype(BF), sequences)
-    queries, keys_part, vals_part = mixed
-    grad_vals = jnp.einsum(
-        "bhqk,bqhe->bkhe", chances.astype(BF), grad_attended, preferred_element_type=F32
-    )
-    grad_chances = jnp.einsum(
-        "bqhe,bkhe->bhqk", grad_attended, vals_part, preferred_element_type=F32
-    )
-    weighted_total = jnp.sum(chances * grad_chances, -1, keepdims=True)
-    grad_scores = (chances * (grad_chances - weighted_total)).astype(BF)
-    grad_queries = SCALE * jnp.einsum(
-        "bhqk,bkhe->bqhe", grad_scores, keys_part, preferred_element_type=F32
-    )
-    grad_keys = SCALE * jnp.einsum(
-        "bhqk,bqhe->bkhe", grad_scores, queries, preferred_element_type=F32
-    )
-    grad_mixed = [
-        part.reshape(token_count, -1).astype(BF) for part in (grad_queries, grad_keys, grad_vals)
-    ]
-    grad_qkv = jnp.stack([t_mm(normed_attn, part) for part in grad_mixed])
-    grad_normed_attn = pair_total(
-        sum(mm_t(part, qkv_layer[:, k]) for k, part in enumerate(grad_mixed))
-    )
-    gain_attn, grad_first = normalize_back(grad_normed_attn, unit_attn, inv_attn, gain_pair[0])
-    return (
-        grad_middle + grad_first,
-        jnp.stack([gain_attn, gain_ffn]),
-        grad_qkv,
-        grad_project,
-        grad_up,
-        grad_down,
-    )
-
-
-def rows_total(parts):
-    count = lax.axis_size("rows")
-    flat = jnp.concatenate([part.astype(BF) for part in parts], axis=0)
-    total = flat.shape[0]
-    flat = jnp.pad(flat, ((0, -total % (16 * count)), (0, 0)))
-    share = lax.psum_scatter(flat, "rows", scatter_dimension=0, tiled=True)
-    whole = lax.all_gather(share, "rows", axis=0, tiled=True)
+def pieces_of(whole, parts):
     pieces = []
     offset = 0
     for part in parts:
         pieces.append(whole[offset : offset + part.shape[0]])
         offset = offset + part.shape[0]
     return pieces
+
+
+def stacked_rows(parts, multiple):
+    flat = jnp.concatenate([part.astype(BF) for part in parts], axis=0)
+    return jnp.pad(flat, ((0, -flat.shape[0] % multiple), (0, 0)))
+
+
+def rows_share(flat):
+    return lax.psum_scatter(flat, "rows", scatter_dimension=0, tiled=True)
+
+
+def rows_whole(share):
+    return lax.all_gather(share, "rows", axis=0, tiled=True)
 
 
 def pack_kernels(outer, first, second, third):
@@ -669,47 +986,53 @@
     enc_t = [t.reshape(2048, 256) for t in enc_t]
     dec_t = [t.reshape(2048, 256) for t in dec_t]
 
-    head_in = with_sibling(features_first(latent_head), 1)
-    head_out = with_sibling(features_first(decode_head.T), 1)
-    embed = with_sibling(token_embed, 0)
-    qkv = with_sibling(qkv_weight, 3)
-    project = with_sibling(out_weight, 1)
-    widen = with_sibling(up_weight, 2)
-    narrow = with_sibling(down_weight, 1)
+    head_in = features_first(latent_head)
+    head_in = (head_in, beside(head_in))
+    head_out = features_first(decode_head.T)
+    head_out = (head_out, beside(head_out))
+    qkv = jnp.transpose(qkv_weight, (0, 2, 1, 3))
+    halves = []
+    for shard in (token_embed, qkv, out_weight, up_weight, down_weight):
+        halves.append((shard, beside(shard)))
+    embed, qkv, project, widen, narrow = halves
 
     pixels = frames_in(frames, 1)
+    hints = frames_in_later(frame_cotangent)
     z1, z2, z3, z4, feat = enc_fwd(pixels, enc_a, *enc_t)
-    feat = jnp.concatenate([feat, across(feat)], axis=1)
-    head_in4 = head_in.reshape(4, 1024, 512)
-    logits = sum(mm(feat[h], head_in4[h]) for h in range(4))
-    chances = grouped_softmax(logits)
-    latent = chances.astype(BF)
-
-    head_out4 = head_out.reshape(4, 1024, 512)
-    spread = jnp.stack([mm_t(latent, head_out4[h]) for h in range(4)]).astype(BF)
-    decoded = (
-        spread[:, :NF].astype(F32) + across(spread[:, NF:]).astype(F32)
-    ).astype(BF)
-    recon_pairs, p3, p2, p1 = dec_fwd(decoded, dec_u[2], dec_u[1], dec_u[0], dec_b)
-    recon = frames_out(recon_pairs, BF, 3)
-
     first = 2 * core
+
     def mine(array, size):
         own = lax.dynamic_slice_in_dim(array, (first + x) * size, size)
         other = lax.dynamic_slice_in_dim(array, (first + 1 - x) * size, size)
         return jnp.concatenate([own, other], axis=0)
-    segments = mine(segment_ids, 1)
-    allowed = make_mask(segments)
-    embedded = pair_total(mm(latent, embed))
-    hidden = embedded.reshape(2, NF, -1) + positions.astype(F32)[None]
-    hidden = hidden.reshape(2 * NF, -1)
-    kept_layers = []
-    for k in range(layers):
-        hidden, kept = layer_forward(
-            hidden, allowed, norm_gains[k], qkv[k], project[k], widen[k], narrow[k]
-        )
-        kept_layers.append(kept)
-    tokens = hidden.astype(BF)
+
+    allowed = make_mask(mine(segment_ids, 1)).astype(F32)
+    blank = jnp.zeros((NF, NF), F32)
+    allowed = jnp.concatenate(
+        [
+            jnp.concatenate([allowed[0], blank], axis=1),
+            jnp.concatenate([blank, allowed[1]], axis=1),
+        ],
+        axis=0,
+    )
+    line = 16 * lax.axis_size("rows")
+    tokens, latent, chances, decoded, t_flat, grad_latent = middle(
+        layers,
+        line,
+        feat,
+        *head_in,
+        *head_out,
+        *embed,
+        positions,
+        norm_gains.reshape(2 * layers, -1),
+        allowed,
+        mine(token_cotangent, NF),
+        *qkv,
+        *project,
+        *widen,
+        *narrow,
+    )
+    t_share = rows_share(t_flat)
     tokens = jnp.where(
         x == 0, tokens, jnp.concatenate([tokens[NF:], tokens[:NF]], axis=0)
     )
@@ -719,37 +1042,14 @@
         jnp.concatenate([tokens, other_tokens]),
         jnp.concatenate([other_tokens, tokens]),
     )
-    grad_hidden = mine(token_cotangent, NF).astype(F32)
-    layer_grads = [None] * layers
-    for k in reversed(range(layers)):
-        grad_hidden, *layer_grads[k] = layer_backward(
-            grad_hidden,
-            allowed,
-            norm_gains[k],
-            qkv[k],
-            project[k],
-            widen[k],
-            narrow[k],
-            kept_layers[k],
-        )
-    gains, g_qkv, g_project, g_widen, g_narrow = [
-        jnp.stack([entry[slot] for entry in layer_grads]) for slot in range(5)
-    ]
-    g_positions = grad_hidden[:NF] + grad_hidden[NF:]
-    embed_low = grad_hidden.astype(BF)
-    g_embed = fold(t_mm(latent, embed_low), 0)
-    grad_latent = mm_t(embed_low, embed)
-    g_qkv = fold(g_qkv, 3)
-    g_project = fold(g_project, 1)
-    g_widen = fold(g_widen, 2)
-    g_narrow = fold(g_narrow, 1)
-    small = jnp.concatenate([g_positions, gains.reshape(-1, 512)], axis=0)
-    small = small + beside(small.astype(BF)).astype(F32)
-
-    hints = frames_in(frame_cotangent, 2)
+
+    recon_pairs, p3, p2, p1 = dec_fwd(decoded, dec_u[2], dec_u[1], dec_u[0], dec_b)
     g_decoded, h2, h3, h4, h_outer = dec_bwd(hints, decoded, p3, p2, p1, dec_a, *dec_t)
     g_spread = jnp.concatenate([g_decoded, across(g_decoded)], axis=1)
     g_head_out = fold(jnp.concatenate([t_mm(g_spread[h], latent) for h in range(4)]), 1)
+    head_out4 = jnp.concatenate(head_out, axis=1).reshape(4, 1024, 512)
+    head_in4 = jnp.concatenate(head_in, axis=1).reshape(4, 1024, 512)
+    feat = jnp.concatenate([feat, across(feat)], axis=1)
     grad_latent = grad_latent + sum(mm(g_spread[h], head_out4[h]) for h in range(4))
     dec_flat = pack_kernels(
         red_to_we(h_outer),
@@ -759,17 +1059,8 @@
     )
     dec_share = strip_share(dec_flat, x, core)
 
-    early_wide = rows_total(
-        [
-            g_widen.reshape(-1, 512),
-            g_narrow.reshape(-1, 512),
-            g_project.reshape(-1, 512),
-            g_embed,
-            small,
-        ]
-    )
-    qkv_rows = jnp.concatenate([g_qkv[0], g_qkv[1]], axis=-1).reshape(-1, 256)
-    early = rows_total([g_head_out, qkv_rows, dec_share])
+    d_parts = [g_head_out, dec_share]
+    d_flat = stacked_rows(d_parts, line)
 
     grouped = chances.reshape(2 * NF, -1, LCLASS)
     grad_grouped = grad_latent.reshape(grouped.shape)
@@ -778,8 +1069,10 @@
     g_head_in = fold(jnp.concatenate([t_mm(feat[h], grad_logits) for h in range(4)]), 1)
     g_feat = jnp.stack([mm_t(grad_logits, head_in4[h]) for h in range(4)]).astype(BF)
     g_feat = (g_feat[:, :NF].astype(F32) + across(g_feat[:, NF:]).astype(F32)).astype(BF)
+    g_feat, t_share, d_flat = lax.optimization_barrier((g_feat, t_share, d_flat))
+    d_share = rows_share(d_flat)
+    t_total = rows_whole(t_share)
     d_pairs, e2, e3, e4, e_outer = enc_bwd(pixels, z1, z2, z3, z4, g_feat, *enc_u, enc_b)
-    frames_grad = frames_out(d_pairs, F32, 4)
     enc_flat = pack_kernels(
         red_to_we(e_outer),
         gt_to_we(e2, 4, 32, 64),
@@ -787,7 +1080,12 @@
         gt_to_we(e4, 1, 128, 256),
     )
     enc_share = strip_share(enc_flat, x, core)
-    late = rows_total([g_head_in, enc_share])
+    late_parts = [g_head_in, enc_share]
+    late_flat = stacked_rows(late_parts, 16)
+    late_flat, d_share = lax.optimization_barrier((late_flat, d_share))
+    d_total = pieces_of(rows_whole(d_share), d_parts)
+    late, recon, frames_grad = finish(late_flat, recon_pairs, d_pairs, 4, 2)
+    late = pieces_of(late, late_parts)
 
     def of_encoder(part, c, o):
         return part.astype(F32).reshape(4, o, 4, c).transpose(1, 3, 0, 2)
@@ -796,8 +1094,12 @@
         return jnp.flip(part.astype(F32).reshape(4, o, 4, c), (0, 2)).transpose(3, 1, 0, 2)
 
     k1, k2, k3, k4 = unpack_kernels(strip_whole(late[1], x, core))
-    j1, j2, j3, j4 = unpack_kernels(strip_whole(early[2], x, core))
-    r_qkv = early[1].astype(F32).reshape(3, 512, 2, 128).transpose(2, 1, 0, 3)
+    j1, j2, j3, j4 = unpack_kernels(strip_whole(d_total[1], x, core))
+    t_total = t_total.astype(F32)
+    t_layers = t_total[: layers * LAYER_ROWS].reshape(layers, LAYER_ROWS, 512)
+    t_rest = t_total[layers * LAYER_ROWS :]
+    r_qkv = t_layers[:, 1152:].reshape(layers, 3, 128, 4, 128).transpose(0, 3, 2, 1, 4)
+    r_qkv = r_qkv.reshape(qkv_weight.shape)
     return (
         tokens_out,
         recon,
@@ -807,14 +1109,14 @@
         of_encoder(k3, 64, 128),
         of_encoder(k4, 128, 256),
         channels_first(late[0].astype(F32)),
-        early_wide[3].astype(F32),
-        early_wide[4][:NF].astype(F32),
-        early_wide[4][NF:].astype(F32).reshape(norm_gains.shape),
+        t_rest[:256],
+        t_rest[256 : 256 + NF],
+        t_rest[256 + NF : 256 + NF + 2 * layers].reshape(norm_gains.shape),
         r_qkv,
-        early_wide[2].astype(F32).reshape(out_weight.shape),
-        early_wide[0].astype(F32).reshape(up_weight.shape),
-        early_wide[1].astype(F32).reshape(down_weight.shape),
-        channels_first(early[0].astype(F32)).T,
+        t_layers[:, 1024:1152],
+        t_layers[:, 512:1024],
+        t_layers[:, :512],
+        channels_first(d_total[0].astype(F32)).T,
         of_decoder(j4, 128, 256),
         of_decoder(j3, 64, 128),
         of_decoder(j2, 32, 64),

time: 972 us -> 747 us (0.77)
  waiting for transfers between devices: 304 us -> 114 us
  Pallas kernels: 211 us -> 352 us
  local copies, waits for them, and re-layouts: 230 us -> 156 us
  other arithmetic: 114 us -> 54.6 us
  matrix products: 62.5 us -> 20 us
    pallas_call x2 -> x3, Pallas kernels: 40.4 us -> 200 us  [the longest x1 114 us: finish(): pl.pallas_call(functools.partial(finish_kernel, count, chunks), out_shape...]
    all_gather x3 -> x2, waiting for transfers between devices: 105 us -> 0.01 us  [rows_whole(): return lax.all_gather(share, 'rows', axis=0, tiled=True)]
    reduce_scatter x3 -> x2, waiting for transfers between devices: 164 us -> 71.3 us  [rows_share(): return lax.psum_scatter(flat, 'rows', scatter_dimension=0, tiled=True)]
    unnamed x471 -> x197, local copies, waits for them, and re-layouts: 64.9 us -> 34.2 us
    convert_element_type x14 -> x0, local copies, waits for them, and re-layouts: 19.4 us -> none  [the longest x12 17.6 us: layer_backward(): part.reshape(token_count, -1).astype(BF)]
    pallas_call x2 -> x1, Pallas kernels: 40.1 us -> 21.2 us  [frames_in(): pl.pallas_call(frames_in_kernel, out_shape=jax.ShapeDtypeStruct((34, NF,...]
    concatenate x5 -> x3, other arithmetic: 20 us -> 2.48 us  [the longest x2 1.77 us: stacked_rows(): flat = jnp.concatenate([part.astype(BF) for part in parts], axis=0)]
    dot_general x12 -> x0, matrix products: 16.1 us -> none  [the longest x2 3.97 us: layer_backward(): jnp.einsum('bhqk,bqhe->bkhe', chances.astype(BF), grad_attended, preferre...]
  transfers between devices with their start and end apart: 43 -> 28, of which waited for: 16 -> 11; matrix products, arithmetic and copies ran while one was open for 31% -> 27% of each run, Pallas kernels for 17% -> 42%
where the time goes in v2:
time: 747 us; the launch traced here: 733 us
  Pallas kernels  352 us (47%)
  local copies, waits for them, and re-layouts  156 us (21%)
  waiting for transfers between devices  114 us (15%)
  other arithmetic  54.6 us (7%)
  starting transfers between devices  21.3 us (3%)
  matrix products  20 us (3%)
  between operations  16 us (2%)
    pallas_call x4, Pallas kernels, run(): pl.pallas_call(kernel, out_shape=outs, in_specs=VM(len(args)), out_specs=...  131 us
    pallas_call x1, Pallas kernels, finish(): pl.pallas_call(functools.partial(finish_kernel, count, chunks), out_shape...  114 us
    pallas_call x1, Pallas kernels, middle(): pl.pallas_call(functools.partial(middle_kernel, layers), out_shape=(S((t,...  84.3 us
    reduce_scatter x2, waiting for transfers between devices, rows_share(): return lax.psum_scatter(flat, 'rows', scatter_dimension=0, tiled=True)  71.3 us
    ppermute x7, waiting for transfers between devices, across(): return lax.ppermute(value, 'strip', [(0, 2), (2, 0), (1, 3), (3, 1)])  38.1 us
    unnamed x197, local copies, waits for them, and re-layouts  34.2 us
    pallas_call x1, Pallas kernels, frames_in(): pl.pallas_call(frames_in_kernel, out_shape=jax.ShapeDtypeStruct((34, NF,...  21.2 us
  transfers between devices with their start and end apart: 28, of which 11 were waited for; matrix products, arithmetic and copies ran while one was open for 27% of the time, Pallas kernels for 42%

profile of v2, /device:TPU:0, one launch (start us, length us, event | category | flops | bytes accessed | tf_op | source)
XLA Modules:
  0.0 733.5 jit_solution(7063277038226797868)
XLA Ops:
  7.3 3.3 copy.162
  26.3 2.8 copy.149
  33.7 21.2 %frames_in.1.xp = bf16[34,64,384]{2,1,0:T(8,128)(2,1)S(1)} custom-call(bf16[3,16,64,256]{3,2,1,0:T(8,128)(2,1)S(1)} %bitcast.308), custom_call_target="tpu_custom_call" | custom-call | tf_op jit(solution)/shard_map/frames_in/pallas_call | solution.py:313
  57.7 21.9 %encode.1 = (bf16[32,64,1024]{2,1,0:T(8,128)(2,1)}, bf16[16,64,1024]{2,1,0:T(8,128)(2,1)}, bf16[8,64,1024]{2,1,0:T(8,128)(2,1)}, bf16[4,64,1024]{2,1,0:T(8,128)(2,1)}, bf16[4,64,1024]{2,1,0:T(8,128)(2,1)}) custom-call(bf16[34,64,384]{2,1,0:T(8,128)(2,1)} %copy-done.2, bf16[1152,1024]{1,0:T(8,128)(2,1)} %bitcast.337, bf16[2048,256]{1,0:T(8,128)(2,1)} %bitcast.351, ...), custom_call_target="tpu_custom_call" | custom-call | flops 10000000000 | bytes 20971520 | tf_op jit(solution)/shard_map/encode/pallas_call | solution.py:244
  80.6 4.9 rev.32
  143.3 4.5 copy.178
  150.0 2.4 copy.180
  163.4 8.5 %collective-permute-start.9 = (bf16[8,64,384]{2,1,0:T(8,128)(2,1)S(1)}, bf16[8,64,384]{2,1,0:T(8,128)(2,1)S(1)}, u32[]{:S(2)}, u32[]{:S(2)}) collective-permute-start(bf16[8,64,384]{2,1,0:T(8,128)(2,1)S(1)} %get-tuple-element.62), channel_id=1, source_target_pairs={{0,1},{1,2},{2,3},{3,0},{4,5},{5,6},{6,7},{7,4},{8,9},{9,10},{10,1... | collective-permute-start | bytes 1179656 | tf_op jit(solution)/shard_map/ppermute | solution.py:358
  172.0 84.3 %middle.1 = (bf16[128,512]{1,0:T(8,128)(2,1)}, bf16[128,512]{1,0:T(8,128)(2,1)}, f32[128,512]{1,0:T(8,128)}, bf16[4,64,1024]{2,1,0:T(8,128)(2,1)}, bf16[3456,512]{1,0:T(8,128)(2,1)}, /*index=5*/f32[128,512]{1,0:T(8,128)}) custom-call(bf16[4,64,1024]{2,1,0:T(8,128)(2,1)} %get-tuple-element.57.feat, bf16[4096,256]{1,0:T(8,128)(2,1)} %bitcast.21.lh0, ...), custom_call_target="tpu_custom_call" | custom-call | tf_op jit(solution)/shard_map/middle/pallas_call | solution.py:795
  256.3 24.4 %decode.1 = (bf16[32,64,384]{2,1,0:T(8,128)(2,1)}, bf16[8,64,1024]{2,1,0:T(8,128)(2,1)}, bf16[16,64,1024]{2,1,0:T(8,128)(2,1)}, bf16[32,64,1024]{2,1,0:T(8,128)(2,1)}) custom-call(bf16[4,64,1024]{2,1,0:T(8,128)(2,1)} %get-tuple-element.65.dec, bf16[2,1536,256]{2,1,0:T(8,128)(2,1)} %pad_maximum_fusion.5.u4, bf16[2,1024,256]{2,1,0:T(8,128)(2,1)} %pad_maximum_fusion.12.u3, ...), custom_call_target="tpu_custom_call" | custom-call | flops 10000000000 | bytes 20971520 | tf_op jit(solution)/shard_map/decode/pallas_call | solution.py:244
  281.7 41.0 %decode_back.1 = (bf16[4,64,1024]{2,1,0:T(8,128)(2,1)}, f32[4,256,512]{2,1,0:T(8,128)}, f32[4,256,512]{2,1,0:T(8,128)}, f32[4,256,512]{2,1,0:T(8,128)}, f32[3,32,384]{2,1,0:T(8,128)}) custom-call(bf16[8,64,384]{2,1,0:T(8,128)(2,1)} %copy-done.5, bf16[8,64,384]{2,1,0:T(8,128)(2,1)} %copy-done.88, bf16[8,64,384]{2,1,0:T(8,128)(2,1)} %copy-done.86, ...), custom_call_target="tpu_custom_call" | custom-call | flops 10000000000 | bytes 20971520 | tf_op jit(solution)/shard_map/decode_back/pallas_call | solution.py:244
  332.0 5.2 collective-permute-done.12
  373.2 8.3 %collective-permute-done.14 = bf16[4,64,1024]{2,1,0:T(8,128)(2,1)} collective-permute-done((bf16[4,64,1024]{2,1,0:T(8,128)(2,1)}, bf16[4,64,1024]{2,1,0:T(8,128)(2,1)}, u32[]{:S(2)}, u32[]{:S(2)}) %collective-permute-start.14) | collective-permute-done | bytes 524320 | tf_op jit(solution)/shard_map/ppermute | solution.py:839
  383.5 5.3 collective-permute-done.17
  389.8 2.4 fusion.3
  393.9 17.6 %reduce-scatter.3.cloned.1.call-done = bf16[432,512]{1,0:T(8,128)(2,1)} async-done(((bf16[3456,512]{1,0:T(8,128)(2,1)}), bf16[432,512]{1,0:T(8,128)(2,1)}) %reduce-scatter.3.cloned.1.call-update) | async-done | bytes 442384 | tf_op jit(solution)/shard_map/reduce_scatter | solution.py:886
  411.5 43.7 %encode_back.1 = (bf16[32,64,384]{2,1,0:T(8,128)(2,1)}, f32[4,256,512]{2,1,0:T(8,128)}, f32[4,256,512]{2,1,0:T(8,128)}, f32[4,256,512]{2,1,0:T(8,128)}, f32[3,32,384]{2,1,0:T(8,128)}) custom-call(bf16[34,64,384]{2,1,0:T(8,128)(2,1)} %copy-done.2, bf16[32,64,1024]{2,1,0:T(8,128)(2,1)} %get-tuple-element.70.z1, bf16[16,64,1024]{2,1,0:T(8,128)(2,1)} %get-tuple-element.71.z2, ...), custom_call_target="tpu_custom_call" | custom-call | flops 10000000000 | bytes 20971520 | tf_op jit(solution)/shard_map/encode_back/pallas_call | solution.py:244
  464.8 3.4 fusion.4
  468.2 5.6 collective-permute-done.19
  474.1 53.7 %reduce-scatter.5.cloned.1.call-done = bf16[608,256]{1,0:T(8,128)(2,1)} async-done(((bf16[4864,256]{1,0:T(8,128)(2,1)}), bf16[608,256]{1,0:T(8,128)(2,1)}) %reduce-scatter.5.cloned.1.call-update) | async-done | bytes 311312 | tf_op jit(solution)/shard_map/reduce_scatter | solution.py:886
  530.0 113.7 %finish.1 = (bf16[4,2,4,160,256]{4,3,2,1,0:T(8,128)(2,1)}, bf16[3,16,64,256]{3,2,1,0:T(8,128)(2,1)}, f32[3,16,64,256]{3,2,1,0:T(8,128)}) custom-call(bf16[4,2,4,160,256]{4,3,2,1,0:T(8,128)(2,1)} %bitcast.314, bf16[32,64,384]{2,1,0:T(8,128)(2,1)} %get-tuple-element.87.recon, bf16[32,64,384]{2,1,0:T(8,128)(2,1)} %get-tuple-element.88.grad), custom_call_target="tpu_custom_call" | custom-call | tf_op jit(solution)/shard_map/finish/pallas_call | solution.py:485
  646.3 7.7 %collective-permute-done.20 = bf16[704,256]{1,0:T(8,128)(2,1)S(1)} collective-permute-done((bf16[704,256]{1,0:T(8,128)(2,1)S(1)}, bf16[704,256]{1,0:T(8,128)(2,1)S(1)}, u32[]{:S(2)}, u32[]{:S(2)}) %collective-permute-start.20) | collective-permute-done | bytes 360480 | tf_op jit(solution)/shard_map/ppermute | solution.py:839
  659.7 4.4 copy.199
  671.1 6.1 collective-permute-done.22
  682.4 2.8 slice.722
  685.3 2.4 copy-done.7
  695.1 4.7 fusion.93
  701.4 3.2 copy.201
  704.6 5.8 copy.210
  714.7 2.7 copy.211
  719.1 2.3 copy.212
  722.1 2.7 copy.242
  (479 shorter events, 194.7 us)
Async XLA Ops:
  7.2 404.3 %reduce-scatter.3.cloned.1.call-start = ((), (), s32[]{:S(2)}) async-start(), calls=%async_computation.2 | async-start | bytes 3981312 | tf_op jit(solution)/shard_map/reduce_scatter | solution.py:886
  12.6 159.3 %collective-permute-start.1 = (bf16[4096,256]{1,0:T(8,128)(2,1)}, bf16[4096,256]{1,0:T(8,128)(2,1)}, u32[]{:S(2)}, u32[]{:S(2)}) collective-permute-start(bf16[4096,256]{1,0:T(8,128)(2,1)} %bitcast.26.dh0), channel_id=1, source_target_pairs={{0,1},{1,0},{2,3},{3,2},{4,5},{5,4},{6,7},{7,6},{8,9},{9,8},{10,11... | collective-permute-start | bytes 6291464 | tf_op jit(solution)/shard_map/ppermute | solution.py:843
  15.2 156.8 %collective-permute-start = (bf16[4096,256]{1,0:T(8,128)(2,1)}, bf16[4096,256]{1,0:T(8,128)(2,1)}, u32[]{:S(2)}, u32[]{:S(2)}) collective-permute-start(bf16[4096,256]{1,0:T(8,128)(2,1)} %bitcast.21.lh0), channel_id=1, source_target_pairs={{0,1},{1,0},{2,3},{3,2},{4,5},{5,4},{6,7},{7,6},{8,9},{9,8},{10,11... | collective-permute-start | bytes 6291464 | tf_op jit(solution)/shard_map/ppermute | solution.py:843
  15.2 140.3 %collective-permute-start.2 = (bf16[256,512]{1,0:T(8,128)(2,1)}, bf16[256,512]{1,0:T(8,128)(2,1)}, u32[]{:S(2)}, u32[]{:S(2)}) collective-permute-start(bf16[256,512]{1,0:T(8,128)(2,1)} %emb0.1), channel_id=1, source_target_pairs={{0,1},{1,0},{2,3},{3,2},{4,5},{5,4},{6,7},{7,6},{8,9},{9,8},{10,11... | collective-permute-start | bytes 786440 | tf_op jit(solution)/shard_map/ppermute | solution.py:843
  15.7 141.5 %collective-permute-start.4 = (bf16[2,128,512]{2,1,0:T(8,128)(2,1)}, bf16[2,128,512]{2,1,0:T(8,128)(2,1)}, u32[]{:S(2)}, u32[]{:S(2)}) collective-permute-start(bf16[2,128,512]{2,1,0:T(8,128)(2,1)} %proj0.1), channel_id=1, source_target_pairs={{0,1},{1,0},{2,3},{3,2},{4,5},{5,4},{6,7},{7,6},{8,9},{9,8},{10,11... | collective-permute-start | bytes 786440 | tf_op jit(solution)/shard_map/ppermute | solution.py:843
  33.7 22.5 %copy-start.15 = (bf16[256,128,4,4]{1,3,2,0:T(4,128)(2,1)S(1)}, bf16[256,128,4,4]{1,3,2,0:T(4,128)(2,1)}, u32[]{:S(2)}) copy-start(bf16[256,128,4,4]{1,3,2,0:T(4,128)(2,1)} %param.26) | copy-start | bytes 3145732
  79.6 77.7 %collective-permute-start.8 = (bf16[4,64,1024]{2,1,0:T(8,128)(2,1)}, bf16[4,64,1024]{2,1,0:T(8,128)(2,1)}, u32[]{:S(2)}, u32[]{:S(2)}) collective-permute-start(bf16[4,64,1024]{2,1,0:T(8,128)(2,1)} %get-tuple-element.57.feat), channel_id=1, source_target_pairs={{0,2},{2,0},{1,3},{3,1},{4,6},{6,4},{5,7},{7,5},{8,10},{10,8},{9,1... | collective-permute-start | bytes 1572872 | tf_op jit(solution)/shard_map/ppermute | solution.py:839
  155.5 6.6 collective-permute-start.5
  157.1 6.3 collective-permute-start.6
  157.4 4.3 collective-permute-start.3
  161.7 119.0 %collective-permute-start.10 = (bf16[8,64,384]{2,1,0:T(8,128)(2,1)S(1)}, bf16[8,64,384]{2,1,0:T(8,128)(2,1)S(1)}, u32[]{:S(2)}, u32[]{:S(2)}) collective-permute-start(bf16[8,64,384]{2,1,0:T(8,128)(2,1)S(1)} %get-tuple-element.63), channel_id=1, source_target_pairs={{0,2},{1,3},{2,0},{3,1},{4,6},{5,7},{6,4},{7,5},{8,10},{9,11},{10,... | collective-permute-start | bytes 1179656 | tf_op jit(solution)/shard_map/ppermute | solution.py:358
  162.1 118.6 %collective-permute-start.11 = (bf16[8,64,384]{2,1,0:T(8,128)(2,1)S(1)}, bf16[8,64,384]{2,1,0:T(8,128)(2,1)S(1)}, u32[]{:S(2)}, u32[]{:S(2)}) collective-permute-start(bf16[8,64,384]{2,1,0:T(8,128)(2,1)S(1)} %get-tuple-element.64), channel_id=1, source_target_pairs={{0,3},{1,0},{2,1},{3,2},{4,7},{5,4},{6,5},{7,6},{8,11},{9,8},{10,9... | collective-permute-start | bytes 1179656 | tf_op jit(solution)/shard_map/ppermute | solution.py:358
  163.4 117.3 %collective-permute-start.9 = (bf16[8,64,384]{2,1,0:T(8,128)(2,1)S(1)}, bf16[8,64,384]{2,1,0:T(8,128)(2,1)S(1)}, u32[]{:S(2)}, u32[]{:S(2)}) collective-permute-start(bf16[8,64,384]{2,1,0:T(8,128)(2,1)S(1)} %get-tuple-element.62), channel_id=1, source_target_pairs={{0,1},{1,2},{2,3},{3,0},{4,5},{5,6},{6,7},{7,4},{8,9},{9,10},{10,1... | collective-permute-start | bytes 1179656 | tf_op jit(solution)/shard_map/ppermute | solution.py:358
  322.7 14.5 %collective-permute-start.12 = (bf16[4,64,1024]{2,1,0:T(8,128)(2,1)}, bf16[4,64,1024]{2,1,0:T(8,128)(2,1)}, u32[]{:S(2)}, u32[]{:S(2)}) collective-permute-start(bf16[4,64,1024]{2,1,0:T(8,128)(2,1)} %get-tuple-element.69), channel_id=1, source_target_pairs={{0,2},{2,0},{1,3},{3,1},{4,6},{6,4},{5,7},{7,5},{8,10},{10,8},{9,1... | collective-permute-start | bytes 1572872 | tf_op jit(solution)/shard_map/ppermute | solution.py:839
  330.9 36.7 %collective-permute-start.16 = (bf16[1408,256]{1,0:T(8,128)(2,1)}, bf16[1408,256]{1,0:T(8,128)(2,1)}, u32[]{:S(2)}, u32[]{:S(2)}) collective-permute-start(bf16[1408,256]{1,0:T(8,128)(2,1)} %constant_dynamic-slice_fusion.3), channel_id=1, source_target_pairs={{0,1},{1,0},{2,3},{3,2},{4,5},{5,4},{6,7},{7,6},{8,9},{9,8},{10,11... | collective-permute-start | bytes 2162696 | tf_op jit(solution)/shard_map/ppermute | solution.py:843
  331.0 196.7 %reduce-scatter.5.cloned.1.call-start = ((), (), s32[]{:S(2)}) async-start(), calls=%async_computation.3 | async-start | bytes 2801664 | tf_op jit(solution)/shard_map/reduce_scatter | solution.py:886
  357.1 32.8 %collective-permute-start.15 = (bf16[4096,256]{1,0:T(8,128)(2,1)}, bf16[4096,256]{1,0:T(8,128)(2,1)}, u32[]{:S(2)}, u32[]{:S(2)}) collective-permute-start(bf16[4096,256]{1,0:T(8,128)(2,1)} %slice.878), channel_id=1, source_target_pairs={{0,1},{1,0},{2,3},{3,2},{4,5},{5,4},{6,7},{7,6},{8,9},{9,8},{10,11... | collective-permute-start | bytes 6291464 | tf_op jit(solution)/shard_map/ppermute | solution.py:843
  366.4 15.0 %collective-permute-start.14 = (bf16[4,64,1024]{2,1,0:T(8,128)(2,1)}, bf16[4,64,1024]{2,1,0:T(8,128)(2,1)}, u32[]{:S(2)}, u32[]{:S(2)}) collective-permute-start(bf16[4,64,1024]{2,1,0:T(8,128)(2,1)} %slice.667), channel_id=1, source_target_pairs={{0,2},{2,0},{1,3},{3,1},{4,6},{6,4},{5,7},{7,5},{8,10},{10,8},{9,1... | collective-permute-start | bytes 1572872 | tf_op jit(solution)/shard_map/ppermute | solution.py:839
  369.1 19.7 %collective-permute-start.17 = (bf16[704,256]{1,0:T(8,128)(2,1)S(1)}, bf16[704,256]{1,0:T(8,128)(2,1)}, u32[]{:S(2)}, u32[]{:S(2)}) collective-permute-start(bf16[704,256]{1,0:T(8,128)(2,1)S(1)} %constant_dynamic-slice_fusion.2), channel_id=1, source_target_pairs={{0,2},{2,0},{1,3},{3,1},{4,6},{6,4},{5,7},{7,5},{8,10},{10,8},{9,1... | collective-permute-start | bytes 1081352 | tf_op jit(solution)/shard_map/ppermute | solution.py:839
  371.4 20.9 %copy-start.6 = (f32[4096,512]{1,0:T(8,128)}, f32[4096,512]{1,0:T(8,128)S(1)}, u32[]{:S(2)}) copy-start(f32[4096,512]{1,0:T(8,128)S(1)} %pad_maximum_fusion) | copy-start | bytes 25165828
  373.2 91.7 %collective-permute-start.13 = (bf16[4096,256]{1,0:T(8,128)(2,1)}, bf16[4096,256]{1,0:T(8,128)(2,1)}, u32[]{:S(2)}, u32[]{:S(2)}) collective-permute-start(bf16[4096,256]{1,0:T(8,128)(2,1)} %slice.879), channel_id=1, source_target_pairs={{0,1},{1,0},{2,3},{3,2},{4,5},{5,4},{6,7},{7,6},{8,9},{9,8},{10,11... | collective-permute-start | bytes 6291464 | tf_op jit(solution)/shard_map/ppermute | solution.py:843
  458.4 207.2 %all-gather.5.cloned.1.call-start = ((), (), s32[]{:S(2)}) async-start(), calls=%async_computation.5 | async-start | bytes 2801664 | tf_op jit(solution)/shard_map/all_gather | solution.py:890
  460.8 2.3 collective-permute-start.18
  463.3 10.5 %collective-permute-start.19 = (bf16[704,256]{1,0:T(8,128)(2,1)S(1)}, bf16[704,256]{1,0:T(8,128)(2,1)S(1)}, u32[]{:S(2)}, u32[]{:S(2)}) collective-permute-start(bf16[704,256]{1,0:T(8,128)(2,1)S(1)} %constant_dynamic-slice_fusion), channel_id=1, source_target_pairs={{0,2},{2,0},{1,3},{3,1},{4,6},{6,4},{5,7},{7,5},{8,10},{10,8},{9,1... | collective-permute-start | bytes 1081352 | tf_op jit(solution)/shard_map/ppermute | solution.py:839
  527.8 154.6 %all-gather.3.cloned.1.call-start = ((), (), s32[]{:S(2)}) async-start(), calls=%async_computation.4 | async-start | bytes 3981312 | tf_op jit(solution)/shard_map/all_gather | solution.py:890
  530.0 116.2 %copy-start.71 = (bf16[128,512]{1,0:T(8,128)(2,1)S(1)}, bf16[128,512]{1,0:T(8,128)(2,1)}, u32[]{:S(2)}) copy-start(bf16[128,512]{1,0:T(8,128)(2,1)} %get-tuple-element.58) | copy-start | bytes 393220
  644.8 9.2 %collective-permute-start.20 = (bf16[704,256]{1,0:T(8,128)(2,1)S(1)}, bf16[704,256]{1,0:T(8,128)(2,1)S(1)}, u32[]{:S(2)}, u32[]{:S(2)}) collective-permute-start(bf16[704,256]{1,0:T(8,128)(2,1)S(1)} %slice.709), channel_id=1, source_target_pairs={{0,2},{2,0},{1,3},{3,1},{4,6},{6,4},{5,7},{7,5},{8,10},{10,8},{9,1... | collective-permute-start | bytes 1081352 | tf_op jit(solution)/shard_map/ppermute | solution.py:839
  654.3 9.8 %collective-permute-start.21 = (bf16[1408,256]{1,0:T(8,128)(2,1)S(1)}, bf16[1408,256]{1,0:T(8,128)(2,1)S(1)}, u32[]{:S(2)}, u32[]{:S(2)}) collective-permute-start(bf16[1408,256]{1,0:T(8,128)(2,1)S(1)} %maximum_select_fusion.2), channel_id=1, source_target_pairs={{0,1},{1,0},{2,3},{3,2},{4,5},{5,4},{6,7},{7,6},{8,9},{9,8},{10,11... | collective-permute-start | bytes 2162696 | tf_op jit(solution)/shard_map/ppermute | solution.py:843
  654.4 2.3 collective-permute-start.7
  666.6 10.6 %collective-permute-start.22 = (bf16[704,256]{1,0:T(8,128)(2,1)S(1)}, bf16[704,256]{1,0:T(8,128)(2,1)}, u32[]{:S(2)}, u32[]{:S(2)}) collective-permute-start(bf16[704,256]{1,0:T(8,128)(2,1)S(1)} %slice.728), channel_id=1, source_target_pairs={{0,2},{2,0},{1,3},{3,1},{4,6},{6,4},{5,7},{7,5},{8,10},{10,8},{9,1... | collective-permute-start | bytes 1081352 | tf_op jit(solution)/shard_map/ppermute | solution.py:839
  668.8 10.6 %copy-start.14 = (bf16[2816,256]{1,0:T(8,128)(2,1)S(1)}, bf16[2816,256]{1,0:T(8,128)(2,1)}, u32[]{:S(2)}) copy-start(bf16[2816,256]{1,0:T(8,128)(2,1)} %copy-done.13) | copy-start | bytes 4325380
  679.4 31.0 %collective-permute-start.23 = (bf16[1408,256]{1,0:T(8,128)(2,1)}, bf16[1408,256]{1,0:T(8,128)(2,1)}, u32[]{:S(2)}, u32[]{:S(2)}) collective-permute-start(bf16[1408,256]{1,0:T(8,128)(2,1)} %maximum_select_fusion.3), channel_id=1, source_target_pairs={{0,1},{1,0},{2,3},{3,2},{4,5},{5,4},{6,7},{7,6},{8,9},{9,8},{10,11... | collective-permute-start | bytes 2162696 | tf_op jit(solution)/shard_map/ppermute | solution.py:843
  (89 other events, 214.2 us)
Sparse Core Ops, SparseCore 0:
  331.2 80.2 reduce-scatter.2
  458.5 69.2 reduce-scatter.4
  530.2 80.7 all-gather.4
  613.2 68.5 all-gather.2

commit v3 on v2

--- a/solution.py
+++ b/solution.py
@@ -19,50 +19,6 @@
 MESH = pl.DeviceIdType.MESH
 
 
-def canon_T(we, a):
-    _,_,c,o=we.shape
-    flat=we.reshape(4,4*c,o)
-    cols=[]
-    for j in range(a):
-        top=(a+2*j-1)*c
-        cols.append(jnp.pad(flat,((0,0),(top,512-top-4*c),(0,0))))
-    return jnp.concatenate(cols,axis=2)
-
-def canon_U(T, a):
-    Tt=jnp.swapaxes(T,1,2)
-    z=jnp.zeros_like(Tt[:,:,:128])
-    left=jnp.concatenate([Tt[:,:,384:512],z],axis=2)
-    mid=Tt[:,:,128:384]
-    right=jnp.concatenate([z,Tt[:,:,0:128]],axis=2)
-    if a>1:
-        left=left[:,128:]; right=right[:,:128]
-    U=jnp.concatenate([left,mid,right],axis=1)
-    return jnp.stack([jnp.concatenate([U[1],U[3]]),jnp.concatenate([U[0],U[2]])])
-
-def outer_A(we):
-    w=jnp.arange(64)[:,None]; j=jnp.arange(32)[None,:]
-    kw=w-2*j+1
-    hot=(kw[None]==jnp.arange(4)[:,None,None]).astype(we.dtype)
-    full=jnp.einsum("kwj,hkco->hcwjo",hot,we,preferred_element_type=F32).astype(we.dtype)
-    full=full.reshape(4,192,1024)
-    z=jnp.zeros_like(full[0])
-    return jnp.stack([jnp.concatenate([z,full[0]]),jnp.concatenate([full[1],full[2]]),jnp.concatenate([full[3],z])])
-
-def outer_B(A):
-    return jnp.swapaxes(A,1,2).reshape(3072,384)
-
-def gt_to_we(GT, a, c, o):
-    tot=0
-    for j in range(a):
-        s=(a+2*j-1)*c
-        tot=tot+GT[:,j*o:(j+1)*o,s:s+4*c]
-    return tot
-
-def red_to_we(red):
-    r=red.reshape(3,32,2,3,64)[...,:4]
-    r=r.transpose(0,2,3,4,1)
-    return jnp.stack([r[0,1],r[1,0],r[1,1],r[2,0]])
-
 def sig(z): return 1.0/(1.0+jnp.exp(-z))
 
 def zero_big(ref,rows):
@@ -112,14 +68,53 @@
     for q in range(4):
         dst[256*q:256*q+256,:]=src[1:rows+1,:,pad+256*q:pad+256*q+256].reshape(rows*NF,256).T
 
-def grad_w(big,yt,rows,out):
-    def body(kh,half):
+def grad_w(big,yt,rows):
+    out=[]
+    for kh in range(4):
         acc=jnp.zeros((256,512),F32)
         for q in range(4):
-            win=big[pl.ds(half,rows),kh-2*half,:,256*q:256*q+512].reshape(rows*NF,512)
+            win=big[pl.ds(kh//2,rows),kh%2,:,256*q:256*q+512].reshape(rows*NF,512)
             acc=acc+jnp.dot(yt[256*q:256*q+256,:],win,preferred_element_type=F32)
-        out[kh]=acc
-    for kh in range(4): body(kh,kh//2)
+        out.append(acc)
+    return out
+
+def pack(pk,base,a,c,o,sums,flipped,swap,turned=False):
+    taps=[]
+    for acc in sums:
+        total=None
+        for j in range(a):
+            first=(a+2*j-1)*c
+            part=acc[j*o:j*o+o]
+            if first: part=pltpu.roll(part,512-first,1)
+            part=part[:,:4*c]
+            total=part if total is None else total+part
+        taps.append(total.astype(BF) if turned else total.T.astype(BF))
+    width,count=(c,o//16) if turned else (o,c//16)
+    held=[]
+    for b in range(count):
+        rows=[]
+        for k in range(16):
+            kh,kw=divmod(15-k if flipped else k,4)
+            if turned: rows.append(taps[kh][16*b:16*b+16,c*kw:c*kw+c])
+            else: rows.append(taps[kh][c*kw+16*b:c*kw+16*b+16])
+        block=jnp.dot(swap,jnp.concatenate(rows,axis=0),preferred_element_type=F32).astype(BF)
+        if width==256: pk[base+256*b:base+256*b+256]=block
+        elif width==128:
+            side,at=divmod(b,count//2)
+            pk[base+256*at:base+256*at+256,128*side:128*side+128]=block
+        else: held.extend([block[:128],block[128:]])
+    if held: pk[base:base+128]=jnp.concatenate(held,axis=1)
+
+def pack_outer(pk,base,red,flipped):
+    r=lax.broadcasted_iota(jnp.int32,(48,1152),0); lane=lax.broadcasted_iota(jnp.int32,(48,1152),1)
+    k=lax.rem(r,16)
+    if flipped: k=15-k
+    kh,kw=lax.div(k,4),lax.rem(k,4)
+    at=384*lax.div(kh+1,2)+192*lax.rem(kh+1,2)+64*lax.div(r,16)+kw
+    pick=(lane==at).astype(BF)
+    value=jnp.concatenate([part.astype(BF) for part in red],axis=1)
+    pk[base:base+128]=jnp.zeros((128,256),BF)
+    pk[base:base+48,0:32]=lax.dot_general(pick,value,(((1,),(1,)),((),())),preferred_element_type=F32).astype(BF)
 
 def outer_down(xp,a_ref,emit,per=4):
     def body(g):
@@ -136,7 +131,8 @@
         emit(i0,jnp.dot(lhs,b_ref[...],preferred_element_type=F32).reshape(per,NF,384))
     loop(32//per,body)
 
-def outer_grad(xp,yt,red):
+def outer_grad(xp,yt):
+    red=[]
     lane=lax.broadcasted_iota(jnp.int32,(32,384),1)%64
     for d in range(3):
         x=xp[d:d+32].reshape(32*NF,384)
@@ -149,7 +145,8 @@
                 if j==0: v=jnp.where(lane==0,0.0,v)
                 if j==31: v=jnp.where(lane==3,0.0,v)
                 tot=tot+v
-        red[d]=tot
+        red.append(tot)
+    return red
 
 def enc_fwd_kernel(xp,a,t2,t3,t4,z1,z2,z3,z4,feat,m1,m2,m3):
     zero_big(m1,32); zero_big(m2,16); zero_big(m3,8)
@@ -166,9 +163,10 @@
     down(m2,t3,8,4,keep(z3,m3))
     down(m3,t4,4,4,keep(z4,None))
 
-def enc_bwd_kernel(xp,z1,z2,z3,z4,df,u2,u3,u4,b,dx,g2,g3,g4,red,m1,m2,m3,s1,s2,s3,s4,yt1,yt2,yt3,yt4):
+def enc_bwd_kernel(xp,z1,z2,z3,z4,df,u2,u3,u4,b,dx,pk,m1,m2,m3,s1,s2,s3,s4,yt1,yt2,yt3,yt4):
     zero_big(m1,32); zero_big(m2,16); zero_big(m3,8)
     zero_small(s1,32,0); zero_small(s2,16,128); zero_small(s3,8,128); zero_small(s4,4,256)
+    swap=exchange_16()
     z=z4[...].astype(F32); s=sig(z)
     s4[1:5,:,256:1280]=(df[...].astype(F32)*(s*(1.0+z*(1.0-s)))).astype(BF)
     def back(z_ref,m,dst,pad):
@@ -182,14 +180,14 @@
                 m[m0+t+odd,1-odd,:,128+256*q:384+256*q]=mm.astype(BF)
         return emit
     up(s4,u4,4,4,back(z3,m3,s3,128))
-    turn(s4,yt4,4,256); grad_w(m3,yt4,4,g4)
+    turn(s4,yt4,4,256); pack(pk,0,1,128,256,grad_w(m3,yt4,4),False,swap,True)
     up(s3,u3,8,4,back(z2,m2,s2,128))
-    turn(s3,yt3,8,128); grad_w(m2,yt3,8,g3)
+    turn(s3,yt3,8,128); pack(pk,2048,2,64,128,grad_w(m2,yt3,8),False,swap)
     up(s2,u2,16,4,back(z1,m1,s1,0))
-    turn(s2,yt2,16,128); grad_w(m1,yt2,16,g2)
+    turn(s2,yt2,16,128); pack(pk,2560,4,32,64,grad_w(m1,yt2,16),False,swap)
     def put(i0,acc): dx[pl.ds(i0,acc.shape[0])]=acc.astype(BF)
     outer_up(s1,b,put)
-    turn(s1,yt1,32,0); outer_grad(xp,yt1,red)
+    turn(s1,yt1,32,0); pack_outer(pk,2688,outer_grad(xp,yt1),False)
 
 def dec_fwd_kernel(dec,u4,u3,u2,b,recon,p3,p2,p1,s4,s3,s2,s1):
     zero_small(s1,32,0); zero_small(s2,16,128); zero_small(s3,8,128); zero_small(s4,4,256)
@@ -209,7 +207,7 @@
     def put(i0,acc): recon[pl.ds(i0,acc.shape[0])]=acc.astype(BF)
     outer_up(s1,b,put)
 
-def dec_bwd_kernel(c0,c1,c2,c3,dec,p3,p2,p1,a,t2,t3,t4,gdec,g2,g3,g4,red,d1,d2,d3,cp,yt1,yt2,yt3,yt4):
+def dec_bwd_kernel(c0,c1,c2,c3,dec,p3,p2,p1,a,t2,t3,t4,gdec,pk,d1,d2,d3,cp,yt1,yt2,yt3,yt4):
     me=lax.axis_index("strip")
     cp[0]=jnp.zeros((NF,384),BF); cp[33]=jnp.zeros((NF,384),BF)
     for k,part in enumerate((c0,c1,c2,c3)):
@@ -228,13 +226,14 @@
             if dst is None: gdec[pl.ds(i0,rows),:,256*q:256*q+256]=val.reshape(rows,NF,256)
             else: put_big(dst,half0,rows,q,val)
         return emit
-    maps(p1,32,yt1); outer_grad(cp,yt1,red)
+    swap=exchange_16()
+    maps(p1,32,yt1); pack_outer(pk,2688,outer_grad(cp,yt1),True)
     outer_down(cp,a,back(p1,d1))
-    maps(p2,16,yt2); grad_w(d1,yt2,16,g2)
+    maps(p2,16,yt2); pack(pk,2560,4,32,64,grad_w(d1,yt2,16),True,swap)
     down(d1,t2,16,4,back(p2,d2))
-    maps(p3,8,yt3); grad_w(d2,yt3,8,g3)
+    maps(p3,8,yt3); pack(pk,2048,2,64,128,grad_w(d2,yt3,8),True,swap)
     down(d2,t3,8,4,back(p3,d3))
-    maps(dec,4,yt4); grad_w(d3,yt4,4,g4)
+    maps(dec,4,yt4); pack(pk,0,1,128,256,grad_w(d3,yt4,4),True,swap)
     down(d3,t4,4,4,back(dec,None))
 
 def S(shape,dt=BF): return jax.ShapeDtypeStruct(shape,dt)
@@ -248,7 +247,7 @@
 def enc_fwd(xp,a,t2,t3,t4):
     return run(enc_fwd_kernel,(S((32,NF,1024)),S((16,NF,1024)),S((8,NF,1024)),S((4,NF,1024)),S((4,NF,1024))),
       [big(32),big(16),big(8)],(xp,a,t2,t3,t4),"encode")
-GS=tuple([S((4,256,512),F32)]*3+[S((3,32,384),F32)])
+GS=(S((2816,256)),)
 small=lambda h,p:V((h+2,NF,1024+2*p))
 yts=[V((1024,32*NF)),V((1024,16*NF)),V((1024,8*NF)),V((1024,4*NF))]
 def enc_bwd(xp,z1,z2,z3,z4,df,u2,u3,u4,b):
@@ -262,6 +261,12 @@
       (*hints,dec,p3,p2,p1,a,t2,t3,t4),"decode_back")
 
 
+def exchange_16():
+    r = lax.broadcasted_iota(jnp.int32, (256, 256), 0)
+    s = lax.broadcasted_iota(jnp.int32, (256, 256), 1)
+    return (s == lax.rem(r, 16) * 16 + lax.div(r, 16)).astype(BF)
+
+
 def first_frame(strip):
     return NF * ((strip % 2) * 2 + strip // 2)
 
@@ -270,11 +275,108 @@
     return jnp.concatenate([x[c, 2 * i + p] for p in range(2) for c in range(3)], axis=0).T
 
 
-def frames_in_kernel(x, out, stage, send_sem, recv_sem):
+def canonical(w, swap, c, o, flipped):
+    parts = {}
+    for b in range(c // 16):
+        block = jnp.dot(swap, w[256 * b : 256 * b + 256, :], preferred_element_type=F32).astype(BF)
+        for k in range(16):
+            parts[(15 - k if flipped else k, b)] = block[16 * k : 16 * k + 16]
+    return [
+        jnp.concatenate(
+            [parts[(4 * kh + kw, b)] for kw in range(4) for b in range(c // 16)], axis=0
+        )
+        for kh in range(4)
+    ]
+
+
+def canonical_turned(w, swap):
+    parts = {}
+    for b in range(16):
+        block = jnp.dot(swap, w[256 * b : 256 * b + 256, :], preferred_element_type=F32).astype(BF)
+        for k in range(16):
+            parts[(k, b)] = block[16 * k : 16 * k + 16]
+    return [
+        jnp.concatenate(
+            [
+                jnp.concatenate([parts[(4 * kh + kw, b)] for b in range(16)], axis=0)
+                for kw in range(4)
+            ],
+            axis=1,
+        )
+        for kh in range(4)
+    ]
+
+
+def band(flat, a, c, o):
+    def shifted(value, first):
+        above = jnp.zeros((first, value.shape[1]), BF)
+        below = jnp.zeros((512 - first - value.shape[0], value.shape[1]), BF)
+        return jnp.concatenate([above, value, below], axis=0)
+
+    if a == 1:
+        return flat
+    if a == 2:
+        return jnp.concatenate([shifted(flat, 64), shifted(flat, 192)], axis=1)
+    twice = jnp.concatenate([flat, flat], axis=1)
+    left = lax.broadcasted_iota(jnp.int32, (512, 128), 1) < 64
+    return jnp.concatenate(
+        [
+            jnp.where(left, shifted(twice, 96), shifted(twice, 160)),
+            jnp.where(left, shifted(twice, 224), shifted(twice, 288)),
+        ],
+        axis=1,
+    )
+
+
+def put_bands(t_ref, u_ref, bands, turned, a):
+    for kh in range(4):
+        t = bands[kh]
+        t_ref[512 * kh : 512 * kh + 512] = t
+        tt = t.T if turned is None else turned[kh]
+        z = jnp.zeros((256, 128), BF)
+        left = jnp.concatenate([tt[:, 384:512], z], axis=1)
+        right = jnp.concatenate([z, tt[:, :128]], axis=1)
+        if a > 1:
+            left, right = left[128:], right[:128]
+        k = 512 if a > 1 else 768
+        u_ref[1 - kh % 2, k * (kh // 2) : k * (kh // 2) + k] = jnp.concatenate(
+            [left, tt[:, 128:384], right], axis=0
+        )
+
+
+def put_outer(a_ref, b_ref, w, flipped):
+    row = lax.broadcasted_iota(jnp.int32, (64, 1024), 0)
+    col = lax.div(lax.broadcasted_iota(jnp.int32, (64, 1024), 1), 32)
+    tap = row - 2 * col + 1
+    for kh in range(4):
+        d, p = (kh + 1) // 2, (kh + 1) % 2
+        for c in range(3):
+            total = jnp.zeros((64, 1024), F32)
+            for kw in range(4):
+                k = 4 * kh + kw
+                r = 16 * c + (15 - k if flipped else k)
+                total = jnp.where(tap == kw, w[r : r + 1, :], total)
+            first = 384 * d + 192 * p + 64 * c
+            a_ref[first : first + 64] = total.astype(BF)
+    a_ref[0:192] = jnp.zeros((192, 1024), BF)
+    a_ref[960:1152] = jnp.zeros((192, 1024), BF)
+    for d in range(3):
+        b_ref[1024 * d : 1024 * d + 1024] = a_ref[384 * d : 384 * d + 384].T
+
+
+def start_kernel(
+    x, e1, e2, e3, e4, d1, d2, d3, d4, lh, dh, emb, qkv, proj, up, down,
+    pixels, ea, eb, et2, et3, et4, eu2, eu3, eu4, da, db, dt2, dt3, dt4, du2, du3, du4,
+    lh0, lh1, dh0, dh1, emb1, qkv1, proj1, up1, down1,
+    stage, send_sem, recv_sem, side_sems,
+    va, vb, vt2, vt3, vt4, vu2, vu3, vu4, wa, wb, wt2, wt3, wt4, wu2, wu3, wu4,
+    vl, vd, out_sems,
+):
     me = lax.axis_index("strip")
     row = lax.axis_index("rows")
-    out[0] = jnp.zeros((NF, 384), BF)
-    out[33] = jnp.zeros((NF, 384), BF)
+    sibling = (row, me + 1 - 2 * lax.rem(me, 2))
+    pixels[0] = jnp.zeros((NF, 384), BF)
+    pixels[33] = jnp.zeros((NF, 384), BF)
 
     def turn_rows(i, carry):
         flat = turned_rows(x, i)
@@ -295,7 +397,7 @@
         copies.append(
             pltpu.make_async_remote_copy(
                 src_ref=stage.at[to],
-                dst_ref=out.at[pl.ds(1 + 8 * me, 8)],
+                dst_ref=pixels.at[pl.ds(1 + 8 * me, 8)],
                 send_sem=send_sem.at[k - 1],
                 recv_sem=recv_sem.at[k - 1],
                 device_id=(row, to),
@@ -304,27 +406,114 @@
         )
     for copy in copies:
         copy.start()
-    out[pl.ds(1 + 8 * me, 8)] = stage[me]
+
+    def to_sibling(src, dst, index):
+        copy = pltpu.make_async_remote_copy(
+            src_ref=src,
+            dst_ref=dst,
+            send_sem=side_sems.at[0, index],
+            recv_sem=side_sems.at[1, index],
+            device_id=sibling,
+            device_id_type=MESH,
+        )
+        copy.start()
+        copies.append(copy)
+
+    for index, (src, dst) in enumerate(
+        ((emb, emb1), (qkv, qkv1), (proj, proj1), (up, up1), (down, down1))
+    ):
+        to_sibling(src, dst, index)
+    pixels[pl.ds(1 + 8 * me, 8)] = stage[me]
+
+    stores = []
+
+    def store(src, dst):
+        copy = pltpu.make_async_copy(src, dst, out_sems.at[len(stores)])
+        copy.start()
+        stores.append(copy)
+
+    swap = exchange_16()
+    put_outer(va, vb, e1, False)
+    store(va, ea)
+    store(vb, eb)
+    put_bands(vt2, vu2, [band(f, 4, 32, 64) for f in canonical(e2, swap, 32, 64, False)], None, 4)
+    store(vt2, et2)
+    store(vu2, eu2)
+    put_bands(vt3, vu3, [band(f, 2, 64, 128) for f in canonical(e3, swap, 64, 128, False)], None, 2)
+    store(vt3, et3)
+    store(vu3, eu3)
+    turned = canonical_turned(e4, swap)
+    put_bands(vt4, vu4, [f.T for f in turned], turned, 1)
+    store(vt4, et4)
+    store(vu4, eu4)
+    for b in range(16):
+        rows = slice(256 * b, 256 * b + 256)
+        for src, dst in ((lh[rows, :], vl), (dh[:, rows].T, vd)):
+            block = jnp.dot(swap, src, preferred_element_type=F32).astype(BF)
+            for k in range(16):
+                dst[256 * k + 16 * b : 256 * k + 16 * b + 16] = block[16 * k : 16 * k + 16]
+    store(vl, lh0)
+    store(vd, dh0)
+    to_sibling(vl, lh1, 5)
+    to_sibling(vd, dh1, 6)
+    put_outer(wa, wb, d4, True)
+    store(wa, da)
+    store(wb, db)
+    put_bands(wt2, wu2, [band(f, 4, 32, 64) for f in canonical(d3, swap, 32, 64, True)], None, 4)
+    store(wt2, dt2)
+    store(wu2, du2)
+    put_bands(wt3, wu3, [band(f, 2, 64, 128) for f in canonical(d2, swap, 64, 128, True)], None, 2)
+    store(wt3, dt3)
+    store(wu3, du3)
+    put_bands(wt4, wu4, canonical(d1, swap, 128, 256, True), None, 1)
+    store(wt4, dt4)
+    store(wu4, du4)
     for copy in copies:
         copy.wait()
-
-
-def frames_in(block, ident):
-    return pl.pallas_call(
-        frames_in_kernel,
-        out_shape=jax.ShapeDtypeStruct((34, NF, 384), BF),
-        in_specs=VM(1),
-        out_specs=VM(1)[0],
+    for copy in stores:
+        copy.wait()
+
+
+def start(frames, kernels, latent_head, decode_head, others):
+    e1, e2, e3, e4, d1, d2, d3, d4 = kernels
+    rows_in = [
+        jnp.tile(jnp.transpose(e1, (1, 2, 3, 0)).reshape(48, 32), (1, 32)).astype(F32),
+        jnp.transpose(e2, (1, 2, 3, 0)).reshape(512, 64),
+        jnp.transpose(e3, (1, 2, 3, 0)).reshape(1024, 128),
+        jnp.transpose(e4, (0, 2, 3, 1)).reshape(4096, 128),
+        jnp.transpose(d1, (0, 2, 3, 1)).reshape(2048, 256),
+        jnp.transpose(d2, (0, 2, 3, 1)).reshape(1024, 128),
+        jnp.transpose(d3, (0, 2, 3, 1)).reshape(512, 64),
+        jnp.tile(jnp.transpose(d4, (0, 2, 3, 1)).reshape(48, 32), (1, 32)).astype(F32),
+    ]
+    dma = pltpu.SemaphoreType.DMA
+    any_spec = pl.BlockSpec(memory_space=pl.ANY)
+    built = [(1152, 1024), (3072, 384)] + [(2048, 256)] * 3
+    built = built + [(2, 1024, 256), (2, 1024, 256), (2, 1536, 256)]
+    heads = [(4096, 256)] * 4
+    shapes = [(34, NF, 384)] + built * 2 + heads + [w.shape for w in others]
+    out = pl.pallas_call(
+        start_kernel,
+        out_shape=tuple(S(shape) for shape in shapes),
+        in_specs=VM(11) + [any_spec] * len(others),
+        out_specs=tuple(VM(1) + [any_spec] * (len(shapes) - 1)),
         scratch_shapes=[
-            pltpu.VMEM((4, 8, NF, 384), BF),
-            pltpu.SemaphoreType.DMA((3,)),
-            pltpu.SemaphoreType.DMA((3,)),
+            V((4, 8, NF, 384)),
+            dma((3,)),
+            dma((3,)),
+            dma((2, 7)),
+            *[V(shape) for shape in built * 2],
+            V((4096, 256)),
+            V((4096, 256)),
+            dma((18,)),
         ],
         compiler_params=pltpu.CompilerParams(
-            collective_id=ident, has_side_effects=True, vmem_limit_bytes=32 * MIB
+            collective_id=1, has_side_effects=True, vmem_limit_bytes=56 * MIB
         ),
-        name="frames_in",
-    )(jnp.transpose(block, (1, 2, 3, 0)))
+        name="start",
+    )(jnp.transpose(frames, (1, 2, 3, 0)), *rows_in, latent_head, decode_head, *others)
+    encode_forms, decode_forms = out[1:9], out[9:17]
+    return out[0], encode_forms, decode_forms, out[17:19], out[19:21], out[21:]
 
 
 def turn_kernel(x, *out):
@@ -345,173 +534,58 @@
     lax.fori_loop(0, 8, turn_rows, 0)
 
 
+def around(parts):
+    return [parts[0]] + [
+        lax.ppermute(parts[k], "strip", [(s, (s + k) % 4) for s in range(4)]) for k in range(1, 4)
+    ]
+
+
 def frames_in_later(block):
     parts = pl.pallas_call(
         turn_kernel,
-        out_shape=(jax.ShapeDtypeStruct((8, NF, 384), BF),) * 4,
+        out_shape=(S((8, NF, 384)),) * 4,
         in_specs=VM(1),
         out_specs=tuple(VM(4)),
         compiler_params=pltpu.CompilerParams(vmem_limit_bytes=32 * MIB),
         name="turn",
     )(jnp.transpose(block, (1, 2, 3, 0)))
-    return [parts[0]] + [
-        lax.ppermute(parts[k], "strip", [(s, (s + k) % 4) for s in range(4)]) for k in range(1, 4)
-    ]
-
-
-def finish_kernel(
-    count, chunks, v, recon, grad, total, recon_out, grad_out,
-    got, from_near, summed, from_far, strip_sems, near_sems, far_sems, back_sems, last_sems,
-):
+    return around(parts)
+
+
+def turned_back(got, out):
+    def turn_rows(i, carry):
+        block = jnp.concatenate([got[(b % 2) * 2 + b // 2, i] for b in range(4)], axis=0)
+        flat = block.T.astype(out.dtype)
+        for p in range(2):
+            for c in range(3):
+                first = 64 * (3 * p + c)
+                out[c, 2 * i + p] = flat[first : first + 64]
+        return carry
+
+    lax.fori_loop(0, 8, turn_rows, 0)
+
+
+def turn_back_kernel(c0, c1, c2, c3, out, got):
     me = lax.axis_index("strip")
-    row = lax.axis_index("rows")
-    half = count // 2
-    near, far = lax.rem(row, 2), lax.div(row, 2)
-    near_device = (row + 1 - 2 * near, me)
-    barrier = pltpu.get_barrier_semaphore()
-    strip_devices = [(row, lax.rem(me + k, 4)) for k in range(1, 4)]
-    far_places = [lax.rem(far + k, half) for k in range(1, half)]
-    far_devices = [(2 * place + near, me) for place in far_places]
-    for device in strip_devices + [near_device] + far_devices:
-        pl.semaphore_signal(barrier, inc=1, device_id=device, device_id_type=MESH)
-    pl.semaphore_wait(barrier, 3 + half)
-
-    def copy(src, dst, sems, index, device):
-        return pltpu.make_async_remote_copy(
-            src_ref=src,
-            dst_ref=dst,
-            send_sem=sems.at[(0,) + index],
-            recv_sem=sems.at[(1,) + index],
-            device_id=device,
-            device_id_type=MESH,
-        )
-
-    near_copies = [
-        copy(v.at[c, 1 - near], from_near.at[c], near_sems, (c,), near_device)
-        for c in range(chunks)
-    ]
-    for one in near_copies:
-        one.start()
-    strip_copies = []
-    for slot, pairs in enumerate((recon, grad)):
-        for k in range(1, 4):
-            to = lax.rem(me + k, 4)
-            strip_copies.append(
-                copy(
-                    pairs.at[pl.ds(8 * to, 8)],
-                    got.at[slot, me],
-                    strip_sems,
-                    (slot, k - 1),
-                    (row, to),
-                )
-            )
-    for one in strip_copies:
-        one.start()
-    for slot, pairs in enumerate((recon, grad)):
-        got[slot, me] = pairs[pl.ds(8 * me, 8)]
-
-    def turn(slot, out):
-        for one in strip_copies[3 * slot : 3 * slot + 3]:
-            one.wait()
-
-        def turn_rows(i, carry):
-            block = jnp.concatenate([got[slot, (b % 2) * 2 + b // 2, i] for b in range(4)], axis=0)
-            flat = block.T.astype(out.dtype)
-            for p in range(2):
-                for c in range(3):
-                    first = 64 * (3 * p + c)
-                    out[c, 2 * i + p] = flat[first : first + 64]
-            return carry
-
-        lax.fori_loop(0, 8, turn_rows, 0)
-
-    far_copies, back_copies, last_copies = {}, {}, {}
-
-    def stage_far(c):
-        near_copies[c].wait()
-        summed[c] = (v[c, near].astype(F32) + from_near[c].astype(F32)).astype(BF)
-        far_copies[c] = [
-            copy(summed.at[c, place], from_far.at[c, k], far_sems, (c, k), device)
-            for k, (place, device) in enumerate(zip(far_places, far_devices))
-        ]
-        for one in far_copies[c]:
-            one.start()
-
-    def stage_back(c):
-        for one in far_copies[c]:
-            one.wait()
-        whole = summed[c, far].astype(F32)
-        for k in range(half - 1):
-            whole = whole + from_far[c, k].astype(F32)
-        total[c, near, far] = whole.astype(BF)
-        back_copies[c] = [
-            copy(total.at[c, near, far], total.at[c, near, far], back_sems, (c, k), device)
-            for k, device in enumerate(far_devices)
-        ]
-        for one in back_copies[c]:
-            one.start()
-
-    def stage_last(c):
-        for one in back_copies[c]:
-            one.wait()
-        last_copies[c] = copy(
-            total.at[c, near], total.at[c, near], last_sems, (c,), near_device
-        )
-        last_copies[c].start()
-
-    for t in range(chunks + 2):
-        if t < chunks:
-            stage_far(t)
-        if t == 1:
-            turn(0, recon_out)
-        if t == 3:
-            turn(1, grad_out)
-        if 0 <= t - 1 < chunks:
-            stage_back(t - 1)
-        if 0 <= t - 2 < chunks:
-            stage_last(t - 2)
-    for c in range(chunks):
-        last_copies[c].wait()
-
-
-def finish(flat, recon, grad, chunks, ident):
-    count = lax.axis_size("rows")
-    half = count // 2
-    rows = flat.shape[0]
-    flat = jnp.pad(flat, ((0, -rows % (16 * count * chunks)), (0, 0)))
-    each = flat.shape[0] // (count * chunks)
-    shape = (chunks, 2, half, each, 256)
-    dma = pltpu.SemaphoreType.DMA
-    total, recon_out, grad_out = pl.pallas_call(
-        functools.partial(finish_kernel, count, chunks),
-        out_shape=(
-            jax.ShapeDtypeStruct(shape, BF),
-            jax.ShapeDtypeStruct((3, 16, 64, 256), BF),
-            jax.ShapeDtypeStruct((3, 16, 64, 256), F32),
-        ),
-        in_specs=VM(3),
-        out_specs=tuple(VM(3)),
-        scratch_shapes=[
-            pltpu.VMEM((2, 4, 8, NF, 384), BF),
-            pltpu.VMEM((chunks, half, each, 256), BF),
-            pltpu.VMEM((chunks, half, each, 256), BF),
-            pltpu.VMEM((chunks, half - 1, each, 256), BF),
-            dma((2, 2, 3)),
-            dma((2, chunks)),
-            dma((2, chunks, half - 1)),
-            dma((2, chunks, half - 1)),
-            dma((2, chunks)),
-        ],
-        compiler_params=pltpu.CompilerParams(
-            collective_id=ident, has_side_effects=True, vmem_limit_bytes=56 * MIB
-        ),
-        name="finish",
-    )(flat.reshape(shape), recon, grad)
-    return (
-        total.reshape(-1, 256)[:rows],
-        jnp.transpose(recon_out, (3, 0, 1, 2)),
-        jnp.transpose(grad_out, (3, 0, 1, 2)),
-    )
+    for k, part in enumerate((c0, c1, c2, c3)):
+        got[lax.rem(me + 4 - k, 4)] = part[...]
+    turned_back(got, out)
+
+
+def frames_out_later(pairs, strip):
+    parts = around(
+        [lax.dynamic_slice_in_dim(pairs, 8 * ((strip + k) % 4), 8) for k in range(4)]
+    )
+    flat = pl.pallas_call(
+        turn_back_kernel,
+        out_shape=S((3, 16, 64, 256)),
+        in_specs=VM(4),
+        out_specs=VM(1)[0],
+        scratch_shapes=[V((4, 8, NF, 384))],
+        compiler_params=pltpu.CompilerParams(vmem_limit_bytes=32 * MIB),
+        name="turn_back",
+    )(*parts)
+    return jnp.transpose(flat, (3, 0, 1, 2))
 
 
 def dot(a, b):
@@ -562,8 +636,8 @@
     layers,
     feat, lh0, lh1, dh0, dh1, emb0, emb1, pos, gains, allow, cot,
     qkv0, qkv1, proj0, proj1, up0, up1, down0, down1,
-    tokens, latent_out, chances_out, decoded, flat, grad_latent,
-    feat_got, feat_sems, keep, send, sent, spread_sems, parts, gots, pair_sems,
+    tokens, latent_out, chances_out, decoded, flat, grad_latent, feat_got,
+    feat_sems, keep, send, sent, spread_sems, parts, gots, pair_sems,
     other, other_got, fold_sems, unit_a, unit_f, normed_a, normed_f, mixed, weights,
     attended, before, inner, gain_rows,
 ):
@@ -801,11 +875,11 @@
             S((4, NF, 1024)),
             S((rows, 512)),
             S((t, 512), F32),
+            S((4, NF, 1024)),
         ),
         in_specs=VM(len(args)),
-        out_specs=tuple(VM(6)),
+        out_specs=tuple(VM(7)),
         scratch_shapes=[
-            V((4, NF, 1024)),
             dma((2, 1)),
             V((4, NF, 1024)),
             V((4, NF, 1024)),
@@ -835,19 +909,313 @@
     )(*args)
 
 
-def across(value):
-    return lax.ppermute(value, "strip", [(0, 2), (2, 0), (1, 3), (3, 1)])
+def back_kernel(
+    grad, latent, chances, grad_embed, feat0, feat1, lh0, lh1, dh0, dh1,
+    grad_feat, out_rows, in_rows,
+    got, got_sems, keep, send, sent, sent_sems, own, other, other_got, fold_sems,
+):
+    strip = lax.axis_index("strip")
+    row = lax.axis_index("rows")
+    partner = (row, lax.rem(strip + 2, 4))
+    sibling = (row, strip + 1 - 2 * lax.rem(strip, 2))
+    barrier = pltpu.get_barrier_semaphore()
+    for device in (partner, sibling):
+        pl.semaphore_signal(barrier, inc=1, device_id=device, device_id_type=MESH)
+    pl.semaphore_wait(barrier, 2)
+
+    def copy(src, dst, sems, index, device):
+        return pltpu.make_async_remote_copy(
+            src_ref=src,
+            dst_ref=dst,
+            send_sem=sems.at[0, index],
+            recv_sem=sems.at[1, index],
+            device_id=device,
+            device_id_type=MESH,
+        )
+
+    grad_copy = copy(grad, got, got_sems, 0, partner)
+    grad_copy.start()
+
+    def through(maps):
+        halves = []
+        for weight in (dh0, dh1):
+            total = jnp.zeros((NF, 256), F32)
+            for h in range(4):
+                total = total + dot(maps[h], weight[1024 * h : 1024 * h + 1024])
+            halves.append(total)
+        return jnp.concatenate(halves, axis=1)
+
+    mine = through(grad)
+    grad_copy.wait()
+    grad_latent = grad_embed[...] + jnp.concatenate([mine, through(got)], axis=0)
+    probs = chances[...]
+    along = over_groups(probs * grad_latent, jnp.add)
+    grad_logits = (probs * (grad_latent - along)).astype(BF)
+    sends = []
+    for h in range(4):
+        for w in range(4):
+            lanes = slice(256 * w, 256 * w + 256)
+            rows = slice(1024 * h + 256 * w, 1024 * h + 256 * w + 256)
+            value = dot_nt(grad_logits[:, :256], lh0[rows]) + dot_nt(grad_logits[:, 256:], lh1[rows])
+            value = value.astype(BF)
+            keep[h, :, lanes] = value[:NF]
+            send[h, :, lanes] = value[NF:]
+        one = copy(send.at[h], sent.at[h], sent_sems, h, partner)
+        one.start()
+        sends.append(one)
+    folds = []
+    for slot, (first, second, rhs) in enumerate(
+        ((grad, got, latent[...]), (feat0, feat1, grad_logits))
+    ):
+        for h in range(4):
+            for w in range(4):
+                lanes = slice(256 * w, 256 * w + 256)
+                rows = slice(1024 * h + 256 * w, 1024 * h + 256 * w + 256)
+                maps = jnp.concatenate([first[h, :, lanes], second[h, :, lanes]], axis=0)
+                value = dot(maps.T, rhs).astype(BF)
+                own[slot, rows] = value[:, :256]
+                other[slot, rows] = value[:, 256:]
+        one = copy(other.at[slot], other_got.at[slot], fold_sems, slot, sibling)
+        one.start()
+        folds.append(one)
+    for one in sends:
+        one.wait()
+    grad_feat[...] = (keep[...].astype(F32) + sent[...].astype(F32)).astype(BF)
+    swap = exchange_16()
+    for slot, (out, one) in enumerate(zip((out_rows, in_rows), folds)):
+        one.wait()
+        for b in range(16):
+            parts = []
+            for k in range(16):
+                rows = slice(256 * k + 16 * b, 256 * k + 16 * b + 16)
+                value = own[slot, rows].astype(F32) + other_got[slot, rows].astype(F32)
+                parts.append(value.astype(BF))
+            block = dot(swap, jnp.concatenate(parts, axis=0)).astype(BF)
+            out[256 * b : 256 * b + 256] = block.T if slot == 0 else block
+
+
+def latents_back(*args):
+    dma = pltpu.SemaphoreType.DMA
+    maps = (4, NF, 1024)
+    rows = (4096, 256)
+    return pl.pallas_call(
+        back_kernel,
+        out_shape=(S(maps), S(rows), S(rows)),
+        in_specs=VM(len(args)),
+        out_specs=tuple(VM(3)),
+        scratch_shapes=[
+            V(maps),
+            dma((2, 1)),
+            V(maps),
+            V(maps),
+            V(maps),
+            dma((2, 4)),
+            V((2,) + rows),
+            V((2,) + rows),
+            V((2,) + rows),
+            dma((2, 2)),
+        ],
+        compiler_params=pltpu.CompilerParams(
+            collective_id=4, has_side_effects=True, vmem_limit_bytes=56 * MIB
+        ),
+        name="latents_back",
+    )(*args)
+
+
+def finish_kernel(
+    count, v, dec, enc, grad, total, conv, grad_out,
+    got, strip_sems, from_near, summed, from_far, conv_v, conv_near, conv_summed, conv_far,
+    side_got, side_sum, cross_got, sems, far_sems, back_sems,
+):
+    me = lax.axis_index("strip")
+    row = lax.axis_index("rows")
+    half = count // 2
+    chunks = v.shape[0]
+    near, far = lax.rem(row, 2), lax.div(row, 2)
+    core, x = lax.rem(me, 2), lax.div(me, 2)
+    near_device = (row + 1 - 2 * near, me)
+    sibling, partner = (row, me + 1 - 2 * core), (row, lax.rem(me + 2, 4))
+    barrier = pltpu.get_barrier_semaphore()
+    strip_devices = [(row, lax.rem(me + k, 4)) for k in range(1, 4)]
+    far_places = [lax.rem(far + k, half) for k in range(1, half)]
+    far_devices = [(2 * place + near, me) for place in far_places]
+    for device in strip_devices + [near_device] + far_devices:
+        pl.semaphore_signal(barrier, inc=1, device_id=device, device_id_type=MESH)
+    pl.semaphore_wait(barrier, 3 + half)
+
+    def copy(src, dst, pair, index, device):
+        one = pltpu.make_async_remote_copy(
+            src_ref=src,
+            dst_ref=dst,
+            send_sem=pair.at[(0,) + index],
+            recv_sem=pair.at[(1,) + index],
+            device_id=device,
+            device_id_type=MESH,
+        )
+        one.start()
+        return one
+
+    places = [
+        (v.at[c], from_near.at[c], summed.at[c], from_far.at[c], total.at[c])
+        for c in range(chunks)
+    ]
+    places.append((conv_v, conv_near, conv_summed, conv_far, conv.at[core, x]))
+    near_copies, far_copies, back_copies, last_copies = {}, {}, {}, {}
+
+    def stage_near(c):
+        near_copies[c] = copy(places[c][0].at[1 - near], places[c][1], sems, (c,), near_device)
+
+    def stage_far(c):
+        values, arrived, both, slots, _ = places[c]
+        near_copies[c].wait()
+        both[...] = (values[near].astype(F32) + arrived[...].astype(F32)).astype(BF)
+        far_copies[c] = [
+            copy(both.at[place], slots.at[k], far_sems, (c, k), device)
+            for k, (place, device) in enumerate(zip(far_places, far_devices))
+        ]
+
+    def stage_back(c):
+        _, _, both, slots, out = places[c]
+        for one in far_copies[c]:
+            one.wait()
+        whole = both[far].astype(F32)
+        for k in range(half - 1):
+            whole = whole + slots[k].astype(F32)
+        out[near, far] = whole.astype(BF)
+        back_copies[c] = [
+            copy(out.at[near, far], out.at[near, far], back_sems, (c, k), device)
+            for k, device in enumerate(far_devices)
+        ]
+
+    def stage_last(c):
+        out = places[c][4]
+        for one in back_copies[c]:
+            one.wait()
+        last_copies[c] = copy(
+            out.at[near], out.at[near], sems, (chunks + 1 + c,), near_device
+        )
+
+    side = 2 * (chunks + 1)
+    side_copies = [
+        copy(part.at[1 - core], side_got.at[k], sems, (side + k,), sibling)
+        for k, part in enumerate((dec, enc))
+    ]
+    for c in range(chunks):
+        stage_near(c)
+    cross_copies = []
+    for k, part in enumerate((dec, enc)):
+        side_copies[k].wait()
+        side_sum[k] = (part[core].astype(F32) + side_got[k].astype(F32)).astype(BF)
+        cross_copies.append(
+            copy(side_sum.at[k, 1 - x], cross_got.at[k], sems, (side + 2 + k,), partner)
+        )
+    strip_copies = []
+    for k in range(1, 4):
+        to = lax.rem(me + k, 4)
+        strip_copies.append(
+            copy(grad.at[pl.ds(8 * to, 8)], got.at[me], strip_sems, (k - 1,), (row, to))
+        )
+    got[me] = grad[pl.ds(8 * me, 8)]
+
+    stage_far(0)
+    stage_far(1)
+    shares = []
+    for k in range(2):
+        cross_copies[k].wait()
+        shares.append(
+            (side_sum[k, x].astype(F32) + cross_got[k].astype(F32)).astype(BF)
+        )
+    share = jnp.concatenate(shares, axis=0)
+    each = conv_v.shape[2]
+    spare = 2 * half * each - share.shape[0]
+    if spare:
+        share = jnp.concatenate([share, jnp.zeros((spare, 256), BF)], axis=0)
+    for piece in range(2 * half):
+        conv_v[piece // half, piece % half] = share[piece * each : piece * each + each]
+    last = chunks
+    stage_near(last)
+    stage_back(0)
+    stage_far(2)
+    stage_back(1)
+    stage_last(0)
+    stage_far(last)
+    stage_far(3)
+    stage_back(2)
+    stage_last(1)
+    for one in strip_copies:
+        one.wait()
+    turned_back(got, grad_out)
+    stage_back(last)
+    stage_last(2)
+    stage_back(3)
+    stage_last(last)
+    stage_last(3)
+    last_copies[last].wait()
+    cross = copy(conv.at[core, x], conv.at[core, x], sems, (side + 4,), partner)
+    cross.wait()
+    beside_copy = copy(conv.at[core], conv.at[core], sems, (side + 5,), sibling)
+    for c in range(chunks):
+        last_copies[c].wait()
+    beside_copy.wait()
+
+
+def finish(flat, dec, enc, grad):
+    count = lax.axis_size("rows")
+    half = count // 2
+    chunks = 4
+    each = flat.shape[0] // (count * chunks)
+    share = dec.shape[0] // 2
+    conv_each = -(-share // (16 * count)) * 16
+    shape = (chunks, 2, half, each, 256)
+    dma = pltpu.SemaphoreType.DMA
+    quarter = dec.shape[0] // 4
+    total, conv, grad_out = pl.pallas_call(
+        functools.partial(finish_kernel, count),
+        out_shape=(
+            S(shape),
+            S((2, 2, 2, half, conv_each, 256)),
+            S((3, 16, 64, 256), F32),
+        ),
+        in_specs=VM(4),
+        out_specs=tuple(VM(3)),
+        scratch_shapes=[
+            V((4, 8, NF, 384)),
+            dma((2, 3)),
+            V((chunks, half, each, 256)),
+            V((chunks, half, each, 256)),
+            V((chunks, half - 1, each, 256)),
+            V((2, half, conv_each, 256)),
+            V((half, conv_each, 256)),
+            V((half, conv_each, 256)),
+            V((half - 1, conv_each, 256)),
+            V((2, 2, quarter, 256)),
+            V((2, 2, quarter, 256)),
+            V((2, quarter, 256)),
+            dma((2, 2 * (chunks + 1) + 6)),
+            dma((2, chunks + 1, half - 1)),
+            dma((2, chunks + 1, half - 1)),
+        ],
+        compiler_params=pltpu.CompilerParams(
+            collective_id=2, has_side_effects=True, vmem_limit_bytes=56 * MIB
+        ),
+        name="finish",
+    )(
+        flat.reshape(shape),
+        dec.reshape(2, 2, quarter, 256),
+        enc.reshape(2, 2, quarter, 256),
+        grad,
+    )
+    conv = conv.reshape(2, 2, -1, 256)
+    return (
+        total.reshape(-1, 256),
+        conv[:, :, :quarter].reshape(-1, 256),
+        conv[:, :, quarter : 2 * quarter].reshape(-1, 256),
+        jnp.transpose(grad_out, (3, 0, 1, 2)),
+    )
 
 
 def beside(value):
     return lax.ppermute(value, "strip", [(0, 1), (1, 0), (2, 3), (3, 2)])
-
-
-def fold(full, axis):
-    half = full.shape[axis] // 2
-    own = lax.slice_in_dim(full, 0, half, axis=axis)
-    other = lax.slice_in_dim(full, half, 2 * half, axis=axis)
-    return own + beside(other.astype(BF)).astype(F32)
 
 
 def make_mask(segment_ids):
@@ -856,32 +1224,6 @@
     return causal[None] & (segment_ids[:, :, None] == segment_ids[:, None, :])
 
 
-def mm(a, b):
-    return jnp.dot(a, b, preferred_element_type=F32)
-
-
-def mm_t(a, b):
-    return lax.dot_general(a, b, (((1,), (1,)), ((), ())), preferred_element_type=F32)
-
-
-def t_mm(a, b):
-    return lax.dot_general(a, b, (((0,), (0,)), ((), ())), preferred_element_type=F32)
-
-
-def pieces_of(whole, parts):
-    pieces = []
-    offset = 0
-    for part in parts:
-        pieces.append(whole[offset : offset + part.shape[0]])
-        offset = offset + part.shape[0]
-    return pieces
-
-
-def stacked_rows(parts, multiple):
-    flat = jnp.concatenate([part.astype(BF) for part in parts], axis=0)
-    return jnp.pad(flat, ((0, -flat.shape[0] % multiple), (0, 0)))
-
-
 def rows_share(flat):
     return lax.psum_scatter(flat, "rows", scatter_dimension=0, tiled=True)
 
@@ -890,56 +1232,16 @@
     return lax.all_gather(share, "rows", axis=0, tiled=True)
 
 
-def pack_kernels(outer, first, second, third):
-    parts = [
-        jnp.concatenate([third[:, :, :256], third[:, :, 256:]], axis=1).reshape(2048, 256),
-        second.reshape(512, 256),
-        jnp.concatenate([first[:2], first[2:]], axis=2).reshape(128, 256),
-        jnp.pad(outer.reshape(6, 256), ((0, 122), (0, 0))),
-    ]
-    return jnp.concatenate(parts, axis=0)
-
-
 def unpack_kernels(flat):
-    third = flat[:2048].reshape(4, 512, 256)
-    third = jnp.concatenate([third[:, :256], third[:, 256:]], axis=2)
-    second = flat[2048:2560].reshape(4, 128, 256)
-    first = flat[2560:2688].reshape(2, 64, 256)
-    first = jnp.concatenate([first[:, :, :128], first[:, :, 128:]], axis=0)
-    outer = flat[2688:2694].reshape(4, 3, 4, 32)
-    return (outer, first, second, third)
-
-
-def strip_share(flat, x, core):
-    half = flat.shape[0] // 2
-    low = flat.astype(BF)
-    mine = lax.dynamic_slice_in_dim(low, core * half, half)
-    theirs = lax.dynamic_slice_in_dim(low, (1 - core) * half, half)
-    summed = mine.astype(F32) + beside(theirs).astype(F32)
-    low = summed.astype(BF)
-    half = half // 2
-    mine = lax.dynamic_slice_in_dim(low, x * half, half)
-    theirs = lax.dynamic_slice_in_dim(low, (1 - x) * half, half)
-    return mine.astype(F32) + across(theirs).astype(F32)
-
-
-def strip_whole(share, x, core):
-    got = across(share)
-    half = jnp.where(
-        x == 0, jnp.concatenate([share, got]), jnp.concatenate([got, share])
-    )
-    got = beside(half)
-    return jnp.where(
-        core == 0, jnp.concatenate([half, got]), jnp.concatenate([got, half])
-    )
-
-
-def features_first(weight):
-    return weight.reshape(256, 16, -1).transpose(1, 0, 2).reshape(weight.shape)
-
-
-def channels_first(weight):
-    return weight.reshape(16, 256, -1).transpose(1, 0, 2).reshape(weight.shape)
+    flat = flat.astype(F32)
+    second = jnp.concatenate([flat[2048:2560, :128], flat[2048:2560, 128:]], axis=0)
+    first = jnp.concatenate([flat[2560:2688, 64 * k : 64 * k + 64] for k in range(4)], axis=0)
+    return (
+        flat[2688:2736, :32].reshape(3, 4, 4, 32),
+        first.reshape(32, 4, 4, 64),
+        second.reshape(64, 4, 4, 128),
+        flat[:2048],
+    )
 
 
 def shards(
@@ -969,36 +1271,27 @@
     x, core = strip // 2, strip % 2
     layers = qkv_weight.shape[0]
 
-    enc = [w.transpose(2, 3, 1, 0) for w in (encode_one, encode_two, encode_three, encode_four)]
-    dec = [
-        jnp.flip(w, (2, 3)).transpose(2, 3, 0, 1)
-        for w in (decode_four, decode_three, decode_two, decode_one)
-    ]
-    folds = (4, 2, 1)
-    enc_a = outer_A(enc[0])
-    dec_a = outer_A(dec[0])
-    enc_b, dec_b = outer_B(enc_a), outer_B(dec_a)
-    enc_a, dec_a = enc_a.reshape(1152, 1024), dec_a.reshape(1152, 1024)
-    enc_t = [canon_T(w, a) for w, a in zip(enc[1:], folds)]
-    dec_t = [canon_T(w, a) for w, a in zip(dec[1:], folds)]
-    enc_u = [canon_U(t, a) for t, a in zip(enc_t, folds)]
-    dec_u = [canon_U(t, a) for t, a in zip(dec_t, folds)]
-    enc_t = [t.reshape(2048, 256) for t in enc_t]
-    dec_t = [t.reshape(2048, 256) for t in dec_t]
-
-    head_in = features_first(latent_head)
-    head_in = (head_in, beside(head_in))
-    head_out = features_first(decode_head.T)
-    head_out = (head_out, beside(head_out))
+    kernels = (
+        encode_one,
+        encode_two,
+        encode_three,
+        encode_four,
+        decode_one,
+        decode_two,
+        decode_three,
+        decode_four,
+    )
     qkv = jnp.transpose(qkv_weight, (0, 2, 1, 3))
-    halves = []
-    for shard in (token_embed, qkv, out_weight, up_weight, down_weight):
-        halves.append((shard, beside(shard)))
-    embed, qkv, project, widen, narrow = halves
-
-    pixels = frames_in(frames, 1)
+    shards_here = (token_embed, qkv, out_weight, up_weight, down_weight)
+    pixels, enc_f, dec_f, head_in, head_out, theirs = start(
+        frames, kernels, latent_head, decode_head, shards_here
+    )
+    enc_a, enc_b, enc_t, enc_u = enc_f[0], enc_f[1], enc_f[2:5], enc_f[5:8]
+    dec_a, dec_b, dec_t, dec_u = dec_f[0], dec_f[1], dec_f[2:5], dec_f[5:8]
+    embed, qkv, project, widen, narrow = zip(shards_here, theirs)
     hints = frames_in_later(frame_cotangent)
     z1, z2, z3, z4, feat = enc_fwd(pixels, enc_a, *enc_t)
+
     first = 2 * core
 
     def mine(array, size):
@@ -1016,7 +1309,7 @@
         axis=0,
     )
     line = 16 * lax.axis_size("rows")
-    tokens, latent, chances, decoded, t_flat, grad_latent = middle(
+    tokens, latent, chances, decoded, t_flat, grad_latent, feat_got = middle(
         layers,
         line,
         feat,
@@ -1044,71 +1337,37 @@
     )
 
     recon_pairs, p3, p2, p1 = dec_fwd(decoded, dec_u[2], dec_u[1], dec_u[0], dec_b)
-    g_decoded, h2, h3, h4, h_outer = dec_bwd(hints, decoded, p3, p2, p1, dec_a, *dec_t)
-    g_spread = jnp.concatenate([g_decoded, across(g_decoded)], axis=1)
-    g_head_out = fold(jnp.concatenate([t_mm(g_spread[h], latent) for h in range(4)]), 1)
-    head_out4 = jnp.concatenate(head_out, axis=1).reshape(4, 1024, 512)
-    head_in4 = jnp.concatenate(head_in, axis=1).reshape(4, 1024, 512)
-    feat = jnp.concatenate([feat, across(feat)], axis=1)
-    grad_latent = grad_latent + sum(mm(g_spread[h], head_out4[h]) for h in range(4))
-    dec_flat = pack_kernels(
-        red_to_we(h_outer),
-        gt_to_we(h2, 4, 32, 64),
-        gt_to_we(h3, 2, 64, 128),
-        gt_to_we(h4, 1, 128, 256),
-    )
-    dec_share = strip_share(dec_flat, x, core)
-
-    d_parts = [g_head_out, dec_share]
-    d_flat = stacked_rows(d_parts, line)
-
-    grouped = chances.reshape(2 * NF, -1, LCLASS)
-    grad_grouped = grad_latent.reshape(grouped.shape)
-    grad_logits = grouped * (grad_grouped - jnp.sum(grouped * grad_grouped, -1, keepdims=True))
-    grad_logits = grad_logits.reshape(2 * NF, -1).astype(BF)
-    g_head_in = fold(jnp.concatenate([t_mm(feat[h], grad_logits) for h in range(4)]), 1)
-    g_feat = jnp.stack([mm_t(grad_logits, head_in4[h]) for h in range(4)]).astype(BF)
-    g_feat = (g_feat[:, :NF].astype(F32) + across(g_feat[:, NF:]).astype(F32)).astype(BF)
-    g_feat, t_share, d_flat = lax.optimization_barrier((g_feat, t_share, d_flat))
-    d_share = rows_share(d_flat)
+    recon = frames_out_later(recon_pairs, strip)
+    g_decoded, dec_flat = dec_bwd(hints, decoded, p3, p2, p1, dec_a, *dec_t)
+    g_decoded, t_share = lax.optimization_barrier((g_decoded, t_share))
     t_total = rows_whole(t_share)
-    d_pairs, e2, e3, e4, e_outer = enc_bwd(pixels, z1, z2, z3, z4, g_feat, *enc_u, enc_b)
-    enc_flat = pack_kernels(
-        red_to_we(e_outer),
-        gt_to_we(e2, 4, 32, 64),
-        gt_to_we(e3, 2, 64, 128),
-        gt_to_we(e4, 1, 128, 256),
-    )
-    enc_share = strip_share(enc_flat, x, core)
-    late_parts = [g_head_in, enc_share]
-    late_flat = stacked_rows(late_parts, 16)
-    late_flat, d_share = lax.optimization_barrier((late_flat, d_share))
-    d_total = pieces_of(rows_whole(d_share), d_parts)
-    late, recon, frames_grad = finish(late_flat, recon_pairs, d_pairs, 4, 2)
-    late = pieces_of(late, late_parts)
-
-    def of_encoder(part, c, o):
-        return part.astype(F32).reshape(4, o, 4, c).transpose(1, 3, 0, 2)
-
-    def of_decoder(part, c, o):
-        return jnp.flip(part.astype(F32).reshape(4, o, 4, c), (0, 2)).transpose(3, 1, 0, 2)
-
-    k1, k2, k3, k4 = unpack_kernels(strip_whole(late[1], x, core))
-    j1, j2, j3, j4 = unpack_kernels(strip_whole(d_total[1], x, core))
+    g_feat, d_rows, l_rows = latents_back(
+        g_decoded, latent, chances, grad_latent, feat, feat_got, *head_in, *head_out
+    )
+    d_share = rows_share(d_rows)
+
+    d_pairs, enc_flat = enc_bwd(pixels, z1, z2, z3, z4, g_feat, *enc_u, enc_b)
+    d_pairs, t_total, d_share = lax.optimization_barrier((d_pairs, t_total, d_share))
+    d_total = rows_whole(d_share)
+    l_total, dec_total, enc_total, frames_grad = finish(l_rows, dec_flat, enc_flat, d_pairs)
+
     t_total = t_total.astype(F32)
     t_layers = t_total[: layers * LAYER_ROWS].reshape(layers, LAYER_ROWS, 512)
     t_rest = t_total[layers * LAYER_ROWS :]
     r_qkv = t_layers[:, 1152:].reshape(layers, 3, 128, 4, 128).transpose(0, 3, 2, 1, 4)
     r_qkv = r_qkv.reshape(qkv_weight.shape)
+    e_one, e_two, e_three, e_four = unpack_kernels(enc_total)
+    d_four, d_three, d_two, d_one = unpack_kernels(dec_total)
+    e_four = jnp.concatenate([e_four[:, :128], e_four[:, 128:]], axis=0)
     return (
         tokens_out,
         recon,
         frames_grad,
-        k1.astype(F32).transpose(3, 1, 0, 2),
-        of_encoder(k2, 32, 64),
-        of_encoder(k3, 64, 128),
-        of_encoder(k4, 128, 256),
-        channels_first(late[0].astype(F32)),
+        e_one.transpose(3, 0, 1, 2),
+        e_two.transpose(3, 0, 1, 2),
+        e_three.transpose(3, 0, 1, 2),
+        e_four.reshape(256, 4, 4, 128).transpose(0, 3, 1, 2),
+        l_total.astype(F32),
         t_rest[:256],
         t_rest[256 : 256 + NF],
         t_rest[256 + NF : 256 + NF + 2 * layers].reshape(norm_gains.shape),
@@ -1116,11 +1375,11 @@
         t_layers[:, 1024:1152],
         t_layers[:, 512:1024],
         t_layers[:, :512],
-        channels_first(d_total[0].astype(F32)).T,
-        of_decoder(j4, 128, 256),
-        of_decoder(j3, 64, 128),
-        of_decoder(j2, 32, 64),
-        jnp.flip(j1.astype(F32), (0, 2)).transpose(1, 3, 0, 2),
+        d_total.astype(F32).reshape(16, 256, 256).transpose(1, 0, 2).reshape(256, 4096),
+        d_one.reshape(128, 4, 4, 256).transpose(0, 3, 1, 2),
+        d_two.transpose(0, 3, 1, 2),
+        d_three.transpose(0, 3, 1, 2),
+        d_four.transpose(0, 3, 1, 2),
     )
 
 

time: 747 us -> 598 us (0.80)
  local copies, waits for them, and re-layouts: 156 us -> 46 us
  other arithmetic: 54.6 us -> 13.4 us
  Pallas kernels: 352 us -> 393 us
  matrix products: 20 us -> 0 us
  starting transfers between devices: 21.3 us -> 5.62 us
    all_gather x2, waiting for transfers between devices: 0.01 us -> 93.3 us  [rows_whole(): return lax.all_gather(share, 'rows', axis=0, tiled=True)]
    reduce_scatter x2, waiting for transfers between devices: 71.3 us -> 6.96 us  [rows_share(): return lax.psum_scatter(flat, 'rows', scatter_dimension=0, tiled=True)]
    pallas_call x3 -> x5, Pallas kernels: 136 us -> 167 us  [the longest x1 102 us: finish(): pl.pallas_call(functools.partial(finish_kernel, count), out_shape=(S(shap...]
    slice x49 -> x9, local copies, waits for them, and re-layouts: 33.2 us -> 6.12 us  [the longest x1 1.99 us: finish(): conv[:, :, :quarter].reshape(-1, 256)]
    unnamed x197 -> x27, local copies, waits for them, and re-layouts: 34.2 us -> 9.13 us
    ppermute x10 -> x6, waiting for transfers between devices: 38.1 us -> 15.7 us  [around(): lax.ppermute(parts[k], 'strip', [(s, (s + k) % 4) for s in range(4)])]
    dot_general x18 -> x0, matrix products: 20 us -> none  [the longest x4 6.86 us: mm_t(): lax.dot_general(a, b, (((1,), (1,)), ((), ())), preferred_element_type=F32)]
    another operation x29 -> x0, other arithmetic: 19.5 us -> none  [the longest x16 8.5 us: canon_U(): jnp.stack([jnp.concatenate([U[1], U[3]]), jnp.concatenate([U[0], U[2]])])]
  transfers between devices with their start and end apart: 28 -> 11, of which waited for: 11 -> 7; matrix products, arithmetic and copies ran while one was open for 27% -> 4% of each run, Pallas kernels for 42% -> 19%
where the time goes in v3:
time: 598 us; the launch traced here: 591 us
  Pallas kernels  393 us (66%)
  waiting for transfers between devices  118 us (20%)
  local copies, waits for them, and re-layouts  46 us (8%)
  between operations  14.6 us (2%)
  other arithmetic  13.4 us (2%)
    pallas_call x4, Pallas kernels, run(): pl.pallas_call(kernel, out_shape=outs, in_specs=VM(len(args)), out_specs=...  132 us
    pallas_call x1, Pallas kernels, finish(): pl.pallas_call(functools.partial(finish_kernel, count), out_shape=(S(shap...  102 us
    pallas_call x1, Pallas kernels, middle(): pl.pallas_call(functools.partial(middle_kernel, layers), out_shape=(S((t,...  94.7 us
    all_gather x2, waiting for transfers between devices, rows_whole(): return lax.all_gather(share, 'rows', axis=0, tiled=True)  93.3 us
    pallas_call x1, Pallas kernels, latents_back(): pl.pallas_call(back_kernel, out_shape=(S(maps), S(rows), S(rows)), in_spe...  34.8 us
    pallas_call x1, Pallas kernels, start(): pl.pallas_call(start_kernel, out_shape=tuple((S(shape) for shape in shape...  26.5 us
    ppermute x6, waiting for transfers between devices, around(): lax.ppermute(parts[k], 'strip', [(s, (s + k) % 4) for s in range(4)])  15.7 us
  transfers between devices with their start and end apart: 11, of which 7 were waited for; matrix products, arithmetic and copies ran while one was open for 4% of the time, Pallas kernels for 19%

profile of v3, /device:TPU:0, one launch (start us, length us, event | category | flops | bytes accessed | tf_op | source)
XLA Modules:
  0.0 590.6 jit_solution(608157637135224101)
XLA Ops:
  15.7 26.5 %start.1 = (bf16[34,64,384]{2,1,0:T(8,128)(2,1)}, bf16[1152,1024]{1,0:T(8,128)(2,1)}, bf16[3072,384]{1,0:T(8,128)(2,1)}, bf16[2048,256]{1,0:T(8,128)(2,1)}, bf16...) custom-call(bf16[3,16,64,256]{3,2,1,0:T(8,128)(2,1)} %bitcast.89, ...), custom_call_target="tpu_custom_call" | custom-call | tf_op jit(solution)/shard_map/start/pallas_call | solution.py:495
  42.2 21.7 %encode.1 = (bf16[32,64,1024]{2,1,0:T(8,128)(2,1)}, bf16[16,64,1024]{2,1,0:T(8,128)(2,1)}, bf16[8,64,1024]{2,1,0:T(8,128)(2,1)}, bf16[4,64,1024]{2,1,0:T(8,128)(2,1)}, bf16[4,64,1024]{2,1,0:T(8,128)(2,1)}) custom-call(bf16[34,64,384]{2,1,0:T(8,128)(2,1)} %get-tuple-element.81.xp, bf16[1152,1024]{1,0:T(8,128)(2,1)} %get-tuple-element.82.a, ...), custom_call_target="tpu_custom_call" | custom-call | flops 10000000000 | bytes 20971520 | tf_op jit(solution)/shard_map/encode/pallas_call | solution.py:243
  63.8 94.7 %middle.1 = (bf16[128,512]{1,0:T(8,128)(2,1)}, bf16[128,512]{1,0:T(8,128)(2,1)}, f32[128,512]{1,0:T(8,128)}, bf16[4,64,1024]{2,1,0:T(8,128)(2,1)}, bf16[3456,512...) custom-call(bf16[4,64,1024]{2,1,0:T(8,128)(2,1)} %get-tuple-element.86.feat.feat0, ...), custom_call_target="tpu_custom_call" | custom-call | tf_op jit(solution)/shard_map/middle/pallas_call | solution.py:869
  160.0 1.5 turn.1
  163.6 1.4 collective-permute-start.6
  165.1 24.1 %decode.1 = (bf16[32,64,384]{2,1,0:T(8,128)(2,1)}, bf16[8,64,1024]{2,1,0:T(8,128)(2,1)}, bf16[16,64,1024]{2,1,0:T(8,128)(2,1)}, bf16[32,64,1024]{2,1,0:T(8,128)(2,1)}) custom-call(bf16[4,64,1024]{2,1,0:T(8,128)(2,1)} %get-tuple-element.97.dec, bf16[2,1536,256]{2,1,0:T(8,128)(2,1)} %get-tuple-element.98.u4, bf16[2,1024,256]{2,1,0:T(8,128)(2,1)} %get-tuple-element.99.u3, ...), custom_call_target="tpu_custom_call" | custom-call | flops 10000000000 | bytes 20971520 | tf_op jit(solution)/shard_map/decode/pallas_call | solution.py:243
  190.2 42.8 %decode_back.1 = (bf16[4,64,1024]{2,1,0:T(8,128)(2,1)}, bf16[2816,256]{1,0:T(8,128)(2,1)}) custom-call(bf16[8,64,384]{2,1,0:T(8,128)(2,1)} %copy-done.1, bf16[8,64,384]{2,1,0:T(8,128)(2,1)} %copy-done.10, bf16[8,64,384]{2,1,0:T(8,128)(2,1)} %copy-done.11, bf16[8,64,384]{2,1,0:T(8,128)(2,1)} %copy-done.12, bf16[4,64,1024]{2,1,0:T(8,128)(2,1)} %get-tuple-element.97.dec, ...), custom_call_target="tpu_custom_call" | custom-call | flops 10000000000 | bytes 20971520 | tf_op jit(solution)/shard_map/decode_back/pallas_call | solution.py:243
  233.0 6.1 %reduce-scatter.3.cloned.1.call-done = bf16[432,512]{1,0:T(8,128)(2,1)} async-done(((bf16[3456,512]{1,0:T(8,128)(2,1)}), bf16[432,512]{1,0:T(8,128)(2,1)}) %reduce-scatter.3.cloned.1.call-update) | async-done | bytes 442384 | tf_op jit(solution)/shard_map/reduce_scatter | solution.py:1228
  239.2 34.8 %latents_back.1 = (bf16[4,64,1024]{2,1,0:T(8,128)(2,1)}, bf16[4096,256]{1,0:T(8,128)(2,1)}, bf16[4096,256]{1,0:T(8,128)(2,1)}) custom-call(bf16[4,64,1024]{2,1,0:T(8,128)(2,1)} %get-tuple-element.116.grad, bf16[128,512]{1,0:T(8,128)(2,1)} %get-tuple-element.117.latent, f32[128,512]{1,0:T(8,128)} %get-tuple-element.118.chances, ...), custom_call_target="tpu_custom_call" | custom-call | tf_op jit(solution)/shard_map/latents_back/pallas_call | solution.py:1001
  276.0 1.7 collective-permute-start.2
  280.1 4.2 collective-permute-done.3.c3
  284.3 11.5 %collective-permute-done.2.c2 = bf16[8,64,384]{2,1,0:T(8,128)(2,1)S(1)} collective-permute-done((bf16[8,64,384]{2,1,0:T(8,128)(2,1)S(1)}, bf16[8,64,384]{2,1,0:T(8,128)(2,1)S(1)}, u32[]{:S(2)}, u32[]{:S(2)}) %collective-permute-start.2) | collective-permute-done | bytes 393248 | tf_op jit(solution)/shard_map/ppermute | solution.py:539
  295.8 2.3 turn_back.1
  298.1 43.1 %encode_back.1 = (bf16[32,64,384]{2,1,0:T(8,128)(2,1)}, bf16[2816,256]{1,0:T(8,128)(2,1)}) custom-call(bf16[34,64,384]{2,1,0:T(8,128)(2,1)} %get-tuple-element.81.xp, bf16[32,64,1024]{2,1,0:T(8,128)(2,1)} %get-tuple-element.123.z1, bf16[16,64,1024]{2,1,0:T(8,128)(2,1)} %get-tuple-element.124.z2, bf16[8,64,1024]{2,1,0:T(8,128)(2,1)} %get-tuple-element.125.z3, ...), custom_call_target="tpu_custom_call" | custom-call | flops 10000000000 | bytes 20971520 | tf_op jit(solution)/shard_map/encode_back/pallas_call | solution.py:243
  342.1 66.4 %all-gather.3.cloned.1.call-done = bf16[3456,512]{1,0:T(8,128)(2,1)} async-done(((bf16[432,512]{1,0:T(8,128)(2,1)}), bf16[3456,512]{1,0:T(8,128)(2,1)}) %all-gather.3.cloned.1.call-update) | async-done | bytes 3538960 | tf_op jit(solution)/shard_map/all_gather | solution.py:1232
  409.2 1.5 slice.144
  410.7 1.8 slice.143
  412.5 2.8 slice.146
  416.1 1.9 copy-done.2
  419.3 101.7 %finish.1 = (bf16[4,2,4,128,256]{4,3,2,1,0:T(8,128)(2,1)}, bf16[2,2,2,4,176,256]{5,4,3,2,1,0:T(8,128)(2,1)}, f32[3,16,64,256]{3,2,1,0:T(8,128)}) custom-call(bf16[4,2,4,128,256]{4,3,2,1,0:T(8,128)(2,1)} %bitcast.85, bf16[2,2,704,256]{3,2,1,0:T(8,128)(2,1)} %bitcast.92, bf16[2,2,704,256]{3,2,1,0:T(8,128)(2,1)} %bitcast.93, ...), custom_call_target="tpu_custom_call" | custom-call | tf_op jit(solution)/shard_map/finish/pallas_call | solution.py:1172
  521.1 2.0 fusion.3
  525.3 1.5 slice.152
  527.4 2.7 reshape.173
  530.1 2.8 copy.43
  533.5 2.8 reshape.178
  540.6 4.7 fusion
  545.5 1.5 pad_maximum_fusion
  547.8 2.5 bitcast_convert_fusion
  550.3 26.9 %all-gather.5.cloned.1.call-done = bf16[4096,256]{1,0:T(8,128)(2,1)} async-done(((bf16[512,256]{1,0:T(8,128)(2,1)}), bf16[4096,256]{1,0:T(8,128)(2,1)}) %all-gather.5.cloned.1.call-update) | async-done | bytes 2097168 | tf_op jit(solution)/shard_map/all_gather | solution.py:1232
  577.2 2.0 convert_bitcast_fusion
  579.2 2.6 copy.45
  582.0 1.7 copy.47
  (80 shorter events, 29.9 us)
Async XLA Ops:
  7.2 6.0 %copy-start.7 = (bf16[128,256,4,4]{1,3,2,0:T(4,128)(2,1)S(1)}, bf16[128,256,4,4]{1,3,2,0:T(4,128)(2,1)}, u32[]{:S(2)}) copy-start(bf16[128,256,4,4]{1,3,2,0:T(4,128)(2,1)} %param.36) | copy-start | bytes 3145732
  7.2 232.0 %reduce-scatter.3.cloned.1.call-start = ((), (), s32[]{:S(2)}) async-start(), calls=%async_computation.2 | async-start | bytes 3981312 | tf_op jit(solution)/shard_map/reduce_scatter | solution.py:1228
  12.1 2.9 copy-start.9
  158.6 1.4 copy-start
  158.6 183.4 %reduce-scatter.5.cloned.1.call-start = ((), (), s32[]{:S(2)}) async-start(), calls=%async_computation.4 | async-start | bytes 2359296 | tf_op jit(solution)/shard_map/reduce_scatter | solution.py:1228
  161.5 0.7 copy-start.1
  162.3 26.9 %collective-permute-start.4 = (bf16[8,64,384]{2,1,0:T(8,128)(2,1)S(1)}, bf16[8,64,384]{2,1,0:T(8,128)(2,1)S(1)}, u32[]{:S(2)}, u32[]{:S(2)}) collective-permute-start(bf16[8,64,384]{2,1,0:T(8,128)(2,1)S(1)} %get-tuple-element.104), channel_id=1, source_target_pairs={{0,1},{1,2},{2,3},{3,0},{4,5},{5,6},{6,7},{7,4},{8,9},{9,10},{10,1... | collective-permute-start | bytes 1179656 | tf_op jit(solution)/shard_map/ppermute | solution.py:539
  162.3 26.9 %collective-permute-start.5 = (bf16[8,64,384]{2,1,0:T(8,128)(2,1)S(1)}, bf16[8,64,384]{2,1,0:T(8,128)(2,1)S(1)}, u32[]{:S(2)}, u32[]{:S(2)}) collective-permute-start(bf16[8,64,384]{2,1,0:T(8,128)(2,1)S(1)} %get-tuple-element.105), channel_id=1, source_target_pairs={{0,2},{1,3},{2,0},{3,1},{4,6},{5,7},{6,4},{7,5},{8,10},{9,11},{10,... | collective-permute-start | bytes 1179656 | tf_op jit(solution)/shard_map/ppermute | solution.py:539
  163.6 25.5 %collective-permute-start.6 = (bf16[8,64,384]{2,1,0:T(8,128)(2,1)S(1)}, bf16[8,64,384]{2,1,0:T(8,128)(2,1)S(1)}, u32[]{:S(2)}, u32[]{:S(2)}) collective-permute-start(bf16[8,64,384]{2,1,0:T(8,128)(2,1)S(1)} %get-tuple-element.106), channel_id=1, source_target_pairs={{0,3},{1,0},{2,1},{3,2},{4,7},{5,4},{6,5},{7,6},{8,11},{9,8},{10,9... | collective-permute-start | bytes 1179656 | tf_op jit(solution)/shard_map/ppermute | solution.py:539
  189.1 0.7 copy-start.10
  189.2 0.9 copy-start.11
  189.2 1.0 copy-start.12
  274.0 1.4 copy-start.6
  274.0 3.8 copy-start.8
  274.0 134.4 %all-gather.3.cloned.1.call-start = ((), (), s32[]{:S(2)}) async-start(), calls=%async_computation.3 | async-start | bytes 3981312 | tf_op jit(solution)/shard_map/all_gather | solution.py:1232
  274.7 302.4 %all-gather.5.cloned.1.call-start = ((), (), s32[]{:S(2)}) async-start(), calls=%async_computation.5 | async-start | bytes 2359296 | tf_op jit(solution)/shard_map/all_gather | solution.py:1232
  275.6 8.8 %collective-permute-start.3 = (bf16[8,64,384]{2,1,0:T(8,128)(2,1)S(1)}, bf16[8,64,384]{2,1,0:T(8,128)(2,1)S(1)}, u32[]{:S(2)}, u32[]{:S(2)}) collective-permute-start(bf16[8,64,384]{2,1,0:T(8,128)(2,1)S(1)} %get-tuple-element.160), channel_id=1, source_target_pairs={{0,3},{1,0},{2,1},{3,2},{4,7},{5,4},{6,5},{7,6},{8,11},{9,8},{10,9... | collective-permute-start | bytes 1179656 | tf_op jit(solution)/shard_map/ppermute | solution.py:539
  276.0 19.8 %collective-permute-start.2 = (bf16[8,64,384]{2,1,0:T(8,128)(2,1)S(1)}, bf16[8,64,384]{2,1,0:T(8,128)(2,1)S(1)}, u32[]{:S(2)}, u32[]{:S(2)}) collective-permute-start(bf16[8,64,384]{2,1,0:T(8,128)(2,1)S(1)} %get-tuple-element.161), channel_id=1, source_target_pairs={{0,2},{1,3},{2,0},{3,1},{4,6},{5,7},{6,4},{7,5},{8,10},{9,11},{10,... | collective-permute-start | bytes 1179656 | tf_op jit(solution)/shard_map/ppermute | solution.py:539
  277.7 18.1 %collective-permute-start.1 = (bf16[8,64,384]{2,1,0:T(8,128)(2,1)S(1)}, bf16[8,64,384]{2,1,0:T(8,128)(2,1)S(1)}, u32[]{:S(2)}, u32[]{:S(2)}) collective-permute-start(bf16[8,64,384]{2,1,0:T(8,128)(2,1)S(1)} %get-tuple-element.162), channel_id=1, source_target_pairs={{0,1},{1,2},{2,3},{3,0},{4,5},{5,6},{6,7},{7,4},{8,9},{9,10},{10,1... | collective-permute-start | bytes 1179656 | tf_op jit(solution)/shard_map/ppermute | solution.py:539
  277.9 1.5 collective-permute-start
  415.2 2.8 copy-start.2
  523.7 1.6 copy-start.3
  545.5 2.4 copy-start.5
  579.2 2.8 copy-start.4
Sparse Core Ops, SparseCore 0:
  158.7 80.3 reduce-scatter.2
  274.1 67.8 reduce-scatter.4
  344.2 64.1 all-gather.2
  526.9 50.2 all-gather.4

commit v4 on v3

--- a/solution.py
+++ b/solution.py
@@ -66,7 +66,7 @@
 
 def turn(src,dst,rows,pad):
     for q in range(4):
-        dst[256*q:256*q+256,:]=src[1:rows+1,:,pad+256*q:pad+256*q+256].reshape(rows*NF,256).T
+        dst[256*q:256*q+256,:rows*NF]=src[1:rows+1,:,pad+256*q:pad+256*q+256].reshape(rows*NF,256).T
 
 def grad_w(big,yt,rows):
     out=[]
@@ -74,7 +74,7 @@
         acc=jnp.zeros((256,512),F32)
         for q in range(4):
             win=big[pl.ds(kh//2,rows),kh%2,:,256*q:256*q+512].reshape(rows*NF,512)
-            acc=acc+jnp.dot(yt[256*q:256*q+256,:],win,preferred_element_type=F32)
+            acc=acc+jnp.dot(yt[256*q:256*q+256,:rows*NF],win,preferred_element_type=F32)
         out.append(acc)
     return out
 
@@ -163,33 +163,12 @@
     down(m2,t3,8,4,keep(z3,m3))
     down(m3,t4,4,4,keep(z4,None))
 
-def enc_bwd_kernel(xp,z1,z2,z3,z4,df,u2,u3,u4,b,dx,pk,m1,m2,m3,s1,s2,s3,s4,yt1,yt2,yt3,yt4):
-    zero_big(m1,32); zero_big(m2,16); zero_big(m3,8)
-    zero_small(s1,32,0); zero_small(s2,16,128); zero_small(s3,8,128); zero_small(s4,4,256)
-    swap=exchange_16()
-    z=z4[...].astype(F32); s=sig(z)
-    s4[1:5,:,256:1280]=(df[...].astype(F32)*(s*(1.0+z*(1.0-s)))).astype(BF)
-    def back(z_ref,m,dst,pad):
-        def emit(m0,odd,q,acc):
-            per=acc.shape[0]
-            for t in range(per):
-                h=2*(m0+t)+odd
-                zz=z_ref[h,:,256*q:256*q+256].astype(F32)
-                ss=sig(zz); mm=zz*ss
-                dst[h+1,:,pad+256*q:pad+256*q+256]=(acc[t]*(ss+mm*(1.0-ss))).astype(BF)
-                m[m0+t+odd,1-odd,:,128+256*q:384+256*q]=mm.astype(BF)
-        return emit
-    up(s4,u4,4,4,back(z3,m3,s3,128))
-    turn(s4,yt4,4,256); pack(pk,0,1,128,256,grad_w(m3,yt4,4),False,swap,True)
-    up(s3,u3,8,4,back(z2,m2,s2,128))
-    turn(s3,yt3,8,128); pack(pk,2048,2,64,128,grad_w(m2,yt3,8),False,swap)
-    up(s2,u2,16,4,back(z1,m1,s1,0))
-    turn(s2,yt2,16,128); pack(pk,2560,4,32,64,grad_w(m1,yt2,16),False,swap)
-    def put(i0,acc): dx[pl.ds(i0,acc.shape[0])]=acc.astype(BF)
-    outer_up(s1,b,put)
-    turn(s1,yt1,32,0); pack_outer(pk,2688,outer_grad(xp,yt1),False)
-
-def dec_fwd_kernel(dec,u4,u3,u2,b,recon,p3,p2,p1,s4,s3,s2,s1):
+def dec_fwd_kernel(count,dec,u4,u3,u2,b,upper_both,lower,recon,p3,p2,p1,upper_piece,lower_both,
+                   s4,s3,s2,s1,upper_slots,lower_near,remote):
+    place=Place(count); sems=Sems(remote,None)
+    place.greet([place.near_device]+place.far_devices)
+    upper_far=far_start(place,sems,upper_both,upper_slots)
+    lower_copy=near_start(place,sems,lower,lower_near)
     zero_small(s1,32,0); zero_small(s2,16,128); zero_small(s3,8,128); zero_small(s4,4,256)
     z=dec[...].astype(F32)
     s4[1:5,:,256:1280]=(z*sig(z)).astype(BF)
@@ -206,9 +185,15 @@
     up(s2,u2,16,4,fwd(p1,s1,0))
     def put(i0,acc): recon[pl.ds(i0,acc.shape[0])]=acc.astype(BF)
     outer_up(s1,b,put)
-
-def dec_bwd_kernel(c0,c1,c2,c3,dec,p3,p2,p1,a,t2,t3,t4,gdec,pk,d1,d2,d3,cp,yt1,yt2,yt3,yt4):
-    me=lax.axis_index("strip")
+    far_end(place,upper_far,upper_both,upper_slots,upper_piece)
+    near_end(place,lower_copy,lower,lower_near,lower_both)
+
+def dec_bwd_kernel(count,c0,c1,c2,c3,dec,p3,p2,p1,a,t2,t3,t4,upper_piece,lower_both,
+                   gdec,pk,upper_half,lower_piece,d1,d2,d3,cp,yt,lower_slots,remote,here):
+    place=Place(count); sems=Sems(remote,here); me=place.me
+    place.greet(place.far_devices)
+    upper_back=back_start(place,sems,upper_piece,upper_half)
+    lower_far=far_start(place,sems,lower_both,lower_slots)
     cp[0]=jnp.zeros((NF,384),BF); cp[33]=jnp.zeros((NF,384),BF)
     for k,part in enumerate((c0,c1,c2,c3)):
         cp[pl.ds(1+8*lax.rem(me+4-k,4),8)]=part[...]
@@ -216,7 +201,7 @@
     def maps(p,rows,yt):
         for q in range(4):
             zz=p[:,:,256*q:256*q+256].reshape(rows*NF,256).astype(F32)
-            yt[256*q:256*q+256,:]=(zz*sig(zz)).astype(BF).T
+            yt[256*q:256*q+256,:rows*NF]=(zz*sig(zz)).astype(BF).T
     def back(p,dst):
         def emit(i0,half0,q,acc):
             rows=acc.shape[0]//NF
@@ -227,38 +212,142 @@
             else: put_big(dst,half0,rows,q,val)
         return emit
     swap=exchange_16()
-    maps(p1,32,yt1); pack_outer(pk,2688,outer_grad(cp,yt1),True)
+    maps(p1,32,yt); pack_outer(pk,2688,outer_grad(cp,yt),True)
     outer_down(cp,a,back(p1,d1))
-    maps(p2,16,yt2); pack(pk,2560,4,32,64,grad_w(d1,yt2,16),True,swap)
+    maps(p2,16,yt); pack(pk,2560,4,32,64,grad_w(d1,yt,16),True,swap)
     down(d1,t2,16,4,back(p2,d2))
-    maps(p3,8,yt3); pack(pk,2048,2,64,128,grad_w(d2,yt3,8),True,swap)
+    maps(p3,8,yt); pack(pk,2048,2,64,128,grad_w(d2,yt,8),True,swap)
     down(d2,t3,8,4,back(p3,d3))
-    maps(dec,4,yt4); pack(pk,0,1,128,256,grad_w(d3,yt4,4),True,swap)
+    maps(dec,4,yt); pack(pk,0,1,128,256,grad_w(d3,yt,4),True,swap)
     down(d3,t4,4,4,back(dec,None))
+    pk[2816-80:2816]=jnp.zeros((80,256),BF)
+    far_end(place,lower_far,lower_both,lower_slots,lower_piece)
+    for one in upper_back: one.wait()
+
+def estimate(us):
+    return pl.CostEstimate(flops=us*1150*10**6,bytes_accessed=MIB,transcendentals=0)
 
 def S(shape,dt=BF): return jax.ShapeDtypeStruct(shape,dt)
 def V(shape,dt=BF): return pltpu.VMEM(shape,dt)
 VM=lambda n:[pl.BlockSpec(memory_space=pltpu.VMEM)]*n
-def run(kernel,outs,scratch,args,name,lim=60,flops=10**10):
+def run(kernel,outs,scratch,args,name,us,lim=60,ident=None):
+    extra={} if ident is None else dict(collective_id=ident,has_side_effects=True)
     return pl.pallas_call(kernel,out_shape=outs,in_specs=VM(len(args)),out_specs=tuple(VM(len(outs))),
-        scratch_shapes=scratch,compiler_params=pltpu.CompilerParams(vmem_limit_bytes=lim*MIB),
-        cost_estimate=pl.CostEstimate(flops=flops,bytes_accessed=20*MIB,transcendentals=0),name=name)(*args)
+        scratch_shapes=scratch,compiler_params=pltpu.CompilerParams(vmem_limit_bytes=lim*MIB,**extra),
+        cost_estimate=estimate(us),name=name)(*args)
 big=lambda h:V((h//2+1,2,NF,1280))
 def enc_fwd(xp,a,t2,t3,t4):
     return run(enc_fwd_kernel,(S((32,NF,1024)),S((16,NF,1024)),S((8,NF,1024)),S((4,NF,1024)),S((4,NF,1024))),
-      [big(32),big(16),big(8)],(xp,a,t2,t3,t4),"encode")
-GS=(S((2816,256)),)
+      [big(32),big(16),big(8)],(xp,a,t2,t3,t4),"encode",22)
+small=lambda h,p:V((h+2,NF,1024+2*p))
+def enc_fwd(xp,a,t2,t3,t4):
+    return run(enc_fwd_kernel,(S((32,NF,1024)),S((16,NF,1024)),S((8,NF,1024)),S((4,NF,1024)),S((4,NF,1024))),
+      [big(32),big(16),big(8)],(xp,a,t2,t3,t4),"encode",22)
 small=lambda h,p:V((h+2,NF,1024+2*p))
 yts=[V((1024,32*NF)),V((1024,16*NF)),V((1024,8*NF)),V((1024,4*NF))]
-def enc_bwd(xp,z1,z2,z3,z4,df,u2,u3,u4,b):
-    return run(enc_bwd_kernel,(S((32,NF,384)),)+GS,[big(32),big(16),big(8),small(32,0),small(16,128),small(8,128),small(4,256)]+yts,
-      (xp,z1,z2,z3,z4,df,u2,u3,u4,b),"encode_back")
-def dec_fwd(dec,u4,u3,u2,b):
-    return run(dec_fwd_kernel,(S((32,NF,384)),S((8,NF,1024)),S((16,NF,1024)),S((32,NF,1024))),
-      [small(4,256),small(8,128),small(16,128),small(32,0)],(dec,u4,u3,u2,b),"decode")
-def dec_bwd(hints,dec,p3,p2,p1,a,t2,t3,t4):
-    return run(dec_bwd_kernel,(S((4,NF,1024)),)+GS,[big(32),big(16),big(8),V((34,NF,384))]+yts,
-      (*hints,dec,p3,p2,p1,a,t2,t3,t4),"decode_back")
+def dec_fwd(dec,u4,u3,u2,b,upper_both,lower):
+    count=lax.axis_size("rows"); half=count//2
+    upper,rows=2*upper_both.shape[0],lower.shape[0]
+    dma=pltpu.SemaphoreType.DMA
+    return run(functools.partial(dec_fwd_kernel,count),
+      (S((32,NF,384)),S((8,NF,1024)),S((16,NF,1024)),S((32,NF,1024)),S((upper//count,512)),S((rows//2,512))),
+      [small(4,256),small(8,128),small(16,128),small(32,0),V((half-1,upper//count,512)),V((rows//2,512)),dma((2,half))],
+      (dec,u4,u3,u2,b,upper_both,lower),"decode",24,ident=5)
+def dec_bwd(hints,dec,p3,p2,p1,a,t2,t3,t4,upper_piece,lower_both):
+    count=lax.axis_size("rows"); half=count//2
+    upper,rows=count*upper_piece.shape[0],2*lower_both.shape[0]
+    dma=pltpu.SemaphoreType.DMA
+    return run(functools.partial(dec_bwd_kernel,count),
+      (S((4,NF,1024)),S((2816,256)),S((upper//2,512)),S((rows//count,512))),
+      [big(32),big(16),big(8),V((34,NF,384)),V((1024,32*NF)),V((half-1,rows//count,512)),dma((2,2*(half-1))),dma((1,))],
+      (*hints,dec,p3,p2,p1,a,t2,t3,t4,upper_piece,lower_both),"decode_back",42,ident=6)
+
+
+def rows_of(ref, index, size):
+    return ref.at[pl.ds(pl.multiple_of(index * size, 16), size)]
+
+
+class Place:
+    def __init__(self, count):
+        self.me, self.row = lax.axis_index("strip"), lax.axis_index("rows")
+        self.half = count // 2
+        self.near, self.far = lax.rem(self.row, 2), lax.div(self.row, 2)
+        self.core, self.x = lax.rem(self.me, 2), lax.div(self.me, 2)
+        self.near_device = (self.row + 1 - 2 * self.near, self.me)
+        self.sibling = (self.row, self.me + 1 - 2 * self.core)
+        self.partner = (self.row, lax.rem(self.me + 2, 4))
+        self.others = [(self.row, lax.rem(self.me + k, 4)) for k in range(1, 4)]
+        self.far_places = [lax.rem(self.far + k, self.half) for k in range(1, self.half)]
+        self.far_devices = [(2 * place + self.near, self.me) for place in self.far_places]
+
+    def greet(self, devices):
+        barrier = pltpu.get_barrier_semaphore()
+        for device in devices:
+            pl.semaphore_signal(barrier, inc=1, device_id=device, device_id_type=MESH)
+        pl.semaphore_wait(barrier, len(devices))
+
+
+class Sems:
+    def __init__(self, remote, local):
+        self.remote, self.local, self.used, self.used_here = remote, local, 0, 0
+
+    def copy(self, src, dst, device):
+        one = pltpu.make_async_remote_copy(
+            src_ref=src,
+            dst_ref=dst,
+            send_sem=self.remote.at[0, self.used],
+            recv_sem=self.remote.at[1, self.used],
+            device_id=device,
+            device_id_type=MESH,
+        )
+        self.used = self.used + 1
+        one.start()
+        return one
+
+    def here(self, src, dst):
+        one = pltpu.make_async_copy(src, dst, self.local.at[self.used_here])
+        self.used_here = self.used_here + 1
+        one.start()
+        return one
+
+
+def near_start(place, sems, values, arrived):
+    half = values.shape[0] // 2
+    return sems.copy(rows_of(values, 1 - place.near, half), arrived, place.near_device)
+
+
+def near_end(place, copy, values, arrived, both):
+    copy.wait()
+    half = values.shape[0] // 2
+    total = rows_of(values, place.near, half)[...].astype(F32) + arrived[...].astype(F32)
+    both[...] = total.astype(BF)
+
+
+def far_start(place, sems, both, slots):
+    each = slots.shape[1]
+    return [
+        sems.copy(rows_of(both, at, each), slots.at[k], device)
+        for k, (at, device) in enumerate(zip(place.far_places, place.far_devices))
+    ]
+
+
+def far_end(place, copies, both, slots, piece):
+    for one in copies:
+        one.wait()
+    total = rows_of(both, place.far, slots.shape[1])[...].astype(F32)
+    for k in range(slots.shape[0]):
+        total = total + slots[k].astype(F32)
+    piece[...] = total.astype(BF)
+
+
+def back_start(place, sems, piece, home):
+    out = rows_of(home, place.far, piece.shape[0])
+    return [sems.here(piece, out)] + [sems.copy(piece, out, d) for d in place.far_devices]
+
+
+def last_start(place, sems, home, out):
+    half = out.shape[0] // 2
+    return sems.copy(home, rows_of(out, place.near, half), place.near_device)
 
 
 def exchange_16():
@@ -365,9 +454,9 @@
 
 
 def start_kernel(
-    x, e1, e2, e3, e4, d1, d2, d3, d4, lh, dh, emb, qkv, proj, up, down,
+    x, later, e1, e2, e3, e4, d1, d2, d3, d4, lh, dh, emb, qkv, proj, up, down,
     pixels, ea, eb, et2, et3, et4, eu2, eu3, eu4, da, db, dt2, dt3, dt4, du2, du3, du4,
-    lh0, lh1, dh0, dh1, emb1, qkv1, proj1, up1, down1,
+    lh0, lh1, dh0, dh1, emb1, qkv1, proj1, up1, down1, t0, t1, t2, t3,
     stage, send_sem, recv_sem, side_sems,
     va, vb, vt2, vt3, vt4, vu2, vu3, vu4, wa, wb, wt2, wt3, wt4, wu2, wu3, wu4,
     vl, vd, out_sems,
@@ -425,6 +514,7 @@
         to_sibling(src, dst, index)
     pixels[pl.ds(1 + 8 * me, 8)] = stage[me]
 
+    turn_kernel(later, t0, t1, t2, t3)
     stores = []
 
     def store(src, dst):
@@ -474,7 +564,7 @@
         copy.wait()
 
 
-def start(frames, kernels, latent_head, decode_head, others):
+def start(frames, later, kernels, latent_head, decode_head, others):
     e1, e2, e3, e4, d1, d2, d3, d4 = kernels
     rows_in = [
         jnp.tile(jnp.transpose(e1, (1, 2, 3, 0)).reshape(48, 32), (1, 32)).astype(F32),
@@ -492,11 +582,12 @@
     built = built + [(2, 1024, 256), (2, 1024, 256), (2, 1536, 256)]
     heads = [(4096, 256)] * 4
     shapes = [(34, NF, 384)] + built * 2 + heads + [w.shape for w in others]
+    shapes = shapes + [(8, NF, 384)] * 4
     out = pl.pallas_call(
         start_kernel,
         out_shape=tuple(S(shape) for shape in shapes),
-        in_specs=VM(11) + [any_spec] * len(others),
-        out_specs=tuple(VM(1) + [any_spec] * (len(shapes) - 1)),
+        in_specs=VM(12) + [any_spec] * len(others),
+        out_specs=tuple(VM(1) + [any_spec] * (len(shapes) - 5) + VM(4)),
         scratch_shapes=[
             V((4, 8, NF, 384)),
             dma((3,)),
@@ -510,10 +601,18 @@
         compiler_params=pltpu.CompilerParams(
             collective_id=1, has_side_effects=True, vmem_limit_bytes=56 * MIB
         ),
+        cost_estimate=estimate(26),
         name="start",
-    )(jnp.transpose(frames, (1, 2, 3, 0)), *rows_in, latent_head, decode_head, *others)
-    encode_forms, decode_forms = out[1:9], out[9:17]
-    return out[0], encode_forms, decode_forms, out[17:19], out[19:21], out[21:]
+    )(
+        jnp.transpose(frames, (1, 2, 3, 0)),
+        jnp.transpose(later, (1, 2, 3, 0)),
+        *rows_in,
+        latent_head,
+        decode_head,
+        *others,
+    )
+    hints = around(out[-4:])
+    return out[0], out[1:9], out[9:17], out[17:19], out[19:21], out[21:-4], hints
 
 
 def turn_kernel(x, *out):
@@ -538,18 +637,6 @@
     return [parts[0]] + [
         lax.ppermute(parts[k], "strip", [(s, (s + k) % 4) for s in range(4)]) for k in range(1, 4)
     ]
-
-
-def frames_in_later(block):
-    parts = pl.pallas_call(
-        turn_kernel,
-        out_shape=(S((8, NF, 384)),) * 4,
-        in_specs=VM(1),
-        out_specs=tuple(VM(4)),
-        compiler_params=pltpu.CompilerParams(vmem_limit_bytes=32 * MIB),
-        name="turn",
-    )(jnp.transpose(block, (1, 2, 3, 0)))
-    return around(parts)
 
 
 def turned_back(got, out):
@@ -572,10 +659,11 @@
     turned_back(got, out)
 
 
-def frames_out_later(pairs, strip):
-    parts = around(
-        [lax.dynamic_slice_in_dim(pairs, 8 * ((strip + k) % 4), 8) for k in range(4)]
-    )
+def blocks_around(pairs, strip):
+    return around([lax.dynamic_slice_in_dim(pairs, 8 * ((strip + k) % 4), 8) for k in range(4)])
+
+
+def frames_out_later(parts):
     flat = pl.pallas_call(
         turn_back_kernel,
         out_shape=S((3, 16, 64, 256)),
@@ -583,6 +671,7 @@
         out_specs=VM(1)[0],
         scratch_shapes=[V((4, 8, NF, 384))],
         compiler_params=pltpu.CompilerParams(vmem_limit_bytes=32 * MIB),
+        cost_estimate=estimate(2),
         name="turn_back",
     )(*parts)
     return jnp.transpose(flat, (3, 0, 1, 2))
@@ -628,27 +717,26 @@
 LAYER_ROWS = 1536
 
 
-def token_rows(layers):
-    return layers * LAYER_ROWS + 256 + NF + 16
+def token_rows(layers, count):
+    upper = max(layers - 1, 1) * LAYER_ROWS
+    lower = LAYER_ROWS + 256 + NF + 16
+    return share_rows(upper, count), share_rows(lower, count)
 
 
 def middle_kernel(
-    layers,
+    layers, count,
     feat, lh0, lh1, dh0, dh1, emb0, emb1, pos, gains, allow, cot,
     qkv0, qkv1, proj0, proj1, up0, up1, down0, down1,
-    tokens, latent_out, chances_out, decoded, flat, grad_latent, feat_got,
+    tokens, latent_out, chances_out, decoded, upper_both, lower, grad_latent, feat_got,
     feat_sems, keep, send, sent, spread_sems, parts, gots, pair_sems,
-    other, other_got, fold_sems, unit_a, unit_f, normed_a, normed_f, mixed, weights,
+    upper, upper_other, upper_got, lower_other, lower_got, upper_near, fold_sems, near_sems, unit_a, unit_f, normed_a, normed_f, mixed, weights,
     attended, before, inner, gain_rows,
 ):
     strip = lax.axis_index("strip")
     row = lax.axis_index("rows")
-    partner = (row, lax.rem(strip + 2, 4))
-    sibling = (row, strip + 1 - 2 * lax.rem(strip, 2))
-    barrier = pltpu.get_barrier_semaphore()
-    for device in (partner, sibling):
-        pl.semaphore_signal(barrier, inc=1, device_id=device, device_id_type=MESH)
-    pl.semaphore_wait(barrier, 2)
+    place_here = Place(count)
+    partner, sibling = place_here.partner, place_here.sibling
+    place_here.greet([partner, sibling, place_here.near_device])
 
     def copy(src, dst, sems, index, device):
         return pltpu.make_async_remote_copy(
@@ -753,17 +841,25 @@
     spread_copy.wait()
     decoded[...] = (keep[...].astype(F32) + sent[...].astype(F32)).astype(BF)
 
-    fold_copies = []
-
-    def fold_start(first, count):
-        rows = pl.ds(first, count)
-        one = copy(other.at[rows], other_got.at[rows], fold_sems, len(fold_copies), sibling)
+    def fold_start(index, part, got):
+        one = copy(part, got, fold_sems, index, sibling)
         one.start()
-        fold_copies.append((first, count, one))
+        return one
+
+    def fold_end(one, own, got, count):
+        one.wait()
+        for first in range(0, count, 128):
+            rows = slice(first, min(first + 128, count))
+            own[rows] = (own[rows].astype(F32) + got[rows].astype(F32)).astype(BF)
+        if own.shape[0] > count:
+            own[count:] = jnp.zeros((own.shape[0] - count, 512), BF)
+
+    lower_rows = LAYER_ROWS + 256 + NF + 16
 
     grad = cot[...].astype(F32)
     for k in reversed(range(layers)):
-        base = LAYER_ROWS * k
+        flat, other = (upper, upper_other) if k else (lower, lower_other)
+        base = LAYER_ROWS * (k - 1) if k else 0
         index = 2 * layers + 1 + 2 * (layers - 1 - k)
         low = grad.astype(BF)
         partial = jnp.zeros((2 * NF, 512), F32)
@@ -781,6 +877,9 @@
             act = inner[k, :, 512 * side : 512 * side + 512]
             dst[base : base + 512] = dot(act.T, low).astype(BF)
             dst[base + 512 : base + 1024] = dot(turned, grads[side]).astype(BF)
+        if k == 0:
+            fold_end(upper_fold, upper, upper_got, LAYER_ROWS * (layers - 1))
+            near_copy = near_start(place_here, Sems(near_sems, None), upper, upper_near)
         grad_normed = total_wait(index, waiting)
         gain_f, grad_rows = unit_back(
             grad_normed, unit_f[k, :, :512], unit_f[k, :, 512:513], gains[2 * k + 1 : 2 * k + 2]
@@ -822,7 +921,8 @@
                     dst[first : first + 128, 128 * b : 128 * b + 128] = value[
                         128 * b : 128 * b + 128
                     ]
-        fold_start(base, LAYER_ROWS)
+        if k == 1:
+            upper_fold = fold_start(0, upper_other, upper_got)
         grad_normed = total_wait(index + 1, waiting)
         gain_a, grad_rows = unit_back(
             grad_normed, unit_a[k, :, :512], unit_a[k, :, 512:513], gains[2 * k : 2 * k + 1]
@@ -831,12 +931,11 @@
         gain_rows[2 * k : 2 * k + 1] = gain_a
         gain_rows[2 * k + 1 : 2 * k + 2] = gain_f
 
-    base = LAYER_ROWS * layers
     low = grad.astype(BF)
     own_latent, other_latent = latent_out[:, :256], latent_out[:, 256:]
-    flat[base : base + 256] = dot(own_latent.T, low).astype(BF)
-    other[base : base + 256] = dot(other_latent.T, low).astype(BF)
-    small = jnp.concatenate(
+    lower[LAYER_ROWS : LAYER_ROWS + 256] = dot(own_latent.T, low).astype(BF)
+    lower_other[LAYER_ROWS : LAYER_ROWS + 256] = dot(other_latent.T, low).astype(BF)
+    rest = jnp.concatenate(
         [
             grad[:NF] + grad[NF:],
             gain_rows[...],
@@ -844,41 +943,35 @@
         ],
         axis=0,
     ).astype(BF)
-    flat[base + 256 : base + 256 + NF + 16] = small
-    other[base + 256 : base + 256 + NF + 16] = small
-    fold_start(base, 256 + NF + 16)
+    lower[LAYER_ROWS + 256 : lower_rows] = rest
+    lower_other[LAYER_ROWS + 256 : lower_rows] = rest
+    lower_fold = fold_start(1, lower_other, lower_got)
     grad_latent[:, :256] = dot_nt(low, emb0[...])
     grad_latent[:, 256:] = dot_nt(low, emb1[...])
-    for first, count, one in fold_copies:
-        one.wait()
-        for start in range(first, first + count, 16 * 7 if count % 112 == 0 else 16 * 8):
-            size = min(128 if count % 112 else 112, first + count - start)
-            rows = slice(start, start + size)
-            flat[rows] = (flat[rows].astype(F32) + other_got[rows].astype(F32)).astype(BF)
-    spare = flat.shape[0] - token_rows(layers)
-    if spare:
-        flat[token_rows(layers) :] = jnp.zeros((spare, 512), BF)
-
-
-def middle(layers, multiple, *args):
-    rows = token_rows(layers)
-    rows = rows + -rows % multiple
+    near_end(place_here, near_copy, upper, upper_near, upper_both)
+    fold_end(lower_fold, lower, lower_got, lower_rows)
+
+
+def middle(layers, *args):
+    count = lax.axis_size("rows")
+    upper, lower = token_rows(layers, count)
     dma = pltpu.SemaphoreType.DMA
     sums = 4 * layers + 1
     t = 2 * NF
     return pl.pallas_call(
-        functools.partial(middle_kernel, layers),
+        functools.partial(middle_kernel, layers, count),
         out_shape=(
             S((t, 512)),
             S((t, 512)),
             S((t, 512), F32),
             S((4, NF, 1024)),
-            S((rows, 512)),
+            S((upper // 2, 512)),
+            S((lower, 512)),
             S((t, 512), F32),
             S((4, NF, 1024)),
         ),
         in_specs=VM(len(args)),
-        out_specs=tuple(VM(7)),
+        out_specs=tuple(VM(8)),
         scratch_shapes=[
             dma((2, 1)),
             V((4, NF, 1024)),
@@ -888,9 +981,14 @@
             V((sums, t, 512)),
             V((sums, t, 512)),
             dma((2, sums)),
-            V((rows, 512)),
-            V((rows, 512)),
-            dma((2, layers + 1)),
+            V((upper, 512)),
+            V((upper, 512)),
+            V((upper, 512)),
+            V((lower, 512)),
+            V((lower, 512)),
+            V((upper // 2, 512)),
+            dma((2, 2)),
+            dma((2, 1)),
             V((layers, t, 640), F32),
             V((layers, t, 640), F32),
             V((layers, t, 512)),
@@ -905,36 +1003,40 @@
         compiler_params=pltpu.CompilerParams(
             collective_id=3, has_side_effects=True, vmem_limit_bytes=56 * MIB
         ),
+        cost_estimate=estimate(84),
         name="middle",
     )(*args)
 
 
 def back_kernel(
-    grad, latent, chances, grad_embed, feat0, feat1, lh0, lh1, dh0, dh1,
-    grad_feat, out_rows, in_rows,
-    got, got_sems, keep, send, sent, sent_sems, own, other, other_got, fold_sems,
+    count, grad, latent, chances, grad_embed, feat0, feat1, lh0, lh1, dh0, dh1, flat, upper_half, lower_piece,
+    grad_feat, in_rows, share, d_both, upper_total, lower_half,
+    side_got, side_sum, cross_got, side_sems, got, got_sems, keep, send, sent, sent_sems,
+    own, other, other_got, fold_sems, values, from_near, remote, here,
 ):
-    strip = lax.axis_index("strip")
-    row = lax.axis_index("rows")
-    partner = (row, lax.rem(strip + 2, 4))
-    sibling = (row, strip + 1 - 2 * lax.rem(strip, 2))
-    barrier = pltpu.get_barrier_semaphore()
-    for device in (partner, sibling):
-        pl.semaphore_signal(barrier, inc=1, device_id=device, device_id_type=MESH)
-    pl.semaphore_wait(barrier, 2)
-
-    def copy(src, dst, sems, index, device):
-        return pltpu.make_async_remote_copy(
+    place = Place(count)
+    near, core, x = place.near, place.core, place.x
+    partner, sibling = place.partner, place.sibling
+    place.greet([partner, sibling, place.near_device] + place.far_devices)
+    sems = Sems(remote, here)
+
+    def copy(src, dst, pair, index, device):
+        one = pltpu.make_async_remote_copy(
             src_ref=src,
             dst_ref=dst,
-            send_sem=sems.at[0, index],
-            recv_sem=sems.at[1, index],
+            send_sem=pair.at[(0,) + index],
+            recv_sem=pair.at[(1,) + index],
             device_id=device,
             device_id_type=MESH,
         )
-
-    grad_copy = copy(grad, got, got_sems, 0, partner)
-    grad_copy.start()
+        one.start()
+        return one
+
+    grad_copy = copy(grad, got, got_sems, (0,), partner)
+    upper_own = sems.here(upper_half, rows_of(upper_total, near, upper_half.shape[0]))
+    upper_last = last_start(place, sems, upper_half, upper_total)
+    lower_back = back_start(place, sems, lower_piece, lower_half)
+    side_copy = copy(flat.at[1 - core], side_got, side_sems, (0,), sibling)
 
     def through(maps):
         halves = []
@@ -945,8 +1047,33 @@
             halves.append(total)
         return jnp.concatenate(halves, axis=1)
 
+    def head_grad(slot, first, second, rhs):
+        for h in range(4):
+            for w in range(4):
+                lanes = slice(256 * w, 256 * w + 256)
+                rows = slice(1024 * h + 256 * w, 1024 * h + 256 * w + 256)
+                maps = jnp.concatenate([first[h, :, lanes], second[h, :, lanes]], axis=0)
+                value = dot(maps.T, rhs).astype(BF)
+                own[slot, rows] = value[:, :256]
+                other[slot, rows] = value[:, 256:]
+        return copy(other.at[slot], other_got.at[slot], fold_sems, (slot,), sibling)
+
+    swap = exchange_16()
+
+    def folded(slot, b):
+        parts = []
+        for k in range(16):
+            rows = slice(256 * k + 16 * b, 256 * k + 16 * b + 16)
+            value = own[slot, rows].astype(F32) + other_got[slot, rows].astype(F32)
+            parts.append(value.astype(BF))
+        return dot(swap, jnp.concatenate(parts, axis=0)).astype(BF)
+
     mine = through(grad)
+    side_copy.wait()
+    side_sum[...] = (flat[core].astype(F32) + side_got[...].astype(F32)).astype(BF)
+    cross_copy = copy(side_sum.at[1 - x], cross_got, side_sems, (1,), partner)
     grad_copy.wait()
+    out_fold = head_grad(0, grad, got, latent[...])
     grad_latent = grad_embed[...] + jnp.concatenate([mine, through(got)], axis=0)
     probs = chances[...]
     along = over_groups(probs * grad_latent, jnp.add)
@@ -960,50 +1087,53 @@
             value = value.astype(BF)
             keep[h, :, lanes] = value[:NF]
             send[h, :, lanes] = value[NF:]
-        one = copy(send.at[h], sent.at[h], sent_sems, h, partner)
-        one.start()
-        sends.append(one)
-    folds = []
-    for slot, (first, second, rhs) in enumerate(
-        ((grad, got, latent[...]), (feat0, feat1, grad_logits))
-    ):
-        for h in range(4):
-            for w in range(4):
-                lanes = slice(256 * w, 256 * w + 256)
-                rows = slice(1024 * h + 256 * w, 1024 * h + 256 * w + 256)
-                maps = jnp.concatenate([first[h, :, lanes], second[h, :, lanes]], axis=0)
-                value = dot(maps.T, rhs).astype(BF)
-                own[slot, rows] = value[:, :256]
-                other[slot, rows] = value[:, 256:]
-        one = copy(other.at[slot], other_got.at[slot], fold_sems, slot, sibling)
-        one.start()
-        folds.append(one)
+        sends.append(copy(send.at[h], sent.at[h], sent_sems, (h,), partner))
+    out_fold.wait()
+    for b in range(16):
+        values[256 * b : 256 * b + 256] = folded(0, b).T
+    near_copy = near_start(place, sems, values, from_near)
+    in_fold = head_grad(1, feat0, feat1, grad_logits)
+    cross_copy.wait()
+    share[...] = (side_sum[x].astype(F32) + cross_got[...].astype(F32)).astype(BF)
     for one in sends:
         one.wait()
     grad_feat[...] = (keep[...].astype(F32) + sent[...].astype(F32)).astype(BF)
-    swap = exchange_16()
-    for slot, (out, one) in enumerate(zip((out_rows, in_rows), folds)):
+    in_fold.wait()
+    for b in range(16):
+        in_rows[256 * b : 256 * b + 256] = folded(1, b)
+    near_end(place, near_copy, values, from_near, d_both)
+    upper_own.wait()
+    upper_last.wait()
+    for one in lower_back:
         one.wait()
-        for b in range(16):
-            parts = []
-            for k in range(16):
-                rows = slice(256 * k + 16 * b, 256 * k + 16 * b + 16)
-                value = own[slot, rows].astype(F32) + other_got[slot, rows].astype(F32)
-                parts.append(value.astype(BF))
-            block = dot(swap, jnp.concatenate(parts, axis=0)).astype(BF)
-            out[256 * b : 256 * b + 256] = block.T if slot == 0 else block
 
 
 def latents_back(*args):
     dma = pltpu.SemaphoreType.DMA
+    count = lax.axis_size("rows")
+    half = count // 2
+    flat, upper_half, lower_piece = args[-3:]
+    quarter = flat.shape[0] // 4
+    args = args[:-3] + (flat.reshape(2, 2, quarter, 256), upper_half, lower_piece)
     maps = (4, NF, 1024)
     rows = (4096, 256)
     return pl.pallas_call(
-        back_kernel,
-        out_shape=(S(maps), S(rows), S(rows)),
+        functools.partial(back_kernel, count),
+        out_shape=(
+            S(maps),
+            S(rows),
+            S((quarter, 256)),
+            S((2048, 256)),
+            S((2 * upper_half.shape[0], 512)),
+            S((half * lower_piece.shape[0], 512)),
+        ),
         in_specs=VM(len(args)),
-        out_specs=tuple(VM(3)),
+        out_specs=tuple(VM(4) + [pl.BlockSpec(memory_space=pl.ANY)] + VM(1)),
         scratch_shapes=[
+            V((2, quarter, 256)),
+            V((2, quarter, 256)),
+            V((quarter, 256)),
+            dma((2, 2)),
             V(maps),
             dma((2, 1)),
             V(maps),
@@ -1014,202 +1144,255 @@
             V((2,) + rows),
             V((2,) + rows),
             dma((2, 2)),
+            V(rows),
+            V((2048, 256)),
+            dma((2, half + 1)),
+            dma((2,)),
         ],
         compiler_params=pltpu.CompilerParams(
-            collective_id=4, has_side_effects=True, vmem_limit_bytes=56 * MIB
+            collective_id=4, has_side_effects=True, vmem_limit_bytes=58 * MIB
         ),
+        cost_estimate=estimate(50),
         name="latents_back",
     )(*args)
 
 
-def finish_kernel(
-    count, v, dec, enc, grad, total, conv, grad_out,
-    got, strip_sems, from_near, summed, from_far, conv_v, conv_near, conv_summed, conv_far,
-    side_got, side_sum, cross_got, sems, far_sems, back_sems,
-):
-    me = lax.axis_index("strip")
-    row = lax.axis_index("rows")
-    half = count // 2
-    chunks = v.shape[0]
-    near, far = lax.rem(row, 2), lax.div(row, 2)
-    core, x = lax.rem(me, 2), lax.div(me, 2)
-    near_device = (row + 1 - 2 * near, me)
-    sibling, partner = (row, me + 1 - 2 * core), (row, lax.rem(me + 2, 4))
-    barrier = pltpu.get_barrier_semaphore()
-    strip_devices = [(row, lax.rem(me + k, 4)) for k in range(1, 4)]
-    far_places = [lax.rem(far + k, half) for k in range(1, half)]
-    far_devices = [(2 * place + near, me) for place in far_places]
-    for device in strip_devices + [near_device] + far_devices:
-        pl.semaphore_signal(barrier, inc=1, device_id=device, device_id_type=MESH)
-    pl.semaphore_wait(barrier, 3 + half)
-
-    def copy(src, dst, pair, index, device):
-        one = pltpu.make_async_remote_copy(
-            src_ref=src,
-            dst_ref=dst,
-            send_sem=pair.at[(0,) + index],
-            recv_sem=pair.at[(1,) + index],
-            device_id=device,
-            device_id_type=MESH,
-        )
-        one.start()
-        return one
-
-    places = [
-        (v.at[c], from_near.at[c], summed.at[c], from_far.at[c], total.at[c])
-        for c in range(chunks)
-    ]
-    places.append((conv_v, conv_near, conv_summed, conv_far, conv.at[core, x]))
-    near_copies, far_copies, back_copies, last_copies = {}, {}, {}, {}
-
-    def stage_near(c):
-        near_copies[c] = copy(places[c][0].at[1 - near], places[c][1], sems, (c,), near_device)
-
-    def stage_far(c):
-        values, arrived, both, slots, _ = places[c]
-        near_copies[c].wait()
-        both[...] = (values[near].astype(F32) + arrived[...].astype(F32)).astype(BF)
-        far_copies[c] = [
-            copy(both.at[place], slots.at[k], far_sems, (c, k), device)
-            for k, (place, device) in enumerate(zip(far_places, far_devices))
-        ]
-
-    def stage_back(c):
-        _, _, both, slots, out = places[c]
-        for one in far_copies[c]:
-            one.wait()
-        whole = both[far].astype(F32)
-        for k in range(half - 1):
-            whole = whole + slots[k].astype(F32)
-        out[near, far] = whole.astype(BF)
-        back_copies[c] = [
-            copy(out.at[near, far], out.at[near, far], back_sems, (c, k), device)
-            for k, device in enumerate(far_devices)
-        ]
-
-    def stage_last(c):
-        out = places[c][4]
-        for one in back_copies[c]:
-            one.wait()
-        last_copies[c] = copy(
-            out.at[near], out.at[near], sems, (chunks + 1 + c,), near_device
-        )
-
-    side = 2 * (chunks + 1)
-    side_copies = [
-        copy(part.at[1 - core], side_got.at[k], sems, (side + k,), sibling)
-        for k, part in enumerate((dec, enc))
-    ]
-    for c in range(chunks):
-        stage_near(c)
-    cross_copies = []
-    for k, part in enumerate((dec, enc)):
-        side_copies[k].wait()
-        side_sum[k] = (part[core].astype(F32) + side_got[k].astype(F32)).astype(BF)
-        cross_copies.append(
-            copy(side_sum.at[k, 1 - x], cross_got.at[k], sems, (side + 2 + k,), partner)
-        )
-    strip_copies = []
-    for k in range(1, 4):
-        to = lax.rem(me + k, 4)
-        strip_copies.append(
-            copy(grad.at[pl.ds(8 * to, 8)], got.at[me], strip_sems, (k - 1,), (row, to))
-        )
-    got[me] = grad[pl.ds(8 * me, 8)]
-
-    stage_far(0)
-    stage_far(1)
-    shares = []
-    for k in range(2):
-        cross_copies[k].wait()
-        shares.append(
-            (side_sum[k, x].astype(F32) + cross_got[k].astype(F32)).astype(BF)
-        )
-    share = jnp.concatenate(shares, axis=0)
-    each = conv_v.shape[2]
-    spare = 2 * half * each - share.shape[0]
+def strip_fold_start(place, sems, flat, first, size, got):
+    half = size // 2
+    return sems.copy(
+        flat.at[pl.ds(pl.multiple_of(first + (1 - place.core) * half, 16), half)], got, place.sibling
+    )
+
+
+def strip_cross_start(place, sems, copy, flat, first, size, got, both, cross):
+    copy.wait()
+    half = size // 2
+    own = flat[pl.ds(pl.multiple_of(first + place.core * half, 16), half)]
+    both[...] = (own.astype(F32) + got[...].astype(F32)).astype(BF)
+    return sems.copy(rows_of(both, 1 - place.x, half // 2), cross, place.partner)
+
+
+def strip_share(place, copy, both, cross):
+    copy.wait()
+    own = rows_of(both, place.x, cross.shape[0])[...]
+    return (own.astype(F32) + cross[...].astype(F32)).astype(BF)
+
+
+def padded_share(ref, parts):
+    share = jnp.concatenate(parts, axis=0)
+    spare = ref.shape[0] - share.shape[0]
     if spare:
         share = jnp.concatenate([share, jnp.zeros((spare, 256), BF)], axis=0)
-    for piece in range(2 * half):
-        conv_v[piece // half, piece % half] = share[piece * each : piece * each + each]
-    last = chunks
-    stage_near(last)
-    stage_back(0)
-    stage_far(2)
-    stage_back(1)
-    stage_last(0)
-    stage_far(last)
-    stage_far(3)
-    stage_back(2)
-    stage_last(1)
-    for one in strip_copies:
-        one.wait()
-    turned_back(got, grad_out)
-    stage_back(last)
-    stage_last(2)
-    stage_back(3)
-    stage_last(last)
-    stage_last(3)
-    last_copies[last].wait()
-    cross = copy(conv.at[core, x], conv.at[core, x], sems, (side + 4,), partner)
-    cross.wait()
-    beside_copy = copy(conv.at[core], conv.at[core], sems, (side + 5,), sibling)
-    for c in range(chunks):
-        last_copies[c].wait()
-    beside_copy.wait()
-
-
-def finish(flat, dec, enc, grad):
+    ref[...] = share
+
+
+def enc_bwd_kernel(
+    count, xp, z1, z2, z3, z4, df, u2, u3, u4, b, dec, d_both, t_half, l_rows,
+    d_total, l_total, t_total, early, late, grad_out,
+    m1, m2, m3, s1, s2, s3, s4, yt, pk, dx, got, rows_out,
+    d_slots, d_piece, l_near, l_both, l_slots, l_piece,
+    e_fold, e_sum, e_cross, e_values, e_near, e_both, e_slots, e_piece,
+    f_fold, f_sum, f_cross, f_values, f_near, f_both, f_slots, f_piece,
+    remote, here,
+):
+    place = Place(count)
+    near, core, x = place.near, place.core, place.x
+    sems = Sems(remote, here)
+    place.greet(place.others + [place.near_device] + place.far_devices)
+
+    def home(ref):
+        return rows_of(ref, near, ref.shape[0] // 2)
+
+    def waits(copies):
+        for one in copies:
+            one.wait()
+
+    d_far = far_start(place, sems, d_both, d_slots)
+    l_copy = near_start(place, sems, l_rows, l_near)
+    l_own = sems.here(rows_of(l_rows, near, l_rows.shape[0] // 2), l_both)
+    t_own = sems.here(t_half, home(t_total))
+    t_last = last_start(place, sems, t_half, t_total)
+
+    zero_big(m1, 32)
+    zero_big(m2, 16)
+    zero_big(m3, 8)
+    zero_small(s1, 32, 0)
+    zero_small(s2, 16, 128)
+    zero_small(s3, 8, 128)
+    zero_small(s4, 4, 256)
+    swap = exchange_16()
+    z = z4[...].astype(F32)
+    s = sig(z)
+    s4[1:5, :, 256:1280] = (df[...].astype(F32) * (s * (1.0 + z * (1.0 - s)))).astype(BF)
+
+    def back(z_ref, m, dst, pad):
+        def emit(m0, odd, q, acc):
+            for t in range(acc.shape[0]):
+                h = 2 * (m0 + t) + odd
+                zz = z_ref[h, :, 256 * q : 256 * q + 256].astype(F32)
+                ss = sig(zz)
+                mm = zz * ss
+                dst[h + 1, :, pad + 256 * q : pad + 256 * q + 256] = (
+                    acc[t] * (ss + mm * (1.0 - ss))
+                ).astype(BF)
+                m[m0 + t + odd, 1 - odd, :, 128 + 256 * q : 384 + 256 * q] = mm.astype(BF)
+
+        return emit
+
+    up(s4, u4, 4, 4, back(z3, m3, s3, 128))
+    turn(s4, yt, 4, 256)
+    pack(pk, 0, 1, 128, 256, grad_w(m3, yt, 4), False, swap, True)
+    up(s3, u3, 8, 4, back(z2, m2, s2, 128))
+    turn(s3, yt, 8, 128)
+    pack(pk, 2048, 2, 64, 128, grad_w(m2, yt, 8), False, swap)
+    e_copy = strip_fold_start(place, sems, pk, 0, 2560, e_fold)
+    far_end(place, d_far, d_both, d_slots, d_piece)
+    d_back = back_start(place, sems, d_piece, home(d_total))
+    up(s2, u2, 16, 4, back(z1, m1, s1, 0))
+    e_copy = strip_cross_start(place, sems, e_copy, pk, 0, 2560, e_fold, e_sum, e_cross)
+    l_own.wait()
+    l_copy.wait()
+    l_both[...] = (l_both[...].astype(F32) + l_near[...].astype(F32)).astype(BF)
+    l_far = far_start(place, sems, l_both, l_slots)
+
+    def put(i0, acc):
+        dx[pl.ds(i0, acc.shape[0])] = acc.astype(BF)
+
+    outer_up(s1, b, put)
+    padded_share(e_values, [dec[...], strip_share(place, e_copy, e_sum, e_cross)])
+    e_copy = near_start(place, sems, e_values, e_near)
+    strips = [
+        sems.copy(dx.at[pl.ds(8 * device[1], 8)], got.at[place.me], device)
+        for device in place.others
+    ]
+    got[place.me] = dx[pl.ds(8 * place.me, 8)]
+    turn(s2, yt, 16, 128)
+    pack(pk, 2560, 4, 32, 64, grad_w(m1, yt, 16), False, swap)
+    waits(d_back)
+    d_last = last_start(place, sems, home(d_total), d_total)
+    near_end(place, e_copy, e_values, e_near, e_both)
+    e_far = far_start(place, sems, e_both, e_slots)
+    turn(s1, yt, 32, 0)
+    pack_outer(pk, 2688, outer_grad(xp, yt), False)
+    f_copy = strip_fold_start(place, sems, pk, 2560, 256, f_fold)
+    f_copy = strip_cross_start(place, sems, f_copy, pk, 2560, 256, f_fold, f_sum, f_cross)
+    padded_share(f_values, [strip_share(place, f_copy, f_sum, f_cross)])
+    f_copy = near_start(place, sems, f_values, f_near)
+    far_end(place, l_far, l_both, l_slots, l_piece)
+    l_back = back_start(place, sems, l_piece, home(l_total))
+    far_end(place, e_far, e_both, e_slots, e_piece)
+    e_out = early.at[core, x]
+    e_back = back_start(place, sems, e_piece, home(e_out))
+    near_end(place, f_copy, f_values, f_near, f_both)
+    f_far = far_start(place, sems, f_both, f_slots)
+    far_end(place, f_far, f_both, f_slots, f_piece)
+    f_out = late.at[core, x]
+    f_back = back_start(place, sems, f_piece, home(f_out))
+    waits(strips)
+    stores = []
+    for i in range(8):
+        slot = i % 2
+        if i > 1:
+            stores[i - 2].wait()
+        block = jnp.concatenate([got[(k % 2) * 2 + k // 2, i] for k in range(4)], axis=0)
+        flat = block.T.astype(F32)
+        for p in range(2):
+            for c in range(3):
+                rows_out[slot, c, p] = flat[64 * (3 * p + c) : 64 * (3 * p + c) + 64]
+        stores.append(sems.here(rows_out.at[slot], grad_out.at[:, 2 * i : 2 * i + 2]))
+    waits(stores[-2:])
+    waits(e_back)
+    e_last = last_start(place, sems, home(e_out), e_out)
+    waits(f_back)
+    f_last = last_start(place, sems, home(f_out), f_out)
+    e_last.wait()
+    e_cross_out = sems.copy(e_out, e_out, place.partner)
+    f_last.wait()
+    f_cross_out = sems.copy(f_out, f_out, place.partner)
+    waits(l_back)
+    l_last = last_start(place, sems, home(l_total), l_total)
+    e_cross_out.wait()
+    e_side = sems.copy(early.at[core], early.at[core], place.sibling)
+    f_cross_out.wait()
+    f_side = sems.copy(late.at[core], late.at[core], place.sibling)
+    t_own.wait()
+    waits([t_last, d_last, e_side, f_side, l_last])
+
+
+def share_rows(rows, count):
+    return rows + -rows % (16 * count)
+
+
+def enc_bwd(maps, dec, d_both, t_half, l_rows):
     count = lax.axis_size("rows")
     half = count // 2
-    chunks = 4
-    each = flat.shape[0] // (count * chunks)
-    share = dec.shape[0] // 2
-    conv_each = -(-share // (16 * count)) * 16
-    shape = (chunks, 2, half, each, 256)
     dma = pltpu.SemaphoreType.DMA
-    quarter = dec.shape[0] // 4
-    total, conv, grad_out = pl.pallas_call(
-        functools.partial(finish_kernel, count),
+    any_spec = pl.BlockSpec(memory_space=pl.ANY)
+    head = l_rows.shape[0]
+    quarter = dec.shape[0]
+    early = share_rows(quarter + 640, count)
+    late = share_rows(64, count)
+
+    def steps(rows):
+        return [
+            V((rows, 256)),
+            V((rows // 2, 256)),
+            V((rows // 2, 256)),
+            V((half - 1, rows // count, 256)),
+            V((rows // count, 256)),
+        ]
+
+    d_total, l_total, t_total, e_out, f_out, grad_out = pl.pallas_call(
+        functools.partial(enc_bwd_kernel, count),
         out_shape=(
-            S(shape),
-            S((2, 2, 2, half, conv_each, 256)),
+            S((head, 256)),
+            S((head, 256)),
+            S((2 * t_half.shape[0], 512)),
+            S((2, 2, early, 256)),
+            S((2, 2, late, 256)),
             S((3, 16, 64, 256), F32),
         ),
-        in_specs=VM(4),
-        out_specs=tuple(VM(3)),
+        in_specs=VM(len(maps) + 2) + [any_spec] * 2,
+        out_specs=tuple([any_spec] * 6),
         scratch_shapes=[
+            big(32),
+            big(16),
+            big(8),
+            small(32, 0),
+            small(16, 128),
+            small(8, 128),
+            small(4, 256),
+            V((1024, 32 * NF)),
+            V((2816, 256)),
+            V((32, NF, 384)),
             V((4, 8, NF, 384)),
-            dma((2, 3)),
-            V((chunks, half, each, 256)),
-            V((chunks, half, each, 256)),
-            V((chunks, half - 1, each, 256)),
-            V((2, half, conv_each, 256)),
-            V((half, conv_each, 256)),
-            V((half, conv_each, 256)),
-            V((half - 1, conv_each, 256)),
-            V((2, 2, quarter, 256)),
-            V((2, 2, quarter, 256)),
-            V((2, quarter, 256)),
-            dma((2, 2 * (chunks + 1) + 6)),
-            dma((2, chunks + 1, half - 1)),
-            dma((2, chunks + 1, half - 1)),
+            V((2, 3, 2, 64, 256), F32),
+            *steps(head)[3:],
+            *steps(head)[1:],
+            V((1280, 256)),
+            V((1280, 256)),
+            V((640, 256)),
+            *steps(early),
+            V((128, 256)),
+            V((128, 256)),
+            V((64, 256)),
+            *steps(late),
+            dma((2, 8 * (half - 1) + 20)),
+            dma((16,)),
         ],
         compiler_params=pltpu.CompilerParams(
-            collective_id=2, has_side_effects=True, vmem_limit_bytes=56 * MIB
+            collective_id=2, has_side_effects=True, vmem_limit_bytes=60 * MIB
         ),
-        name="finish",
-    )(
-        flat.reshape(shape),
-        dec.reshape(2, 2, quarter, 256),
-        enc.reshape(2, 2, quarter, 256),
-        grad,
-    )
-    conv = conv.reshape(2, 2, -1, 256)
+        cost_estimate=estimate(110),
+        name="encode_back",
+    )(*maps, dec, d_both, t_half, l_rows)
+    enc = [e_out[:, :, quarter : quarter + 640], f_out[:, :, :64]]
     return (
-        total.reshape(-1, 256),
-        conv[:, :, :quarter].reshape(-1, 256),
-        conv[:, :, quarter : 2 * quarter].reshape(-1, 256),
+        d_total,
+        l_total,
+        t_total,
+        e_out[:, :, :quarter].reshape(-1, 256),
+        jnp.concatenate([part.reshape(-1, 256) for part in enc], axis=0),
         jnp.transpose(grad_out, (3, 0, 1, 2)),
     )
 
@@ -1222,14 +1405,6 @@
     places = jnp.arange(segment_ids.shape[1])
     causal = places[:, None] >= places[None, :]
     return causal[None] & (segment_ids[:, :, None] == segment_ids[:, None, :])
-
-
-def rows_share(flat):
-    return lax.psum_scatter(flat, "rows", scatter_dimension=0, tiled=True)
-
-
-def rows_whole(share):
-    return lax.all_gather(share, "rows", axis=0, tiled=True)
 
 
 def unpack_kernels(flat):
@@ -1283,13 +1458,12 @@
     )
     qkv = jnp.transpose(qkv_weight, (0, 2, 1, 3))
     shards_here = (token_embed, qkv, out_weight, up_weight, down_weight)
-    pixels, enc_f, dec_f, head_in, head_out, theirs = start(
-        frames, kernels, latent_head, decode_head, shards_here
+    pixels, enc_f, dec_f, head_in, head_out, theirs, hints = start(
+        frames, frame_cotangent, kernels, latent_head, decode_head, shards_here
     )
     enc_a, enc_b, enc_t, enc_u = enc_f[0], enc_f[1], enc_f[2:5], enc_f[5:8]
     dec_a, dec_b, dec_t, dec_u = dec_f[0], dec_f[1], dec_f[2:5], dec_f[5:8]
     embed, qkv, project, widen, narrow = zip(shards_here, theirs)
-    hints = frames_in_later(frame_cotangent)
     z1, z2, z3, z4, feat = enc_fwd(pixels, enc_a, *enc_t)
 
     first = 2 * core
@@ -1308,10 +1482,8 @@
         ],
         axis=0,
     )
-    line = 16 * lax.axis_size("rows")
-    tokens, latent, chances, decoded, t_flat, grad_latent, feat_got = middle(
+    tokens, latent, chances, decoded, upper, lower, grad_latent, feat_got = middle(
         layers,
-        line,
         feat,
         *head_in,
         *head_out,
@@ -1325,7 +1497,6 @@
         *widen,
         *narrow,
     )
-    t_share = rows_share(t_flat)
     tokens = jnp.where(
         x == 0, tokens, jnp.concatenate([tokens[NF:], tokens[:NF]], axis=0)
     )
@@ -1336,24 +1507,27 @@
         jnp.concatenate([other_tokens, tokens]),
     )
 
-    recon_pairs, p3, p2, p1 = dec_fwd(decoded, dec_u[2], dec_u[1], dec_u[0], dec_b)
-    recon = frames_out_later(recon_pairs, strip)
-    g_decoded, dec_flat = dec_bwd(hints, decoded, p3, p2, p1, dec_a, *dec_t)
-    g_decoded, t_share = lax.optimization_barrier((g_decoded, t_share))
-    t_total = rows_whole(t_share)
-    g_feat, d_rows, l_rows = latents_back(
-        g_decoded, latent, chances, grad_latent, feat, feat_got, *head_in, *head_out
-    )
-    d_share = rows_share(d_rows)
-
-    d_pairs, enc_flat = enc_bwd(pixels, z1, z2, z3, z4, g_feat, *enc_u, enc_b)
-    d_pairs, t_total, d_share = lax.optimization_barrier((d_pairs, t_total, d_share))
-    d_total = rows_whole(d_share)
-    l_total, dec_total, enc_total, frames_grad = finish(l_rows, dec_flat, enc_flat, d_pairs)
-
-    t_total = t_total.astype(F32)
-    t_layers = t_total[: layers * LAYER_ROWS].reshape(layers, LAYER_ROWS, 512)
-    t_rest = t_total[layers * LAYER_ROWS :]
+    recon_pairs, p3, p2, p1, upper, lower = dec_fwd(
+        decoded, dec_u[2], dec_u[1], dec_u[0], dec_b, upper, lower
+    )
+    recon_parts = blocks_around(recon_pairs, strip)
+    g_decoded, dec_flat, upper, lower = dec_bwd(
+        hints, decoded, p3, p2, p1, dec_a, *dec_t, upper, lower
+    )
+    recon_parts, g_decoded = lax.optimization_barrier((recon_parts, g_decoded))
+    recon = frames_out_later(recon_parts)
+    g_feat, l_rows, dec_share, d_both, upper, lower = latents_back(
+        g_decoded, latent, chances, grad_latent, feat, feat_got, *head_in, *head_out, dec_flat,
+        upper, lower,
+    )
+
+    d_total, l_total, lower, dec_total, enc_total, frames_grad = enc_bwd(
+        (pixels, z1, z2, z3, z4, g_feat, *enc_u, enc_b), dec_share, d_both, lower, l_rows
+    )
+
+    t_layers = jnp.concatenate([lower[:LAYER_ROWS], upper[: LAYER_ROWS * (layers - 1)]], axis=0)
+    t_layers = t_layers.astype(F32).reshape(layers, LAYER_ROWS, 512)
+    t_rest = lower[LAYER_ROWS:].astype(F32)
     r_qkv = t_layers[:, 1152:].reshape(layers, 3, 128, 4, 128).transpose(0, 3, 2, 1, 4)
     r_qkv = r_qkv.reshape(qkv_weight.shape)
     e_one, e_two, e_three, e_four = unpack_kernels(enc_total)

time: 598 us -> 493 us (0.82)
  waiting for transfers between devices: 118 us -> 0.02 us
  Pallas kernels: 393 us -> 431 us
  local copies, waits for them, and re-layouts: 46 us -> 31.3 us
  between operations: 14.6 us -> 1.6 us
    all_gather x2 -> x0, waiting for transfers between devices: 93.3 us -> none  [rows_whole(): return lax.all_gather(share, 'rows', axis=0, tiled=True)]
    pallas_call x4 -> x3, Pallas kernels: 233 us -> 299 us  [the longest x1 152 us: enc_bwd(): pl.pallas_call(functools.partial(enc_bwd_kernel, count), out_shape=(S((he...]
    pallas_call x4 -> x3, Pallas kernels: 132 us -> 103 us  [run(): pl.pallas_call(kernel, out_shape=outs, in_specs=VM(len(args)), out_specs=...]
    ppermute x6, waiting for transfers between devices: 15.7 us -> 0.02 us  [around(): lax.ppermute(parts[k], 'strip', [(s, (s + k) % 4) for s in range(4)])]
    reduce_scatter x2 -> x0, waiting for transfers between devices: 6.96 us -> none  [rows_share(): return lax.psum_scatter(flat, 'rows', scatter_dimension=0, tiled=True)]
  transfers between devices with their start and end apart: 11 -> 7, of which waited for: 7 -> 0; matrix products, arithmetic and copies ran while one was open for 4% -> 1% of each run, Pallas kernels for 19% -> 40%
where the time goes in v4:
time: 493 us; the launch traced here: 486 us
  Pallas kernels  431 us (87%)
  local copies, waits for them, and re-layouts  31.3 us (6%)
  other arithmetic  17.3 us (4%)
    pallas_call x1, Pallas kernels, enc_bwd(): pl.pallas_call(functools.partial(enc_bwd_kernel, count), out_shape=(S((he...  152 us
    pallas_call x3, Pallas kernels, run(): pl.pallas_call(kernel, out_shape=outs, in_specs=VM(len(args)), out_specs=...  103 us
    pallas_call x1, Pallas kernels, middle(): pl.pallas_call(functools.partial(middle_kernel, layers, count), out_shape...  89.9 us
    pallas_call x1, Pallas kernels, latents_back(): pl.pallas_call(functools.partial(back_kernel, count), out_shape=(S(maps),...  56.8 us
    pallas_call x1, Pallas kernels, start(): pl.pallas_call(start_kernel, out_shape=tuple((S(shape) for shape in shape...  27.4 us
  transfers between devices with their start and end apart: 7, of which 0 were waited for; matrix products, arithmetic and copies ran while one was open for 1% of the time, Pallas kernels for 40%

profile of v4, /device:TPU:0, one launch (start us, length us, event | category | flops | bytes accessed | tf_op | source)
XLA Modules:
  0.0 485.6 jit_solution(13594263832328612122)
XLA Ops:
  0.7 2.1 reshape.151.d1
  2.9 1.0 convert_element_type.47.e1
  4.0 1.0 convert_element_type.51.d4
  5.1 27.4 %start.1 = (bf16[34,64,384]{2,1,0:T(8,128)(2,1)}, bf16[1152,1024]{1,0:T(8,128)(2,1)}, bf16[3072,384]{1,0:T(8,128)(2,1)}, bf16[2048,256]{1,0:T(8,128)(2,1)}, bf16...) custom-call(bf16[3,16,64,256]{3,2,1,0:T(8,128)(2,1)} %bitcast.96, ...), custom_call_target="tpu_custom_call" | custom-call | flops 29899999232 | bytes 1048576 | tf_op jit(solution)/shard_map/start/pallas_call | solution.py:586
  33.1 1.7 collective-permute-start.5
  37.0 21.6 %encode.1 = (bf16[32,64,1024]{2,1,0:T(8,128)(2,1)}, bf16[16,64,1024]{2,1,0:T(8,128)(2,1)}, bf16[8,64,1024]{2,1,0:T(8,128)(2,1)}, bf16[4,64,1024]{2,1,0:T(8,128)(2,1)}, bf16[4,64,1024]{2,1,0:T(8,128)(2,1)}) custom-call(bf16[34,64,384]{2,1,0:T(8,128)(2,1)} %get-tuple-element.90.xp, bf16[1152,1024]{1,0:T(8,128)(2,1)} %get-tuple-element.91.a, ...), custom_call_target="tpu_custom_call" | custom-call | flops 25300000768 | bytes 1048576 | tf_op jit(solution)/shard_map/encode/pallas_call | solution.py:235
  58.6 89.9 %middle.1 = (bf16[128,512]{1,0:T(8,128)(2,1)}, bf16[128,512]{1,0:T(8,128)(2,1)}, f32[128,512]{1,0:T(8,128)}, bf16[4,64,1024]{2,1,0:T(8,128)(2,1)}, bf16[768,512]...) custom-call(bf16[4,64,1024]{2,1,0:T(8,128)(2,1)} %get-tuple-element.95.feat.feat0, ...), custom_call_target="tpu_custom_call" | custom-call | flops 96599998464 | bytes 1048576 | tf_op jit(solution)/shard_map/middle/pallas_call | solution.py:961
  148.6 0.9 fusion.4
  149.4 0.9 maximum_select_fusion.1
  150.5 35.6 %decode.1 = (bf16[32,64,384]{2,1,0:T(8,128)(2,1)}, bf16[8,64,1024]{2,1,0:T(8,128)(2,1)}, bf16[16,64,1024]{2,1,0:T(8,128)(2,1)}, bf16[32,64,1024]{2,1,0:T(8,128)(...) custom-call(bf16[4,64,1024]{2,1,0:T(8,128)(2,1)} %get-tuple-element.106.dec, ...), custom_call_target="tpu_custom_call" | custom-call | flops 27599998976 | bytes 1048576 | tf_op jit(solution)/shard_map/decode/pallas_call | solution.py:235
  186.1 1.5 constant_dynamic-slice_fusion
  188.6 1.6 collective-permute-start.3
  190.3 45.5 %decode_back.1 = (bf16[4,64,1024]{2,1,0:T(8,128)(2,1)}, bf16[2816,256]{1,0:T(8,128)(2,1)}, bf16[768,512]{1,0:T(8,128)(2,1)}, bf16[240,512]{1,0:T(8,128)(2,1)}) custom-call(bf16[8,64,384]{2,1,0:T(8,128)(2,1)} %get-tuple-element.114.c0, bf16[8,64,384]{2,1,0:T(8,128)(2,1)} %collective-permute-done.4.c1, bf16[8,64,384]{2,1,0:T(8,128)(2,1)} %collective-permute-done.5.c2, ...), custom_call_target="tpu_custom_call" | custom-call | flops 48299999232 | bytes 1048576 | tf_op jit(solution)/shard_map/decode_back/pallas_call | solution.py:235
  235.8 56.8 %latents_back.1 = (bf16[4,64,1024]{2,1,0:T(8,128)(2,1)}, bf16[4096,256]{1,0:T(8,128)(2,1)}, bf16[704,256]{1,0:T(8,128)(2,1)}, bf16[2048,256]{1,0:T(8,128)(2,1)},...) custom-call(bf16[4,64,1024]{2,1,0:T(8,128)(2,1)} %get-tuple-element.136.grad, ...), custom_call_target="tpu_custom_call" | custom-call | flops 57500000256 | bytes 1048576 | tf_op jit(solution)/shard_map/latents_back/pallas_call | solution.py:1120
  292.6 152.3 %encode_back.1 = (bf16[4096,256]{1,0:T(8,128)(2,1)}, bf16[4096,256]{1,0:T(8,128)(2,1)}, bf16[1920,512]{1,0:T(8,128)(2,1)}, bf16[2,2,1408,256]{3,2,1,0:T(8,128)(2...) custom-call(bf16[34,64,384]{2,1,0:T(8,128)(2,1)} %get-tuple-element.90.xp, ...), custom_call_target="tpu_custom_call" | custom-call | flops 126500003840 | bytes 1048576 | tf_op jit(solution)/shard_map/encode_back/pallas_call | solution.py:1345
  444.9 1.5 slice.126
  448.6 1.2 copy-done.9
  450.2 2.6 fusion.1
  453.7 1.4 slice.106
  455.1 0.9 copy-done.20
  456.0 1.5 maximum_convert_fusion
  460.3 0.9 slice.137
  461.9 1.6 reshape.163
  463.5 2.9 copy.43
  466.4 1.6 reshape.168
  468.1 2.0 convert_bitcast_fusion
  470.1 2.6 copy.45
  472.7 2.3 convert_element_type.54
  475.7 1.9 pad_maximum_fusion.4
  477.6 1.5 pad_maximum_fusion.1
  481.4 2.1 turn_back.1
  483.5 1.7 copy.47
  (96 shorter events, 13.8 us)
Async XLA Ops:
  0.7 2.2 copy-start.21
  0.7 3.3 copy-start.22
  5.1 29.8 %copy-start.24 = (s32[4,64]{1,0:T(4,128)S(1)}, s32[4,64]{1,0:T(4,128)}, u32[]{:S(2)}) copy-start(s32[4,64]{1,0:T(4,128)} %param.22) | copy-start | bytes 3076
  5.1 30.0 %copy-start.23 = (f32[2,2,512]{2,1,0:T(2,128)S(1)}, f32[2,2,512]{2,1,0:T(2,128)}, u32[]{:S(2)}) copy-start(f32[2,2,512]{2,1,0:T(2,128)} %param.30) | copy-start | bytes 24580
  5.1 31.3 %copy-start.19 = (bf16[256,512]{1,0:T(8,128)(2,1)S(1)}, bf16[256,512]{1,0:T(8,128)(2,1)}, u32[]{:S(2)}) copy-start(bf16[256,512]{1,0:T(8,128)(2,1)} %param.40) | copy-start | bytes 786436
  32.5 156.1 %collective-permute-start.4 = (bf16[8,64,384]{2,1,0:T(8,128)(2,1)}, bf16[8,64,384]{2,1,0:T(8,128)(2,1)}, u32[]{:S(2)}, u32[]{:S(2)}) collective-permute-start(bf16[8,64,384]{2,1,0:T(8,128)(2,1)} %get-tuple-element.115), channel_id=1, source_target_pairs={{0,1},{1,2},{2,3},{3,0},{4,5},{5,6},{6,7},{7,4},{8,9},{9,10},{10,1... | collective-permute-start | bytes 1179656 | tf_op jit(solution)/shard_map/ppermute | solution.py:638
  33.1 157.1 %collective-permute-start.5 = (bf16[8,64,384]{2,1,0:T(8,128)(2,1)}, bf16[8,64,384]{2,1,0:T(8,128)(2,1)}, u32[]{:S(2)}, u32[]{:S(2)}) collective-permute-start(bf16[8,64,384]{2,1,0:T(8,128)(2,1)} %get-tuple-element.116), channel_id=1, source_target_pairs={{0,2},{1,3},{2,0},{3,1},{4,6},{5,7},{6,4},{7,5},{8,10},{9,11},{10,... | collective-permute-start | bytes 1179656 | tf_op jit(solution)/shard_map/ppermute | solution.py:638
  34.8 155.4 %collective-permute-start.6 = (bf16[8,64,384]{2,1,0:T(8,128)(2,1)}, bf16[8,64,384]{2,1,0:T(8,128)(2,1)}, u32[]{:S(2)}, u32[]{:S(2)}) collective-permute-start(bf16[8,64,384]{2,1,0:T(8,128)(2,1)} %get-tuple-element.117), channel_id=1, source_target_pairs={{0,3},{1,0},{2,1},{3,2},{4,7},{5,4},{6,5},{7,6},{8,11},{9,8},{10,9... | collective-permute-start | bytes 1179656 | tf_op jit(solution)/shard_map/ppermute | solution.py:638
  150.4 37.4 %collective-permute-start = (bf16[128,512]{1,0:T(8,128)(2,1)S(1)}, bf16[128,512]{1,0:T(8,128)(2,1)S(1)}, u32[]{:S(2)}, u32[]{:S(2)}) collective-permute-start(bf16[128,512]{1,0:T(8,128)(2,1)S(1)} %maximum_select_fusion.1), channel_id=1, source_target_pairs={{0,1},{1,0},{2,3},{3,2},{4,5},{5,4},{6,7},{7,6},{8,9},{9,8},{10,11... | collective-permute-start | bytes 393224 | tf_op jit(solution)/shard_map/ppermute | solution.py:1401
  187.7 48.1 %collective-permute-start.1 = (bf16[8,64,384]{2,1,0:T(8,128)(2,1)S(1)}, bf16[8,64,384]{2,1,0:T(8,128)(2,1)S(1)}, u32[]{:S(2)}, u32[]{:S(2)}) collective-permute-start(bf16[8,64,384]{2,1,0:T(8,128)(2,1)S(1)} %get-tuple-element.170), channel_id=1, source_target_pairs={{0,1},{1,2},{2,3},{3,0},{4,5},{5,6},{6,7},{7,4},{8,9},{9,10},{10,1... | collective-permute-start | bytes 1179656 | tf_op jit(solution)/shard_map/ppermute | solution.py:638
  187.8 48.0 %collective-permute-start.2 = (bf16[8,64,384]{2,1,0:T(8,128)(2,1)S(1)}, bf16[8,64,384]{2,1,0:T(8,128)(2,1)S(1)}, u32[]{:S(2)}, u32[]{:S(2)}) collective-permute-start(bf16[8,64,384]{2,1,0:T(8,128)(2,1)S(1)} %get-tuple-element.169), channel_id=1, source_target_pairs={{0,2},{1,3},{2,0},{3,1},{4,6},{5,7},{6,4},{7,5},{8,10},{9,11},{10,... | collective-permute-start | bytes 1179656 | tf_op jit(solution)/shard_map/ppermute | solution.py:638
  188.6 47.2 %collective-permute-start.3 = (bf16[8,64,384]{2,1,0:T(8,128)(2,1)S(1)}, bf16[8,64,384]{2,1,0:T(8,128)(2,1)S(1)}, u32[]{:S(2)}, u32[]{:S(2)}) collective-permute-start(bf16[8,64,384]{2,1,0:T(8,128)(2,1)S(1)} %get-tuple-element.168), channel_id=1, source_target_pairs={{0,3},{1,0},{2,1},{3,2},{4,7},{5,4},{6,5},{7,6},{8,11},{9,8},{10,9... | collective-permute-start | bytes 1179656 | tf_op jit(solution)/shard_map/ppermute | solution.py:638
  235.8 56.8 %copy-start = (bf16[8,64,384]{2,1,0:T(8,128)(2,1)}, bf16[8,64,384]{2,1,0:T(8,128)(2,1)S(1)}, u32[]{:S(2)}) copy-start(bf16[8,64,384]{2,1,0:T(8,128)(2,1)S(1)} %collective-permute-done.2.c2) | copy-start | bytes 1179652
  446.4 2.1 copy-start.8
  446.7 12.9 %copy-start.2 = (f32[2816,256]{1,0:T(8,128)}, f32[2816,256]{1,0:T(8,128)S(1)}, u32[]{:S(2)}) copy-start(f32[2816,256]{1,0:T(8,128)S(1)} %bitcast_convert_fusion) | copy-start | bytes 8650756
  447.5 2.3 copy-start.9
  460.3 1.6 copy-start.6
  463.5 2.9 slice-start
  470.1 2.6 copy-start.7
  472.7 2.4 slice-start.1
  472.7 4.8 copy-start.3
  472.7 4.8 copy-start.4
  477.5 2.4 copy-start.11
  477.5 2.4 copy-start.12
  477.5 2.4 copy-start.13
  477.6 2.3 copy-start.14
  477.6 3.1 copy-start.15
  477.6 3.1 copy-start.16
  477.6 3.1 copy-start.17
  477.6 3.0 copy-start.18
  479.1 2.3 copy-start.1
  481.4 2.1 copy-start.5
  (2 other events, 2.5 us)

commit v5 on v4

--- a/solution.py
+++ b/solution.py
@@ -292,6 +292,7 @@
         self.remote, self.local, self.used, self.used_here = remote, local, 0, 0
 
     def copy(self, src, dst, device):
+        assert self.used < self.remote.shape[1]
         one = pltpu.make_async_remote_copy(
             src_ref=src,
             dst_ref=dst,
@@ -305,6 +306,7 @@
         return one
 
     def here(self, src, dst):
+        assert self.used_here < self.local.shape[0]
         one = pltpu.make_async_copy(src, dst, self.local.at[self.used_here])
         self.used_here = self.used_here + 1
         one.start()
@@ -343,6 +345,24 @@
 def back_start(place, sems, piece, home):
     out = rows_of(home, place.far, piece.shape[0])
     return [sems.here(piece, out)] + [sems.copy(piece, out, d) for d in place.far_devices]
+
+
+def back_part(place, sems, piece, home, part):
+    size = piece.shape[0] // 2
+    src = piece.at[pl.ds(part * size, size)]
+    first = place.far * piece.shape[0] + part * size
+    out = home.at[pl.ds(pl.multiple_of(first, 16), size)]
+    return [sems.here(src, out)] + [sems.copy(src, out, d) for d in place.far_devices]
+
+
+def last_part(place, sems, home, each, part):
+    size = each // 2
+    refs = [home.at[pl.ds(each * k + part * size, size)] for k in range(place.half)]
+    return [sems.copy(ref, ref, place.near_device) for ref in refs]
+
+
+def half_lanes(place, w):
+    return pl.ds(pl.multiple_of(256 * w + 128 * (1 - place.near), 128), 128)
 
 
 def last_start(place, sems, home, out):
@@ -728,6 +748,7 @@
     feat, lh0, lh1, dh0, dh1, emb0, emb1, pos, gains, allow, cot,
     qkv0, qkv1, proj0, proj1, up0, up1, down0, down1,
     tokens, latent_out, chances_out, decoded, upper_both, lower, grad_latent, feat_got,
+    latent_near, feat_near, got_near,
     feat_sems, keep, send, sent, spread_sems, parts, gots, pair_sems,
     upper, upper_other, upper_got, lower_other, lower_got, upper_near, fold_sems, near_sems, unit_a, unit_f, normed_a, normed_f, mixed, weights,
     attended, before, inner, gain_rows,
@@ -773,12 +794,23 @@
 
     mine = logits_of(feat)
     feat_copy.wait()
+    near_sends = Sems(near_sems, None)
+    near_copies = [
+        near_sends.copy(
+            src.at[:, :, half_lanes(place_here, w)],
+            dst.at[:, :, 128 * w : 128 * w + 128],
+            place_here.near_device,
+        )
+        for src, dst in ((feat, feat_near), (feat_got, got_near))
+        for w in range(4)
+    ]
     logits = jnp.concatenate([mine, logits_of(feat_got)], axis=0)
     raised = jnp.exp(logits - over_groups(logits, jnp.maximum))
     chances = raised / over_groups(raised, jnp.add)
     latent = chances.astype(BF)
     chances_out[...] = chances
     latent_out[...] = latent
+    near_copies.append(near_sends.copy(latent_out, latent_near, place_here.near_device))
 
     waiting = total_start(0, dot(latent[:, :256], emb0[...]) + dot(latent[:, 256:], emb1[...]))
     for hw in range(16):
@@ -879,7 +911,7 @@
             dst[base + 512 : base + 1024] = dot(turned, grads[side]).astype(BF)
         if k == 0:
             fold_end(upper_fold, upper, upper_got, LAYER_ROWS * (layers - 1))
-            near_copy = near_start(place_here, Sems(near_sems, None), upper, upper_near)
+            near_copy = near_start(place_here, near_sends, upper, upper_near)
         grad_normed = total_wait(index, waiting)
         gain_f, grad_rows = unit_back(
             grad_normed, unit_f[k, :, :512], unit_f[k, :, 512:513], gains[2 * k + 1 : 2 * k + 2]
@@ -950,6 +982,8 @@
     grad_latent[:, 256:] = dot_nt(low, emb1[...])
     near_end(place_here, near_copy, upper, upper_near, upper_both)
     fold_end(lower_fold, lower, lower_got, lower_rows)
+    for one in near_copies:
+        one.wait()
 
 
 def middle(layers, *args):
@@ -969,9 +1003,12 @@
             S((lower, 512)),
             S((t, 512), F32),
             S((4, NF, 1024)),
+            S((t, 512)),
+            S((4, NF, 512)),
+            S((4, NF, 512)),
         ),
         in_specs=VM(len(args)),
-        out_specs=tuple(VM(8)),
+        out_specs=tuple(VM(11)),
         scratch_shapes=[
             dma((2, 1)),
             V((4, NF, 1024)),
@@ -988,7 +1025,7 @@
             V((lower, 512)),
             V((upper // 2, 512)),
             dma((2, 2)),
-            dma((2, 1)),
+            dma((2, 10)),
             V((layers, t, 640), F32),
             V((layers, t, 640), F32),
             V((layers, t, 512)),
@@ -1009,34 +1046,31 @@
 
 
 def back_kernel(
-    count, grad, latent, chances, grad_embed, feat0, feat1, lh0, lh1, dh0, dh1, flat, upper_half, lower_piece,
-    grad_feat, in_rows, share, d_both, upper_total, lower_half,
-    side_got, side_sum, cross_got, side_sems, got, got_sems, keep, send, sent, sent_sems,
-    own, other, other_got, fold_sems, values, from_near, remote, here,
+    count, grad, latent, latent_near, chances, grad_embed, feat0, feat1, feat2, feat3,
+    lh0, lh1, dh0, dh1, flat, upper_half, lower_piece,
+    grad_feat, share, d_piece, l_both, upper_total, lower_half,
+    got, got_near, got_cross, keep, send, sent, logits_here, logits_near, own, other, other_got,
+    d_both, d_slots, side_got, side_sum, cross_got, remote, here,
 ):
     place = Place(count)
     near, core, x = place.near, place.core, place.x
-    partner, sibling = place.partner, place.sibling
-    place.greet([partner, sibling, place.near_device] + place.far_devices)
+    cross_device = (place.near_device[0], place.partner[1])
+    place.greet(
+        [place.partner, place.sibling, place.near_device, cross_device] + place.far_devices
+    )
     sems = Sems(remote, here)
-
-    def copy(src, dst, pair, index, device):
-        one = pltpu.make_async_remote_copy(
-            src_ref=src,
-            dst_ref=dst,
-            send_sem=pair.at[(0,) + index],
-            recv_sem=pair.at[(1,) + index],
-            device_id=device,
-            device_id_type=MESH,
-        )
-        one.start()
-        return one
-
-    grad_copy = copy(grad, got, got_sems, (0,), partner)
+    grad_copies = [sems.copy(grad, got, place.partner)]
+    for device, dst in ((place.near_device, got_near), (cross_device, got_cross)):
+        for w in range(4):
+            grad_copies.append(
+                sems.copy(
+                    grad.at[:, :, half_lanes(place, w)], dst.at[:, :, 128 * w : 128 * w + 128], device
+                )
+            )
     upper_own = sems.here(upper_half, rows_of(upper_total, near, upper_half.shape[0]))
     upper_last = last_start(place, sems, upper_half, upper_total)
     lower_back = back_start(place, sems, lower_piece, lower_half)
-    side_copy = copy(flat.at[1 - core], side_got, side_sems, (0,), sibling)
+    side_copy = sems.copy(flat.at[1 - core], side_got, place.sibling)
 
     def through(maps):
         halves = []
@@ -1047,23 +1081,24 @@
             halves.append(total)
         return jnp.concatenate(halves, axis=1)
 
-    def head_grad(slot, first, second, rhs):
+    def head_grad(slot, wide, narrow, rhs):
         for h in range(4):
             for w in range(4):
-                lanes = slice(256 * w, 256 * w + 256)
-                rows = slice(1024 * h + 256 * w, 1024 * h + 256 * w + 256)
-                maps = jnp.concatenate([first[h, :, lanes], second[h, :, lanes]], axis=0)
-                value = dot(maps.T, rhs).astype(BF)
+                lanes = pl.ds(pl.multiple_of(256 * w + 128 * near, 128), 128)
+                maps = [ref[h, :, lanes] for ref in wide]
+                maps = maps + [ref[h, :, 128 * w : 128 * w + 128] for ref in narrow]
+                rows = slice(512 * h + 128 * w, 512 * h + 128 * w + 128)
+                value = dot(jnp.concatenate(maps, axis=0).T, rhs).astype(BF)
                 own[slot, rows] = value[:, :256]
                 other[slot, rows] = value[:, 256:]
-        return copy(other.at[slot], other_got.at[slot], fold_sems, (slot,), sibling)
+        return sems.copy(other.at[slot], other_got.at[slot], place.sibling)
 
     swap = exchange_16()
 
     def folded(slot, b):
         parts = []
         for k in range(16):
-            rows = slice(256 * k + 16 * b, 256 * k + 16 * b + 16)
+            rows = slice(128 * k + 16 * b, 128 * k + 16 * b + 16)
             value = own[slot, rows].astype(F32) + other_got[slot, rows].astype(F32)
             parts.append(value.astype(BF))
         return dot(swap, jnp.concatenate(parts, axis=0)).astype(BF)
@@ -1071,13 +1106,24 @@
     mine = through(grad)
     side_copy.wait()
     side_sum[...] = (flat[core].astype(F32) + side_got[...].astype(F32)).astype(BF)
-    cross_copy = copy(side_sum.at[1 - x], cross_got, side_sems, (1,), partner)
-    grad_copy.wait()
-    out_fold = head_grad(0, grad, got, latent[...])
+    for one in grad_copies:
+        one.wait()
+    cross_copy = sems.copy(side_sum.at[1 - x], cross_got, place.partner)
+    both_latents = jnp.concatenate([latent[...], latent_near[...]], axis=0)
+    out_fold = head_grad(0, (grad, got), (got_near, got_cross), both_latents)
     grad_latent = grad_embed[...] + jnp.concatenate([mine, through(got)], axis=0)
     probs = chances[...]
     along = over_groups(probs * grad_latent, jnp.add)
     grad_logits = (probs * (grad_latent - along)).astype(BF)
+    logits_here[...] = grad_logits
+    logits_copy = sems.copy(logits_here, logits_near, place.near_device)
+    out_fold.wait()
+    for b in range(8):
+        d_both[256 * b : 256 * b + 256] = folded(0, b).T
+    d_far = far_start(place, sems, d_both, d_slots)
+    logits_copy.wait()
+    both_logits = jnp.concatenate([grad_logits, logits_near[...]], axis=0)
+    in_fold = head_grad(1, (feat0, feat1), (feat2, feat3), both_logits)
     sends = []
     for h in range(4):
         for w in range(4):
@@ -1087,25 +1133,18 @@
             value = value.astype(BF)
             keep[h, :, lanes] = value[:NF]
             send[h, :, lanes] = value[NF:]
-        sends.append(copy(send.at[h], sent.at[h], sent_sems, (h,), partner))
-    out_fold.wait()
-    for b in range(16):
-        values[256 * b : 256 * b + 256] = folded(0, b).T
-    near_copy = near_start(place, sems, values, from_near)
-    in_fold = head_grad(1, feat0, feat1, grad_logits)
+        sends.append(sems.copy(send.at[h], sent.at[h], place.partner))
+    in_fold.wait()
+    for b in range(8):
+        l_both[256 * b : 256 * b + 256] = folded(1, b)
     cross_copy.wait()
     share[...] = (side_sum[x].astype(F32) + cross_got[...].astype(F32)).astype(BF)
-    for one in sends:
+    upper_own.wait()
+    upper_last.wait()
+    for one in lower_back + sends:
         one.wait()
     grad_feat[...] = (keep[...].astype(F32) + sent[...].astype(F32)).astype(BF)
-    in_fold.wait()
-    for b in range(16):
-        in_rows[256 * b : 256 * b + 256] = folded(1, b)
-    near_end(place, near_copy, values, from_near, d_both)
-    upper_own.wait()
-    upper_last.wait()
-    for one in lower_back:
-        one.wait()
+    far_end(place, d_far, d_both, d_slots, d_piece)
 
 
 def latents_back(*args):
@@ -1116,43 +1155,44 @@
     quarter = flat.shape[0] // 4
     args = args[:-3] + (flat.reshape(2, 2, quarter, 256), upper_half, lower_piece)
     maps = (4, NF, 1024)
-    rows = (4096, 256)
+    narrow = (4, NF, 512)
+    rows = (2048, 256)
     return pl.pallas_call(
         functools.partial(back_kernel, count),
         out_shape=(
             S(maps),
+            S((quarter, 256)),
+            S((4096 // count, 256)),
             S(rows),
-            S((quarter, 256)),
-            S((2048, 256)),
             S((2 * upper_half.shape[0], 512)),
             S((half * lower_piece.shape[0], 512)),
         ),
         in_specs=VM(len(args)),
         out_specs=tuple(VM(4) + [pl.BlockSpec(memory_space=pl.ANY)] + VM(1)),
         scratch_shapes=[
+            V(maps),
+            V(narrow),
+            V(narrow),
+            V(maps),
+            V(maps),
+            V(maps),
+            V((2 * NF, 512)),
+            V((2 * NF, 512)),
+            V((2,) + rows),
+            V((2,) + rows),
+            V((2,) + rows),
+            V(rows),
+            V((half - 1, 4096 // count, 256)),
             V((2, quarter, 256)),
             V((2, quarter, 256)),
             V((quarter, 256)),
-            dma((2, 2)),
-            V(maps),
-            dma((2, 1)),
-            V(maps),
-            V(maps),
-            V(maps),
-            dma((2, 4)),
-            V((2,) + rows),
-            V((2,) + rows),
-            V((2,) + rows),
-            dma((2, 2)),
-            V(rows),
-            V((2048, 256)),
-            dma((2, half + 1)),
+            dma((2, 2 * half + 20)),
             dma((2,)),
         ],
         compiler_params=pltpu.CompilerParams(
             collective_id=4, has_side_effects=True, vmem_limit_bytes=58 * MIB
         ),
-        cost_estimate=estimate(50),
+        cost_estimate=estimate(55),
         name="latents_back",
     )(*args)
 
@@ -1187,18 +1227,21 @@
 
 
 def enc_bwd_kernel(
-    count, xp, z1, z2, z3, z4, df, u2, u3, u4, b, dec, d_both, t_half, l_rows,
+    count, xp, z1, z2, z3, z4, df, u2, u3, u4, b, dec, d_piece, l_both, t_half,
     d_total, l_total, t_total, early, late, grad_out,
     m1, m2, m3, s1, s2, s3, s4, yt, pk, dx, got, rows_out,
-    d_slots, d_piece, l_near, l_both, l_slots, l_piece,
+    l_slots, l_piece,
     e_fold, e_sum, e_cross, e_values, e_near, e_both, e_slots, e_piece,
-    f_fold, f_sum, f_cross, f_values, f_near, f_both, f_slots, f_piece,
+    f_fold, f_sum, f_cross, f_values, f_slots, f_piece,
     remote, here,
 ):
     place = Place(count)
     near, core, x = place.near, place.core, place.x
     sems = Sems(remote, here)
-    place.greet(place.others + [place.near_device] + place.far_devices)
+    row_places = [lax.rem(place.row + k, count) for k in range(1, count)]
+    row_devices = [(at, place.me) for at in row_places]
+    cross_device = (place.near_device[0], place.partner[1])
+    place.greet(place.others + row_devices + [cross_device])
 
     def home(ref):
         return rows_of(ref, near, ref.shape[0] // 2)
@@ -1207,9 +1250,7 @@
         for one in copies:
             one.wait()
 
-    d_far = far_start(place, sems, d_both, d_slots)
-    l_copy = near_start(place, sems, l_rows, l_near)
-    l_own = sems.here(rows_of(l_rows, near, l_rows.shape[0] // 2), l_both)
+    l_far = far_start(place, sems, l_both, l_slots)
     t_own = sems.here(t_half, home(t_total))
     t_last = last_start(place, sems, t_half, t_total)
 
@@ -1246,89 +1287,99 @@
     turn(s3, yt, 8, 128)
     pack(pk, 2048, 2, 64, 128, grad_w(m2, yt, 8), False, swap)
     e_copy = strip_fold_start(place, sems, pk, 0, 2560, e_fold)
-    far_end(place, d_far, d_both, d_slots, d_piece)
-    d_back = back_start(place, sems, d_piece, home(d_total))
+    far_end(place, l_far, l_both, l_slots, l_piece)
+    l_back = [back_part(place, sems, l_piece, home(l_total), part) for part in range(2)]
+    e_copy = strip_cross_start(place, sems, e_copy, pk, 0, 2560, e_fold, e_sum, e_cross)
     up(s2, u2, 16, 4, back(z1, m1, s1, 0))
-    e_copy = strip_cross_start(place, sems, e_copy, pk, 0, 2560, e_fold, e_sum, e_cross)
-    l_own.wait()
-    l_copy.wait()
-    l_both[...] = (l_both[...].astype(F32) + l_near[...].astype(F32)).astype(BF)
-    l_far = far_start(place, sems, l_both, l_slots)
+    padded_share(e_values, [dec[...], strip_share(place, e_copy, e_sum, e_cross)])
+    e_copy = near_start(place, sems, e_values, e_near)
 
     def put(i0, acc):
         dx[pl.ds(i0, acc.shape[0])] = acc.astype(BF)
 
     outer_up(s1, b, put)
-    padded_share(e_values, [dec[...], strip_share(place, e_copy, e_sum, e_cross)])
-    e_copy = near_start(place, sems, e_values, e_near)
     strips = [
         sems.copy(dx.at[pl.ds(8 * device[1], 8)], got.at[place.me], device)
         for device in place.others
     ]
     got[place.me] = dx[pl.ds(8 * place.me, 8)]
+    near_end(place, e_copy, e_values, e_near, e_both)
+    e_far = far_start(place, sems, e_both, e_slots)
+    waits(l_back[0])
+    l_last = last_part(place, sems, home(l_total), l_piece.shape[0], 0)
     turn(s2, yt, 16, 128)
     pack(pk, 2560, 4, 32, 64, grad_w(m1, yt, 16), False, swap)
-    waits(d_back)
-    d_last = last_start(place, sems, home(d_total), d_total)
-    near_end(place, e_copy, e_values, e_near, e_both)
-    e_far = far_start(place, sems, e_both, e_slots)
+    far_end(place, e_far, e_both, e_slots, e_piece)
+    e_out = early.at[core, x]
+    e_back = back_start(place, sems, e_piece, home(e_out))
+    waits(l_back[1])
+    l_last = l_last + last_part(place, sems, home(l_total), l_piece.shape[0], 1)
+    d_back = [back_part(place, sems, d_piece, home(d_total), part) for part in range(2)]
     turn(s1, yt, 32, 0)
     pack_outer(pk, 2688, outer_grad(xp, yt), False)
     f_copy = strip_fold_start(place, sems, pk, 2560, 256, f_fold)
+    waits(e_back)
+    e_last = [
+        sems.copy(home(e_out), home(e_out), device)
+        for device in (place.near_device, place.partner, cross_device)
+    ]
     f_copy = strip_cross_start(place, sems, f_copy, pk, 2560, 256, f_fold, f_sum, f_cross)
-    padded_share(f_values, [strip_share(place, f_copy, f_sum, f_cross)])
-    f_copy = near_start(place, sems, f_values, f_near)
-    far_end(place, l_far, l_both, l_slots, l_piece)
-    l_back = back_start(place, sems, l_piece, home(l_total))
-    far_end(place, e_far, e_both, e_slots, e_piece)
-    e_out = early.at[core, x]
-    e_back = back_start(place, sems, e_piece, home(e_out))
-    near_end(place, f_copy, f_values, f_near, f_both)
-    f_far = far_start(place, sems, f_both, f_slots)
-    far_end(place, f_far, f_both, f_slots, f_piece)
-    f_out = late.at[core, x]
-    f_back = back_start(place, sems, f_piece, home(f_out))
     waits(strips)
     stores = []
-    for i in range(8):
-        slot = i % 2
-        if i > 1:
-            stores[i - 2].wait()
-        block = jnp.concatenate([got[(k % 2) * 2 + k // 2, i] for k in range(4)], axis=0)
-        flat = block.T.astype(F32)
-        for p in range(2):
-            for c in range(3):
-                rows_out[slot, c, p] = flat[64 * (3 * p + c) : 64 * (3 * p + c) + 64]
-        stores.append(sems.here(rows_out.at[slot], grad_out.at[:, 2 * i : 2 * i + 2]))
-    waits(stores[-2:])
-    waits(e_back)
-    e_last = last_start(place, sems, home(e_out), e_out)
+
+    def turn_out(first, count_here):
+        for i in range(first, first + count_here):
+            slot = i % 2
+            if i > 1:
+                stores[i - 2].wait()
+            block = jnp.concatenate([got[(k % 2) * 2 + k // 2, i] for k in range(4)], axis=0)
+            flat = block.T.astype(F32)
+            for p in range(2):
+                for c in range(3):
+                    rows_out[slot, c, p] = flat[64 * (3 * p + c) : 64 * (3 * p + c) + 64]
+            stores.append(sems.here(rows_out.at[slot], grad_out.at[:, 2 * i : 2 * i + 2]))
+
+    turn_out(0, 4)
+    waits(d_back[0])
+    d_last = last_part(place, sems, home(d_total), d_piece.shape[0], 0)
+    padded_share(f_values, [strip_share(place, f_copy, f_sum, f_cross)])
+    each = f_piece.shape[0]
+    f_rows = [
+        sems.copy(rows_of(f_values, at, each), f_slots.at[k], device)
+        for k, (at, device) in enumerate(zip(row_places, row_devices))
+    ]
+    turn_out(4, 4)
+    waits(f_rows)
+    whole = rows_of(f_values, place.row, each)[...].astype(F32)
+    for k in range(count - 1):
+        whole = whole + f_slots[k].astype(F32)
+    f_piece[...] = whole.astype(BF)
+    f_out = rows_of(late.at[core, x], place.row, each)
+    f_back = [sems.here(f_piece, f_out)]
+    f_back = f_back + [sems.copy(f_piece, f_out, device) for device in row_devices]
+    waits(d_back[1])
+    d_last = d_last + last_part(place, sems, home(d_total), d_piece.shape[0], 1)
+    waits(e_last)
+    e_side = sems.copy(early.at[core], early.at[core], place.sibling)
     waits(f_back)
-    f_last = last_start(place, sems, home(f_out), f_out)
-    e_last.wait()
-    e_cross_out = sems.copy(e_out, e_out, place.partner)
-    f_last.wait()
-    f_cross_out = sems.copy(f_out, f_out, place.partner)
-    waits(l_back)
-    l_last = last_start(place, sems, home(l_total), l_total)
-    e_cross_out.wait()
-    e_side = sems.copy(early.at[core], early.at[core], place.sibling)
+    f_cross_out = sems.copy(late.at[core, x], late.at[core, x], place.partner)
     f_cross_out.wait()
     f_side = sems.copy(late.at[core], late.at[core], place.sibling)
+    waits(stores[-2:])
     t_own.wait()
-    waits([t_last, d_last, e_side, f_side, l_last])
+    waits([t_last, e_side, f_side] + d_last + l_last)
 
 
 def share_rows(rows, count):
     return rows + -rows % (16 * count)
 
 
-def enc_bwd(maps, dec, d_both, t_half, l_rows):
+def enc_bwd(maps, dec, d_piece, l_both, t_half):
     count = lax.axis_size("rows")
     half = count // 2
     dma = pltpu.SemaphoreType.DMA
     any_spec = pl.BlockSpec(memory_space=pl.ANY)
-    head = l_rows.shape[0]
+    head = 2 * l_both.shape[0]
     quarter = dec.shape[0]
     early = share_rows(quarter + 640, count)
     late = share_rows(64, count)
@@ -1352,7 +1403,7 @@
             S((2, 2, late, 256)),
             S((3, 16, 64, 256), F32),
         ),
-        in_specs=VM(len(maps) + 2) + [any_spec] * 2,
+        in_specs=VM(len(maps) + 4),
         out_specs=tuple([any_spec] * 6),
         scratch_shapes=[
             big(32),
@@ -1368,7 +1419,6 @@
             V((4, 8, NF, 384)),
             V((2, 3, 2, 64, 256), F32),
             *steps(head)[3:],
-            *steps(head)[1:],
             V((1280, 256)),
             V((1280, 256)),
             V((640, 256)),
@@ -1376,25 +1426,126 @@
             V((128, 256)),
             V((128, 256)),
             V((64, 256)),
-            *steps(late),
-            dma((2, 8 * (half - 1) + 20)),
-            dma((16,)),
+            V((late, 256)),
+            V((count - 1, late // count, 256)),
+            V((late // count, 256)),
+            dma((2, 7 * (half - 1) + 4 * half + 2 * (count - 1) + 15)),
+            dma((18,)),
         ],
         compiler_params=pltpu.CompilerParams(
             collective_id=2, has_side_effects=True, vmem_limit_bytes=60 * MIB
         ),
         cost_estimate=estimate(110),
         name="encode_back",
-    )(*maps, dec, d_both, t_half, l_rows)
-    enc = [e_out[:, :, quarter : quarter + 640], f_out[:, :, :64]]
-    return (
-        d_total,
-        l_total,
-        t_total,
-        e_out[:, :, :quarter].reshape(-1, 256),
-        jnp.concatenate([part.reshape(-1, 256) for part in enc], axis=0),
-        jnp.transpose(grad_out, (3, 0, 1, 2)),
-    )
+    )(*maps, dec, d_piece, l_both, t_half)
+    return d_total, l_total, t_total, e_out, f_out, jnp.transpose(grad_out, (3, 0, 1, 2))
+
+
+def unpack_kernel(
+    layers, quarter, d_total, l_total, upper, lower, early, late,
+    latent_out, head_out, down_out, up_out, project_out, qkv_out, embed_out, rest_out, *outs,
+):
+    kernels, scratch, sems = outs[:8], outs[8:-1], outs[-1]
+    (
+        latent_v, head_v, down_v, up_v, project_v, qkv_v, embed_v, rest_v, *kernel_v
+    ) = scratch
+    stores = []
+
+    def store(src, dst):
+        one = pltpu.make_async_copy(src, dst, sems.at[len(stores)])
+        one.start()
+        stores.append(one)
+
+    for k in range(layers):
+        src, base = (upper, LAYER_ROWS * (k - 1)) if k else (lower, 0)
+        down_v[k] = src[base : base + 512].astype(F32)
+        up_v[k] = src[base + 512 : base + 1024].astype(F32)
+        project_v[k] = src[base + 1024 : base + 1152].astype(F32)
+        for part in range(3):
+            first = base + 1152 + 128 * part
+            for b in range(4):
+                qkv_v[k, part, 128 * b : 128 * b + 128] = src[
+                    first : first + 128, 128 * b : 128 * b + 128
+                ].astype(F32)
+    embed_v[...] = lower[LAYER_ROWS : LAYER_ROWS + 256].astype(F32)
+    rest_v[...] = lower[LAYER_ROWS + 256 : LAYER_ROWS + 256 + NF + 16].astype(F32)
+    for src, dst in (
+        (down_v, down_out), (up_v, up_out), (project_v, project_out), (qkv_v, qkv_out),
+        (embed_v, embed_out), (rest_v, rest_out),
+    ):
+        store(src, dst)
+    for b in range(16):
+        rows = slice(256 * b, 256 * b + 256)
+        head_v[:, rows] = d_total[rows].astype(F32)
+        latent_v[rows] = l_total[rows].astype(F32)
+    store(head_v, head_out)
+    store(latent_v, latent_out)
+
+    def piece(first, is_enc):
+        if not is_enc:
+            at, place = divmod(first, quarter)
+            return early[at // 2, at % 2, place : place + 64].astype(F32)
+        if first < 2560:
+            at, place = divmod(first, 640)
+            return early[at // 2, at % 2, quarter + place : quarter + place + 64].astype(F32)
+        at = (first - 2560) // 64
+        return late[at // 2, at % 2, 0:64].astype(F32)
+
+    for is_enc in (False, True):
+        outer, first, second, third = kernel_v[4:] if is_enc else kernel_v[:4]
+        for r in range(0, 2048, 64):
+            value = piece(r, is_enc)
+            if is_enc:
+                third[r : r + 64] = value[:, :128]
+                third[2048 + r : 2048 + r + 64] = value[:, 128:]
+            else:
+                third[r : r + 64] = value
+        for r in range(0, 512, 64):
+            value = piece(2048 + r, is_enc)
+            second[r : r + 64] = value[:, :128]
+            second[512 + r : 512 + r + 64] = value[:, 128:]
+        for r in range(0, 128, 64):
+            value = piece(2560 + r, is_enc)
+            for k in range(4):
+                first[128 * k + r : 128 * k + r + 64] = value[:, 64 * k : 64 * k + 64]
+        outer[...] = piece(2688, is_enc)[:48, :32]
+        for src, dst in zip(kernel_v[4:] if is_enc else kernel_v[:4], kernels[4:] if is_enc else kernels[:4]):
+            store(src, dst)
+    for one in stores:
+        one.wait()
+
+
+def unpack(layers, quarter, *args):
+    dma = pltpu.SemaphoreType.DMA
+    any_spec = pl.BlockSpec(memory_space=pl.ANY)
+    shapes = [
+        (4096, 256),
+        (256, 4096),
+        (layers, 512, 512),
+        (layers, 512, 512),
+        (layers, 128, 512),
+        (layers, 3, 512, 128),
+        (256, 512),
+        (NF + 16, 512),
+        (48, 32),
+        (512, 64),
+        (1024, 128),
+        (2048, 256),
+        (48, 32),
+        (512, 64),
+        (1024, 128),
+        (4096, 128),
+    ]
+    return pl.pallas_call(
+        functools.partial(unpack_kernel, layers, quarter),
+        out_shape=tuple(S(shape, F32) for shape in shapes),
+        in_specs=VM(len(args)),
+        out_specs=tuple([any_spec] * len(shapes)),
+        scratch_shapes=[V(shape, F32) for shape in shapes] + [dma((len(shapes),))],
+        compiler_params=pltpu.CompilerParams(vmem_limit_bytes=56 * MIB),
+        cost_estimate=estimate(12),
+        name="unpack",
+    )(*args)
 
 
 def beside(value):
@@ -1405,18 +1556,6 @@
     places = jnp.arange(segment_ids.shape[1])
     causal = places[:, None] >= places[None, :]
     return causal[None] & (segment_ids[:, :, None] == segment_ids[:, None, :])
-
-
-def unpack_kernels(flat):
-    flat = flat.astype(F32)
-    second = jnp.concatenate([flat[2048:2560, :128], flat[2048:2560, 128:]], axis=0)
-    first = jnp.concatenate([flat[2560:2688, 64 * k : 64 * k + 64] for k in range(4)], axis=0)
-    return (
-        flat[2688:2736, :32].reshape(3, 4, 4, 32),
-        first.reshape(32, 4, 4, 64),
-        second.reshape(64, 4, 4, 128),
-        flat[:2048],
-    )
 
 
 def shards(
@@ -1482,7 +1621,10 @@
         ],
         axis=0,
     )
-    tokens, latent, chances, decoded, upper, lower, grad_latent, feat_got = middle(
+    (
+        tokens, latent, chances, decoded, upper, lower, grad_latent, feat_got,
+        latent_near, feat_near, got_near,
+    ) = middle(
         layers,
         feat,
         *head_in,
@@ -1516,44 +1658,46 @@
     )
     recon_parts, g_decoded = lax.optimization_barrier((recon_parts, g_decoded))
     recon = frames_out_later(recon_parts)
-    g_feat, l_rows, dec_share, d_both, upper, lower = latents_back(
-        g_decoded, latent, chances, grad_latent, feat, feat_got, *head_in, *head_out, dec_flat,
-        upper, lower,
+    g_feat, dec_share, d_piece, l_both, upper, lower = latents_back(
+        g_decoded, latent, latent_near, chances, grad_latent, feat, feat_got, feat_near, got_near,
+        *head_in, *head_out, dec_flat, upper, lower,
     )
 
-    d_total, l_total, lower, dec_total, enc_total, frames_grad = enc_bwd(
-        (pixels, z1, z2, z3, z4, g_feat, *enc_u, enc_b), dec_share, d_both, lower, l_rows
+    d_total, l_total, lower, early, late, frames_grad = enc_bwd(
+        (pixels, z1, z2, z3, z4, g_feat, *enc_u, enc_b), dec_share, d_piece, l_both, lower
     )
-
-    t_layers = jnp.concatenate([lower[:LAYER_ROWS], upper[: LAYER_ROWS * (layers - 1)]], axis=0)
-    t_layers = t_layers.astype(F32).reshape(layers, LAYER_ROWS, 512)
-    t_rest = lower[LAYER_ROWS:].astype(F32)
-    r_qkv = t_layers[:, 1152:].reshape(layers, 3, 128, 4, 128).transpose(0, 3, 2, 1, 4)
-    r_qkv = r_qkv.reshape(qkv_weight.shape)
-    e_one, e_two, e_three, e_four = unpack_kernels(enc_total)
-    d_four, d_three, d_two, d_one = unpack_kernels(dec_total)
-    e_four = jnp.concatenate([e_four[:, :128], e_four[:, 128:]], axis=0)
+    (
+        g_latent_head, g_decode_head, g_down, g_up, g_out, g_qkv, g_embed, g_rest,
+        d_four, d_three, d_two, d_one, e_one, e_two, e_three, e_four,
+    ) = unpack(layers, dec_share.shape[0], d_total, l_total, upper, lower, early, late)
+
+    def of_input(rows, count):
+        return rows.reshape(count, 4, 4, -1).transpose(3, 0, 1, 2)
+
+    def of_output(rows, count):
+        return rows.reshape(count, 4, 4, -1).transpose(0, 3, 1, 2)
+
     return (
         tokens_out,
         recon,
         frames_grad,
-        e_one.transpose(3, 0, 1, 2),
-        e_two.transpose(3, 0, 1, 2),
-        e_three.transpose(3, 0, 1, 2),
-        e_four.reshape(256, 4, 4, 128).transpose(0, 3, 1, 2),
-        l_total.astype(F32),
-        t_rest[:256],
-        t_rest[256 : 256 + NF],
-        t_rest[256 + NF : 256 + NF + 2 * layers].reshape(norm_gains.shape),
-        r_qkv,
-        t_layers[:, 1024:1152],
-        t_layers[:, 512:1024],
-        t_layers[:, :512],
-        d_total.astype(F32).reshape(16, 256, 256).transpose(1, 0, 2).reshape(256, 4096),
-        d_one.reshape(128, 4, 4, 256).transpose(0, 3, 1, 2),
-        d_two.transpose(0, 3, 1, 2),
-        d_three.transpose(0, 3, 1, 2),
-        d_four.transpose(0, 3, 1, 2),
+        of_input(e_one, 3),
+        of_input(e_two, 32),
+        of_input(e_three, 64),
+        of_output(e_four, 256),
+        g_latent_head,
+        g_embed,
+        g_rest[:NF],
+        g_rest[NF : NF + 2 * layers].reshape(norm_gains.shape),
+        g_qkv.transpose(0, 2, 1, 3),
+        g_out,
+        g_up,
+        g_down,
+        g_decode_head,
+        of_output(d_one, 128),
+        of_output(d_two, 64),
+        of_output(d_three, 32),
+        of_output(d_four, 3),
     )
 
 

time: 493 us -> 443 us (0.90)
  Pallas kernels: 431 us -> 412 us
  local copies, waits for them, and re-layouts: 31.3 us -> 14.9 us
  other arithmetic: 17.3 us -> 3.19 us
    pallas_call x1, Pallas kernels: 152 us -> 122 us  [enc_bwd(): pl.pallas_call(functools.partial(enc_bwd_kernel, count), out_shape=(S((he...]
    pallas_call x0 -> x1, Pallas kernels: none -> 11.7 us  [unpack(): pl.pallas_call(functools.partial(unpack_kernel, layers, quarter), out_sha...]
    slice x16 -> x2, local copies, waits for them, and re-layouts: 10.4 us -> 2.29 us  [the longest x1 1.57 us: shards(): g_rest[:NF]]
    concatenate x6 -> x0, other arithmetic: 5.79 us -> none  [the longest x2 2.68 us: unpack_kernels(): jnp.concatenate([flat[2048:2560, :128], flat[2048:2560, 128:]], axis=0)]
  transfers between devices with their start and end apart: 7 -> 7, of which waited for: 0 -> 0; matrix products, arithmetic and copies ran while one was open for 1% -> 1% of each run, Pallas kernels for 40% -> 44%
where the time goes in v5:
time: 443 us; the launch traced here: 436 us
  Pallas kernels  412 us (93%)
  local copies, waits for them, and re-layouts  14.9 us (3%)
    pallas_call x1, Pallas kernels, enc_bwd(): pl.pallas_call(functools.partial(enc_bwd_kernel, count), out_shape=(S((he...  122 us
    pallas_call x3, Pallas kernels, run(): pl.pallas_call(kernel, out_shape=outs, in_specs=VM(len(args)), out_specs=...  103 us
    pallas_call x1, Pallas kernels, middle(): pl.pallas_call(functools.partial(middle_kernel, layers, count), out_shape...  91.2 us
    pallas_call x1, Pallas kernels, latents_back(): pl.pallas_call(functools.partial(back_kernel, count), out_shape=(S(maps),...  55.1 us
    pallas_call x1, Pallas kernels, start(): pl.pallas_call(start_kernel, out_shape=tuple((S(shape) for shape in shape...  27.4 us
    pallas_call x1, Pallas kernels, unpack(): pl.pallas_call(functools.partial(unpack_kernel, layers, quarter), out_sha...  11.7 us
  transfers between devices with their start and end apart: 7, of which 0 were waited for; matrix products, arithmetic and copies ran while one was open for 1% of the time, Pallas kernels for 44%

profile of v5, /device:TPU:0, one launch (start us, length us, event | category | flops | bytes accessed | tf_op | source)
XLA Modules:
  0.0 436.0 jit_solution(17893585738155466610)
XLA Ops:
  0.7 2.1 reshape.122.d1
  2.9 1.0 convert_element_type.24.e1
  3.9 0.1 tile.5
  4.0 1.0 convert_element_type.28.d4
  5.1 27.4 %start.1 = (bf16[34,64,384]{2,1,0:T(8,128)(2,1)}, bf16[1152,1024]{1,0:T(8,128)(2,1)}, bf16[3072,384]{1,0:T(8,128)(2,1)}, bf16[2048,256]{1,0:T(8,128)(2,1)}, bf16...) custom-call(bf16[3,16,64,256]{3,2,1,0:T(8,128)(2,1)} %bitcast.60, ...), custom_call_target="tpu_custom_call" | custom-call | flops 29899999232 | bytes 1048576 | tf_op jit(solution)/shard_map/start/pallas_call | solution.py:606
  32.5 0.7 collective-permute-start.4
  33.2 1.7 collective-permute-start.5
  34.9 0.1 and_convert_fusion
  35.0 0.6 reshape.125.gains
  35.7 0.7 select_maximum_fusion.allow
  36.4 0.7 pad_maximum_fusion.cot
  37.0 21.6 %encode.1 = (bf16[32,64,1024]{2,1,0:T(8,128)(2,1)}, bf16[16,64,1024]{2,1,0:T(8,128)(2,1)}, bf16[8,64,1024]{2,1,0:T(8,128)(2,1)}, bf16[4,64,1024]{2,1,0:T(8,128)(2,1)}, bf16[4,64,1024]{2,1,0:T(8,128)(2,1)}) custom-call(bf16[34,64,384]{2,1,0:T(8,128)(2,1)} %get-tuple-element.109.xp, bf16[1152,1024]{1,0:T(8,128)(2,1)} %get-tuple-element.110.a, ...), custom_call_target="tpu_custom_call" | custom-call | flops 25300000768 | bytes 1048576 | tf_op jit(solution)/shard_map/encode/pallas_call | solution.py:235
  58.6 91.2 %middle.1 = (bf16[128,512]{1,0:T(8,128)(2,1)}, bf16[128,512]{1,0:T(8,128)(2,1)}, f32[128,512]{1,0:T(8,128)}, bf16[4,64,1024]{2,1,0:T(8,128)(2,1)}, bf16[768,512]...) custom-call(bf16[4,64,1024]{2,1,0:T(8,128)(2,1)} %get-tuple-element., ...), custom_call_target="tpu_custom_call" | custom-call | flops 96599998464 | bytes 1048576 | tf_op jit(solution)/shard_map/middle/pallas_call | solution.py:995
  149.8 0.9 fusion
  150.7 0.9 maximum_select_fusion.1
  151.6 0.1 collective-permute-start
  151.7 35.7 %decode.1 = (bf16[32,64,384]{2,1,0:T(8,128)(2,1)}, bf16[8,64,1024]{2,1,0:T(8,128)(2,1)}, bf16[16,64,1024]{2,1,0:T(8,128)(2,1)}, bf16[32,64,1024]{2,1,0:T(8,128)(...) custom-call(bf16[4,64,1024]{2,1,0:T(8,128)(2,1)} %get-tuple-element.125.dec, ...), custom_call_target="tpu_custom_call" | custom-call | flops 27599998976 | bytes 1048576 | tf_op jit(solution)/shard_map/decode/pallas_call | solution.py:235
  187.5 1.5 constant_dynamic-slice_fusion
  189.0 0.1 collective-permute-start.1
  189.1 0.1 collective-permute-start.2
  189.2 0.8 maximum_select_fusion
  189.9 1.6 collective-permute-start.3
  191.6 45.5 %decode_back.1 = (bf16[4,64,1024]{2,1,0:T(8,128)(2,1)}, bf16[2816,256]{1,0:T(8,128)(2,1)}, bf16[768,512]{1,0:T(8,128)(2,1)}, bf16[240,512]{1,0:T(8,128)(2,1)}) custom-call(bf16[8,64,384]{2,1,0:T(8,128)(2,1)} %get-tuple-element.133.c0, bf16[8,64,384]{2,1,0:T(8,128)(2,1)} %collective-permute-done.4.c1, bf16[8,64,384]{2,1,0:T(8,128)(2,1)} %collective-permute-done.5.c2, ...), custom_call_target="tpu_custom_call" | custom-call | flops 48299999232 | bytes 1048576 | tf_op jit(solution)/shard_map/decode_back/pallas_call | solution.py:235
  237.1 55.1 %latents_back.1 = (bf16[4,64,1024]{2,1,0:T(8,128)(2,1)}, bf16[704,256]{1,0:T(8,128)(2,1)}, bf16[512,256]{1,0:T(8,128)(2,1)}, bf16[2048,256]{1,0:T(8,128)(2,1)}, ...) custom-call(bf16[4,64,1024]{2,1,0:T(8,128)(2,1)} %get-tuple-element.155.grad, ...), custom_call_target="tpu_custom_call" | custom-call | flops 63250001920 | bytes 1048576 | tf_op jit(solution)/shard_map/latents_back/pallas_call | solution.py:1160
  292.2 121.9 %encode_back.1 = (bf16[4096,256]{1,0:T(8,128)(2,1)}, bf16[4096,256]{1,0:T(8,128)(2,1)}, bf16[1920,512]{1,0:T(8,128)(2,1)}, bf16[2,2,1408,256]{3,2,1,0:T(8,128)(2...) custom-call(bf16[34,64,384]{2,1,0:T(8,128)(2,1)} %get-tuple-element.109.xp, ...), custom_call_target="tpu_custom_call" | custom-call | flops 126500003840 | bytes 1048576 | tf_op jit(solution)/shard_map/encode_back/pallas_call | solution.py:1396
  414.2 11.7 %unpack.1 = (f32[4096,256]{1,0:T(8,128)}, f32[256,4096]{1,0:T(8,128)}, f32[2,512,512]{2,1,0:T(8,128)}, f32[2,512,512]{2,1,0:T(8,128)}, f32[2,128,512]{2,1,0:T(8,...) custom-call(bf16[4096,256]{1,0:T(8,128)(2,1)} %get-tuple-element.176, ...), custom_call_target="tpu_custom_call" | custom-call | flops 13799999488 | bytes 1048576 | tf_op jit(solution)/shard_map/unpack/pallas_call | solution.py:1539
  425.9 1.6 slice.22
  427.5 0.7 slice.23
  428.2 2.9 reshape.132
  431.1 0.6 reshape.131
  431.7 2.1 turn_back.1
  433.9 1.7 copy.42
  (36 shorter events, 0.2 us)
Async XLA Ops:
  0.7 2.2 copy-start.6
  0.7 3.3 copy-start.7
  5.1 29.8 %copy-start.9 = (s32[4,64]{1,0:T(4,128)S(1)}, s32[4,64]{1,0:T(4,128)}, u32[]{:S(2)}) copy-start(s32[4,64]{1,0:T(4,128)} %param.22) | copy-start | bytes 3076
  5.1 30.0 %copy-start.8 = (f32[2,2,512]{2,1,0:T(2,128)S(1)}, f32[2,2,512]{2,1,0:T(2,128)}, u32[]{:S(2)}) copy-start(f32[2,2,512]{2,1,0:T(2,128)} %param.30) | copy-start | bytes 24580
  5.1 31.3 %copy-start.5 = (bf16[256,512]{1,0:T(8,128)(2,1)S(1)}, bf16[256,512]{1,0:T(8,128)(2,1)}, u32[]{:S(2)}) copy-start(bf16[256,512]{1,0:T(8,128)(2,1)} %param.40) | copy-start | bytes 786436
  32.5 157.5 %collective-permute-start.4 = (bf16[8,64,384]{2,1,0:T(8,128)(2,1)}, bf16[8,64,384]{2,1,0:T(8,128)(2,1)}, u32[]{:S(2)}, u32[]{:S(2)}) collective-permute-start(bf16[8,64,384]{2,1,0:T(8,128)(2,1)} %get-tuple-element.134), channel_id=1, source_target_pairs={{0,1},{1,2},{2,3},{3,0},{4,5},{5,6},{6,7},{7,4},{8,9},{9,10},{10,1... | collective-permute-start | bytes 1179656 | tf_op jit(solution)/shard_map/ppermute | solution.py:658
  33.2 158.4 %collective-permute-start.5 = (bf16[8,64,384]{2,1,0:T(8,128)(2,1)}, bf16[8,64,384]{2,1,0:T(8,128)(2,1)}, u32[]{:S(2)}, u32[]{:S(2)}) collective-permute-start(bf16[8,64,384]{2,1,0:T(8,128)(2,1)} %get-tuple-element.135), channel_id=1, source_target_pairs={{0,2},{1,3},{2,0},{3,1},{4,6},{5,7},{6,4},{7,5},{8,10},{9,11},{10,... | collective-permute-start | bytes 1179656 | tf_op jit(solution)/shard_map/ppermute | solution.py:658
  34.8 156.8 %collective-permute-start.6 = (bf16[8,64,384]{2,1,0:T(8,128)(2,1)}, bf16[8,64,384]{2,1,0:T(8,128)(2,1)}, u32[]{:S(2)}, u32[]{:S(2)}) collective-permute-start(bf16[8,64,384]{2,1,0:T(8,128)(2,1)} %get-tuple-element.136), channel_id=1, source_target_pairs={{0,3},{1,0},{2,1},{3,2},{4,7},{5,4},{6,5},{7,6},{8,11},{9,8},{10,9... | collective-permute-start | bytes 1179656 | tf_op jit(solution)/shard_map/ppermute | solution.py:658
  151.6 37.5 %collective-permute-start = (bf16[128,512]{1,0:T(8,128)(2,1)S(1)}, bf16[128,512]{1,0:T(8,128)(2,1)S(1)}, u32[]{:S(2)}, u32[]{:S(2)}) collective-permute-start(bf16[128,512]{1,0:T(8,128)(2,1)S(1)} %maximum_select_fusion.1), channel_id=1, source_target_pairs={{0,1},{1,0},{2,3},{3,2},{4,5},{5,4},{6,7},{7,6},{8,9},{9,8},{10,11... | collective-permute-start | bytes 393224 | tf_op jit(solution)/shard_map/ppermute | solution.py:1552
  189.0 48.1 %collective-permute-start.1 = (bf16[8,64,384]{2,1,0:T(8,128)(2,1)S(1)}, bf16[8,64,384]{2,1,0:T(8,128)(2,1)S(1)}, u32[]{:S(2)}, u32[]{:S(2)}) collective-permute-start(bf16[8,64,384]{2,1,0:T(8,128)(2,1)S(1)} %get-tuple-element.200), channel_id=1, source_target_pairs={{0,1},{1,2},{2,3},{3,0},{4,5},{5,6},{6,7},{7,4},{8,9},{9,10},{10,1... | collective-permute-start | bytes 1179656 | tf_op jit(solution)/shard_map/ppermute | solution.py:658
  189.1 48.0 %collective-permute-start.2 = (bf16[8,64,384]{2,1,0:T(8,128)(2,1)S(1)}, bf16[8,64,384]{2,1,0:T(8,128)(2,1)S(1)}, u32[]{:S(2)}, u32[]{:S(2)}) collective-permute-start(bf16[8,64,384]{2,1,0:T(8,128)(2,1)S(1)} %get-tuple-element.199), channel_id=1, source_target_pairs={{0,2},{1,3},{2,0},{3,1},{4,6},{5,7},{6,4},{7,5},{8,10},{9,11},{10,... | collective-permute-start | bytes 1179656 | tf_op jit(solution)/shard_map/ppermute | solution.py:658
  189.9 47.2 %collective-permute-start.3 = (bf16[8,64,384]{2,1,0:T(8,128)(2,1)S(1)}, bf16[8,64,384]{2,1,0:T(8,128)(2,1)S(1)}, u32[]{:S(2)}, u32[]{:S(2)}) collective-permute-start(bf16[8,64,384]{2,1,0:T(8,128)(2,1)S(1)} %get-tuple-element.198), channel_id=1, source_target_pairs={{0,3},{1,0},{2,1},{3,2},{4,7},{5,4},{6,5},{7,6},{8,11},{9,8},{10,9... | collective-permute-start | bytes 1179656 | tf_op jit(solution)/shard_map/ppermute | solution.py:658
  237.1 55.1 %copy-start = (bf16[8,64,384]{2,1,0:T(8,128)(2,1)}, bf16[8,64,384]{2,1,0:T(8,128)(2,1)S(1)}, u32[]{:S(2)}) copy-start(bf16[8,64,384]{2,1,0:T(8,128)(2,1)S(1)} %collective-permute-done.2.c2) | copy-start | bytes 1179652
  237.1 55.1 %copy-start.2 = (bf16[8,64,384]{2,1,0:T(8,128)(2,1)}, bf16[8,64,384]{2,1,0:T(8,128)(2,1)S(1)}, u32[]{:S(2)}) copy-start(bf16[8,64,384]{2,1,0:T(8,128)(2,1)S(1)} %collective-permute-done.3.c3) | copy-start | bytes 1179652
  428.2 3.5 copy-start.1
  428.2 3.5 copy-start.3
  431.7 2.1 copy-start.4

commit v6 on v5

--- a/solution.py
+++ b/solution.py
@@ -19,7 +19,7 @@
 MESH = pl.DeviceIdType.MESH
 
 
-def sig(z): return 1.0/(1.0+jnp.exp(-z))
+def sig(z): return 0.5*jnp.tanh(0.5*z)+0.5
 
 def zero_big(ref,rows):
     z=jnp.zeros((NF,1280),BF)
@@ -163,13 +163,17 @@
     down(m2,t3,8,4,keep(z3,m3))
     down(m3,t4,4,4,keep(z4,None))
 
-def dec_fwd_kernel(count,dec,u4,u3,u2,b,upper_both,lower,recon,p3,p2,p1,upper_piece,lower_both,
-                   s4,s3,s2,s1,upper_slots,lower_near,remote):
-    place=Place(count); sems=Sems(remote,None)
-    place.greet([place.near_device]+place.far_devices)
+def dec_kernel(count,c0,c1,c2,c3,dec,u4,u3,u2,b,a,t2,t3,t4,upper_both,lower,
+               gdec,pk,recon_out,upper_total,got,lower_piece,
+               p3,p2,p1,s4,s3,s2,s1,d1,d2,d3,cp,yt,recon,
+               upper_slots,upper_piece,rows_out,lower_near,lower_both,lower_slots,remote,here):
+    place=Place(count); sems=Sems(remote,here); me=place.me
+    place.greet(place.others+[place.near_device]+place.far_devices)
     upper_far=far_start(place,sems,upper_both,upper_slots)
     lower_copy=near_start(place,sems,lower,lower_near)
+    lower_own=sems.here(rows_of(lower,place.near,lower.shape[0]//2),lower_both)
     zero_small(s1,32,0); zero_small(s2,16,128); zero_small(s3,8,128); zero_small(s4,4,256)
+    zero_big(d1,32); zero_big(d2,16); zero_big(d3,8)
     z=dec[...].astype(F32)
     s4[1:5,:,256:1280]=(z*sig(z)).astype(BF)
     def fwd(p,dst,pad):
@@ -183,25 +187,15 @@
     up(s4,u4,4,4,fwd(p3,s3,128))
     up(s3,u3,8,4,fwd(p2,s2,128))
     up(s2,u2,16,4,fwd(p1,s1,0))
+    far_end(place,upper_far,upper_both,upper_slots,upper_piece)
+    upper_home=rows_of(upper_total,place.near,upper_total.shape[0]//2)
+    upper_back=back_start(place,sems,upper_piece,upper_home)
     def put(i0,acc): recon[pl.ds(i0,acc.shape[0])]=acc.astype(BF)
     outer_up(s1,b,put)
-    far_end(place,upper_far,upper_both,upper_slots,upper_piece)
-    near_end(place,lower_copy,lower,lower_near,lower_both)
-
-def dec_bwd_kernel(count,c0,c1,c2,c3,dec,p3,p2,p1,a,t2,t3,t4,upper_piece,lower_both,
-                   gdec,pk,upper_half,lower_piece,d1,d2,d3,cp,yt,lower_slots,remote,here):
-    place=Place(count); sems=Sems(remote,here); me=place.me
-    place.greet(place.far_devices)
-    upper_back=back_start(place,sems,upper_piece,upper_half)
-    lower_far=far_start(place,sems,lower_both,lower_slots)
+    strips=[sems.copy(recon.at[pl.ds(8*device[1],8)],got.at[pl.ds(8*me,8)],device) for device in place.others]
     cp[0]=jnp.zeros((NF,384),BF); cp[33]=jnp.zeros((NF,384),BF)
-    for k,part in enumerate((c0,c1,c2,c3)):
-        cp[pl.ds(1+8*lax.rem(me+4-k,4),8)]=part[...]
-    zero_big(d1,32); zero_big(d2,16); zero_big(d3,8)
-    def maps(p,rows,yt):
-        for q in range(4):
-            zz=p[:,:,256*q:256*q+256].reshape(rows*NF,256).astype(F32)
-            yt[256*q:256*q+256,:rows*NF]=(zz*sig(zz)).astype(BF).T
+    for k,part in enumerate((c0,c1,c2,c3)): cp[pl.ds(1+8*lax.rem(me+4-k,4),8)]=part[...]
+    swap=exchange_16()
     def back(p,dst):
         def emit(i0,half0,q,acc):
             rows=acc.shape[0]//NF
@@ -211,18 +205,32 @@
             if dst is None: gdec[pl.ds(i0,rows),:,256*q:256*q+256]=val.reshape(rows,NF,256)
             else: put_big(dst,half0,rows,q,val)
         return emit
-    swap=exchange_16()
-    maps(p1,32,yt); pack_outer(pk,2688,outer_grad(cp,yt),True)
+    lower_own.wait(); lower_copy.wait()
+    lower_both[...]=(lower_both[...].astype(F32)+lower_near[...].astype(F32)).astype(BF)
+    turn(s1,yt,32,0); pack_outer(pk,2688,outer_grad(cp,yt),True)
+    for one in upper_back: one.wait()
+    upper_last=last_start(place,sems,upper_home,upper_total)
+    lower_far=far_start(place,sems,lower_both,lower_slots)
     outer_down(cp,a,back(p1,d1))
-    maps(p2,16,yt); pack(pk,2560,4,32,64,grad_w(d1,yt,16),True,swap)
+    turn(s2,yt,16,128); pack(pk,2560,4,32,64,grad_w(d1,yt,16),True,swap)
     down(d1,t2,16,4,back(p2,d2))
-    maps(p3,8,yt); pack(pk,2048,2,64,128,grad_w(d2,yt,8),True,swap)
+    for one in strips: one.wait()
+    arrived=[sems.here(got.at[pl.ds(8*device[1],8)],recon.at[pl.ds(8*device[1],8)]) for device in place.others]
+    for one in arrived: one.wait()
+    stores=[]
+    for i in range(8):
+        if i: stores[i-1].wait()
+        block=jnp.concatenate([recon[8*((k%2)*2+k//2)+i] for k in range(4)],axis=0).T
+        for p in range(2):
+            for c in range(3): rows_out[c,p]=block[64*(3*p+c):64*(3*p+c)+64]
+        stores.append(sems.here(rows_out,recon_out.at[:,2*i:2*i+2]))
+    turn(s3,yt,8,128); pack(pk,2048,2,64,128,grad_w(d2,yt,8),True,swap)
     down(d2,t3,8,4,back(p3,d3))
-    maps(dec,4,yt); pack(pk,0,1,128,256,grad_w(d3,yt,4),True,swap)
+    turn(s4,yt,4,256); pack(pk,0,1,128,256,grad_w(d3,yt,4),True,swap)
     down(d3,t4,4,4,back(dec,None))
     pk[2816-80:2816]=jnp.zeros((80,256),BF)
     far_end(place,lower_far,lower_both,lower_slots,lower_piece)
-    for one in upper_back: one.wait()
+    for one in stores[-1:]+[upper_last]: one.wait()
 
 def estimate(us):
     return pl.CostEstimate(flops=us*1150*10**6,bytes_accessed=MIB,transcendentals=0)
@@ -245,22 +253,25 @@
       [big(32),big(16),big(8)],(xp,a,t2,t3,t4),"encode",22)
 small=lambda h,p:V((h+2,NF,1024+2*p))
 yts=[V((1024,32*NF)),V((1024,16*NF)),V((1024,8*NF)),V((1024,4*NF))]
-def dec_fwd(dec,u4,u3,u2,b,upper_both,lower):
+def decode(hints,dec,u4,u3,u2,b,a,t2,t3,t4,upper_both,lower):
     count=lax.axis_size("rows"); half=count//2
     upper,rows=2*upper_both.shape[0],lower.shape[0]
     dma=pltpu.SemaphoreType.DMA
-    return run(functools.partial(dec_fwd_kernel,count),
-      (S((32,NF,384)),S((8,NF,1024)),S((16,NF,1024)),S((32,NF,1024)),S((upper//count,512)),S((rows//2,512))),
-      [small(4,256),small(8,128),small(16,128),small(32,0),V((half-1,upper//count,512)),V((rows//2,512)),dma((2,half))],
-      (dec,u4,u3,u2,b,upper_both,lower),"decode",24,ident=5)
-def dec_bwd(hints,dec,p3,p2,p1,a,t2,t3,t4,upper_piece,lower_both):
-    count=lax.axis_size("rows"); half=count//2
-    upper,rows=count*upper_piece.shape[0],2*lower_both.shape[0]
-    dma=pltpu.SemaphoreType.DMA
-    return run(functools.partial(dec_bwd_kernel,count),
-      (S((4,NF,1024)),S((2816,256)),S((upper//2,512)),S((rows//count,512))),
-      [big(32),big(16),big(8),V((34,NF,384)),V((1024,32*NF)),V((half-1,rows//count,512)),dma((2,2*(half-1))),dma((1,))],
-      (*hints,dec,p3,p2,p1,a,t2,t3,t4,upper_piece,lower_both),"decode_back",42,ident=6)
+    args=(*hints,dec,u4,u3,u2,b,a,t2,t3,t4,upper_both,lower)
+    return pl.pallas_call(
+        functools.partial(dec_kernel,count),
+        out_shape=(S((4,NF,1024)),S((2816,256)),S((3,16,64,256)),S((upper,512)),S((32,NF,384)),S((rows//count,512))),
+        in_specs=VM(len(args)-1)+[pl.BlockSpec(memory_space=pl.ANY)],
+        out_specs=tuple(VM(2)+[pl.BlockSpec(memory_space=pl.ANY)]*3+VM(1)),
+        scratch_shapes=[V((8,NF,1024)),V((16,NF,1024)),V((32,NF,1024)),small(4,256),small(8,128),small(16,128),small(32,0),
+            big(32),big(16),big(8),V((34,NF,384)),V((1024,32*NF)),V((32,NF,384)),
+            V((half-1,upper//count,512)),V((upper//count,512)),V((3,2,64,256)),
+            V((rows//2,512)),V((rows//2,512)),V((half-1,rows//count,512)),
+            dma((2,3*(half-1)+5)),dma((13,))],
+        compiler_params=pltpu.CompilerParams(collective_id=5,has_side_effects=True,vmem_limit_bytes=60*MIB),
+        cost_estimate=estimate(65),
+        name="decode",
+    )(*args)
 
 
 def rows_of(ref, index, size):
@@ -474,11 +485,11 @@
 
 
 def start_kernel(
-    x, later, e1, e2, e3, e4, d1, d2, d3, d4, lh, dh, emb, qkv, proj, up, down,
-    pixels, ea, eb, et2, et3, et4, eu2, eu3, eu4, da, db, dt2, dt3, dt4, du2, du3, du4,
+    x, later, e1, e2, e3, e4, lh, dh, emb, qkv, proj, up, down,
+    pixels, ea, eb, et2, et3, et4, eu2, eu3, eu4,
     lh0, lh1, dh0, dh1, emb1, qkv1, proj1, up1, down1, t0, t1, t2, t3,
     stage, send_sem, recv_sem, side_sems,
-    va, vb, vt2, vt3, vt4, vu2, vu3, vu4, wa, wb, wt2, wt3, wt4, wu2, wu3, wu4,
+    va, vb, vt2, vt3, vt4, vu2, vu3, vu4,
     vl, vd, out_sems,
 ):
     me = lax.axis_index("strip")
@@ -493,28 +504,32 @@
             stage[k, i] = flat[first_frame(k) : first_frame(k) + NF]
         return carry
 
-    lax.fori_loop(0, 8, turn_rows, 0)
     barrier = pltpu.get_barrier_semaphore()
     for k in range(1, 4):
         pl.semaphore_signal(
             barrier, inc=1, device_id=(row, lax.rem(me + k, 4)), device_id_type=MESH
         )
+    lax.fori_loop(0, 4, turn_rows, 0)
     pl.semaphore_wait(barrier, 3)
     copies = []
-    for k in range(1, 4):
-        to = lax.rem(me + k, 4)
-        copies.append(
-            pltpu.make_async_remote_copy(
-                src_ref=stage.at[to],
-                dst_ref=pixels.at[pl.ds(1 + 8 * me, 8)],
-                send_sem=send_sem.at[k - 1],
-                recv_sem=recv_sem.at[k - 1],
+
+    def send(part):
+        for k in range(1, 4):
+            to = lax.rem(me + k, 4)
+            copy = pltpu.make_async_remote_copy(
+                src_ref=stage.at[to, pl.ds(4 * part, 4)],
+                dst_ref=pixels.at[pl.ds(1 + 8 * me + 4 * part, 4)],
+                send_sem=send_sem.at[3 * part + k - 1],
+                recv_sem=recv_sem.at[3 * part + k - 1],
                 device_id=(row, to),
                 device_id_type=MESH,
             )
-        )
-    for copy in copies:
-        copy.start()
+            copy.start()
+            copies.append(copy)
+
+    send(0)
+    lax.fori_loop(4, 8, turn_rows, 0)
+    send(1)
 
     def to_sibling(src, dst, index):
         copy = pltpu.make_async_remote_copy(
@@ -566,62 +581,48 @@
     store(vd, dh0)
     to_sibling(vl, lh1, 5)
     to_sibling(vd, dh1, 6)
-    put_outer(wa, wb, d4, True)
-    store(wa, da)
-    store(wb, db)
-    put_bands(wt2, wu2, [band(f, 4, 32, 64) for f in canonical(d3, swap, 32, 64, True)], None, 4)
-    store(wt2, dt2)
-    store(wu2, du2)
-    put_bands(wt3, wu3, [band(f, 2, 64, 128) for f in canonical(d2, swap, 64, 128, True)], None, 2)
-    store(wt3, dt3)
-    store(wu3, du3)
-    put_bands(wt4, wu4, canonical(d1, swap, 128, 256, True), None, 1)
-    store(wt4, dt4)
-    store(wu4, du4)
     for copy in copies:
         copy.wait()
     for copy in stores:
         copy.wait()
 
 
+BUILT = [(1152, 1024), (3072, 384)] + [(2048, 256)] * 3
+BUILT = BUILT + [(2, 1024, 256), (2, 1024, 256), (2, 1536, 256)]
+
+
 def start(frames, later, kernels, latent_head, decode_head, others):
-    e1, e2, e3, e4, d1, d2, d3, d4 = kernels
+    e1, e2, e3, e4 = kernels
     rows_in = [
         jnp.tile(jnp.transpose(e1, (1, 2, 3, 0)).reshape(48, 32), (1, 32)).astype(F32),
         jnp.transpose(e2, (1, 2, 3, 0)).reshape(512, 64),
         jnp.transpose(e3, (1, 2, 3, 0)).reshape(1024, 128),
         jnp.transpose(e4, (0, 2, 3, 1)).reshape(4096, 128),
-        jnp.transpose(d1, (0, 2, 3, 1)).reshape(2048, 256),
-        jnp.transpose(d2, (0, 2, 3, 1)).reshape(1024, 128),
-        jnp.transpose(d3, (0, 2, 3, 1)).reshape(512, 64),
-        jnp.tile(jnp.transpose(d4, (0, 2, 3, 1)).reshape(48, 32), (1, 32)).astype(F32),
     ]
     dma = pltpu.SemaphoreType.DMA
     any_spec = pl.BlockSpec(memory_space=pl.ANY)
-    built = [(1152, 1024), (3072, 384)] + [(2048, 256)] * 3
-    built = built + [(2, 1024, 256), (2, 1024, 256), (2, 1536, 256)]
     heads = [(4096, 256)] * 4
-    shapes = [(34, NF, 384)] + built * 2 + heads + [w.shape for w in others]
+    shapes = [(34, NF, 384)] + BUILT + heads + [w.shape for w in others]
     shapes = shapes + [(8, NF, 384)] * 4
     out = pl.pallas_call(
         start_kernel,
         out_shape=tuple(S(shape) for shape in shapes),
-        in_specs=VM(12) + [any_spec] * len(others),
+        in_specs=VM(8) + [any_spec] * len(others),
         out_specs=tuple(VM(1) + [any_spec] * (len(shapes) - 5) + VM(4)),
         scratch_shapes=[
             V((4, 8, NF, 384)),
-            dma((3,)),
-            dma((3,)),
+            dma((6,)),
+            dma((6,)),
             dma((2, 7)),
-            *[V(shape) for shape in built * 2],
+            *[V(shape) for shape in BUILT],
             V((4096, 256)),
             V((4096, 256)),
-            dma((18,)),
+            dma((10,)),
         ],
         compiler_params=pltpu.CompilerParams(
             collective_id=1, has_side_effects=True, vmem_limit_bytes=56 * MIB
         ),
-        cost_estimate=estimate(26),
+        cost_estimate=estimate(22),
         name="start",
     )(
         jnp.transpose(frames, (1, 2, 3, 0)),
@@ -632,7 +633,17 @@
         *others,
     )
     hints = around(out[-4:])
-    return out[0], out[1:9], out[9:17], out[17:19], out[19:21], out[21:-4], hints
+    return out[0], out[1:9], out[9:11], out[11:13], out[13:-4], hints
+
+
+def decoder_rows(kernels):
+    d1, d2, d3, d4 = kernels
+    return (
+        jnp.transpose(d1, (0, 2, 3, 1)).reshape(2048, 256),
+        jnp.transpose(d2, (0, 2, 3, 1)).reshape(1024, 128),
+        jnp.transpose(d3, (0, 2, 3, 1)).reshape(512, 64),
+        jnp.tile(jnp.transpose(d4, (0, 2, 3, 1)).reshape(48, 32), (1, 32)).astype(F32),
+    )
 
 
 def turn_kernel(x, *out):
@@ -657,44 +668,6 @@
     return [parts[0]] + [
         lax.ppermute(parts[k], "strip", [(s, (s + k) % 4) for s in range(4)]) for k in range(1, 4)
     ]
-
-
-def turned_back(got, out):
-    def turn_rows(i, carry):
-        block = jnp.concatenate([got[(b % 2) * 2 + b // 2, i] for b in range(4)], axis=0)
-        flat = block.T.astype(out.dtype)
-        for p in range(2):
-            for c in range(3):
-                first = 64 * (3 * p + c)
-                out[c, 2 * i + p] = flat[first : first + 64]
-        return carry
-
-    lax.fori_loop(0, 8, turn_rows, 0)
-
-
-def turn_back_kernel(c0, c1, c2, c3, out, got):
-    me = lax.axis_index("strip")
-    for k, part in enumerate((c0, c1, c2, c3)):
-        got[lax.rem(me + 4 - k, 4)] = part[...]
-    turned_back(got, out)
-
-
-def blocks_around(pairs, strip):
-    return around([lax.dynamic_slice_in_dim(pairs, 8 * ((strip + k) % 4), 8) for k in range(4)])
-
-
-def frames_out_later(parts):
-    flat = pl.pallas_call(
-        turn_back_kernel,
-        out_shape=S((3, 16, 64, 256)),
-        in_specs=VM(4),
-        out_specs=VM(1)[0],
-        scratch_shapes=[V((4, 8, NF, 384))],
-        compiler_params=pltpu.CompilerParams(vmem_limit_bytes=32 * MIB),
-        cost_estimate=estimate(2),
-        name="turn_back",
-    )(*parts)
-    return jnp.transpose(flat, (3, 0, 1, 2))
 
 
 def dot(a, b):
@@ -746,12 +719,12 @@
 def middle_kernel(
     layers, count,
     feat, lh0, lh1, dh0, dh1, emb0, emb1, pos, gains, allow, cot,
-    qkv0, qkv1, proj0, proj1, up0, up1, down0, down1,
+    qkv0, qkv1, proj0, proj1, up0, up1, down0, down1, d1, d2, d3, d4,
     tokens, latent_out, chances_out, decoded, upper_both, lower, grad_latent, feat_got,
-    latent_near, feat_near, got_near,
+    latent_near, feat_near, got_near, da, db, dt2, dt3, dt4, du2, du3, du4,
     feat_sems, keep, send, sent, spread_sems, parts, gots, pair_sems,
     upper, upper_other, upper_got, lower_other, lower_got, upper_near, fold_sems, near_sems, unit_a, unit_f, normed_a, normed_f, mixed, weights,
-    attended, before, inner, gain_rows,
+    attended, before, inner, gain_rows, wa, wb, wt2, wt3, wt4, wu2, wu3, wu4, form_sems,
 ):
     strip = lax.axis_index("strip")
     row = lax.axis_index("rows")
@@ -825,6 +798,34 @@
     embedded = total_wait(0, waiting)
     place = pos[...].astype(F32)
     hidden = embedded + jnp.concatenate([place, place], axis=0)
+    swap = exchange_16()
+    forms = []
+
+    def store(src, dst):
+        one = pltpu.make_async_copy(src, dst, form_sems.at[len(forms)])
+        one.start()
+        forms.append(one)
+
+    def build(step):
+        if step == 0:
+            put_outer(wa, wb, d4, True)
+            store(wa, da)
+            store(wb, db)
+        if step == 1:
+            bands = [band(f, 4, 32, 64) for f in canonical(d3, swap, 32, 64, True)]
+            put_bands(wt2, wu2, bands, None, 4)
+            store(wt2, dt2)
+            store(wu2, du2)
+        if step == 2:
+            bands = [band(f, 2, 64, 128) for f in canonical(d2, swap, 64, 128, True)]
+            put_bands(wt3, wu3, bands, None, 2)
+            store(wt3, dt3)
+            store(wu3, du3)
+        if step == 3:
+            put_bands(wt4, wu4, canonical(d1, swap, 128, 256, True), None, 1)
+            store(wt4, dt4)
+            store(wu4, du4)
+
     head_lane = lax.div(lax.broadcasted_iota(jnp.int32, (2 * NF, 128), 1), HEAD_DIM)
     allowed = allow[...] > 0.5
 
@@ -855,7 +856,9 @@
                 both = both + of_head(dot(weight.astype(BF), mixed[k, 2, :, lanes]), h)
             attended[k, :, 128 * p : 128 * p + 128] = both.astype(BF)
         partial = dot(attended[k, :, :128], proj0[k]) + dot(attended[k, :, 128:], proj1[k])
-        middle = hidden + total_wait(2 * k + 1, total_start(2 * k + 1, partial))
+        waiting = total_start(2 * k + 1, partial)
+        build(2 * k)
+        middle = hidden + total_wait(2 * k + 1, waiting)
         unit, inv = unit_of(middle)
         unit_f[k] = jnp.concatenate([unit, jnp.broadcast_to(inv, (2 * NF, 128))], axis=1)
         normed = (unit * gains[2 * k + 1 : 2 * k + 2]).astype(BF)
@@ -867,7 +870,9 @@
             act = (value * sig(value)).astype(BF)
             inner[k, :, 512 * side : 512 * side + 512] = act
             partial = partial + dot(act, down[k])
-        hidden = middle + total_wait(2 * k + 2, total_start(2 * k + 2, partial))
+        waiting = total_start(2 * k + 2, partial)
+        build(2 * k + 1)
+        hidden = middle + total_wait(2 * k + 2, waiting)
     tokens[...] = hidden.astype(BF)
 
     spread_copy.wait()
@@ -982,7 +987,9 @@
     grad_latent[:, 256:] = dot_nt(low, emb1[...])
     near_end(place_here, near_copy, upper, upper_near, upper_both)
     fold_end(lower_fold, lower, lower_got, lower_rows)
-    for one in near_copies:
+    for step in range(2 * layers, 4):
+        build(step)
+    for one in near_copies + forms:
         one.wait()
 
 
@@ -1006,9 +1013,10 @@
             S((t, 512)),
             S((4, NF, 512)),
             S((4, NF, 512)),
+            *[S(shape) for shape in BUILT],
         ),
         in_specs=VM(len(args)),
-        out_specs=tuple(VM(11)),
+        out_specs=tuple(VM(11) + [pl.BlockSpec(memory_space=pl.ANY)] * 8),
         scratch_shapes=[
             dma((2, 1)),
             V((4, NF, 1024)),
@@ -1036,6 +1044,8 @@
             V((layers, t, 1024), F32),
             V((layers, t, 1024)),
             V((2 * layers, 512), F32),
+            *[V(shape) for shape in BUILT],
+            dma((8,)),
         ],
         compiler_params=pltpu.CompilerParams(
             collective_id=3, has_side_effects=True, vmem_limit_bytes=56 * MIB
@@ -1047,9 +1057,9 @@
 
 def back_kernel(
     count, grad, latent, latent_near, chances, grad_embed, feat0, feat1, feat2, feat3,
-    lh0, lh1, dh0, dh1, flat, upper_half, lower_piece,
-    grad_feat, share, d_piece, l_both, upper_total, lower_half,
-    got, got_near, got_cross, keep, send, sent, logits_here, logits_near, own, other, other_got,
+    lh0, lh1, dh0, dh1, flat, lower_piece,
+    grad_feat, share, d_piece, l_both, lower_total,
+    lower_half, got, got_near, got_cross, keep, send, sent, logits_here, logits_near, own, other, other_got,
     d_both, d_slots, side_got, side_sum, cross_got, remote, here,
 ):
     place = Place(count)
@@ -1067,8 +1077,6 @@
                     grad.at[:, :, half_lanes(place, w)], dst.at[:, :, 128 * w : 128 * w + 128], device
                 )
             )
-    upper_own = sems.here(upper_half, rows_of(upper_total, near, upper_half.shape[0]))
-    upper_last = last_start(place, sems, upper_half, upper_total)
     lower_back = back_start(place, sems, lower_piece, lower_half)
     side_copy = sems.copy(flat.at[1 - core], side_got, place.sibling)
 
@@ -1122,6 +1130,10 @@
         d_both[256 * b : 256 * b + 256] = folded(0, b).T
     d_far = far_start(place, sems, d_both, d_slots)
     logits_copy.wait()
+    for one in lower_back:
+        one.wait()
+    lower_own = sems.here(lower_half, rows_of(lower_total, near, lower_half.shape[0]))
+    lower_last = last_start(place, sems, lower_half, lower_total)
     both_logits = jnp.concatenate([grad_logits, logits_near[...]], axis=0)
     in_fold = head_grad(1, (feat0, feat1), (feat2, feat3), both_logits)
     sends = []
@@ -1139,9 +1151,8 @@
         l_both[256 * b : 256 * b + 256] = folded(1, b)
     cross_copy.wait()
     share[...] = (side_sum[x].astype(F32) + cross_got[...].astype(F32)).astype(BF)
-    upper_own.wait()
-    upper_last.wait()
-    for one in lower_back + sends:
+    lower_own.wait()
+    for one in sends + [lower_last]:
         one.wait()
     grad_feat[...] = (keep[...].astype(F32) + sent[...].astype(F32)).astype(BF)
     far_end(place, d_far, d_both, d_slots, d_piece)
@@ -1151,9 +1162,9 @@
     dma = pltpu.SemaphoreType.DMA
     count = lax.axis_size("rows")
     half = count // 2
-    flat, upper_half, lower_piece = args[-3:]
+    flat, lower_piece = args[-2:]
     quarter = flat.shape[0] // 4
-    args = args[:-3] + (flat.reshape(2, 2, quarter, 256), upper_half, lower_piece)
+    args = args[:-2] + (flat.reshape(2, 2, quarter, 256), lower_piece)
     maps = (4, NF, 1024)
     narrow = (4, NF, 512)
     rows = (2048, 256)
@@ -1164,12 +1175,12 @@
             S((quarter, 256)),
             S((4096 // count, 256)),
             S(rows),
-            S((2 * upper_half.shape[0], 512)),
-            S((half * lower_piece.shape[0], 512)),
+            S((count * lower_piece.shape[0], 512)),
         ),
         in_specs=VM(len(args)),
-        out_specs=tuple(VM(4) + [pl.BlockSpec(memory_space=pl.ANY)] + VM(1)),
+        out_specs=tuple(VM(4) + [pl.BlockSpec(memory_space=pl.ANY)]),
         scratch_shapes=[
+            V((half * lower_piece.shape[0], 512)),
             V(maps),
             V(narrow),
             V(narrow),
@@ -1227,8 +1238,8 @@
 
 
 def enc_bwd_kernel(
-    count, xp, z1, z2, z3, z4, df, u2, u3, u4, b, dec, d_piece, l_both, t_half,
-    d_total, l_total, t_total, early, late, grad_out,
+    count, xp, z1, z2, z3, z4, df, u2, u3, u4, b, dec, d_piece, l_both,
+    d_total, l_total, early, late, grad_out,
     m1, m2, m3, s1, s2, s3, s4, yt, pk, dx, got, rows_out,
     l_slots, l_piece,
     e_fold, e_sum, e_cross, e_values, e_near, e_both, e_slots, e_piece,
@@ -1251,8 +1262,6 @@
             one.wait()
 
     l_far = far_start(place, sems, l_both, l_slots)
-    t_own = sems.here(t_half, home(t_total))
-    t_last = last_start(place, sems, t_half, t_total)
 
     zero_big(m1, 32)
     zero_big(m2, 16)
@@ -1366,15 +1375,14 @@
     f_cross_out.wait()
     f_side = sems.copy(late.at[core], late.at[core], place.sibling)
     waits(stores[-2:])
-    t_own.wait()
-    waits([t_last, e_side, f_side] + d_last + l_last)
+    waits([e_side, f_side] + d_last + l_last)
 
 
 def share_rows(rows, count):
     return rows + -rows % (16 * count)
 
 
-def enc_bwd(maps, dec, d_piece, l_both, t_half):
+def enc_bwd(maps, dec, d_piece, l_both):
     count = lax.axis_size("rows")
     half = count // 2
     dma = pltpu.SemaphoreType.DMA
@@ -1393,18 +1401,17 @@
             V((rows // count, 256)),
         ]
 
-    d_total, l_total, t_total, e_out, f_out, grad_out = pl.pallas_call(
+    d_total, l_total, e_out, f_out, grad_out = pl.pallas_call(
         functools.partial(enc_bwd_kernel, count),
         out_shape=(
             S((head, 256)),
             S((head, 256)),
-            S((2 * t_half.shape[0], 512)),
             S((2, 2, early, 256)),
             S((2, 2, late, 256)),
             S((3, 16, 64, 256), F32),
         ),
-        in_specs=VM(len(maps) + 4),
-        out_specs=tuple([any_spec] * 6),
+        in_specs=VM(len(maps) + 3),
+        out_specs=tuple([any_spec] * 5),
         scratch_shapes=[
             big(32),
             big(16),
@@ -1437,17 +1444,17 @@
         ),
         cost_estimate=estimate(110),
         name="encode_back",
-    )(*maps, dec, d_piece, l_both, t_half)
-    return d_total, l_total, t_total, e_out, f_out, jnp.transpose(grad_out, (3, 0, 1, 2))
+    )(*maps, dec, d_piece, l_both)
+    return d_total, l_total, e_out, f_out, jnp.transpose(grad_out, (3, 0, 1, 2))
 
 
 def unpack_kernel(
     layers, quarter, d_total, l_total, upper, lower, early, late,
-    latent_out, head_out, down_out, up_out, project_out, qkv_out, embed_out, rest_out, *outs,
+    latent_out, head_out, down_out, up_out, project_out, qkv_out, embed_out, place_out, gain_out, *outs,
 ):
     kernels, scratch, sems = outs[:8], outs[8:-1], outs[-1]
     (
-        latent_v, head_v, down_v, up_v, project_v, qkv_v, embed_v, rest_v, *kernel_v
+        latent_v, head_v, down_v, up_v, project_v, qkv_v, embed_v, place_v, gain_v, *kernel_v
     ) = scratch
     stores = []
 
@@ -1468,10 +1475,11 @@
                     first : first + 128, 128 * b : 128 * b + 128
                 ].astype(F32)
     embed_v[...] = lower[LAYER_ROWS : LAYER_ROWS + 256].astype(F32)
-    rest_v[...] = lower[LAYER_ROWS + 256 : LAYER_ROWS + 256 + NF + 16].astype(F32)
+    place_v[...] = lower[LAYER_ROWS + 256 : LAYER_ROWS + 256 + NF].astype(F32)
+    gain_v[...] = lower[LAYER_ROWS + 256 + NF : LAYER_ROWS + 256 + NF + 16].astype(F32)[: 2 * layers]
     for src, dst in (
         (down_v, down_out), (up_v, up_out), (project_v, project_out), (qkv_v, qkv_out),
-        (embed_v, embed_out), (rest_v, rest_out),
+        (embed_v, embed_out), (place_v, place_out), (gain_v, gain_out),
     ):
         store(src, dst)
     for b in range(16):
@@ -1526,7 +1534,8 @@
         (layers, 128, 512),
         (layers, 3, 512, 128),
         (256, 512),
-        (NF + 16, 512),
+        (NF, 512),
+        (2 * layers, 512),
         (48, 32),
         (512, 64),
         (1024, 128),
@@ -1585,23 +1594,14 @@
     x, core = strip // 2, strip % 2
     layers = qkv_weight.shape[0]
 
-    kernels = (
-        encode_one,
-        encode_two,
-        encode_three,
-        encode_four,
-        decode_one,
-        decode_two,
-        decode_three,
-        decode_four,
-    )
+    kernels = (encode_one, encode_two, encode_three, encode_four)
+    dec_rows = decoder_rows((decode_one, decode_two, decode_three, decode_four))
     qkv = jnp.transpose(qkv_weight, (0, 2, 1, 3))
     shards_here = (token_embed, qkv, out_weight, up_weight, down_weight)
-    pixels, enc_f, dec_f, head_in, head_out, theirs, hints = start(
+    pixels, enc_f, head_in, head_out, theirs, hints = start(
         frames, frame_cotangent, kernels, latent_head, decode_head, shards_here
     )
     enc_a, enc_b, enc_t, enc_u = enc_f[0], enc_f[1], enc_f[2:5], enc_f[5:8]
-    dec_a, dec_b, dec_t, dec_u = dec_f[0], dec_f[1], dec_f[2:5], dec_f[5:8]
     embed, qkv, project, widen, narrow = zip(shards_here, theirs)
     z1, z2, z3, z4, feat = enc_fwd(pixels, enc_a, *enc_t)
 
@@ -1623,7 +1623,7 @@
     )
     (
         tokens, latent, chances, decoded, upper, lower, grad_latent, feat_got,
-        latent_near, feat_near, got_near,
+        latent_near, feat_near, got_near, *dec_f,
     ) = middle(
         layers,
         feat,
@@ -1638,7 +1638,9 @@
         *project,
         *widen,
         *narrow,
+        *dec_rows,
     )
+    dec_a, dec_b, dec_t, dec_u = dec_f[0], dec_f[1], dec_f[2:5], dec_f[5:8]
     tokens = jnp.where(
         x == 0, tokens, jnp.concatenate([tokens[NF:], tokens[:NF]], axis=0)
     )
@@ -1649,25 +1651,20 @@
         jnp.concatenate([other_tokens, tokens]),
     )
 
-    recon_pairs, p3, p2, p1, upper, lower = dec_fwd(
-        decoded, dec_u[2], dec_u[1], dec_u[0], dec_b, upper, lower
+    g_decoded, dec_flat, recon, upper, _, lower = decode(
+        hints, decoded, dec_u[2], dec_u[1], dec_u[0], dec_b, dec_a, *dec_t, upper, lower
     )
-    recon_parts = blocks_around(recon_pairs, strip)
-    g_decoded, dec_flat, upper, lower = dec_bwd(
-        hints, decoded, p3, p2, p1, dec_a, *dec_t, upper, lower
+    recon = jnp.transpose(recon, (3, 0, 1, 2))
+    g_feat, dec_share, d_piece, l_both, lower = latents_back(
+        g_decoded, latent, latent_near, chances, grad_latent, feat, feat_got, feat_near, got_near,
+        *head_in, *head_out, dec_flat, lower,
     )
-    recon_parts, g_decoded = lax.optimization_barrier((recon_parts, g_decoded))
-    recon = frames_out_later(recon_parts)
-    g_feat, dec_share, d_piece, l_both, upper, lower = latents_back(
-        g_decoded, latent, latent_near, chances, grad_latent, feat, feat_got, feat_near, got_near,
-        *head_in, *head_out, dec_flat, upper, lower,
-    )
-
-    d_total, l_total, lower, early, late, frames_grad = enc_bwd(
-        (pixels, z1, z2, z3, z4, g_feat, *enc_u, enc_b), dec_share, d_piece, l_both, lower
+
+    d_total, l_total, early, late, frames_grad = enc_bwd(
+        (pixels, z1, z2, z3, z4, g_feat, *enc_u, enc_b), dec_share, d_piece, l_both
     )
     (
-        g_latent_head, g_decode_head, g_down, g_up, g_out, g_qkv, g_embed, g_rest,
+        g_latent_head, g_decode_head, g_down, g_up, g_out, g_qkv, g_embed, g_place, g_gain,
         d_four, d_three, d_two, d_one, e_one, e_two, e_three, e_four,
     ) = unpack(layers, dec_share.shape[0], d_total, l_total, upper, lower, early, late)
 
@@ -1687,8 +1684,8 @@
         of_output(e_four, 256),
         g_latent_head,
         g_embed,
-        g_rest[:NF],
-        g_rest[NF : NF + 2 * layers].reshape(norm_gains.shape),
+        g_place,
+        g_gain.reshape(norm_gains.shape),
         g_qkv.transpose(0, 2, 1, 3),
         g_out,
         g_up,

time: 443 us -> 435 us (0.982)
  Pallas kernels: 412 us -> 405 us
    pallas_call x3 -> x1, Pallas kernels: 103 us -> 21.1 us  [run(): pl.pallas_call(kernel, out_shape=outs, in_specs=VM(len(args)), out_specs=...]
    pallas_call x1, Pallas kernels: 2.13 us -> 76.8 us  [decode(): pl.pallas_call(functools.partial(dec_kernel, count), out_shape=(S((4, NF,...]
  transfers between devices with their start and end apart: 7 -> 4, of which waited for: 0 -> 1; matrix products, arithmetic and copies ran while one was open for 1% -> 2% of each run, Pallas kernels for 44% -> 26%
where the time goes in v6:
time: 435 us; the launch traced here: 427 us
  Pallas kernels  405 us (93%)
  local copies, waits for them, and re-layouts  14.2 us (3%)
    pallas_call x1, Pallas kernels, enc_bwd(): pl.pallas_call(functools.partial(enc_bwd_kernel, count), out_shape=(S((he...  118 us
    pallas_call x1, Pallas kernels, middle(): pl.pallas_call(functools.partial(middle_kernel, layers, count), out_shape...  91.6 us
    pallas_call x1, Pallas kernels, decode(): pl.pallas_call(functools.partial(dec_kernel, count), out_shape=(S((4, NF,...  76.8 us
    pallas_call x1, Pallas kernels, latents_back(): pl.pallas_call(functools.partial(back_kernel, count), out_shape=(S(maps),...  59.2 us
    pallas_call x1, Pallas kernels, start(): pl.pallas_call(start_kernel, out_shape=tuple((S(shape) for shape in shape...  26.1 us
    pallas_call x1, Pallas kernels, run(): pl.pallas_call(kernel, out_shape=outs, in_specs=VM(len(args)), out_specs=...  21.1 us
    pallas_call x1, Pallas kernels, unpack(): pl.pallas_call(functools.partial(unpack_kernel, layers, quarter), out_sha...  11.7 us
  transfers between devices with their start and end apart: 4, of which 1 were waited for; matrix products, arithmetic and copies ran while one was open for 2% of the time, Pallas kernels for 26%

profile of v6, /device:TPU:0, one launch (start us, length us, event | category | flops | bytes accessed | tf_op | source)
XLA Modules:
  0.0 427.4 jit_solution(2769641181796110899)
XLA Ops:
  0.7 0.7 convert_element_type.32
  1.4 0.1 tile.4
  1.4 1.0 convert_element_type.24.e1
  2.5 26.1 %start.1 = (bf16[34,64,384]{2,1,0:T(8,128)(2,1)}, bf16[1152,1024]{1,0:T(8,128)(2,1)}, bf16[3072,384]{1,0:T(8,128)(2,1)}, bf16[2048,256]{1,0:T(8,128)(2,1)}, bf16...) custom-call(bf16[3,16,64,256]{3,2,1,0:T(8,128)(2,1)} %bitcast.61, ...), custom_call_target="tpu_custom_call" | custom-call | flops 25300000768 | bytes 1048576 | tf_op jit(solution)/shard_map/start/pallas_call | solution.py:607
  28.6 0.7 collective-permute-start.1
  29.2 1.7 collective-permute-start.2
  30.9 0.6 reshape.122.gains
  31.6 0.1 and_convert_fusion
  31.7 0.1 tile.5
  31.8 1.0 convert_element_type.29.d4
  32.8 1.1 reshape.123.d1
  33.9 0.7 select_maximum_fusion.allow
  34.6 0.7 pad_maximum_fusion.cot
  35.3 21.1 %encode.1 = (bf16[32,64,1024]{2,1,0:T(8,128)(2,1)}, bf16[16,64,1024]{2,1,0:T(8,128)(2,1)}, bf16[8,64,1024]{2,1,0:T(8,128)(2,1)}, bf16[4,64,1024]{2,1,0:T(8,128)(2,1)}, bf16[4,64,1024]{2,1,0:T(8,128)(2,1)}) custom-call(bf16[34,64,384]{2,1,0:T(8,128)(2,1)} %get-tuple-element.98.xp, bf16[1152,1024]{1,0:T(8,128)(2,1)} %get-tuple-element.99.a, ...), custom_call_target="tpu_custom_call" | custom-call | flops 25300000768 | bytes 1048576 | tf_op jit(solution)/shard_map/encode/pallas_call | solution.py:243
  56.4 91.6 %middle.1 = (bf16[128,512]{1,0:T(8,128)(2,1)}, bf16[128,512]{1,0:T(8,128)(2,1)}, f32[128,512]{1,0:T(8,128)}, bf16[4,64,1024]{2,1,0:T(8,128)(2,1)}, bf16[768,512]...) custom-call(bf16[4,64,1024]{2,1,0:T(8,128)(2,1)} %get-tuple-element., ...), custom_call_target="tpu_custom_call" | custom-call | flops 96599998464 | bytes 1048576 | tf_op jit(solution)/shard_map/middle/pallas_call | solution.py:1002
  148.0 0.9 fusion
  148.9 0.9 maximum_select_fusion.1
  149.9 0.1 collective-permute-start
  150.0 1.3 collective-permute-done
  151.3 0.8 maximum_select_fusion
  152.1 0.7 copy-done.7
  152.8 0.1 copy-done.8
  152.9 0.1 copy-done.9
  153.1 76.8 %decode.1 = (bf16[4,64,1024]{2,1,0:T(8,128)(2,1)}, bf16[2816,256]{1,0:T(8,128)(2,1)}, bf16[3,16,64,256]{3,2,1,0:T(8,128)(2,1)}, bf16[1536,512]{1,0:T(8,128)(2,1)...) custom-call(bf16[8,64,384]{2,1,0:T(8,128)(2,1)} %get-tuple-element.114.c0, bf16[8,64,384]{2,1,0:T(8,128)(2,1)} %copy-done.7, ...), custom_call_target="tpu_custom_call" | custom-call | flops 74750001152 | bytes 1048576 | tf_op jit(solution)/shard_map/decode/pallas_call | solution.py:261
  229.9 59.2 %latents_back.1 = (bf16[4,64,1024]{2,1,0:T(8,128)(2,1)}, bf16[704,256]{1,0:T(8,128)(2,1)}, bf16[512,256]{1,0:T(8,128)(2,1)}, bf16[2048,256]{1,0:T(8,128)(2,1)}, bf16[1920,512]{1,0:T(8,128)(2,1)}) custom-call(bf16[4,64,1024]{2,1,0:T(8,128)(2,1)} %get-tuple-element.134.grad, bf16[128,512]{1,0:T(8,128)(2,1)} %get-tuple-element.135.latent, ...), custom_call_target="tpu_custom_call" | custom-call | flops 63250001920 | bytes 1048576 | tf_op jit(solution)/shard_map/latents_back/pallas_call | solution.py:1171
  289.1 117.9 %encode_back.1 = (bf16[4096,256]{1,0:T(8,128)(2,1)}, bf16[4096,256]{1,0:T(8,128)(2,1)}, bf16[2,2,1408,256]{3,2,1,0:T(8,128)(2,1)}, bf16[2,2,128,256]{3,2,1,0:T(8,128)(2,1)}, f32[3,16,64,256]{3,2,1,0:T(8,128)}) custom-call(bf16[34,64,384]{2,1,0:T(8,128)(2,1)} %get-tuple-element.98.xp, bf16[32,64,1024]{2,1,0:T(8,128)(2,1)} %get-tuple-element.130.z1, ...), custom_call_target="tpu_custom_call" | custom-call | flops 126500003840 | bytes 1048576 | tf_op jit(solution)/shard_map/encode_back/pallas_call | solution.py:1404
  407.1 11.7 %unpack.1 = (f32[4096,256]{1,0:T(8,128)}, f32[256,4096]{1,0:T(8,128)}, f32[2,512,512]{2,1,0:T(8,128)}, f32[2,512,512]{2,1,0:T(8,128)}, f32[2,128,512]{2,1,0:T(8,...) custom-call(bf16[4096,256]{1,0:T(8,128)(2,1)} %get-tuple-element.153, ...), custom_call_target="tpu_custom_call" | custom-call | flops 13799999488 | bytes 1048576 | tf_op jit(solution)/shard_map/unpack/pallas_call | solution.py:1548
  418.8 1.3 reshape.131
  420.1 3.0 reshape.132
  423.1 1.1 copy.43
  424.2 1.3 copy-done
  425.6 1.7 copy.44
  (26 shorter events, 0.1 us)
Async XLA Ops:
  2.5 28.4 %copy-start.5 = (f32[2,2,512]{2,1,0:T(2,128)S(1)}, f32[2,2,512]{2,1,0:T(2,128)}, u32[]{:S(2)}) copy-start(f32[2,2,512]{2,1,0:T(2,128)} %param.30) | copy-start | bytes 24580
  2.5 29.1 %copy-start.4 = (bf16[3,32,4,4]{1,3,2,0:T(4,128)(2,1)S(1)}, bf16[3,32,4,4]{1,3,2,0:T(4,128)(2,1)}, u32[]{:S(2)}) copy-start(bf16[3,32,4,4]{1,3,2,0:T(4,128)(2,1)} %param.39) | copy-start | bytes 9220
  2.5 29.1 %copy-start.6 = (s32[4,64]{1,0:T(4,128)S(1)}, s32[4,64]{1,0:T(4,128)}, u32[]{:S(2)}) copy-start(s32[4,64]{1,0:T(4,128)} %param.22) | copy-start | bytes 3076
  28.5 4.3 %copy-start.2 = (bf16[128,256,4,4]{1,3,2,0:T(4,128)(2,1)S(1)}, bf16[128,256,4,4]{1,3,2,0:T(4,128)(2,1)}, u32[]{:S(2)}) copy-start(bf16[128,256,4,4]{1,3,2,0:T(4,128)(2,1)} %param.36) | copy-start | bytes 3145732
  28.6 123.5 %collective-permute-start.1 = (bf16[8,64,384]{2,1,0:T(8,128)(2,1)}, bf16[8,64,384]{2,1,0:T(8,128)(2,1)S(1)}, u32[]{:S(2)}, u32[]{:S(2)}) collective-permute-start(bf16[8,64,384]{2,1,0:T(8,128)(2,1)} %get-tuple-element.115), channel_id=1, source_target_pairs={{0,1},{1,2},{2,3},{3,0},{4,5},{5,6},{6,7},{7,4},{8,9},{9,10},{10,1... | collective-permute-start | bytes 1179656 | tf_op jit(solution)/shard_map/ppermute | solution.py:669
  29.2 122.8 %collective-permute-start.2 = (bf16[8,64,384]{2,1,0:T(8,128)(2,1)}, bf16[8,64,384]{2,1,0:T(8,128)(2,1)S(1)}, u32[]{:S(2)}, u32[]{:S(2)}) collective-permute-start(bf16[8,64,384]{2,1,0:T(8,128)(2,1)} %get-tuple-element.116), channel_id=1, source_target_pairs={{0,2},{1,3},{2,0},{3,1},{4,6},{5,7},{6,4},{7,5},{8,10},{9,11},{10,... | collective-permute-start | bytes 1179656 | tf_op jit(solution)/shard_map/ppermute | solution.py:669
  30.9 121.2 %collective-permute-start.3 = (bf16[8,64,384]{2,1,0:T(8,128)(2,1)}, bf16[8,64,384]{2,1,0:T(8,128)(2,1)S(1)}, u32[]{:S(2)}, u32[]{:S(2)}) collective-permute-start(bf16[8,64,384]{2,1,0:T(8,128)(2,1)} %get-tuple-element.117), channel_id=1, source_target_pairs={{0,3},{1,0},{2,1},{3,2},{4,7},{5,4},{6,5},{7,6},{8,11},{9,8},{10,9... | collective-permute-start | bytes 1179656 | tf_op jit(solution)/shard_map/ppermute | solution.py:669
  31.7 2.9 copy-start.3
  149.9 1.4 collective-permute-start
  152.1 0.7 copy-start.7
  152.1 0.9 copy-start.8
  152.1 1.0 copy-start.9
  420.1 3.0 copy-start.1
  423.1 2.5 copy-start

commit v7 on v6

--- a/solution.py
+++ b/solution.py
@@ -158,9 +158,9 @@
             if m is None: feat[pl.ds(i0,rows),:,256*q:256*q+256]=val.reshape(rows,NF,256)
             else: put_big(m,half0,rows,q,val)
         return emit
-    outer_down(xp,a,keep(z1,m1))
-    down(m1,t2,16,4,keep(z2,m2))
-    down(m2,t3,8,4,keep(z3,m3))
+    outer_down(xp,a,keep(z1,m1),8)
+    down(m1,t2,16,8,keep(z2,m2))
+    down(m2,t3,8,8,keep(z3,m3))
     down(m3,t4,4,4,keep(z4,None))
 
 def dec_kernel(count,c0,c1,c2,c3,dec,u4,u3,u2,b,a,t2,t3,t4,upper_both,lower,
@@ -1058,8 +1058,8 @@
 def back_kernel(
     count, grad, latent, latent_near, chances, grad_embed, feat0, feat1, feat2, feat3,
     lh0, lh1, dh0, dh1, flat, lower_piece,
-    grad_feat, share, d_piece, l_both, lower_total,
-    lower_half, got, got_near, got_cross, keep, send, sent, logits_here, logits_near, own, other, other_got,
+    grad_feat, share, d_piece, l_both, lower_half,
+    got, got_near, got_cross, keep, send, sent, logits_here, logits_near, own, other, other_got,
     d_both, d_slots, side_got, side_sum, cross_got, remote, here,
 ):
     place = Place(count)
@@ -1130,10 +1130,6 @@
         d_both[256 * b : 256 * b + 256] = folded(0, b).T
     d_far = far_start(place, sems, d_both, d_slots)
     logits_copy.wait()
-    for one in lower_back:
-        one.wait()
-    lower_own = sems.here(lower_half, rows_of(lower_total, near, lower_half.shape[0]))
-    lower_last = last_start(place, sems, lower_half, lower_total)
     both_logits = jnp.concatenate([grad_logits, logits_near[...]], axis=0)
     in_fold = head_grad(1, (feat0, feat1), (feat2, feat3), both_logits)
     sends = []
@@ -1151,8 +1147,7 @@
         l_both[256 * b : 256 * b + 256] = folded(1, b)
     cross_copy.wait()
     share[...] = (side_sum[x].astype(F32) + cross_got[...].astype(F32)).astype(BF)
-    lower_own.wait()
-    for one in sends + [lower_last]:
+    for one in sends + lower_back:
         one.wait()
     grad_feat[...] = (keep[...].astype(F32) + sent[...].astype(F32)).astype(BF)
     far_end(place, d_far, d_both, d_slots, d_piece)
@@ -1175,12 +1170,11 @@
             S((quarter, 256)),
             S((4096 // count, 256)),
             S(rows),
-            S((count * lower_piece.shape[0], 512)),
+            S((half * lower_piece.shape[0], 512)),
         ),
         in_specs=VM(len(args)),
-        out_specs=tuple(VM(4) + [pl.BlockSpec(memory_space=pl.ANY)]),
+        out_specs=tuple(VM(5)),
         scratch_shapes=[
-            V((half * lower_piece.shape[0], 512)),
             V(maps),
             V(narrow),
             V(narrow),
@@ -1238,8 +1232,8 @@
 
 
 def enc_bwd_kernel(
-    count, xp, z1, z2, z3, z4, df, u2, u3, u4, b, dec, d_piece, l_both,
-    d_total, l_total, early, late, grad_out,
+    count, xp, z1, z2, z3, z4, df, u2, u3, u4, b, dec, d_piece, l_both, t_half,
+    d_total, l_total, t_total, early, late, grad_out,
     m1, m2, m3, s1, s2, s3, s4, yt, pk, dx, got, rows_out,
     l_slots, l_piece,
     e_fold, e_sum, e_cross, e_values, e_near, e_both, e_slots, e_piece,
@@ -1262,6 +1256,8 @@
             one.wait()
 
     l_far = far_start(place, sems, l_both, l_slots)
+    t_own = sems.here(t_half, home(t_total))
+    t_last = last_start(place, sems, t_half, t_total)
 
     zero_big(m1, 32)
     zero_big(m2, 16)
@@ -1375,14 +1371,15 @@
     f_cross_out.wait()
     f_side = sems.copy(late.at[core], late.at[core], place.sibling)
     waits(stores[-2:])
-    waits([e_side, f_side] + d_last + l_last)
+    t_own.wait()
+    waits([t_last, e_side, f_side] + d_last + l_last)
 
 
 def share_rows(rows, count):
     return rows + -rows % (16 * count)
 
 
-def enc_bwd(maps, dec, d_piece, l_both):
+def enc_bwd(maps, dec, d_piece, l_both, t_half):
     count = lax.axis_size("rows")
     half = count // 2
     dma = pltpu.SemaphoreType.DMA
@@ -1401,17 +1398,18 @@
             V((rows // count, 256)),
         ]
 
-    d_total, l_total, e_out, f_out, grad_out = pl.pallas_call(
+    d_total, l_total, t_total, e_out, f_out, grad_out = pl.pallas_call(
         functools.partial(enc_bwd_kernel, count),
         out_shape=(
             S((head, 256)),
             S((head, 256)),
+            S((2 * t_half.shape[0], 512)),
             S((2, 2, early, 256)),
             S((2, 2, late, 256)),
             S((3, 16, 64, 256), F32),
         ),
-        in_specs=VM(len(maps) + 3),
-        out_specs=tuple([any_spec] * 5),
+        in_specs=VM(len(maps) + 4),
+        out_specs=tuple([any_spec] * 6),
         scratch_shapes=[
             big(32),
             big(16),
@@ -1444,8 +1442,8 @@
         ),
         cost_estimate=estimate(110),
         name="encode_back",
-    )(*maps, dec, d_piece, l_both)
-    return d_total, l_total, e_out, f_out, jnp.transpose(grad_out, (3, 0, 1, 2))
+    )(*maps, dec, d_piece, l_both, t_half)
+    return d_total, l_total, t_total, e_out, f_out, jnp.transpose(grad_out, (3, 0, 1, 2))
 
 
 def unpack_kernel(
@@ -1660,8 +1658,8 @@
         *head_in, *head_out, dec_flat, lower,
     )
 
-    d_total, l_total, early, late, frames_grad = enc_bwd(
-        (pixels, z1, z2, z3, z4, g_feat, *enc_u, enc_b), dec_share, d_piece, l_both
+    d_total, l_total, lower, early, late, frames_grad = enc_bwd(
+        (pixels, z1, z2, z3, z4, g_feat, *enc_u, enc_b), dec_share, d_piece, l_both, lower
     )
     (
         g_latent_head, g_decode_head, g_down, g_up, g_out, g_qkv, g_embed, g_place, g_gain,

time: 435 us -> 434 us (level)
  no operation moved by 1% of the time
where the time goes in v7:
time: 434 us; the launch traced here: 426 us
  Pallas kernels  404 us (93%)
  local copies, waits for them, and re-layouts  14.2 us (3%)
    pallas_call x1, Pallas kernels, enc_bwd(): pl.pallas_call(functools.partial(enc_bwd_kernel, count), out_shape=(S((he...  122 us
    pallas_call x1, Pallas kernels, middle(): pl.pallas_call(functools.partial(middle_kernel, layers, count), out_shape...  91.7 us
    pallas_call x1, Pallas kernels, decode(): pl.pallas_call(functools.partial(dec_kernel, count), out_shape=(S((4, NF,...  76.8 us
    pallas_call x1, Pallas kernels, latents_back(): pl.pallas_call(functools.partial(back_kernel, count), out_shape=(S(maps),...  55.9 us
    pallas_call x1, Pallas kernels, start(): pl.pallas_call(start_kernel, out_shape=tuple((S(shape) for shape in shape...  26.1 us
    pallas_call x1, Pallas kernels, run(): pl.pallas_call(kernel, out_shape=outs, in_specs=VM(len(args)), out_specs=...  19.5 us
    pallas_call x1, Pallas kernels, unpack(): pl.pallas_call(functools.partial(unpack_kernel, layers, quarter), out_sha...  11.7 us
  transfers between devices with their start and end apart: 4, of which 1 were waited for; matrix products, arithmetic and copies ran while one was open for 2% of the time, Pallas kernels for 26%

profile of v7, /device:TPU:0, one launch (start us, length us, event | category | flops | bytes accessed | tf_op | source)
XLA Modules:
  0.0 426.5 jit_solution(10791502236922827131)
XLA Ops:
  0.7 0.7 convert_element_type.32
  1.4 0.1 tile.4
  1.4 1.0 convert_element_type.24.e1
  2.5 26.1 %start.1 = (bf16[34,64,384]{2,1,0:T(8,128)(2,1)}, bf16[1152,1024]{1,0:T(8,128)(2,1)}, bf16[3072,384]{1,0:T(8,128)(2,1)}, bf16[2048,256]{1,0:T(8,128)(2,1)}, bf16...) custom-call(bf16[3,16,64,256]{3,2,1,0:T(8,128)(2,1)} %bitcast.61, ...), custom_call_target="tpu_custom_call" | custom-call | flops 25300000768 | bytes 1048576 | tf_op jit(solution)/shard_map/start/pallas_call | solution.py:607
  28.6 0.7 collective-permute-start.1
  29.2 1.7 collective-permute-start.2
  30.9 0.6 reshape.122.gains
  31.6 0.1 and_convert_fusion
  31.7 0.1 tile.5
  31.8 1.0 convert_element_type.29.d4
  32.8 1.1 reshape.123.d1
  33.9 0.7 select_maximum_fusion.allow
  34.6 0.7 pad_maximum_fusion.cot
  35.3 19.5 %encode.1 = (bf16[32,64,1024]{2,1,0:T(8,128)(2,1)}, bf16[16,64,1024]{2,1,0:T(8,128)(2,1)}, bf16[8,64,1024]{2,1,0:T(8,128)(2,1)}, bf16[4,64,1024]{2,1,0:T(8,128)(2,1)}, bf16[4,64,1024]{2,1,0:T(8,128)(2,1)}) custom-call(bf16[34,64,384]{2,1,0:T(8,128)(2,1)} %get-tuple-element.99.xp, bf16[1152,1024]{1,0:T(8,128)(2,1)} %get-tuple-element.100.a, ...), custom_call_target="tpu_custom_call" | custom-call | flops 25300000768 | bytes 1048576 | tf_op jit(solution)/shard_map/encode/pallas_call | solution.py:243
  54.8 91.7 %middle.1 = (bf16[128,512]{1,0:T(8,128)(2,1)}, bf16[128,512]{1,0:T(8,128)(2,1)}, f32[128,512]{1,0:T(8,128)}, bf16[4,64,1024]{2,1,0:T(8,128)(2,1)}, bf16[768,512]...) custom-call(bf16[4,64,1024]{2,1,0:T(8,128)(2,1)} %get-tuple-element., ...), custom_call_target="tpu_custom_call" | custom-call | flops 96599998464 | bytes 1048576 | tf_op jit(solution)/shard_map/middle/pallas_call | solution.py:1002
  146.5 0.9 fusion
  147.4 0.9 maximum_select_fusion.1
  148.3 0.1 collective-permute-start
  148.4 1.3 collective-permute-done
  149.8 0.8 maximum_select_fusion
  150.6 0.7 copy-done.7
  151.3 0.1 copy-done.8
  151.4 0.1 copy-done.9
  151.5 76.8 %decode.1 = (bf16[4,64,1024]{2,1,0:T(8,128)(2,1)}, bf16[2816,256]{1,0:T(8,128)(2,1)}, bf16[3,16,64,256]{3,2,1,0:T(8,128)(2,1)}, bf16[1536,512]{1,0:T(8,128)(2,1)...) custom-call(bf16[8,64,384]{2,1,0:T(8,128)(2,1)} %get-tuple-element.115.c0, bf16[8,64,384]{2,1,0:T(8,128)(2,1)} %copy-done.7, ...), custom_call_target="tpu_custom_call" | custom-call | flops 74750001152 | bytes 1048576 | tf_op jit(solution)/shard_map/decode/pallas_call | solution.py:261
  228.3 55.9 %latents_back.1 = (bf16[4,64,1024]{2,1,0:T(8,128)(2,1)}, bf16[704,256]{1,0:T(8,128)(2,1)}, bf16[512,256]{1,0:T(8,128)(2,1)}, bf16[2048,256]{1,0:T(8,128)(2,1)}, bf16[960,512]{1,0:T(8,128)(2,1)}) custom-call(bf16[4,64,1024]{2,1,0:T(8,128)(2,1)} %get-tuple-element.135.grad, bf16[128,512]{1,0:T(8,128)(2,1)} %get-tuple-element.136.latent, ...), custom_call_target="tpu_custom_call" | custom-call | flops 63250001920 | bytes 1048576 | tf_op jit(solution)/shard_map/latents_back/pallas_call | solution.py:1166
  284.2 121.9 %encode_back.1 = (bf16[4096,256]{1,0:T(8,128)(2,1)}, bf16[4096,256]{1,0:T(8,128)(2,1)}, bf16[1920,512]{1,0:T(8,128)(2,1)}, bf16[2,2,1408,256]{3,2,1,0:T(8,128)(2...) custom-call(bf16[34,64,384]{2,1,0:T(8,128)(2,1)} %get-tuple-element.99.xp, ...), custom_call_target="tpu_custom_call" | custom-call | flops 126500003840 | bytes 1048576 | tf_op jit(solution)/shard_map/encode_back/pallas_call | solution.py:1401
  406.1 11.7 %unpack.1 = (f32[4096,256]{1,0:T(8,128)}, f32[256,4096]{1,0:T(8,128)}, f32[2,512,512]{2,1,0:T(8,128)}, f32[2,512,512]{2,1,0:T(8,128)}, f32[2,128,512]{2,1,0:T(8,...) custom-call(bf16[4096,256]{1,0:T(8,128)(2,1)} %get-tuple-element.155, ...), custom_call_target="tpu_custom_call" | custom-call | flops 13799999488 | bytes 1048576 | tf_op jit(solution)/shard_map/unpack/pallas_call | solution.py:1546
  417.8 1.3 reshape.131
  419.1 3.0 reshape.132
  422.1 1.1 copy.43
  423.3 1.3 copy-done
  424.6 1.7 copy.44
  (26 shorter events, 0.1 us)
Async XLA Ops:
  2.5 28.4 %copy-start.5 = (f32[2,2,512]{2,1,0:T(2,128)S(1)}, f32[2,2,512]{2,1,0:T(2,128)}, u32[]{:S(2)}) copy-start(f32[2,2,512]{2,1,0:T(2,128)} %param.30) | copy-start | bytes 24580
  2.5 29.1 %copy-start.4 = (bf16[3,32,4,4]{1,3,2,0:T(4,128)(2,1)S(1)}, bf16[3,32,4,4]{1,3,2,0:T(4,128)(2,1)}, u32[]{:S(2)}) copy-start(bf16[3,32,4,4]{1,3,2,0:T(4,128)(2,1)} %param.39) | copy-start | bytes 9220
  2.5 29.1 %copy-start.6 = (s32[4,64]{1,0:T(4,128)S(1)}, s32[4,64]{1,0:T(4,128)}, u32[]{:S(2)}) copy-start(s32[4,64]{1,0:T(4,128)} %param.22) | copy-start | bytes 3076
  28.5 4.3 %copy-start.2 = (bf16[128,256,4,4]{1,3,2,0:T(4,128)(2,1)S(1)}, bf16[128,256,4,4]{1,3,2,0:T(4,128)(2,1)}, u32[]{:S(2)}) copy-start(bf16[128,256,4,4]{1,3,2,0:T(4,128)(2,1)} %param.36) | copy-start | bytes 3145732
  28.6 122.0 %collective-permute-start.1 = (bf16[8,64,384]{2,1,0:T(8,128)(2,1)}, bf16[8,64,384]{2,1,0:T(8,128)(2,1)S(1)}, u32[]{:S(2)}, u32[]{:S(2)}) collective-permute-start(bf16[8,64,384]{2,1,0:T(8,128)(2,1)} %get-tuple-element.116), channel_id=1, source_target_pairs={{0,1},{1,2},{2,3},{3,0},{4,5},{5,6},{6,7},{7,4},{8,9},{9,10},{10,1... | collective-permute-start | bytes 1179656 | tf_op jit(solution)/shard_map/ppermute | solution.py:669
  29.2 121.3 %collective-permute-start.2 = (bf16[8,64,384]{2,1,0:T(8,128)(2,1)}, bf16[8,64,384]{2,1,0:T(8,128)(2,1)S(1)}, u32[]{:S(2)}, u32[]{:S(2)}) collective-permute-start(bf16[8,64,384]{2,1,0:T(8,128)(2,1)} %get-tuple-element.117), channel_id=1, source_target_pairs={{0,2},{1,3},{2,0},{3,1},{4,6},{5,7},{6,4},{7,5},{8,10},{9,11},{10,... | collective-permute-start | bytes 1179656 | tf_op jit(solution)/shard_map/ppermute | solution.py:669
  30.9 119.6 %collective-permute-start.3 = (bf16[8,64,384]{2,1,0:T(8,128)(2,1)}, bf16[8,64,384]{2,1,0:T(8,128)(2,1)S(1)}, u32[]{:S(2)}, u32[]{:S(2)}) collective-permute-start(bf16[8,64,384]{2,1,0:T(8,128)(2,1)} %get-tuple-element.118), channel_id=1, source_target_pairs={{0,3},{1,0},{2,1},{3,2},{4,7},{5,4},{6,5},{7,6},{8,11},{9,8},{10,9... | collective-permute-start | bytes 1179656 | tf_op jit(solution)/shard_map/ppermute | solution.py:669
  31.7 2.9 copy-start.3
  148.3 1.4 collective-permute-start
  150.5 0.7 copy-start.7
  150.5 0.9 copy-start.8
  150.6 1.0 copy-start.9
  419.1 3.0 copy-start.1
  422.1 2.5 copy-start
